TPU v7x, 32 devices: a whole 2x2x4 slice. The times are simulated.
32 devices in a mesh: dp: 16 (over z, x, core), mp: 2 (over y).
Axes of the slice: x: 2, y: 2, z: 4, core: 2. Of those that a mesh axis runs over, the one named last changes fastest.
Arguments:
- tokens: bfloat16 [16384, 512], P(('dp', 'mp')), may hold values from -6 to 6
- pos_table: bfloat16 [512, 512], replicated, may hold values from -3 to 3
- qkv_weight: bfloat16 [512, 3, 512], P(None, None, 'mp'), may hold values from -0.25 to 0.25
- out_weight: bfloat16 [512, 512], P('mp'), may hold values from -2 to 2
- out_bias: bfloat16 [512], replicated, may hold values from -3 to 3
- norm1_gain: bfloat16 [512], replicated, may hold values from 0.5 to 1.5
- norm1_shift: bfloat16 [512], replicated, may hold values from -2 to 2
- up_weight: bfloat16 [512, 2048], P(None, 'mp'), may hold values from -0.25 to 0.25
- up_bias: bfloat16 [2048], P('mp'), may hold values from -3 to 3
- down_weight: bfloat16 [2048, 512], P('mp'), may hold values from -0.125 to 0.125
- down_bias: bfloat16 [512], replicated, may hold values from -3 to 3
- norm2_gain: bfloat16 [512], replicated, may hold values from 0.5 to 1.5
- norm2_shift: bfloat16 [512], replicated, may hold values from -2 to 2
- window: int32 [16], P('dp'), may hold values from 256 to 512, as said below
- cotangent: bfloat16 [16384, 512], P(('dp', 'mp')), may hold values from -6 to 6
Outputs:
- layer_out: bfloat16 [16384, 512], P(('dp', 'mp'))
- grad_tokens: bfloat16 [16384, 512], P(('dp', 'mp'))
- grad_pos_table: float32 [512, 512], replicated
- grad_qkv_weight: float32 [512, 3, 512], P(None, None, 'mp')
- grad_out_weight: float32 [512, 512], P('mp')
- grad_out_bias: float32 [512], replicated
- grad_norm1_gain: float32 [512], replicated
- grad_norm1_shift: float32 [512], replicated
- grad_up_weight: float32 [512, 2048], P(None, 'mp')
- grad_up_bias: float32 [2048], P('mp')
- grad_down_weight: float32 [2048, 512], P('mp')
- grad_down_bias: float32 [512], replicated
- grad_norm2_gain: float32 [512], replicated
- grad_norm2_shift: float32 [512], replicated
Inputs may be any that keep to these rules, and one draw needn't show every extreme that they name: `window`: every entry is 256 or 512, each for exactly half of the rows.
All inputs are finite; a program needn't handle non-finite values.
Results may differ from a plain program's by a relative error of at most 0.019.
The roundings to bfloat16 on the way count: a program that leaves them out, or rounds other values in their place, can miss the bound.
Values may be sent and summed in bfloat16 or wider, within the bound.
No kernel may reach another device: no remote copies, remote signals or barrier semaphores. Data moves between devices by JAX's collectives and lax.ppermute only.
A program may use at most 128 MiB of HBM per device.

v0:
```python
import jax
import jax.numpy as jnp
from jax import lax
from jax.sharding import PartitionSpec as P

HD = 64
W_SHORT = 256
W_LONG = 512
ROW = 1024


epsilon = 1e-05


def layer_norm(values_in, norm_gain, norm_shift):
    average = jnp.mean(values_in, axis=-1, keepdims=True)
    centred = values_in - average
    variance = jnp.mean(centred * centred, axis=-1, keepdims=True)
    return centred * lax.rsqrt(variance + epsilon) * norm_gain + norm_shift


def smooth_act(values_in):
    return jax.nn.gelu(values_in, approximate=False)


def smooth_back(pre_values, grad_values):
    return jax.vjp(smooth_act, pre_values)[1](grad_values)[0]


def block_windows(window, first_token, blocks):
    starts = first_token + jnp.arange(blocks, dtype=jnp.int32) * W_LONG
    picked = (starts // ROW)[:, None] == jnp.arange(window.shape[0], dtype=jnp.int32)[None, :]
    return jnp.sum(jnp.where(picked, window[None, :], 0), axis=1)


def table_rows(table_full, window_sizes):
    short_rows = jnp.concatenate([table_full[:W_SHORT], table_full[:W_SHORT]], axis=0)
    chosen = jnp.where((window_sizes == W_LONG)[:, None, None], table_full[None], short_rows[None])
    return chosen.reshape(-1, table_full.shape[1])


def table_grad(grad_rows, window_sizes):
    block_grads = grad_rows.reshape(window_sizes.shape[0], W_LONG, grad_rows.shape[1])
    folded = block_grads[:, :W_SHORT] + block_grads[:, W_SHORT:]
    folded = jnp.concatenate([folded, jnp.zeros_like(folded)], axis=1)
    chosen = jnp.where((window_sizes == W_LONG)[:, None, None], block_grads, folded)
    return jnp.sum(chosen, axis=0)


def causal_mask(window_size):
    offsets = jnp.arange(W_LONG, dtype=jnp.int32)
    causal = offsets[:, None] >= offsets[None, :]
    same_window = offsets[:, None] // window_size == offsets[None, :] // window_size
    return causal & same_window


def block_scores(query_block, key_block, window_size):
    allowed = causal_mask(window_size)[None]
    scores = jnp.einsum(
        "qhe,khe->hqk", query_block, key_block, preferred_element_type=jnp.float32
    ) * HD ** (-0.5)
    diagonal = jnp.sum(
        jnp.where(jnp.eye(W_LONG, dtype=jnp.bool_)[None], scores, 0.0), axis=-1, keepdims=True
    )
    return (jnp.where(allowed, scores, diagonal), allowed)


def project_heads(rows_in, qkv_weight):
    return jnp.einsum(
        "sd,dcf->scf", rows_in, qkv_weight, preferred_element_type=jnp.float32
    ).astype(jnp.bfloat16)


def split_heads(mixed):
    blocks = mixed.shape[0] // W_LONG
    head_count = mixed.shape[2] // HD
    shaped = mixed.reshape(blocks, W_LONG, 3, head_count, HD)
    return (shaped[:, :, 0], shaped[:, :, 1], shaped[:, :, 2])


def attend_forward(mixed, window_sizes):
    query_rows, key_rows, value_rows = split_heads(mixed)

    def one_block(block_items):
        query_block, key_block, value_block, window_size = block_items
        scores, allowed = block_scores(query_block, key_block, window_size)
        top_score = jnp.max(scores, axis=-1, keepdims=True)
        weights = jnp.where(allowed, jnp.exp(scores - top_score), 0.0)
        log_total = jnp.log(jnp.sum(weights, axis=-1, keepdims=True)) + top_score
        probs = jnp.where(allowed, jnp.exp(scores - log_total), 0.0).astype(jnp.bfloat16)
        context = jnp.einsum("hqk,khe->qhe", probs, value_block, preferred_element_type=jnp.float32)
        return (context.astype(jnp.bfloat16), log_total[..., 0])

    context, log_totals = lax.map(one_block, (query_rows, key_rows, value_rows, window_sizes))
    return (context.reshape(mixed.shape[0], mixed.shape[2]), log_totals)


def attend_backward(mixed, grad_context, log_totals, window_sizes):
    query_rows, key_rows, value_rows = split_heads(mixed)
    grad_rows = grad_context.reshape(query_rows.shape)

    def one_block(block_items):
        query_block, key_block, value_block, grad_block, log_block, window_size = block_items
        scores, allowed = block_scores(query_block, key_block, window_size)
        probs = jnp.where(allowed, jnp.exp(scores - log_block[..., None]), 0.0)
        grad_probs = jnp.einsum(
            "qhe,khe->hqk", grad_block, value_block, preferred_element_type=jnp.float32
        )
        inner_sum = jnp.sum(probs * grad_probs, axis=-1, keepdims=True)
        grad_scores = (probs * (grad_probs - inner_sum)).astype(jnp.bfloat16)
        grad_query = jnp.einsum(
            "hqk,khe->qhe", grad_scores, key_block, preferred_element_type=jnp.float32
        ) * HD ** (-0.5)
        grad_key = jnp.einsum(
            "hqk,qhe->khe", grad_scores, query_block, preferred_element_type=jnp.float32
        ) * HD ** (-0.5)
        grad_value = jnp.einsum(
            "hqk,qhe->khe",
            probs.astype(jnp.bfloat16),
            grad_block,
            preferred_element_type=jnp.float32,
        )
        return jnp.stack([grad_query, grad_key, grad_value], axis=1).astype(jnp.bfloat16)

    grad_blocks = lax.map(
        one_block, (query_rows, key_rows, value_rows, grad_rows, log_totals, window_sizes)
    )
    return grad_blocks.reshape(mixed.shape)


def ffn_forward(normed_rows, up_weight, bias_up):
    pre_act = jnp.dot(normed_rows, up_weight, preferred_element_type=jnp.float32) + bias_up
    return (pre_act, smooth_act(pre_act).astype(jnp.bfloat16))


def per_device(
    tokens,
    pos_table,
    qkv_weight,
    out_weight,
    out_bias,
    norm1_gain,
    norm1_shift,
    up_weight,
    up_bias,
    down_weight,
    down_bias,
    norm2_gain,
    norm2_shift,
    window,
    cotangent,
):
    tok_rows = tokens.shape[0]
    first_token = lax.axis_index("mp") * tok_rows
    local_wins = block_windows(window, first_token, tok_rows // W_LONG)
    hidden_in = tokens.astype(jnp.float32) + table_rows(pos_table.astype(jnp.float32), local_wins)
    hidden_low = hidden_in.astype(jnp.bfloat16)
    bias_out = out_bias.astype(jnp.float32)
    bias_down = down_bias.astype(jnp.float32)
    gain_one = norm1_gain.astype(jnp.float32)
    shift_one = norm1_shift.astype(jnp.float32)
    gain_two = norm2_gain.astype(jnp.float32)
    shift_two = norm2_shift.astype(jnp.float32)
    grad_final = cotangent.astype(jnp.float32)
    bias_up = up_bias.astype(jnp.float32)
    all_wins = block_windows(window, jnp.int32(0), tok_rows * lax.axis_size("mp") // W_LONG)
    gathered = lax.all_gather(hidden_low, "mp", axis=0, tiled=True)
    mixed = project_heads(gathered, qkv_weight)
    context, log_totals = attend_forward(mixed, all_wins)
    resid1 = (
        hidden_in
        + lax.psum_scatter(
            jnp.dot(context, out_weight, preferred_element_type=jnp.float32),
            "mp",
            scatter_dimension=0,
            tiled=True,
        )
        + bias_out
    )
    normed1, norm1_back = jax.vjp(layer_norm, resid1, gain_one, shift_one)
    normed_low = normed1.astype(jnp.bfloat16)
    ffn_inputs = lax.all_gather(normed_low, "mp", axis=0, tiled=True)
    pre_act, act_low = ffn_forward(ffn_inputs, up_weight, bias_up)
    resid2 = (
        normed1
        + lax.psum_scatter(
            jnp.dot(act_low, down_weight, preferred_element_type=jnp.float32),
            "mp",
            scatter_dimension=0,
            tiled=True,
        )
        + bias_down
    )
    layer_out, norm2_back = jax.vjp(layer_norm, resid2, gain_two, shift_two)
    grad_resid2, grad_gain_two, grad_shift_two = norm2_back(grad_final)
    grad_ffn_low = grad_resid2.astype(jnp.bfloat16)
    ffn_again, grad_ffn_all = (
        lax.all_gather(normed_low, "mp", axis=0, tiled=True),
        lax.all_gather(grad_ffn_low, "mp", axis=0, tiled=True),
    )
    pre_again, act_again = ffn_forward(ffn_again, up_weight, bias_up)
    grad_down_part = jnp.einsum(
        "sf,sd->fd", act_again, grad_ffn_all, preferred_element_type=jnp.float32
    )
    grad_act = jnp.einsum(
        "sd,fd->sf", grad_ffn_all, down_weight, preferred_element_type=jnp.float32
    )
    grad_pre = smooth_back(pre_again, grad_act).astype(jnp.bfloat16)
    grad_up_part = jnp.einsum("sd,sf->df", ffn_again, grad_pre, preferred_element_type=jnp.float32)
    grad_up_bias_part = jnp.sum(grad_pre, axis=0, dtype=jnp.float32)

    def normed_rows(first_row, row_count):
        return jnp.einsum("sf,df->sd", grad_pre, up_weight, preferred_element_type=jnp.float32)

    grad_normed1 = grad_resid2 + lax.psum_scatter(
        normed_rows(jnp.int32(0), lax.axis_size("mp") * tok_rows),
        "mp",
        scatter_dimension=0,
        tiled=True,
    )
    grad_resid1, grad_gain_one, grad_shift_one = norm1_back(grad_normed1)
    grad_attn_low = grad_resid1.astype(jnp.bfloat16)
    gathered_again, grad_attn_all = (
        lax.all_gather(hidden_low, "mp", axis=0, tiled=True),
        lax.all_gather(grad_attn_low, "mp", axis=0, tiled=True),
    )
    mixed_again = project_heads(gathered_again, qkv_weight)
    context_again, log_again = attend_forward(mixed_again, all_wins)
    grad_out_part = jnp.einsum(
        "sf,sd->fd", context_again, grad_attn_all, preferred_element_type=jnp.float32
    )
    grad_context = jnp.einsum(
        "sd,fd->sf", grad_attn_all, out_weight, preferred_element_type=jnp.float32
    ).astype(jnp.bfloat16)
    grad_mixed = attend_backward(mixed_again, grad_context, log_again, all_wins)
    grad_qkv_part = jnp.einsum(
        "sd,scf->dcf", gathered_again, grad_mixed, preferred_element_type=jnp.float32
    )
    grad_hidden = grad_resid1 + lax.psum_scatter(
        jnp.einsum("scf,dcf->sd", grad_mixed, qkv_weight, preferred_element_type=jnp.float32),
        "mp",
        scatter_dimension=0,
        tiled=True,
    )
    weight_parts = (grad_qkv_part, grad_out_part, grad_up_part, grad_up_bias_part, grad_down_part)
    grad_bias_out = jnp.sum(grad_resid1, axis=0)
    grad_bias_down = jnp.sum(grad_resid2, axis=0)
    summed_weights = (
        lax.psum(weight_parts[0].astype(jnp.bfloat16), "dp").astype(jnp.float32),
        lax.psum(weight_parts[1].astype(jnp.bfloat16), "dp").astype(jnp.float32),
        lax.psum(weight_parts[2].astype(jnp.bfloat16), "dp").astype(jnp.float32),
        lax.psum(weight_parts[3].astype(jnp.bfloat16), "dp").astype(jnp.float32),
        lax.psum(weight_parts[4].astype(jnp.bfloat16), "dp").astype(jnp.float32),
    )
    shared = lax.psum(
        (
            table_grad(grad_hidden, local_wins),
            grad_gain_one,
            grad_shift_one,
            grad_bias_out,
            grad_gain_two,
            grad_shift_two,
            grad_bias_down,
        ),
        ("dp", "mp"),
    )
    return (
        layer_out.astype(jnp.bfloat16),
        grad_hidden.astype(jnp.bfloat16),
        shared[0],
        summed_weights[0],
        summed_weights[1],
        shared[3],
        shared[1],
        shared[2],
        summed_weights[2],
        summed_weights[3],
        summed_weights[4],
        shared[6],
        shared[4],
        shared[5],
    )


def solution(mesh):
    placed = (
        P(("dp", "mp"), None),
        P(),
        P(None, None, "mp"),
        P("mp", None),
        P(),
        P(),
        P(),
        P(None, "mp"),
        P("mp"),
        P("mp", None),
        P(),
        P(),
        P(),
        P("dp"),
        P(("dp", "mp"), None),
    )
    return jax.shard_map(
        per_device,
        mesh=mesh,
        in_specs=placed,
        out_specs=(
            P(("dp", "mp"), None),
            P(("dp", "mp"), None),
            P(),
            P(None, None, "mp"),
            P("mp", None),
            P(),
            P(),
            P(),
            P(None, "mp"),
            P("mp"),
            P("mp", None),
            P(),
            P(),
            P(),
        ),
        check_vma=False,
    )
```

profile of v0, /device:TPU:0, one launch (start us, length us, event | category | flops | bytes accessed | tf_op | source)
XLA Modules:
  0.0 651.4 jit_solution(10920312022065734653)
XLA Ops:
  12.1 24.1 %all-gather.5.cloned.1.call-done = bf16[1024,512]{1,0:T(8,128)(2,1)} async-done(((bf16[512,512]{1,0:T(8,128)(2,1)}), bf16[1024,512]{1,0:T(8,128)(2,1)}) %all-gather.5.cloned.1.call-update) | async-done | bytes 1048592 | tf_op jit(solution)/shard_map/all_gather | solution.py:167
  36.2 2.4 convolution_convert_fusion
  40.4 2.9 reshape.542
  45.6 43.8 %while.41 = (s32[]{:T(128)}, bf16[2,512,4,64]{1,3,2,0:T(8,128)(2,1)}, bf16[2,512,4,64]{1,3,2,0:T(8,128)(2,1)S(1)}, s32[2]{0:T(128)S(1)}, bf16[2,512,4,64]{1,3,2,...) while((s32[]{:T(128)}, bf16[2,512,4,64]{1,3,2,0:T(8,128)(2,1)}, ...), condition=%wide.region_4.5_spmd, body=%wide.region_0.0_spmd.sunk | while | flops 421665792 | bytes 32832616 | solution.py:94
  47.9 2.7 fusion.258
  50.6 6.2 select_reduce_fusion.11
  56.8 4.6 select_reduce_fusion.12
  61.4 6.1 fusion.259
  69.8 2.7 fusion.258
  72.5 6.2 select_reduce_fusion.11
  78.7 4.6 select_reduce_fusion.12
  83.3 6.1 fusion.259
  93.3 31.9 %reduce-scatter.5.cloned.1.call-done = f32[512,512]{1,0:T(8,128)} async-done(((f32[1024,512]{1,0:T(8,128)}), f32[512,512]{1,0:T(8,128)}) %reduce-scatter.5.cloned.1.call-update) | async-done | bytes 1048592 | tf_op jit(solution)/shard_map/reduce_scatter | solution.py:172
  128.8 21.2 %all-gather.7.cloned.1.call-done = bf16[1024,512]{1,0:T(8,128)(2,1)} async-done(((bf16[512,512]{1,0:T(8,128)(2,1)}), bf16[1024,512]{1,0:T(8,128)(2,1)}) %all-gather.7.cloned.1.call-update) | async-done | bytes 1048592 | tf_op jit(solution)/shard_map/all_gather | solution.py:182
  150.1 12.6 %multiply_convert_fusion.1 = (bf16[1024,1024]{1,0:T(8,128)(2,1)S(1)}, f32[1024,1024]{1,0:T(8,128)}, f32[1024,1024]{1,0:T(8,128)}) fusion(f32[1024]{0:T(1024)S(1)} %convert_element_type.159, bf16[1024,512]{1,0:T(8,128)(2,1)} %all-gather.7.cloned.1.call-done, bf16[512,1024]{1,0:T(8,128)(2,1)S(1)} %copy-done), kind=kOutput, calls=%fused_computation.146 | convolution fusion | flops 1142947840 | bytes 12587008 | tf_op jit(solution)/shard_map/dot_general | solution.py:132
  164.1 2.6 fusion.194
  166.8 31.9 %reduce-scatter.7.cloned.1.call-done = f32[512,512]{1,0:T(8,128)} async-done(((f32[1024,512]{1,0:T(8,128)}), f32[512,512]{1,0:T(8,128)}) %reduce-scatter.7.cloned.1.call-update) | async-done | bytes 1048592 | tf_op jit(solution)/shard_map/reduce_scatter | solution.py:186
  204.4 21.4 %all-gather.9.cloned.1.call-done = bf16[1024,512]{1,0:T(8,128)(2,1)} async-done(((bf16[512,512]{1,0:T(8,128)(2,1)}), bf16[1024,512]{1,0:T(8,128)(2,1)}) %all-gather.9.cloned.1.call-update) | async-done | bytes 1048592 | tf_op jit(solution)/shard_map/all_gather | solution.py:199
  225.8 6.6 %fusion.192 = (bf16[1024]{0:T(1024)(128)(2,1)S(1)}, bf16[1024,1024]{1,0:T(8,128)(2,1)S(1)}) fusion(f32[1024,1024]{1,0:T(8,128)} %get-tuple-element.443, bf16[1024,512]{1,0:T(8,128)(2,1)} %all-gather.9.cloned.1.call-done, bf16[1024,512]{1,0:T(8,128)(2,1)} %param.30, f32[1024,1024]{1,0:T(8,128)} %get-tuple-element.468, f32[1024]{0:T(1024)S(1)} %convert_element_type.159), kind=kOutput, calls=%fused_computation.222 | convolution fusion | flops 1090518016 | bytes 12589056 | tf_op jit(solution)/shard_map/sd,fd->sf/dot_general | solution.py:205
  233.8 2.6 fusion.195
  236.5 31.9 %reduce-scatter.9.cloned.1.call-done = f32[512,512]{1,0:T(8,128)} async-done(((f32[1024,512]{1,0:T(8,128)}), f32[512,512]{1,0:T(8,128)}) %reduce-scatter.9.cloned.1.call-update) | async-done | bytes 1048592 | tf_op jit(solution)/shard_map/reduce_scatter | solution.py:215
  272.4 42.8 %while.42 = (s32[]{:T(128)}, bf16[2,512,4,64]{1,3,2,0:T(8,128)(2,1)S(1)}, f32[2,4,512]{2,1,0:T(4,128)S(1)}, bf16[2,512,4,64]{1,3,2,0:T(8,128)(2,1)}, s32[2]{0:T(...) while((s32[]{:T(128)}, ...), condition=%wide.region_20.21_spmd, body=%wide.region_16.20_spmd.sunk | while | flops 421665792 | bytes 34938000 | solution.py:94
  274.7 2.7 fusion.266
  277.4 6.5 select_reduce_fusion.13
  283.9 4.6 select_reduce_fusion.14
  288.6 5.4 fusion.267
  296.3 2.7 fusion.266
  299.0 6.2 select_reduce_fusion.13
  305.2 4.6 select_reduce_fusion.14
  309.9 5.4 fusion.267
  318.9 38.1 %while.43 = (s32[]{:T(128)}, bf16[2,512,3,4,64]{1,4,3,2,0:T(8,128)(2,1)}, bf16[2,512,4,64]{1,3,2,0:T(8,128)(2,1)S(1)}, s32[2]{0:T(128)S(1)}, bf16[2,512,4,64]{1,...) while((s32[]{:T(128)}, ...), condition=%wide.region_24.25_spmd, body=%wide.region_21.24_spmd.sunk | while | flops 821957120 | bytes 54050468 | solution.py:125
  321.2 2.7 fusion.280
  323.9 5.5 multiply_reduce_fusion.6
  329.3 4.6 multiply_convert_fusion.3
  340.1 2.7 fusion.280
  342.8 5.5 multiply_reduce_fusion.6
  348.3 4.6 multiply_convert_fusion.3
  357.0 3.1 copy.57
  360.1 2.3 reshape.545
  362.4 3.8 convolution_bitcast_fusion
  367.5 4.1 convolution_convert_fusion.1
  377.0 21.2 %reduce-scatter.11.cloned.1.call-done = f32[512,512]{1,0:T(8,128)} async-done(((f32[1024,512]{1,0:T(8,128)}), f32[512,512]{1,0:T(8,128)}) %reduce-scatter.11.cloned.1.call-update) | async-done | bytes 1048592 | tf_op jit(solution)/shard_map/reduce_scatter | solution.py:239
  401.7 33.9 %psum.91 = bf16[1024]{0:T(1024)(128)(2,1)S(1)} all-reduce(bf16[1024]{0:T(1024)(128)(2,1)S(1)} %get-tuple-element.469), channel_id=1, replica_groups=mesh['dp'=16,'mp'=2] {'dp'}, use_global_device_ids=true, to_apply=%region_37.38 | all-reduce | flops 1024 | bytes 4096 | tf_op jit(solution)/shard_map/psum | solution.py:252
  436.2 37.1 %all-reduce.1 = (f32[512]{0:T(512)}, f32[512]{0:T(512)}, f32[512]{0:T(512)}, f32[512]{0:T(512)}, f32[512]{0:T(512)}, /*index=5*/f32[512]{0:T(512)}) all-reduce(f32[512]{0:T(512)S(1)} %get-tuple-element.466, f32[512]{0:T(512)S(1)} %get-tuple-element.375, f32[512]{0:T(512)S(1)} %get-tuple-element.379, ...), channel_id=1, replica_groups=mesh['dp'=16,'mp'=2] {'dp','mp'}, use_global_device_ids=true, to_apply=%region_30.31 | all-reduce | flops 3072 | bytes 24576 | tf_op jit(solution)/shard_map/psum | solution.py:255
  473.3 34.3 %all-reduce.8.cloned.1.call-done = (bf16[512,3,256]{2,0,1:T(8,128)(2,1)}, bf16[256,512]{1,0:T(8,128)(2,1)}, bf16[512,1024]{1,0:T(8,128)(2,1)}, bf16[1024,512]{1,0:T(8,128)(2,1)}) async-done(((bf16[512,3,256]{2,0,1:T(8,128)(2,1)}, bf16[256,512]{1,0:T(8,128)(2,1)}, bf16[512,1024]{1,0:T(8,128)(2,1)}, bf16[1024,512]{1,0:T(8,128)(2,1)}), (bf16[512,3,256]{2,0,1:T(8,128)(2,1)}, bf16[256,512]{1,0:T(8,128)(2,1)}, ...) | async-done | bytes 3145744 | tf_op jit(solution)/shard_map/psum | solution.py:249
  507.6 2.9 convert_element_type.176
  510.5 2.9 convert_element_type.179
  515.5 126.3 %all-reduce.6.cloned.1.call-done = f32[512,512]{1,0:T(8,128)} async-done(((f32[512,512]{1,0:T(8,128)}), f32[512,512]{1,0:T(8,128)}) %all-reduce.6.cloned.1.call-update) | async-done | bytes 1048592 | tf_op jit(solution)/shard_map/psum | solution.py:255
  (179 shorter events, 64.4 us)
Async XLA Ops:
  7.2 142.9 %copy-start = (bf16[512,1024]{1,0:T(8,128)(2,1)S(1)}, bf16[512,1024]{1,0:T(8,128)(2,1)}, u32[]{:S(2)}) copy-start(bf16[512,1024]{1,0:T(8,128)(2,1)} %param.28) | copy-start | bytes 3145732
  7.2 29.0 %all-gather.5.cloned.1.call-start = ((), (), s32[]{:S(2)}) async-start(), calls=%async_computation.4 | async-start | bytes 1572864 | tf_op jit(solution)/shard_map/all_gather | solution.py:167
  9.0 0.8 copy-start.9
  12.0 113.1 %reduce-scatter.5.cloned.1.call-start = ((), (), s32[]{:S(2)}) async-start(), calls=%async_computation.5 | async-start | bytes 3145728 | tf_op jit(solution)/shard_map/reduce_scatter | solution.py:172
  45.6 45.7 %copy-start.18 = (bf16[256,512]{1,0:T(8,128)(2,1)S(1)}, bf16[256,512]{1,0:T(8,128)(2,1)}, u32[]{:S(2)}) copy-start(bf16[256,512]{1,0:T(8,128)(2,1)} %param.24) | copy-start | bytes 786436
  89.4 3.8 copy-start.6
  89.4 3.8 copy-start.22
  89.4 3.8 copy-start.23
  89.4 3.8 copy-start.24
  93.1 35.7 %copy-start.21 = (bf16[1024]{0:T(1024)(128)(2,1)S(1)}, bf16[1024]{0:T(1024)(128)(2,1)}, u32[]{:S(2)}) copy-start(bf16[1024]{0:T(1024)(128)(2,1)} %param.29) | copy-start | bytes 6148
  93.1 56.9 %all-gather.7.cloned.1.call-start = ((), (), s32[]{:S(2)}) async-start(), calls=%async_computation.6 | async-start | bytes 1572864 | tf_op jit(solution)/shard_map/all_gather | solution.py:182
  128.6 70.0 %reduce-scatter.7.cloned.1.call-start = ((), (), s32[]{:S(2)}) async-start(), calls=%async_computation.7 | async-start | bytes 3145728 | tf_op jit(solution)/shard_map/reduce_scatter | solution.py:186
  150.1 14.0 %copy-start.28 = (bf16[1024,512]{1,0:T(8,128)(2,1)S(1)}, bf16[1024,512]{1,0:T(8,128)(2,1)}, u32[]{:S(2)}) copy-start(bf16[1024,512]{1,0:T(8,128)(2,1)} %param.30) | copy-start | bytes 3145732
  162.7 1.4 copy-start.32
  164.0 2.6 copy-start.25
  164.1 2.7 copy-start.26
  164.1 2.7 copy-start.27
  166.6 59.2 %all-gather.9.cloned.1.call-start = ((), (), s32[]{:S(2)}) async-start(), calls=%async_computation.8 | async-start | bytes 1572864 | tf_op jit(solution)/shard_map/all_gather | solution.py:199
  198.6 2.0 copy-start.13
  202.4 1.0 copy-start.3
  204.4 64.0 %reduce-scatter.9.cloned.1.call-start = ((), (), s32[]{:S(2)}) async-start(), calls=%async_computation.9 | async-start | bytes 3145728 | tf_op jit(solution)/shard_map/reduce_scatter | solution.py:215
  232.4 1.3 copy-start.11
  236.4 79.6 %all-gather.11.cloned.1.call-start = ((), (), s32[]{:S(2)}) async-start(), calls=%async_computation.10 | async-start | bytes 1572864 | tf_op jit(solution)/shard_map/all_gather | solution.py:225
  270.9 1.5 copy-start.4
  272.1 126.2 %reduce-scatter.11.cloned.1.call-start = ((), (), s32[]{:S(2)}) async-start(), calls=%async_computation.11 | async-start | bytes 3145728 | tf_op jit(solution)/shard_map/reduce_scatter | solution.py:239
  283.9 4.7 copy-start.7
  305.2 4.7 copy-start.7
  315.2 0.8 copy-start.14
  316.0 2.8 copy-start.8
  333.9 2.2 copy-start.2
  352.9 2.2 copy-start.2
  357.0 5.5 copy-start.31
  362.4 3.9 copy-start.15
  366.3 1.2 copy-start.30
  366.3 141.3 %all-reduce.8.cloned.1.call-start = ((), (), s32[]{:S(2)}) async-start(), calls=%async_computation.13 | async-start | bytes 6291456 | tf_op jit(solution)/shard_map/psum | solution.py:249
  367.5 4.1 copy-start.12
  367.5 4.1 copy-start.17
  371.6 2.3 copy-start.10
  371.6 3.4 copy-start.16
  371.6 3.4 copy-start.29
  375.0 23.3 %copy-start.5 = (f32[512,512]{1,0:T(8,128)S(1)}, f32[512,512]{1,0:T(8,128)}, u32[]{:S(2)}) copy-start(f32[512,512]{1,0:T(8,128)} %copy-done.4) | copy-start | bytes 3145732
  377.0 264.9 %all-reduce.6.cloned.1.call-start = ((), (), s32[]{:S(2)}) async-start(), calls=%async_computation.12 | async-start | bytes 2097152 | tf_op jit(solution)/shard_map/psum | solution.py:255
  507.6 5.8 copy-start.19
  507.6 7.1 %copy-start.20 = (bf16[256,512]{1,0:T(8,128)(2,1)S(1)}, bf16[256,512]{1,0:T(8,128)(2,1)}, u32[]{:S(2)}) copy-start(bf16[256,512]{1,0:T(8,128)(2,1)} %get-tuple-element.430) | copy-start | bytes 786436
  510.5 133.6 %copy-start.1 = (bf16[512,1024]{1,0:T(8,128)(2,1)S(1)}, bf16[512,1024]{1,0:T(8,128)(2,1)}, u32[]{:S(2)}) copy-start(bf16[512,1024]{1,0:T(8,128)(2,1)} %param.28) | copy-start | bytes 3145732
Sparse Core Ops, SparseCore 0:
  12.1 23.9 all-gather.4
  93.3 31.8 reduce-scatter.4
  128.7 21.2 all-gather.6
  166.8 31.8 reduce-scatter.6
  204.5 21.2 all-gather.8
  236.5 31.8 reduce-scatter.8
  272.2 21.2 all-gather.10
  366.4 31.8 reduce-scatter.10
  403.3 104.2 all-reduce.7
  513.2 128.5 all-reduce.5
where the time goes:
time: 660 us; the launch traced here: 651 us
  waiting for transfers between devices  344 us (52%)
  matrix products  123 us (19%)
  blocking collectives  71 us (11%)
  other arithmetic  61.9 us (9%)
  local copies, waits for them, and re-layouts  30.5 us (5%)
  between operations  15.8 us (2%)
    psum x1, waiting for transfers between devices, per_device(): lax.psum((table_grad(grad_hidden, local_wins), grad_gain_one, grad_shift_...  126 us
    psum x1, blocking collectives, per_device(): lax.psum((table_grad(grad_hidden, local_wins), grad_gain_one, grad_shift_...  37.1 us
    broadcast_in_dim x6, matrix products, block_scores(): return (jnp.where(allowed, scores, diagonal), allowed)  36.2 us
    psum x1, waiting for transfers between devices, per_device(): lax.psum(weight_parts[0].astype(jnp.bfloat16), 'dp').astype(jnp.float32)  34.3 us
    psum x1, blocking collectives, per_device(): lax.psum(weight_parts[3].astype(jnp.bfloat16), 'dp').astype(jnp.float32)  33.9 us
    reduce_scatter x1, waiting for transfers between devices, per_device(): lax.psum_scatter(normed_rows(jnp.int32(0), lax.axis_size('mp') * tok_rows...  31.9 us
    reduce_scatter x1, waiting for transfers between devices, per_device(): lax.psum_scatter(jnp.dot(act_low, down_weight, preferred_element_type=jnp...  31.9 us
    reduce_scatter x1, waiting for transfers between devices, per_device(): lax.psum_scatter(jnp.dot(context, out_weight, preferred_element_type=jnp....  31.9 us
  transfers between devices with their start and end apart: 10, of which 9 were waited for; matrix products, arithmetic and copies ran while one was open for 10% of the time, Pallas kernels for 0%

commit v1 on v0

v1 whole, which is shorter than its diff:
```python
import functools

import jax
import jax.numpy as jnp
from jax import lax
from jax.experimental import pallas as pl
from jax.experimental.pallas import tpu as pltpu
from jax.sharding import PartitionSpec as P

HD = 64
W_SHORT = 256
W_LONG = 512
ROW = 1024
LANES = 128
EXTRA = 16
EPSILON = 1e-05
MASKED = -1e30
F32 = jnp.float32
BF16 = jnp.bfloat16
VMEM_BYTES = 48 * 1024 * 1024

vmem = pl.BlockSpec(memory_space=pltpu.VMEM)
smem = pl.BlockSpec(memory_space=pltpu.SMEM)


def call(kernel, outs, args, specs=None, scratch=(), flops=0, bytes_accessed=0, name=None):
    return pl.pallas_call(
        kernel,
        out_shape=[jax.ShapeDtypeStruct(shape, dtype) for shape, dtype in outs],
        in_specs=specs or [vmem] * len(args),
        out_specs=[vmem] * len(outs),
        scratch_shapes=list(scratch),
        compiler_params=pltpu.CompilerParams(vmem_limit_bytes=VMEM_BYTES),
        cost_estimate=pl.CostEstimate(
            flops=flops, bytes_accessed=bytes_accessed, transcendentals=0
        ),
        name=name,
    )(*args)


def mm(a, b):
    return lax.dot_general(a, b, (((1,), (0,)), ((), ())), preferred_element_type=F32)


def mm_nt(a, b):
    return lax.dot_general(a, b, (((1,), (1,)), ((), ())), preferred_element_type=F32)


def mm_tn(a, b):
    return lax.dot_general(a, b, (((0,), (0,)), ((), ())), preferred_element_type=F32)


def position_rows(pos_ref, is_long):
    first = pos_ref[0:W_SHORT, :].astype(F32)
    second = jnp.where(is_long, pos_ref[W_SHORT:W_LONG, :].astype(F32), first)
    return first, second


def hidden_rows(tokens_ref, pos_ref, windows):
    parts = []
    for block, is_long in enumerate(windows):
        first, second = position_rows(pos_ref, is_long)
        start = block * W_LONG
        parts.append(tokens_ref[start : start + W_SHORT, :].astype(F32) + first)
        parts.append(tokens_ref[start + W_SHORT : start + W_LONG, :].astype(F32) + second)
    return jnp.concatenate(parts, axis=0)


def read_windows(win_ref, blocks):
    return [win_ref[block] == W_LONG for block in range(blocks)]


def norm_stats(values):
    average = jnp.mean(values, axis=-1, keepdims=True)
    centred = values - average
    variance = jnp.mean(centred * centred, axis=-1, keepdims=True)
    scale = lax.rsqrt(variance + EPSILON)
    return centred * scale, scale


def norm_grad(grad_hat, hat, scale):
    mean_grad = jnp.mean(grad_hat, axis=-1, keepdims=True)
    mean_both = jnp.mean(grad_hat * hat, axis=-1, keepdims=True)
    return scale * (grad_hat - mean_grad - hat * mean_both)


def head_mask(rows):
    return lax.broadcasted_iota(jnp.int32, (rows, LANES), 1) < HD


def own_head(value, is_low, head):
    zero = jnp.zeros_like(value)
    return jnp.where(is_low, value, zero) if head == 0 else jnp.where(is_low, zero, value)


def attend_forward(hidden_low, weight_ref, windows, mixed_ref, probs_ref, context_ref):
    rows, width = context_ref.shape
    for c in range(3):
        part = mm(hidden_low, weight_ref[c]).astype(BF16)
        mixed_ref[c] = part * BF16(HD**-0.5) if c == 0 else part
    causal = lax.broadcasted_iota(jnp.int32, (W_SHORT, W_SHORT), 0) >= lax.broadcasted_iota(
        jnp.int32, (W_SHORT, W_SHORT), 1
    )
    is_low = head_mask(W_SHORT)
    for block, is_long in enumerate(windows):
        lo = slice(block * W_LONG, block * W_LONG + W_SHORT)
        hi = slice(block * W_LONG + W_SHORT, (block + 1) * W_LONG)
        for pair in range(width // LANES):
            lanes = slice(pair * LANES, (pair + 1) * LANES)
            key_lo, key_hi = mixed_ref[1, lo, lanes], mixed_ref[1, hi, lanes]
            val_lo, val_hi = mixed_ref[2, lo, lanes], mixed_ref[2, hi, lanes]
            query_lo, query_hi = mixed_ref[0, lo, lanes], mixed_ref[0, hi, lanes]
            results = []
            for head in range(2):
                slot = ((block * (width // LANES) + pair) * 2 + head) * 3
                q_lo = own_head(query_lo, is_low, head)
                q_hi = own_head(query_hi, is_low, head)
                s_a = jnp.where(causal, mm_nt(q_lo, key_lo), MASKED)
                e_a = jnp.exp(s_a - jnp.max(s_a, axis=-1, keepdims=True))
                p_a = (e_a * (1.0 / jnp.sum(e_a, axis=-1, keepdims=True))).astype(BF16)
                s_b = jnp.where(is_long, mm_nt(q_hi, key_lo), MASKED)
                s_c = jnp.where(causal, mm_nt(q_hi, key_hi), MASKED)
                top = jnp.max(jnp.maximum(s_b, s_c), axis=-1, keepdims=True)
                e_b = jnp.exp(s_b - top)
                e_c = jnp.exp(s_c - top)
                inverse = 1.0 / jnp.sum(e_b + e_c, axis=-1, keepdims=True)
                p_b = (e_b * inverse).astype(BF16)
                p_c = (e_c * inverse).astype(BF16)
                probs_ref[slot] = p_a
                probs_ref[slot + 1] = p_b
                probs_ref[slot + 2] = p_c
                results.append((mm(p_a, val_lo), mm(p_b, val_lo) + mm(p_c, val_hi)))
            context_ref[lo, lanes] = jnp.where(is_low, results[0][0], results[1][0]).astype(BF16)
            context_ref[hi, lanes] = jnp.where(is_low, results[0][1], results[1][1]).astype(BF16)


def attend_backward(grad_context, mixed_ref, probs_ref, blocks, grad_mixed_ref):
    width = mixed_ref.shape[2]
    is_low = head_mask(W_SHORT)
    for block in range(blocks):
        lo = slice(block * W_LONG, block * W_LONG + W_SHORT)
        hi = slice(block * W_LONG + W_SHORT, (block + 1) * W_LONG)
        for pair in range(width // LANES):
            lanes = slice(pair * LANES, (pair + 1) * LANES)
            q_lo, q_hi = mixed_ref[0, lo, lanes], mixed_ref[0, hi, lanes]
            k_lo, k_hi = mixed_ref[1, lo, lanes], mixed_ref[1, hi, lanes]
            v_lo, v_hi = mixed_ref[2, lo, lanes], mixed_ref[2, hi, lanes]
            g_lo, g_hi = grad_context[lo, lanes], grad_context[hi, lanes]
            results = []
            for head in range(2):
                slot = ((block * (width // LANES) + pair) * 2 + head) * 3
                gm_lo = own_head(g_lo, is_low, head)
                gm_hi = own_head(g_hi, is_low, head)
                pb_a, pb_b, pb_c = probs_ref[slot], probs_ref[slot + 1], probs_ref[slot + 2]
                p_a, p_b, p_c = pb_a.astype(F32), pb_b.astype(F32), pb_c.astype(F32)
                g_a = mm_nt(gm_lo, v_lo)
                g_b = mm_nt(gm_hi, v_lo)
                g_c = mm_nt(gm_hi, v_hi)
                inner_a = jnp.sum(p_a * g_a, axis=-1, keepdims=True)
                inner_b = jnp.sum(p_b * g_b + p_c * g_c, axis=-1, keepdims=True)
                s_a = (p_a * (g_a - inner_a)).astype(BF16)
                s_b = (p_b * (g_b - inner_b)).astype(BF16)
                s_c = (p_c * (g_c - inner_b)).astype(BF16)
                results.append(
                    (
                        mm(s_a, k_lo),
                        mm(s_b, k_lo) + mm(s_c, k_hi),
                        mm_tn(s_a, q_lo) + mm_tn(s_b, q_hi),
                        mm_tn(s_c, q_hi),
                        mm_tn(pb_a, g_lo) + mm_tn(pb_b, g_hi),
                        mm_tn(pb_c, g_hi),
                    )
                )
            both = [jnp.where(is_low, a, b) for a, b in zip(*results)]
            grad_mixed_ref[0, lo, lanes] = (both[0] * HD**-0.5).astype(BF16)
            grad_mixed_ref[0, hi, lanes] = (both[1] * HD**-0.5).astype(BF16)
            grad_mixed_ref[1, lo, lanes] = both[2].astype(BF16)
            grad_mixed_ref[1, hi, lanes] = both[3].astype(BF16)
            grad_mixed_ref[2, lo, lanes] = both[4].astype(BF16)
            grad_mixed_ref[2, hi, lanes] = both[5].astype(BF16)


def normal_parts(x):
    density = jnp.exp(x * x * -0.5)
    t = 1.0 / (1.0 + jnp.abs(x) * 0.23164189)
    poly = t * (
        0.127414796
        + t * (-0.142248368 + t * (0.7107068705 + t * (-0.7265760135 + t * 0.5307027145)))
    )
    tail = poly * density
    return jnp.where(x > 0, 1.0 - tail, tail), density * 0.3989422804


def first_kernel(win_ref, tokens_ref, pos_ref, weight_ref, mixed_ref, probs_ref, context_ref):
    windows = read_windows(win_ref, tokens_ref.shape[0] // W_LONG)
    hidden_low = hidden_rows(tokens_ref, pos_ref, windows).astype(BF16)
    attend_forward(hidden_low, weight_ref, windows, mixed_ref, probs_ref, context_ref)


def second_kernel(
    win_ref,
    tokens_ref,
    pos_ref,
    weight_ref,
    context_own_ref,
    out_own_ref,
    out_oth_ref,
    vec_ref,
    mixed_ref,
    probs_ref,
    context_ref,
    resid_ref,
):
    windows = read_windows(win_ref, tokens_ref.shape[0] // W_LONG)
    hidden_in = hidden_rows(tokens_ref, pos_ref, windows)
    attend_forward(
        hidden_in.astype(BF16), weight_ref, windows, mixed_ref, probs_ref, context_ref
    )
    branch = mm(context_own_ref[...], out_own_ref[...]) + mm(context_ref[...], out_oth_ref[...])
    hidden_in = hidden_rows(tokens_ref, pos_ref, windows)
    resid_ref[...] = hidden_in + branch + vec_ref[0:1, :]


def ffn_kernel(
    resid_ref,
    cot_ref,
    up_own_ref,
    up_oth_ref,
    down_own_ref,
    down_oth_ref,
    bias_ref,
    vec_ref,
    layer_ref,
    down_own_grad,
    down_oth_grad,
    up_own_grad,
    up_oth_grad,
    small_ref,
    bias_grad_ref,
    grad_resid_ref,
    act_ref,
    slope_ref,
    low_ref,
    hat_ref,
    grad_ref,
):
    rows, width = resid_ref.shape
    units = up_own_ref.shape[1]
    chunk = 256
    hat, scale = norm_stats(resid_ref[...])
    hat_ref[...] = hat
    normed = hat * vec_ref[1:2, :] + vec_ref[2:3, :]
    low_ref[...] = normed.astype(BF16)
    for half, up in enumerate((up_own_ref, up_oth_ref)):
        for start in range(0, units, chunk):
            cols = slice(start, start + chunk)
            pre = mm(low_ref[...], up[:, cols]) + bias_ref[half : half + 1, cols]
            total, density = normal_parts(pre)
            act_ref[half, :, cols] = (pre * total).astype(BF16)
            slope_ref[half, :, cols] = total + pre * density
    branch = mm(act_ref[0], down_own_ref[...]) + mm(act_ref[1], down_oth_ref[...])
    normed = hat_ref[...] * vec_ref[1:2, :] + vec_ref[2:3, :]
    hat2, scale2 = norm_stats(normed + branch + vec_ref[3:4, :])
    layer_ref[...] = (hat2 * vec_ref[4:5, :] + vec_ref[5:6, :]).astype(BF16)
    cot = cot_ref[...].astype(F32)
    small_ref[4:5, :] = jnp.sum(cot * hat2, axis=0, keepdims=True)
    small_ref[5:6, :] = jnp.sum(cot, axis=0, keepdims=True)
    grad = norm_grad(cot * vec_ref[4:5, :], hat2, scale2)
    small_ref[3:4, :] = jnp.sum(grad, axis=0, keepdims=True)
    grad_ref[...] = grad
    grad_low = grad.astype(BF16)
    for half, up, down, down_grad, up_grad in (
        (1, up_oth_ref, down_oth_ref, down_oth_grad, up_oth_grad),
        (0, up_own_ref, down_own_ref, down_own_grad, up_own_grad),
    ):
        for start in range(0, units, chunk):
            cols = slice(start, start + chunk)
            act = act_ref[half, :, cols]
            down_grad[cols, :] = mm_tn(act, grad_low).astype(BF16)
            pre_grad = (mm_nt(grad_low, down[cols, :]) * slope_ref[half, :, cols]).astype(BF16)
            act_ref[half, :, cols] = pre_grad
            bias_grad_ref[half : half + 1, cols] = jnp.sum(
                pre_grad.astype(F32), axis=0, keepdims=True
            )
        for start in range(0, units, width):
            cols = slice(start, start + width)
            up_grad[start : start + width, :] = mm_tn(low_ref[...], act_ref[half, :, cols]).astype(
                BF16
            )
        grad_ref[...] += mm_nt(act_ref[half], up[...])
    grad = grad_ref[...]
    hat, scale = norm_stats(resid_ref[...])
    small_ref[1:2, :] = jnp.sum(grad * hat, axis=0, keepdims=True)
    small_ref[2:3, :] = jnp.sum(grad, axis=0, keepdims=True)
    grad = norm_grad(grad * vec_ref[1:2, :], hat, scale)
    small_ref[0:1, :] = jnp.sum(grad, axis=0, keepdims=True)
    small_ref[6:8, :] = jnp.zeros((2, width), F32)
    grad_resid_ref[...] = grad


def last_kernel(
    win_ref,
    tokens_ref,
    pos_ref,
    grad_resid_ref,
    w_own_ref,
    w_oth_ref,
    out_own_ref,
    out_oth_ref,
    mixed_own_ref,
    mixed_oth_ref,
    probs_own_ref,
    probs_oth_ref,
    context_own_ref,
    context_oth_ref,
    own_grad,
    oth_grad,
    tokens_grad_ref,
    table_ref,
    gm_ref,
    grad_ref,
):
    rows, width = tokens_ref.shape
    half_width = width // 2
    blocks = rows // W_LONG
    windows = read_windows(win_ref, blocks)
    hidden_low = hidden_rows(tokens_ref, pos_ref, windows).astype(BF16)
    grad_low = grad_resid_ref[...].astype(BF16)
    grad_ref[...] = grad_resid_ref[...]
    for weight, out_w, mixed, probs, context, grads in (
        (w_oth_ref, out_oth_ref, mixed_oth_ref, probs_oth_ref, context_oth_ref, oth_grad),
        (w_own_ref, out_own_ref, mixed_own_ref, probs_own_ref, context_own_ref, own_grad),
    ):
        grads[width + half_width :, :] = mm_tn(context[...], grad_low).astype(BF16)
        grad_context = mm_nt(grad_low, out_w[...]).astype(BF16)
        attend_backward(grad_context, mixed, probs, blocks, gm_ref)
        grads[0:width, 0:half_width] = mm_tn(hidden_low, gm_ref[0]).astype(BF16)
        grads[0:width, half_width:] = mm_tn(hidden_low, gm_ref[1]).astype(BF16)
        value_grad = mm_tn(hidden_low, gm_ref[2]).astype(BF16)
        grads[width : width + half_width, 0:half_width] = value_grad[0:half_width, :]
        grads[width : width + half_width, half_width:] = value_grad[half_width:, :]
        grad_ref[...] += (
            mm_nt(gm_ref[0], weight[0]) + mm_nt(gm_ref[1], weight[1]) + mm_nt(gm_ref[2], weight[2])
        )
    grad = grad_ref[...]
    tokens_grad_ref[...] = grad.astype(BF16)
    first, second = None, None
    for block, is_long in enumerate(windows):
        top = grad[block * W_LONG : block * W_LONG + W_SHORT]
        bottom = grad[block * W_LONG + W_SHORT : (block + 1) * W_LONG]
        zero = jnp.zeros_like(top)
        part_first = top + jnp.where(is_long, zero, bottom)
        part_second = jnp.where(is_long, bottom, zero)
        first = part_first if first is None else first + part_first
        second = part_second if second is None else second + part_second
    table_ref[0:W_SHORT, :] = first.astype(BF16)
    table_ref[W_SHORT:, :] = second.astype(BF16)


def per_device(
    tokens,
    pos_table,
    qkv_weight,
    out_weight,
    out_bias,
    norm1_gain,
    norm1_shift,
    up_weight,
    up_bias,
    down_weight,
    down_bias,
    norm2_gain,
    norm2_shift,
    window,
    cotangent,
):
    rows, width = tokens.shape
    blocks = rows // W_LONG
    half_width = width // 2
    heads_half = half_width // HD
    starts = lax.axis_index("mp") * rows + jnp.arange(blocks, dtype=jnp.int32) * W_LONG
    win = window[starts // ROW]
    vectors = jnp.stack(
        [out_bias, norm1_gain, norm1_shift, down_bias, norm2_gain, norm2_shift]
    ).astype(F32)

    qkv = lax.all_gather(jnp.transpose(qkv_weight, (1, 0, 2)), "mp", axis=2, tiled=True)
    out_w = lax.all_gather(out_weight, "mp", axis=0, tiled=True)
    up_w = lax.all_gather(up_weight, "mp", axis=1, tiled=True)
    bias = lax.all_gather(up_bias, "mp", axis=0, tiled=True)
    down_w = lax.all_gather(down_weight, "mp", axis=0, tiled=True)
    units = up_w.shape[1] // 2
    w_own, w_oth = qkv[:, :, :half_width], qkv[:, :, half_width:]
    out_own, out_oth = out_w[:half_width], out_w[half_width:]
    up_own, up_oth = up_w[:, :units], up_w[:, units:]
    down_own, down_oth = down_w[:units], down_w[units:]
    bias2 = bias.reshape(2, units).astype(F32)

    mixed_shape = ((3, rows, half_width), BF16)
    probs_shape = ((blocks * heads_half * 3, W_SHORT, W_SHORT), BF16)
    context_shape = ((rows, half_width), BF16)
    wide = ((rows, width), F32)
    mixed_own, probs_own, context_own = call(
        first_kernel,
        [mixed_shape, probs_shape, context_shape],
        [win, tokens, pos_table, w_own],
        [smem, vmem, vmem, vmem],
        name="attend_first",
    )
    mixed_oth, probs_oth, context_oth, resid = call(
        second_kernel,
        [mixed_shape, probs_shape, context_shape, wide],
        [win, tokens, pos_table, w_oth, context_own, out_own, out_oth, vectors],
        [smem] + [vmem] * 7,
        name="attend_second",
    )
    package = ((width * 2, width), BF16)
    layer_out, down_own_g, down_oth_g, up_own_g, up_oth_g, small, bias_g, grad_resid = call(
        ffn_kernel,
        [
            ((rows, width), BF16),
            package,
            package,
            package,
            package,
            ((8, width), F32),
            ((2, units), F32),
            wide,
        ],
        [resid, cotangent, up_own, up_oth, down_own, down_oth, bias2, vectors],
        scratch=[
            pltpu.VMEM((2, rows, units), BF16),
            pltpu.VMEM((2, rows, units), F32),
            pltpu.VMEM((rows, width), BF16),
            pltpu.VMEM((rows, width), F32),
            pltpu.VMEM((rows, width), F32),
        ],
        name="feed_forward",
    )
    att_own_g, att_oth_g, grad_tokens, table = call(
        last_kernel,
        [package, package, ((rows, width), BF16), ((W_LONG, width), BF16)],
        [
            win,
            tokens,
            pos_table,
            grad_resid,
            w_own,
            w_oth,
            out_own,
            out_oth,
            mixed_own,
            mixed_oth,
            probs_own,
            probs_oth,
            context_own,
            context_oth,
        ],
        [smem] + [vmem] * 13,
        scratch=[pltpu.VMEM((3, rows, half_width), BF16), pltpu.VMEM((rows, width), F32)],
        name="attend_backward",
    )

    def summed(own, oth, make, dim):
        whole = jnp.concatenate([make(own), make(oth)], axis=dim)
        part = lax.psum_scatter(whole, "mp", scatter_dimension=dim, tiled=True)
        return lax.psum(part, "dp").astype(F32)

    def qkv_part(g):
        value = jnp.concatenate(
            [g[width : width + half_width, :half_width], g[width : width + half_width, half_width:]],
            axis=0,
        )
        return jnp.stack([g[:width, :half_width], g[:width, half_width:], value])

    def up_part(g):
        return jnp.concatenate([g[s : s + width] for s in range(0, g.shape[0], width)], axis=1)

    qkv_g = jnp.transpose(summed(att_own_g, att_oth_g, qkv_part, 2), (1, 0, 2))
    out_g = summed(att_own_g, att_oth_g, lambda g: g[width + half_width :], 0)
    up_g = summed(up_own_g, up_oth_g, up_part, 1)
    down_g = summed(down_own_g, down_oth_g, lambda g: g, 0)
    bias_part = lax.psum_scatter(bias_g.reshape(-1), "mp", scatter_dimension=0, tiled=True)
    bias_sum = lax.psum(bias_part, "dp")
    small = lax.psum(small, ("dp", "mp"))
    table = lax.psum(table.astype(F32), ("dp", "mp"))
    return (
        layer_out,
        grad_tokens,
        table,
        qkv_g,
        out_g,
        small[0],
        small[1],
        small[2],
        up_g,
        bias_sum,
        down_g,
        small[3],
        small[4],
        small[5],
    )


def solution(mesh):
    placed = (
        P(("dp", "mp"), None),
        P(),
        P(None, None, "mp"),
        P("mp", None),
        P(),
        P(),
        P(),
        P(None, "mp"),
        P("mp"),
        P("mp", None),
        P(),
        P(),
        P(),
        P("dp"),
        P(("dp", "mp"), None),
    )
    return jax.shard_map(
        per_device,
        mesh=mesh,
        in_specs=placed,
        out_specs=(
            P(("dp", "mp"), None),
            P(("dp", "mp"), None),
            P(),
            P(None, None, "mp"),
            P("mp", None),
            P(),
            P(),
            P(),
            P(None, "mp"),
            P("mp"),
            P("mp", None),
            P(),
            P(),
            P(),
        ),
        check_vma=False,
    )
```

time: 660 us -> 384 us (0.58); the launches traced: 651 us -> 384 us
  waiting for transfers between devices: 344 us -> 191 us
  matrix products: 123 us -> 0 us
  other arithmetic: 61.9 us -> 11.9 us
  blocking collectives: 71 us -> 111 us
  Pallas kernels: 0 us -> 31.3 us
  local copies, waits for them, and re-layouts: 30.5 us -> 21.9 us
    psum x2 -> x1, waiting for transfers between devices: 161 us -> 15.3 us  [summed(): return lax.psum(part, 'dp').astype(F32)]
    dot_general x28 -> x0, matrix products: 86.5 us -> none  [the longest x4 22.9 us: one_block(): jnp.einsum('hqk,khe->qhe', probs, value_block, preferred_element_type=jnp...]
    broadcast_in_dim x6 -> x0, matrix products: 36.2 us -> none  [block_scores(): return (jnp.where(allowed, scores, diagonal), allowed)]
    pallas_call x0 -> x4, Pallas kernels: none -> 31.3 us  [call(): pl.pallas_call(kernel, out_shape=[jax.ShapeDtypeStruct(shape, dtype) for...]
    reduce_sum x15 -> x0, other arithmetic: 30.3 us -> none  [the longest x4 18.5 us: one_block(): log_total = jnp.log(jnp.sum(weights, axis=-1, keepdims=True)) + top_score]
    psum x2, blocking collectives: 71 us -> 89.2 us  [the longest x1 56.1 us: per_device(): table = lax.psum(table.astype(F32), ('dp', 'mp'))]
    all_gather x0 -> x2, blocking collectives: none -> 17.3 us  [the longest x1 12 us: per_device(): out_w = lax.all_gather(out_weight, 'mp', axis=0, tiled=True)]
    convert_element_type x16 -> x4, other arithmetic: 21 us -> 5.35 us  [the longest x3 5.34 us: summed(): return lax.psum(part, 'dp').astype(F32)]
  transfers between devices with their start and end apart: 10 -> 8, of which waited for: 9 -> 8; matrix products, arithmetic and copies ran while one was open for 10% -> 3% of each run, Pallas kernels for 0% -> 2%
where the time goes in v1:
time: 384 us
  waiting for transfers between devices  191 us (50%)
  blocking collectives  111 us (29%)
  Pallas kernels  31.3 us (8%)
  local copies, waits for them, and re-layouts  21.9 us (6%)
  between operations  15.8 us (4%)
  other arithmetic  11.9 us (3%)
    reduce_scatter x4, waiting for transfers between devices, summed(): part = lax.psum_scatter(whole, 'mp', scatter_dimension=dim, tiled=True)  106 us
    psum x1, blocking collectives, per_device(): table = lax.psum(table.astype(F32), ('dp', 'mp'))  56.1 us
    psum x1, blocking collectives, per_device(): bias_sum = lax.psum(bias_part, 'dp')  33.1 us
    all_gather x1, waiting for transfers between devices, per_device(): up_w = lax.all_gather(up_weight, 'mp', axis=1, tiled=True)  31.7 us
    pallas_call x4, Pallas kernels, call(): pl.pallas_call(kernel, out_shape=[jax.ShapeDtypeStruct(shape, dtype) for...  31.3 us
    all_gather x1, waiting for transfers between devices, per_device(): down_w = lax.all_gather(down_weight, 'mp', axis=0, tiled=True)  23.7 us
    psum x1, waiting for transfers between devices, summed(): return lax.psum(part, 'dp').astype(F32)  15.3 us
    all_gather x1, waiting for transfers between devices, per_device(): lax.all_gather(jnp.transpose(qkv_weight, (1, 0, 2)), 'mp', axis=2, tiled=...  12.9 us
  transfers between devices with their start and end apart: 8, of which 8 were waited for; matrix products, arithmetic and copies ran while one was open for 3% of the time, Pallas kernels for 2%

profile of v1, /device:TPU:0, one launch (start us, length us, event | category | flops | bytes accessed | tf_op | source)
XLA Modules:
  0.0 384.0 jit_solution(11226135480534102772)
XLA Ops:
  7.3 0.7 all-gather.4.cloned.1.call-update
  8.0 0.7 all-gather.8.cloned.1.call-update
  8.8 0.7 all-gather.6.cloned.1.call-update
  10.4 5.3 %all_gather.19 = bf16[2048]{0:T(1024)(128)(2,1)S(1)} all-gather(bf16[1024]{0:T(1024)(128)(2,1)S(1)} %copy-done.28), channel_id=1, replica_groups=mesh['dp'=16,'mp'=2] {'mp'}, dimensions={0}, use_global_device_ids=true | all-gather | bytes 6144 | tf_op jit(solution)/shard_map/all_gather | solution.py:390
  15.6 12.0 %all_gather.16 = bf16[512,512]{1,0:T(8,128)(2,1)S(1)} all-gather(bf16[256,512]{1,0:T(8,128)(2,1)S(1)} %copy-done.26), channel_id=1, replica_groups=mesh['dp'=16,'mp'=2] {'mp'}, dimensions={0}, use_global_device_ids=true | all-gather | bytes 786432 | tf_op jit(solution)/shard_map/all_gather | solution.py:388
  27.7 12.9 %all-gather.4.cloned.1.call-done = bf16[3,512,512]{2,1,0:T(8,128)(2,1)} async-done(((bf16[3,512,256]{2,1,0:T(8,128)(2,1)}), bf16[3,512,512]{2,1,0:T(8,128)(2,1)}) %all-gather.4.cloned.1.call-update) | async-done | bytes 1572880 | tf_op jit(solution)/shard_map/all_gather | solution.py:387
  40.6 1.5 fusion.2
  42.1 2.6 attend_first.1
  44.7 1.1 copy-done.2
  45.9 0.9 copy-done.13
  46.7 3.6 attend_second.1
  50.4 1.0 copy-done.12
  51.4 1.0 copy-done.15
  52.3 0.7 copy-done.20
  53.0 23.7 %all-gather.8.cloned.1.call-done = bf16[2048,512]{1,0:T(8,128)(2,1)} async-done(((bf16[1024,512]{1,0:T(8,128)(2,1)}), bf16[2048,512]{1,0:T(8,128)(2,1)}) %all-gather.8.cloned.1.call-update) | async-done | bytes 2097168 | tf_op jit(solution)/shard_map/all_gather | solution.py:391
  76.8 3.0 fusion
  79.8 31.7 %all-gather.6.cloned.1.call-done = bf16[512,2048]{1,0:T(8,128)(2,1)} async-done(((bf16[512,1024]{1,0:T(8,128)(2,1)}), bf16[512,2048]{1,0:T(8,128)(2,1)}) %all-gather.6.cloned.1.call-update) | async-done | bytes 2097168 | tf_op jit(solution)/shard_map/all_gather | solution.py:389
  111.5 3.1 fusion.1
  114.6 12.9 %feed_forward.1 = (bf16[512,512]{1,0:T(8,128)(2,1)}, bf16[1024,512]{1,0:T(8,128)(2,1)S(1)}, bf16[1024,512]{1,0:T(8,128)(2,1)S(1)}, bf16[1024,512]{1,0:T(8,128)(2...) custom-call(f32[512,512]{1,0:T(8,128)} %copy-done.12, ...), custom_call_target="tpu_custom_call" | custom-call | tf_op jit(solution)/shard_map/feed_forward/pallas_call | solution.py:27
  127.4 1.0 copy-done.3
  128.4 1.0 copy-done.6
  129.4 1.0 copy-done.10
  130.4 12.2 %attend_backward.1 = (bf16[1024,512]{1,0:T(8,128)(2,1)}, bf16[1024,512]{1,0:T(8,128)(2,1)}, bf16[512,512]{1,0:T(8,128)(2,1)}, bf16[512,512]{1,0:T(8,128)(2,1)S(1)}) custom-call(s32[1]{0:T(128)S(6)} %copy.39.win_ref, bf16[512,512]{1,0:T(8,128)(2,1)S(1)} %copy-done, bf16[512,512]{1,0:T(8,128)(2,1)S(1)} %copy-done.1, f32[512,512]{1,0:T(8,128)} %copy-done.3, ...), custom_call_target="tpu_custom_call" | custom-call | tf_op jit(solution)/shard_map/attend_backward/pallas_call | solution.py:27
  142.5 0.8 copy-done.17
  143.3 1.1 slice.100
  144.5 1.0 slice.101
  145.4 0.8 pad_maximum_fusion.2
  146.5 1.3 maximum_maximum_fusion
  147.9 0.2 copy-done.9
  148.1 0.5 copy-done.11
  148.8 1.6 pad_maximum_fusion
  150.5 1.1 copy-done.5
  151.6 0.3 copy-done.7
  151.9 1.5 pad_maximum_fusion.1
  153.5 7.5 %reduce-scatter.7.cloned.1.call-done = bf16[256,512]{1,0:T(8,128)(2,1)} async-done(((bf16[512,512]{1,0:T(8,128)(2,1)}), bf16[256,512]{1,0:T(8,128)(2,1)}) %reduce-scatter.7.cloned.1.call-update) | async-done | bytes 262160 | tf_op jit(solution)/shard_map/reduce_scatter | solution.py:466
  161.0 28.9 %reduce-scatter.5.cloned.1.call-done = bf16[3,512,256]{2,1,0:T(8,128)(2,1)} async-done(((bf16[3,512,512]{2,1,0:T(8,128)(2,1)}), bf16[3,512,256]{2,1,0:T(8,128)(2,1)}) %reduce-scatter.5.cloned.1.call-update) | async-done | bytes 786448 | tf_op jit(solution)/shard_map/reduce_scatter | solution.py:466
  189.9 34.5 %reduce-scatter.9.cloned.1.call-done = bf16[512,1024]{1,0:T(8,128)(2,1)} async-done(((bf16[512,2048]{1,0:T(8,128)(2,1)}), bf16[512,1024]{1,0:T(8,128)(2,1)}) %reduce-scatter.9.cloned.1.call-update) | async-done | bytes 1048592 | tf_op jit(solution)/shard_map/reduce_scatter | solution.py:466
  224.4 34.8 %reduce-scatter.11.cloned.1.call-done = bf16[1024,512]{1,0:T(8,128)(2,1)} async-done(((bf16[2048,512]{1,0:T(8,128)(2,1)}), bf16[1024,512]{1,0:T(8,128)(2,1)}) %reduce-scatter.11.cloned.1.call-update) | async-done | bytes 1048592 | tf_op jit(solution)/shard_map/reduce_scatter | solution.py:466
  259.2 0.6 dynamic-slice
  260.4 5.0 %all-reduce = f32[2048]{0:T(1024)S(1)} all-reduce(f32[2048]{0:T(1024)S(1)} %bitcast.28), channel_id=5, replica_groups=mesh['dp'=16,'mp'=2] {'mp'}, use_global_device_ids=true, to_apply=%region_8.9.clone | all-reduce | flops 2048 | bytes 16384
  265.5 33.1 %psum.54 = f32[1024]{0:T(1024)} all-reduce(f32[1024]{0:T(1024)S(1)} %dynamic-slice.1), channel_id=1, replica_groups=mesh['dp'=16,'mp'=2] {'dp'}, use_global_device_ids=true, to_apply=%region_9.10 | all-reduce | flops 1024 | bytes 8192 | tf_op jit(solution)/shard_map/psum | solution.py:484
  298.6 56.1 %all-reduce.7 = (f32[512,512]{1,0:T(8,128)}, f32[8,512]{1,0:T(8,128)S(1)}) all-reduce(bf16[512,512]{1,0:T(8,128)(2,1)S(1)} %copy-done.18, f32[8,512]{1,0:T(8,128)S(1)} %get-tuple-element.46), channel_id=1, replica_groups=mesh['dp'=16,'mp'=2] {'dp','mp'}, use_global_device_ids=true, to_apply=%region_0.1 | all-reduce | flops 266240 | bytes 1605632 | tf_op jit(solution)/shard_map/psum | solution.py:486
  354.7 0.6 fusion.8
  355.3 15.3 %all-reduce.6.cloned.1.call-done = (bf16[512,3,256]{2,0,1:T(8,128)(2,1)}, bf16[256,512]{1,0:T(8,128)(2,1)}, bf16[512,1024]{1,0:T(8,128)(2,1)}, bf16[1024,512]{1,0:T(8,128)(2,1)}) async-done(((bf16[512,3,256]{2,0,1:T(8,128)(2,1)}, bf16[256,512]{1,0:T(8,128)(2,1)}, bf16[512,1024]{1,0:T(8,128)(2,1)}, bf16[1024,512]{1,0:T(8,128)(2,1)}), (bf16[512,3,256]{2,0,1:T(8,128)(2,1)}, bf16[256,512]{1,0:T(8,128)(2,1)}, ...) | async-done | bytes 3145744 | tf_op jit(solution)/shard_map/psum | solution.py:467
  370.5 2.9 convert_element_type.26
  373.4 1.6 convert_element_type.27
  375.0 1.3 transpose.11
  376.3 0.9 convert_element_type.25
  (89 shorter events, 0.9 us)
Async XLA Ops:
  7.2 3.0 copy-start.29
  7.2 3.0 copy-start.30
  7.2 3.0 copy-start.31
  7.2 3.0 copy-start.32
  7.2 3.0 copy-start.33
  7.2 3.0 copy-start.34
  7.2 3.1 copy-start.28
  7.3 8.4 %copy-start.26 = (bf16[256,512]{1,0:T(8,128)(2,1)S(1)}, bf16[256,512]{1,0:T(8,128)(2,1)}, u32[]{:S(2)}) copy-start(bf16[256,512]{1,0:T(8,128)(2,1)} %param.18) | copy-start | bytes 786436
  7.3 33.3 %all-gather.4.cloned.1.call-start = ((), (), s32[]{:S(2)}) async-start(), calls=%async_computation.4 | async-start | bytes 2359296 | tf_op jit(solution)/shard_map/all_gather | solution.py:387
  8.0 68.8 %all-gather.8.cloned.1.call-start = ((), (), s32[]{:S(2)}) async-start(), calls=%async_computation.6 | async-start | bytes 3145728 | tf_op jit(solution)/shard_map/all_gather | solution.py:391
  8.7 102.7 %all-gather.6.cloned.1.call-start = ((), (), s32[]{:S(2)}) async-start(), calls=%async_computation.5 | async-start | bytes 3145728 | tf_op jit(solution)/shard_map/all_gather | solution.py:389
  9.5 151.5 %reduce-scatter.7.cloned.1.call-start = ((), (), s32[]{:S(2)}) async-start(), calls=%async_computation.8 | async-start | bytes 786432 | tf_op jit(solution)/shard_map/reduce_scatter | solution.py:466
  27.6 14.4 %copy-start = (bf16[512,512]{1,0:T(8,128)(2,1)S(1)}, bf16[512,512]{1,0:T(8,128)(2,1)}, u32[]{:S(2)}) copy-start(bf16[512,512]{1,0:T(8,128)(2,1)} %tokens_ref.5) | copy-start | bytes 1572868
  27.6 14.4 %copy-start.1 = (bf16[512,512]{1,0:T(8,128)(2,1)S(1)}, bf16[512,512]{1,0:T(8,128)(2,1)}, u32[]{:S(2)}) copy-start(bf16[512,512]{1,0:T(8,128)(2,1)} %pos_ref.5) | copy-start | bytes 1572868
  44.7 1.1 copy-start.2
  45.9 0.9 copy-start.13
  50.4 1.0 copy-start.12
  51.4 1.0 copy-start.15
  52.3 0.7 copy-start.20
  111.5 3.1 copy-start.19
  114.5 15.8 %copy-start.14 = (bf16[3,512,256]{2,1,0:T(8,128)(2,1)S(1)}, bf16[3,512,256]{2,1,0:T(8,128)(2,1)}, u32[]{:S(2)}) copy-start(bf16[3,512,256]{2,1,0:T(8,128)(2,1)} %copy-done.13) | copy-start | bytes 2359300
  114.5 15.8 %copy-start.16 = (bf16[3,512,256]{2,1,0:T(8,128)(2,1)S(1)}, bf16[3,512,256]{2,1,0:T(8,128)(2,1)}, u32[]{:S(2)}) copy-start(bf16[3,512,256]{2,1,0:T(8,128)(2,1)} %copy-done.15) | copy-start | bytes 2359300
  114.5 15.8 %copy-start.21 = (bf16[512,256]{1,0:T(8,128)(2,1)S(1)}, bf16[512,256]{1,0:T(8,128)(2,1)}, u32[]{:S(2)}) copy-start(bf16[512,256]{1,0:T(8,128)(2,1)} %copy-done.20) | copy-start | bytes 786436
  127.4 1.0 copy-start.3
  128.4 1.0 copy-start.6
  129.4 1.0 copy-start.10
  130.3 12.2 %copy-start.4 = (bf16[1024,512]{1,0:T(8,128)(2,1)}, bf16[1024,512]{1,0:T(8,128)(2,1)S(1)}, u32[]{:S(2)}) copy-start(bf16[1024,512]{1,0:T(8,128)(2,1)S(1)} %get-tuple-element.50) | copy-start | bytes 3145732
  130.3 12.2 %copy-start.8 = (bf16[1024,512]{1,0:T(8,128)(2,1)}, bf16[1024,512]{1,0:T(8,128)(2,1)S(1)}, u32[]{:S(2)}) copy-start(bf16[1024,512]{1,0:T(8,128)(2,1)S(1)} %get-tuple-element.47) | copy-start | bytes 3145732
  142.5 0.8 copy-start.17
  143.3 3.0 copy-start.23
  143.3 3.0 copy-start.24
  146.3 43.6 %reduce-scatter.5.cloned.1.call-start = ((), (), s32[]{:S(2)}) async-start(), calls=%async_computation.7 | async-start | bytes 2359296 | tf_op jit(solution)/shard_map/reduce_scatter | solution.py:466
  146.5 1.6 copy-start.9
  146.5 2.1 copy-start.11
  147.8 76.5 %reduce-scatter.9.cloned.1.call-start = ((), (), s32[]{:S(2)}) async-start(), calls=%async_computation.9 | async-start | bytes 3145728 | tf_op jit(solution)/shard_map/reduce_scatter | solution.py:466
  150.4 1.2 copy-start.5
  150.4 1.5 copy-start.7
  150.4 108.7 %reduce-scatter.11.cloned.1.call-start = ((), (), s32[]{:S(2)}) async-start(), calls=%async_computation.10 | async-start | bytes 3145728 | tf_op jit(solution)/shard_map/reduce_scatter | solution.py:466
  153.4 105.8 %copy-start.35 = (u32[32]{0:T(128)S(1)}, u32[32]{0:T(128)}, u32[]{:S(2)}) copy-start(u32[32]{0:T(128)} %constant.6) | copy-start | bytes 388
  153.4 145.2 %copy-start.18 = (bf16[512,512]{1,0:T(8,128)(2,1)S(1)}, bf16[512,512]{1,0:T(8,128)(2,1)}, u32[]{:S(2)}) copy-start(bf16[512,512]{1,0:T(8,128)(2,1)} %copy-done.17) | copy-start | bytes 1572868
  153.5 217.1 %all-reduce.6.cloned.1.call-start = ((), (), s32[]{:S(2)}) async-start(), calls=%async_computation.11 | async-start | bytes 6291456 | tf_op jit(solution)/shard_map/psum | solution.py:467
  370.5 2.9 copy-start.22
  373.4 1.6 copy-start.25
  373.4 2.9 copy-start.27
Sparse Core Ops, SparseCore 0:
  9.6 30.8 all-gather.3
  42.1 34.5 all-gather.7
  78.3 33.1 all-gather.5
  146.4 14.5 reduce-scatter.6
  163.7 26.0 reduce-scatter.4
  192.5 31.8 reduce-scatter.8
  227.3 31.8 reduce-scatter.10
  263.1 107.4 all-reduce.5

commit v2 on v1

v2 whole, which is shorter than its diff:
```python
import functools

import jax
import jax.numpy as jnp
from jax import lax
from jax.experimental import pallas as pl
from jax.experimental.pallas import tpu as pltpu
from jax.sharding import Mesh
from jax.sharding import PartitionSpec as P

HD = 64
W_SHORT = 256
W_LONG = 512
ROW = 1024
LANES = 128
EXTRA = 16
CHUNK = 256
EPSILON = 1e-05
MASKED = -1e30
F32 = jnp.float32
BF16 = jnp.bfloat16
MIB = 1024 * 1024
FLOPS_PER_US = 10**9

vmem = pl.BlockSpec(memory_space=pltpu.VMEM)
smem = pl.BlockSpec(memory_space=pltpu.SMEM)
anywhere = pl.BlockSpec(memory_space=pl.ANY)


def call(kernel, outs, args, after=(), scratch=(), us=1, mib=32, smem_args=0, name=None):
    flat, tree = jax.tree.flatten(tuple(args))
    count, extra = len(flat), len(after)

    def flat_kernel(*refs):
        kernel(*jax.tree.unflatten(tree, refs[:count]), *refs[count + extra :])

    return pl.pallas_call(
        flat_kernel,
        out_shape=[
            jax.ShapeDtypeStruct(out, BF16) if isinstance(out[0], int) else jax.ShapeDtypeStruct(*out)
            for out in outs
        ],
        in_specs=[smem] * smem_args + [vmem] * (count - smem_args) + [anywhere] * extra,
        out_specs=[vmem] * len(outs),
        scratch_shapes=[pltpu.VMEM(shape, dtype) for shape, dtype in scratch],
        compiler_params=pltpu.CompilerParams(vmem_limit_bytes=mib * MIB),
        cost_estimate=pl.CostEstimate(
            flops=us * FLOPS_PER_US, bytes_accessed=0, transcendentals=0
        ),
        name=name,
    )(*flat, *after)


def place(axis):
    return lax.axis_index(axis)


def row(ref, start=0, size=None):
    size = ref.shape[0] if size is None else size
    return ref[start : start + size].astype(F32).reshape(1, size)


def mm(a, b):
    return lax.dot_general(a, b, (((1,), (0,)), ((), ())), preferred_element_type=F32)


def mm_nt(a, b):
    return lax.dot_general(a, b, (((1,), (1,)), ((), ())), preferred_element_type=F32)


def mm_tn(a, b):
    return lax.dot_general(a, b, (((0,), (0,)), ((), ())), preferred_element_type=F32)


def position_rows(pos_ref, is_long):
    first = pos_ref[0:W_SHORT, :].astype(F32)
    second = jnp.where(is_long, pos_ref[W_SHORT:W_LONG, :].astype(F32), first)
    return first, second


def hidden_rows(tokens_ref, pos_ref, windows):
    parts = []
    for block, is_long in enumerate(windows):
        first, second = position_rows(pos_ref, is_long)
        start = block * W_LONG
        parts.append(tokens_ref[start : start + W_SHORT, :].astype(F32) + first)
        parts.append(tokens_ref[start + W_SHORT : start + W_LONG, :].astype(F32) + second)
    return jnp.concatenate(parts, axis=0)


def read_windows(win_ref, rows):
    first = place("mp") * rows
    return [
        win_ref[lax.div(first + block * W_LONG, ROW)] == W_LONG for block in range(rows // W_LONG)
    ]


def norm_stats(values):
    average = jnp.mean(values, axis=-1, keepdims=True)
    centred = values - average
    variance = jnp.mean(centred * centred, axis=-1, keepdims=True)
    scale = lax.rsqrt(variance + EPSILON)
    return centred * scale, scale


def norm_grad(grad_hat, hat, scale):
    mean_grad = jnp.mean(grad_hat, axis=-1, keepdims=True)
    mean_both = jnp.mean(grad_hat * hat, axis=-1, keepdims=True)
    return scale * (grad_hat - mean_grad - hat * mean_both)


def head_mask(rows):
    return lax.broadcasted_iota(jnp.int32, (rows, LANES), 1) < HD


def own_head(value, is_low, head):
    zero = jnp.zeros_like(value)
    return jnp.where(is_low, value, zero) if head == 0 else jnp.where(is_low, zero, value)


def attend_forward(hidden_low, weight_ref, windows, mixed_ref, probs_ref, context_ref):
    rows, width = context_ref.shape
    for c in range(3):
        part = mm(hidden_low, weight_ref[c]).astype(BF16)
        mixed_ref[c] = part * BF16(HD**-0.5) if c == 0 else part
    causal = lax.broadcasted_iota(jnp.int32, (W_SHORT, W_SHORT), 0) >= lax.broadcasted_iota(
        jnp.int32, (W_SHORT, W_SHORT), 1
    )
    is_low = head_mask(W_SHORT)
    for block, is_long in enumerate(windows):
        lo = slice(block * W_LONG, block * W_LONG + W_SHORT)
        hi = slice(block * W_LONG + W_SHORT, (block + 1) * W_LONG)
        for pair in range(width // LANES):
            lanes = slice(pair * LANES, (pair + 1) * LANES)
            key_lo, key_hi = mixed_ref[1, lo, lanes], mixed_ref[1, hi, lanes]
            val_lo, val_hi = mixed_ref[2, lo, lanes], mixed_ref[2, hi, lanes]
            query_lo, query_hi = mixed_ref[0, lo, lanes], mixed_ref[0, hi, lanes]
            results = []
            for head in range(2):
                slot = ((block * (width // LANES) + pair) * 2 + head) * 3
                q_lo = own_head(query_lo, is_low, head)
                q_hi = own_head(query_hi, is_low, head)
                s_a = jnp.where(causal, mm_nt(q_lo, key_lo), MASKED)
                e_a = jnp.exp(s_a - jnp.max(s_a, axis=-1, keepdims=True))
                p_a = (e_a * (1.0 / jnp.sum(e_a, axis=-1, keepdims=True))).astype(BF16)
                s_b = jnp.where(is_long, mm_nt(q_hi, key_lo), MASKED)
                s_c = jnp.where(causal, mm_nt(q_hi, key_hi), MASKED)
                top = jnp.max(jnp.maximum(s_b, s_c), axis=-1, keepdims=True)
                e_b = jnp.exp(s_b - top)
                e_c = jnp.exp(s_c - top)
                inverse = 1.0 / jnp.sum(e_b + e_c, axis=-1, keepdims=True)
                p_b = (e_b * inverse).astype(BF16)
                p_c = (e_c * inverse).astype(BF16)
                probs_ref[slot] = p_a
                probs_ref[slot + 1] = p_b
                probs_ref[slot + 2] = p_c
                results.append((mm(p_a, val_lo), mm(p_b, val_lo) + mm(p_c, val_hi)))
            context_ref[lo, lanes] = jnp.where(is_low, results[0][0], results[1][0]).astype(BF16)
            context_ref[hi, lanes] = jnp.where(is_low, results[0][1], results[1][1]).astype(BF16)


def attend_backward(grad_context, mixed_ref, probs_ref, blocks, grad_mixed_ref):
    width = mixed_ref.shape[2]
    is_low = head_mask(W_SHORT)
    for block in range(blocks):
        lo = slice(block * W_LONG, block * W_LONG + W_SHORT)
        hi = slice(block * W_LONG + W_SHORT, (block + 1) * W_LONG)
        for pair in range(width // LANES):
            lanes = slice(pair * LANES, (pair + 1) * LANES)
            q_lo, q_hi = mixed_ref[0, lo, lanes], mixed_ref[0, hi, lanes]
            k_lo, k_hi = mixed_ref[1, lo, lanes], mixed_ref[1, hi, lanes]
            v_lo, v_hi = mixed_ref[2, lo, lanes], mixed_ref[2, hi, lanes]
            g_lo, g_hi = grad_context[lo, lanes], grad_context[hi, lanes]
            results = []
            for head in range(2):
                slot = ((block * (width // LANES) + pair) * 2 + head) * 3
                gm_lo = own_head(g_lo, is_low, head)
                gm_hi = own_head(g_hi, is_low, head)
                pb_a, pb_b, pb_c = probs_ref[slot], probs_ref[slot + 1], probs_ref[slot + 2]
                p_a, p_b, p_c = pb_a.astype(F32), pb_b.astype(F32), pb_c.astype(F32)
                g_a = mm_nt(gm_lo, v_lo)
                g_b = mm_nt(gm_hi, v_lo)
                g_c = mm_nt(gm_hi, v_hi)
                inner_a = jnp.sum(p_a * g_a, axis=-1, keepdims=True)
                inner_b = jnp.sum(p_b * g_b + p_c * g_c, axis=-1, keepdims=True)
                s_a = (p_a * (g_a - inner_a)).astype(BF16)
                s_b = (p_b * (g_b - inner_b)).astype(BF16)
                s_c = (p_c * (g_c - inner_b)).astype(BF16)
                results.append(
                    (
                        mm(s_a, k_lo),
                        mm(s_b, k_lo) + mm(s_c, k_hi),
                        mm_tn(s_a, q_lo) + mm_tn(s_b, q_hi),
                        mm_tn(s_c, q_hi),
                        mm_tn(pb_a, g_lo) + mm_tn(pb_b, g_hi),
                        mm_tn(pb_c, g_hi),
                    )
                )
            both = [jnp.where(is_low, a, b) for a, b in zip(*results)]
            grad_mixed_ref[0, lo, lanes] = (both[0] * HD**-0.5).astype(BF16)
            grad_mixed_ref[0, hi, lanes] = (both[1] * HD**-0.5).astype(BF16)
            grad_mixed_ref[1, lo, lanes] = both[2].astype(BF16)
            grad_mixed_ref[1, hi, lanes] = both[3].astype(BF16)
            grad_mixed_ref[2, lo, lanes] = both[4].astype(BF16)
            grad_mixed_ref[2, hi, lanes] = both[5].astype(BF16)


def normal_parts(x):
    density = jnp.exp(x * x * -0.5)
    t = 1.0 / (1.0 + jnp.abs(x) * 0.23164189)
    poly = t * (
        0.127414796
        + t * (-0.142248368 + t * (0.7107068705 + t * (-0.7265760135 + t * 0.5307027145)))
    )
    tail = poly * density
    return jnp.where(x > 0, 1.0 - tail, tail), density * 0.3989422804


def first_kernel(win_ref, tokens_ref, pos_ref, weight_ref, mixed_ref, probs_ref, context_ref):
    windows = read_windows(win_ref, tokens_ref.shape[0])
    hidden_low = hidden_rows(tokens_ref, pos_ref, windows).astype(BF16)
    attend_forward(hidden_low, weight_ref, windows, mixed_ref, probs_ref, context_ref)


def quarter():
    return place("core") * 2 + place("x")


def part(index, size):
    return pl.ds(pl.multiple_of(index * size, size), size)


def pack_attend_kernel(qkv_ref, out_ref, bias_ref, send_ref):
    _, width, half = qkv_ref.shape
    depth, mine = width // 4, quarter()
    send_ref[0:depth, 0:half] = qkv_ref[0, part(mine, depth), :]
    send_ref[0:depth, half:] = qkv_ref[1, part(mine, depth), :]
    value = qkv_ref[2, part(mine, depth), :]
    send_ref[depth : depth + depth // 2, 0:half] = value[0 : depth // 2]
    send_ref[depth : depth + depth // 2, half:] = value[depth // 2 :]
    start = depth + depth // 2
    send_ref[start : 2 * depth, :] = out_ref[part(mine, depth // 2), :]
    for i in range(EXTRA):
        index = i if (i + 1) * width <= bias_ref.shape[0] else 0
        send_ref[2 * depth + i : 2 * depth + i + 1, :] = row(bias_ref, index * width, width).astype(
            BF16
        )


def pack_ffn_kernel(up_ref, down_ref, up_to, down_to):
    width, units = up_ref.shape
    depth, mine = width // 4, quarter()
    for i in range(units // width):
        up_to[i * depth : (i + 1) * depth, :] = up_ref[
            part(mine, depth), i * width : (i + 1) * width
        ]
    down_to[...] = down_ref[part(mine, units // 4), :]


def places(pieces):
    x, core = place("x"), place("core")
    from_y, from_x, core_y, core_x = pieces
    return (
        (from_y, core * 2 + x),
        (from_x, core * 2 + 1 - x),
        (core_y, (1 - core) * 2 + x),
        (core_x, (1 - core) * 2 + 1 - x),
    )


def second_kernel(
    win_ref,
    tokens_ref,
    pos_ref,
    pieces,
    context_own_ref,
    out_own_ref,
    out_bias_ref,
    mixed_ref,
    probs_ref,
    context_ref,
    resid_ref,
    w_oth_ref,
    out_oth_ref,
    bias_oth_ref,
):
    width = tokens_ref.shape[1]
    half, depth = width // 2, width // 4
    windows = read_windows(win_ref, tokens_ref.shape[0])
    if len(pieces) == 4:
        for ref, index in places(pieces):
            rows = part(index, depth)
            w_oth_ref[0, rows, :] = ref[0:depth, 0:half]
            w_oth_ref[1, rows, :] = ref[0:depth, half:]
            middle = depth + depth // 2
            w_oth_ref[2, part(index * 2, depth // 2), :] = ref[depth:middle, 0:half]
            w_oth_ref[2, part(index * 2 + 1, depth // 2), :] = ref[depth:middle, half:]
            out_oth_ref[part(index, depth // 2), :] = ref[middle : 2 * depth, :]
        for i in range(bias_oth_ref.shape[0] // width):
            bias_row = pieces[0][2 * depth + i : 2 * depth + i + 1, :].astype(F32)
            bias_oth_ref[i * width : (i + 1) * width] = bias_row.reshape(width)
    else:
        w_oth_ref[...] = pieces[0][...]
        out_oth_ref[...] = pieces[1][...]
        bias_oth_ref[...] = pieces[2][...].astype(F32)
    hidden_in = hidden_rows(tokens_ref, pos_ref, windows)
    attend_forward(
        hidden_in.astype(BF16), w_oth_ref, windows, mixed_ref, probs_ref, context_ref
    )
    branch = mm(context_own_ref[...], out_own_ref[...]) + mm(context_ref[...], out_oth_ref[...])
    hidden_in = hidden_rows(tokens_ref, pos_ref, windows)
    resid_ref[...] = hidden_in + branch + row(out_bias_ref)


def core_split(whole_ref, keep_ref, send_ref, start, split):
    half = whole_ref.shape[0] // 2
    core = place("core") if split else 0
    keep_ref[start : start + half, :] = whole_ref[part(core, half), :]
    send_ref[start : start + half, :] = whole_ref[part(1 - core, half), :]


def ffn_forward(low_ref, up_ref, bias_ref, act_ref, slope_ref):
    for start in range(0, up_ref.shape[1], CHUNK):
        cols = slice(start, start + CHUNK)
        pre = mm(low_ref[...], up_ref[:, cols]) + row(bias_ref, start, CHUNK)
        total, density = normal_parts(pre)
        act_ref[:, cols] = (pre * total).astype(BF16)
        slope_ref[:, cols] = (total + pre * density).astype(BF16)


def ffn_own_kernel(
    resid_ref,
    up_ref,
    down_ref,
    bias_ref,
    gain_ref,
    shift_ref,
    low_ref,
    act_ref,
    slope_ref,
    branch_ref,
):
    hat, _ = norm_stats(resid_ref[...])
    normed = hat * row(gain_ref) + row(shift_ref)
    low_ref[...] = normed.astype(BF16)
    ffn_forward(low_ref, up_ref, bias_ref, act_ref, slope_ref)
    branch_ref[...] = normed + mm(act_ref[...], down_ref[...])


def ffn_other_kernel(
    split,
    cot_ref,
    low_ref,
    act_own_ref,
    branch_ref,
    up_refs,
    down_refs,
    bias_ref,
    down_bias_ref,
    gain_ref,
    shift_ref,
    layer_ref,
    keep_ref,
    send_ref,
    slope_ref,
    up_ref,
    down_ref,
    grad_ref,
    vec_ref,
    act_ref,
    package_ref,
):
    width = cot_ref.shape[1]
    units = up_ref.shape[1]
    if len(up_refs) == 4:
        for ref, index in places(up_refs):
            depth = ref.shape[0] * width // units
            for i in range(units // width):
                up_ref[part(index, depth), i * width : (i + 1) * width] = ref[
                    i * depth : (i + 1) * depth, :
                ]
        for ref, index in places(down_refs):
            down_ref[part(index, ref.shape[0]), :] = ref[...]
    else:
        up_ref[...] = up_refs[0][...]
        down_ref[...] = down_refs[0][...]
    ffn_forward(low_ref, up_ref, bias_ref, act_ref, slope_ref)
    resid = branch_ref[...] + mm(act_ref[...], down_ref[...]) + row(down_bias_ref)
    hat, scale = norm_stats(resid)
    layer_ref[...] = (hat * row(gain_ref) + row(shift_ref)).astype(BF16)
    cot = cot_ref[...].astype(F32)
    vec_ref[1:2, :] = jnp.sum(cot * hat, axis=0, keepdims=True)
    vec_ref[2:3, :] = jnp.sum(cot, axis=0, keepdims=True)
    grad = norm_grad(cot * row(gain_ref), hat, scale)
    vec_ref[0:1, :] = jnp.sum(grad, axis=0, keepdims=True)
    grad_ref[...] = grad
    grad_low = grad.astype(BF16)
    for half, act in ((0, act_own_ref), (1, act_ref)):
        for start in range(0, units, CHUNK):
            cols = slice(start, start + CHUNK)
            package_ref[cols, :] = mm_tn(act[:, cols], grad_low).astype(BF16)
        core_split(package_ref, keep_ref, send_ref, half * (units // 2), split)


def ffn_back_kernel(
    split,
    resid_ref,
    grad_ref,
    low_ref,
    slopes,
    ups,
    downs,
    vec_ref,
    gain_ref,
    keep_ref,
    send_ref,
    small_ref,
    grad_resid_ref,
    work_ref,
    total_ref,
    package_ref,
    bias_sum_ref,
):
    width = resid_ref.shape[1]
    units = ups[0].shape[1]
    grad_low = grad_ref[...].astype(BF16)
    for half in range(2):
        for start in range(0, units, CHUNK):
            cols = slice(start, start + CHUNK)
            grad_act = mm_nt(grad_low, downs[half][cols, :])
            pre_grad = (grad_act * slopes[half][:, cols].astype(F32)).astype(BF16)
            work_ref[:, cols] = pre_grad
            at = half * (units // width) + start // width
            bias_sum_ref[at : at + 1, start % width : start % width + CHUNK] = jnp.sum(
                pre_grad.astype(F32), axis=0, keepdims=True
            )
        for start in range(0, units, width):
            cols = slice(start, start + width)
            package_ref[cols, :] = mm_tn(low_ref[...], work_ref[:, cols]).astype(BF16)
        core_split(package_ref, keep_ref, send_ref, half * (units // 2), split)
        before = grad_ref[...] if half == 0 else total_ref[...]
        total_ref[...] = before + mm_nt(work_ref[...], ups[half][...])
    grad = total_ref[...]
    hat, scale = norm_stats(resid_ref[...])
    small_ref[1:2, :] = jnp.sum(grad * hat, axis=0, keepdims=True)
    small_ref[2:3, :] = jnp.sum(grad, axis=0, keepdims=True)
    grad = norm_grad(grad * row(gain_ref), hat, scale)
    small_ref[0:1, :] = jnp.sum(grad, axis=0, keepdims=True)
    small_ref[3:6, :] = vec_ref[0:3, :]
    span = units // width
    first_half = (place("mp") if split else 0) == 0
    ours, theirs = bias_sum_ref[0:span, :], bias_sum_ref[span : 2 * span, :]
    small_ref[6 : 6 + span, :] = jnp.where(first_half, ours, theirs)
    small_ref[6 + span : 6 + 2 * span, :] = jnp.where(first_half, theirs, ours)
    used = 6 + 2 * span
    small_ref[used:, :] = jnp.zeros((small_ref.shape[0] - used, width), F32)
    keep_ref[units:, :] = small_ref[...].astype(BF16)
    send_ref[units:, :] = small_ref[...].astype(BF16)
    grad_resid_ref[...] = grad


def half_backward(
    split,
    hidden_low,
    grad_low,
    weight_ref,
    out_ref,
    mixed_ref,
    probs_ref,
    context_ref,
    keep_ref,
    send_ref,
    gm_ref,
    package_ref,
):
    rows, width = hidden_low.shape
    half_width = width // 2
    package_ref[width + half_width :, :] = mm_tn(context_ref[...], grad_low).astype(BF16)
    grad_context = mm_nt(grad_low, out_ref[...]).astype(BF16)
    attend_backward(grad_context, mixed_ref, probs_ref, rows // W_LONG, gm_ref)
    package_ref[0:width, 0:half_width] = mm_tn(hidden_low, gm_ref[0]).astype(BF16)
    package_ref[0:width, half_width:] = mm_tn(hidden_low, gm_ref[1]).astype(BF16)
    value_grad = mm_tn(hidden_low, gm_ref[2]).astype(BF16)
    package_ref[width : width + half_width, 0:half_width] = value_grad[0:half_width, :]
    package_ref[width : width + half_width, half_width:] = value_grad[half_width:, :]
    core_split(package_ref, keep_ref, send_ref, 0, split)
    return (
        mm_nt(gm_ref[0], weight_ref[0])
        + mm_nt(gm_ref[1], weight_ref[1])
        + mm_nt(gm_ref[2], weight_ref[2])
    )


def attend_back_kernel(
    split,
    win_ref,
    tokens_ref,
    pos_ref,
    grad_resid_ref,
    own_refs,
    other_refs,
    other_keep_ref,
    other_send_ref,
    own_keep_ref,
    own_send_ref,
    table_keep_ref,
    table_send_ref,
    tokens_grad_ref,
    grad_ref,
    gm_ref,
    package_ref,
    table_ref,
):
    rows, width = tokens_ref.shape
    windows = read_windows(win_ref, rows)
    hidden_low = hidden_rows(tokens_ref, pos_ref, windows).astype(BF16)
    grad_low = grad_resid_ref[...].astype(BF16)
    for before_ref, refs, to_refs in (
        (grad_resid_ref, other_refs, (other_keep_ref, other_send_ref)),
        (grad_ref, own_refs, (own_keep_ref, own_send_ref)),
    ):
        part_grad = half_backward(
            split, hidden_low, grad_low, *refs, *to_refs, gm_ref, package_ref
        )
        grad_ref[...] = before_ref[...] + part_grad
    grad = grad_ref[...]
    tokens_grad_ref[...] = grad.astype(BF16)
    first, second = None, None
    for block, is_long in enumerate(windows):
        top = grad[block * W_LONG : block * W_LONG + W_SHORT]
        bottom = grad[block * W_LONG + W_SHORT : (block + 1) * W_LONG]
        zero = jnp.zeros_like(top)
        part_first = top + jnp.where(is_long, zero, bottom)
        part_second = jnp.where(is_long, bottom, zero)
        first = part_first if first is None else first + part_first
        second = part_second if second is None else second + part_second
    table_ref[0:W_SHORT, :] = first.astype(BF16)
    table_ref[W_SHORT:, :] = second.astype(BF16)
    core_split(table_ref, table_keep_ref, table_send_ref, 0, split)


def total_of(*values):
    total = values[0].astype(F32)
    for value in values[1:]:
        total = total + value.astype(F32)
    return total


def bit_split(bit, value, work_ref, keep_ref, send_ref, start=0):
    half = value.shape[0] // 2
    work_ref[...] = value.astype(BF16)
    keep_ref[start : start + half, :] = work_ref[part(bit, half), :]
    send_ref[start : start + half, :] = work_ref[part(1 - bit, half), :]


def z_bit():
    return lax.rem(place("z"), 2)


def other_half_kernel(keep_ref, recv_ref, send_ref):
    start = keep_ref.shape[0] - send_ref.shape[0]
    send_ref[...] = total_of(keep_ref[start:, :], recv_ref[start:, :]).astype(BF16)


def down_split_kernel(keep_ref, recv_ref, from_y_ref, x_keep_ref, x_send_ref, work_ref):
    rows = from_y_ref.shape[0]
    total = total_of(keep_ref[0:rows, :], recv_ref[0:rows, :], from_y_ref[...])
    bit_split(place("x"), total, work_ref, x_keep_ref, x_send_ref)


def pair_kernel(a_ref, b_ref, out_ref):
    out_ref[...] = total_of(a_ref[...], b_ref[...]).astype(BF16)


def spread_kernel(parts_ref, out_ref):
    total = total_of(*[parts_ref[i] for i in range(parts_ref.shape[0])]).astype(BF16)
    for i in range(out_ref.shape[0]):
        out_ref[i] = total


def up_split_kernel(keep_ref, recv_ref, x_keep_ref, x_send_ref, work_ref):
    rows = work_ref.shape[0]
    for half in range(2):
        rows_of = slice(half * rows, (half + 1) * rows)
        total = total_of(keep_ref[rows_of, :], recv_ref[rows_of, :])
        start = half * (rows // 2)
        bit_split(place("x"), total, work_ref, x_keep_ref, x_send_ref, start)
    small = total_of(keep_ref[2 * rows :, :], recv_ref[2 * rows :, :]).astype(BF16)
    x_keep_ref[rows:, :] = small
    x_send_ref[rows:, :] = small


def down_x_kernel(keep_ref, recv_ref, z_keep_ref, z_send_ref, work_ref):
    bit_split(z_bit(), total_of(keep_ref[...], recv_ref[...]), work_ref, z_keep_ref, z_send_ref)


def up_x_kernel(keep_ref, recv_ref, z_keep_ref, z_send_ref, work_ref):
    rows = work_ref.shape[0]
    for half in range(2):
        rows_of = slice(half * rows, (half + 1) * rows)
        total = total_of(keep_ref[rows_of, :], recv_ref[rows_of, :])
        bit_split(z_bit(), total, work_ref, z_keep_ref, z_send_ref, half * (rows // 2))
    small = total_of(keep_ref[2 * rows :, :], recv_ref[2 * rows :, :]).astype(BF16)
    z_keep_ref[rows:, :] = small
    z_send_ref[rows:, :] = small


def up_z_kernel(keep_ref, recv_ref, y_keep_ref, y_send_ref):
    rows = y_keep_ref.shape[0] - EXTRA
    y_keep_ref[0:rows, :] = total_of(keep_ref[0:rows, :], recv_ref[0:rows, :]).astype(BF16)
    y_send_ref[...] = total_of(keep_ref[rows:, :], recv_ref[rows:, :]).astype(BF16)
    y_keep_ref[rows:, :] = y_send_ref[rows:, :]


def up_last_kernel(own_ref, recv_ref, out_ref, *small_refs):
    *vector_refs, bias_ref, work_ref = small_refs
    rows, width = out_ref.shape
    out_ref[...] = total_of(own_ref[0:rows, :], recv_ref[0:rows, :]).astype(BF16)
    work_ref[...] = total_of(own_ref[rows:, :], recv_ref[rows:, :])
    for i, ref in enumerate(vector_refs):
        ref[...] = work_ref[i : i + 1, :].reshape(width)
    span = bias_ref.shape[0] // width
    for i in range(span):
        value = work_ref[pl.ds(6 + place("mp") * span + i, 1), :]
        bias_ref[i * width : (i + 1) * width] = value.reshape(width)


def join_kernel(own_ref, recv_ref, out_ref):
    rows = own_ref.shape[0]
    out_ref[part(z_bit(), rows), :] = own_ref[...]
    out_ref[part(1 - z_bit(), rows), :] = recv_ref[...]


def attend_core_kernel(
    keep_ref, recv_ref, table_keep_ref, table_recv_ref, to_y_ref, table_ref, work_ref
):
    rows = keep_ref.shape[0]
    to_y_ref[0:rows, :] = total_of(keep_ref[...], recv_ref[...]).astype(BF16)
    total = total_of(table_keep_ref[...], table_recv_ref[...])
    bit_split(place("mp"), total, work_ref, table_ref, to_y_ref.at[rows:, :])


def attend_pieces_kernel(keep_ref, recv_ref, from_y_ref, table_ref, out_ref):
    devices, rows, _ = out_ref.shape
    size = keep_ref.shape[0]
    piece = size // devices
    spare = rows - piece
    for i in range(devices):
        rows_of = slice(i * piece, (i + 1) * piece)
        out_ref[i, 0:piece, :] = total_of(
            keep_ref[rows_of, :], recv_ref[rows_of, :], from_y_ref[rows_of, :]
        ).astype(BF16)
        rows_of = slice(i * spare, (i + 1) * spare)
        other = from_y_ref[size + i * spare : size + (i + 1) * spare, :]
        out_ref[i, piece:, :] = total_of(table_ref[rows_of, :], other).astype(BF16)


def spread_kernel(parts_ref, out_ref):
    total = total_of(*[parts_ref[i] for i in range(parts_ref.shape[0])]).astype(BF16)
    for i in range(out_ref.shape[0]):
        out_ref[i] = total


def cut_kernel(parts_ref, out_ref):
    devices, rows, _ = parts_ref.shape
    size = out_ref.shape[0] // devices
    for i in range(devices):
        out_ref[i * size : (i + 1) * size, :] = parts_ref[i, rows - size :, :]


def down_out_kernel(own_ref, from_x_ref, core_own_ref, core_x_ref, out_ref):
    x, core = place("x"), place("core")
    rows = own_ref.shape[0]
    for ref, at_x, at_core in (
        (own_ref, x, core),
        (from_x_ref, 1 - x, core),
        (core_own_ref, x, 1 - core),
        (core_x_ref, 1 - x, 1 - core),
    ):
        start = pl.multiple_of((at_core * 2 + at_x) * rows, rows)
        out_ref[pl.ds(start, rows), :] = ref[...].astype(F32)


def up_out_kernel(own_ref, from_x_ref, core_own_ref, core_x_ref, out_ref):
    x, core = place("x"), place("core")
    rows, width = own_ref.shape
    for index in range(2):
        cols = slice(index * width, (index + 1) * width)
        mine = core == index
        for a_ref, b_ref, at_x in ((own_ref, core_own_ref, x), (from_x_ref, core_x_ref, 1 - x)):
            start = pl.multiple_of(at_x * rows, rows)
            out_ref[pl.ds(start, rows), cols] = jnp.where(
                mine, a_ref[...].astype(F32), b_ref[...].astype(F32)
            )


def attend_out_kernel(own_ref, recv_ref, qkv_ref, out_ref):
    first_core = place("core") == 0
    devices, rows, width = own_ref.shape
    half = width // 2
    piece = width // devices
    for i in range(devices):
        ours, theirs = own_ref[i, 0:piece].astype(F32), recv_ref[i, 0:piece].astype(F32)
        low = jnp.where(first_core, ours, theirs)
        high = jnp.where(first_core, theirs, ours)
        rows_of = slice(i * piece, (i + 1) * piece)
        qkv_ref[0, rows_of, :] = low[:, 0:half]
        qkv_ref[1, rows_of, :] = low[:, half:]
        if i < devices // 2:
            qkv_ref[2, rows_of, :] = high[:, 0:half]
            qkv_ref[2, half + i * piece : half + (i + 1) * piece, :] = high[:, half:]
        else:
            out_ref[(i - devices // 2) * piece : (i - devices // 2 + 1) * piece, :] = high


def table_out_kernel(own_ref, from_y_ref, core_own_ref, core_y_ref, out_ref):
    y, core = place("mp"), place("core")
    rows = own_ref.shape[0]
    for ref, at_y, at_core in (
        (own_ref, y, core),
        (from_y_ref, 1 - y, core),
        (core_own_ref, y, 1 - core),
        (core_y_ref, 1 - y, 1 - core),
    ):
        out_ref[part(at_core * 2 + at_y, rows), :] = ref[...].astype(F32)


def swap(value, axis, name="swap", distance=1):
    pairs = [(i, i ^ distance) for i in range(lax.axis_size(axis))]
    with jax.named_scope(f"{name}_{axis}{distance}"):
        return lax.ppermute(value, axis, pairs)


def exchange(value, axes, name="exchange"):
    with jax.named_scope(name):
        return lax.all_to_all(value, axes, 0, 0, tiled=True)


class Chain:
    def __init__(self):
        self.last = ()

    def gate(self, value):
        value = pl.pallas_call(
            lambda *refs: None,
            out_shape=jax.ShapeDtypeStruct(value.shape, value.dtype),
            in_specs=[anywhere] * (1 + len(self.last)),
            out_specs=anywhere,
            input_output_aliases={0: 0},
            compiler_params=pltpu.CompilerParams(vmem_limit_bytes=MIB),
            cost_estimate=pl.CostEstimate(
                flops=FLOPS_PER_US, bytes_accessed=0, transcendentals=0
            ),
            name="gate",
        )(value, *self.last)
        self.last = (value,)
        return value

    def __call__(self, kernel, outs, args, us, name, scratch=(), smem_args=0):
        mib = 28 if us > 2 else 8
        results = call(kernel, outs, args, self.last, scratch, us, mib, smem_args, name)
        self.last = (min(results, key=lambda value: value.size),)
        return results


def per_device(
    fast,
    mp_size,
    tokens,
    pos_table,
    qkv_weight,
    out_weight,
    out_bias,
    norm1_gain,
    norm1_shift,
    up_weight,
    up_bias,
    down_weight,
    down_bias,
    norm2_gain,
    norm2_shift,
    window,
    cotangent,
):
    step = Chain()
    rows, width = tokens.shape
    blocks = rows // W_LONG
    half_width = width // 2
    units = up_weight.shape[1] * mp_size // 2
    n, spare = width, W_LONG // 2
    qkv_weight = jnp.transpose(qkv_weight, (1, 0, 2))
    wide = ((rows, width), F32)

    attend_outs = [
        (3, rows, half_width),
        (blocks * half_width // HD * 3, W_SHORT, W_SHORT),
        (rows, half_width),
    ]

    def attend_own():
        return step(
            first_kernel,
            attend_outs,
            [window, tokens, pos_table, w_own],
            3,
            "attend_first",
            smem_args=1,
        )

    def attend_other():
        return step(
            second_kernel,
            attend_outs
            + [wide, (3, width, half_width), (half_width, width), ((units,), F32)],
            [window, tokens, pos_table, attend_in, context_own, out_own, out_bias],
            5,
            "attend_second",
            smem_args=1,
        )

    def ffn_own():
        return step(
            ffn_own_kernel,
            [(rows, width), (rows, units), (rows, units), wide],
            [resid, up_own, down_own, bias_own, norm1_gain, norm1_shift],
            4,
            "ffn_own",
        )

    if fast:
        w_own, out_own, up_own, down_own = qkv_weight, out_weight, up_weight, down_weight
        bias_own = up_bias
        (message,) = step(
            pack_attend_kernel,
            [(width // 2 + EXTRA, width)],
            [qkv_weight, out_weight, up_bias],
            1,
            "pack_attend",
        )
        attend_y = swap(message, "mp", "attend_y")
        up_message, down_message = step(
            pack_ffn_kernel,
            [(units // 4, width), (units // 4, width)],
            [up_weight, down_weight],
            1,
            "pack_ffn",
        )
        up_y = swap(up_message, "mp", "up_y")
        down_y = swap(down_message, "mp", "down_y")
        attend_y = step.gate(attend_y)
        attend_x = swap(attend_y, "x", "attend_x")
        attend_cy = swap(attend_y, "core", "attend_cy")
        mixed_own, probs_own, context_own = attend_own()
        up_y = step.gate(up_y)
        up_x = swap(up_y, "x", "up_x")
        up_cy = swap(up_y, "core", "up_cy")
        attend_x = step.gate(attend_x)
        attend_cx = swap(attend_x, "core", "attend_cx")
        down_y = step.gate(down_y)
        down_x = swap(down_y, "x", "down_x")
        down_cy = swap(down_y, "core", "down_cy")
        attend_in = (attend_y, attend_x, attend_cy, attend_cx)
        mixed_oth, probs_oth, context_oth, resid, w_oth, out_oth, bias_oth = attend_other()
        up_x = step.gate(up_x)
        up_cx = swap(up_x, "core", "up_cx")
        low, act_own, slope_own, branch = ffn_own()
        down_x = step.gate(down_x)
        down_cx = swap(down_x, "core", "down_cx")
        up_in = (up_y, up_x, up_cy, up_cx)
        down_in = (down_y, down_x, down_cy, down_cx)
    else:
        qkv = lax.all_gather(qkv_weight, "mp", axis=2, tiled=True)
        out_w = lax.all_gather(out_weight, "mp", axis=0, tiled=True)
        up_w = lax.all_gather(up_weight, "mp", axis=1, tiled=True)
        bias = lax.all_gather(up_bias, "mp", axis=0, tiled=True)
        down_w = lax.all_gather(down_weight, "mp", axis=0, tiled=True)
        w_own, out_own = qkv[:, :, :half_width], out_w[:half_width]
        attend_in = (qkv[:, :, half_width:], out_w[half_width:], bias[units:])
        up_own, up_in = up_w[:, :units], (up_w[:, units:],)
        down_own, down_in = down_w[:units], (down_w[units:],)
        bias_own = bias[:units]
        mixed_own, probs_own, context_own = attend_own()
        mixed_oth, probs_oth, context_oth, resid, w_oth, out_oth, bias_oth = attend_other()
        low, act_own, slope_own, branch = ffn_own()

    layer_out, down_keep, down_send, slope_oth, up_oth, down_oth, grad2, vec = step(
        functools.partial(ffn_other_kernel, fast),
        [
            (rows, width),
            (units, width),
            (units, width),
            (rows, units),
            (width, units),
            (units, width),
            wide,
            ((8, width), F32),
        ],
        [
            cotangent,
            low,
            act_own,
            branch,
            up_in,
            down_in,
            bias_oth,
            down_bias,
            norm2_gain,
            norm2_shift,
        ],
        6,
        "ffn_other",
        scratch=[((rows, units), BF16), ((units, width), BF16)],
    )
    down_recv = swap(down_send, "core", "down_recv") if fast else None
    up_keep, up_send, small, grad1 = step(
        functools.partial(ffn_back_kernel, fast),
        [
            (units + EXTRA, width),
            (units + EXTRA, width),
            ((EXTRA, width), F32),
            wide,
        ],
        [
            resid,
            grad2,
            low,
            (slope_own, slope_oth),
            (up_own, up_oth),
            (down_own, down_oth),
            vec,
            norm1_gain,
        ],
        6,
        "ffn_back",
        scratch=[
            ((rows, units), BF16),
            ((rows, width), F32),
            ((units, width), BF16),
            ((8, width), F32),
        ],
    )

    def attend_back():
        return step(
            functools.partial(attend_back_kernel, fast),
            [(n, width)] * 4 + [(spare, width)] * 2 + [(rows, width)],
            [
                window,
                tokens,
                pos_table,
                grad1,
                (w_own, out_own, mixed_own, probs_own, context_own),
                (w_oth, out_oth, mixed_oth, probs_oth, context_oth),
            ],
            13,
            "attend_back",
            scratch=[
                ((rows, width), F32),
                ((3, rows, half_width), BF16),
                ((2 * n, width), BF16),
                ((W_LONG, width), BF16),
            ],
            smem_args=1,
        )

    if not fast:
        *att_parts, grad_tokens = attend_back()
        qkv_g, out_g, up_g, down_g, small, table = reduce_plain(
            n, width, down_keep, down_send, up_keep, up_send, small, *att_parts
        )
        vectors = [small[i] for i in range(6)]
        bias_all = small[6 : 6 + 2 * units // width].reshape(-1)
        start = lax.axis_index("mp") * up_bias.shape[0]
        bias_g = lax.dynamic_slice_in_dim(bias_all, start, up_bias.shape[0])
    else:
        zx = lax.axis_size("z") * lax.axis_size("x")
        half, piece, strip = n // 2, n // 4, spare // 2
        up_recv = swap(up_send, "core", "up_recv")
        (to_y,) = step(other_half_kernel, [(n, width)], [down_keep, down_recv], 1, "down_core")
        down_from_y = swap(to_y, "mp", "down_from_y")
        up_x, to_x = step(
            up_split_kernel,
            [(n + EXTRA, width)] * 2,
            [up_keep, up_recv],
            2,
            "up_core",
            scratch=[((n, width), BF16)],
        )
        up_from_x = swap(to_x, "x", "up_from_x")
        oth_keep, oth_send, own_keep, own_send, tab_keep, tab_send, grad_tokens = attend_back()
        oth_recv = swap(oth_send, "core", "oth_recv")
        tab_recv = swap(tab_send, "core", "tab_recv")
        own_recv = swap(own_send, "core", "own_recv")
        down_x, to_x = step(
            down_split_kernel,
            [(half, width)] * 2,
            [down_keep, down_recv, down_from_y],
            1,
            "down_mp",
            scratch=[((n, width), BF16)],
        )
        down_from_x = swap(to_x, "x", "down_from_x")
        up_z, to_z = step(
            up_x_kernel,
            [(half + EXTRA, width)] * 2,
            [up_x, up_from_x],
            1,
            "up_x",
            scratch=[((half, width), BF16)],
        )
        up_from_z = swap(to_z, "z", "up_from_z")
        to_y, table = step(
            attend_core_kernel,
            [(n + strip, width), (strip, width)],
            [oth_keep, oth_recv, tab_keep, tab_recv],
            1,
            "attend_core",
            scratch=[((spare, width), BF16)],
        )
        att_from_y = swap(to_y, "mp", "att_from_y")
        down_z, to_z = step(
            down_x_kernel,
            [(piece, width)] * 2,
            [down_x, down_from_x],
            1,
            "down_x",
            scratch=[((half, width), BF16)],
        )
        down_from_z = swap(to_z, "z", "down_from_z")
        up_y, to_y = step(
            up_z_kernel, [(piece + EXTRA, width)] * 2, [up_z, up_from_z], 1, "up_z"
        )
        up_from_y = swap(to_y, "mp", "up_from_y")
        (down_z,) = step(pair_kernel, [(piece, width)], [down_z, down_from_z], 1, "down_z")
        down_far = swap(down_z, "z", "down_far", 2)
        (att,) = step(
            attend_pieces_kernel,
            [(zx, (n + strip) // zx, width)],
            [own_keep, own_recv, att_from_y, table],
            1,
            "attend_mp",
        )
        att = exchange(att, ("z", "x"), "att_parts")
        (up_y,) = step(pair_kernel, [(piece + EXTRA, width)], [up_y, up_from_y], 1, "up_mp")
        up_far = swap(up_y, "z", "up_far", 2)
        (down_z,) = step(pair_kernel, [(piece, width)], [down_z, down_far], 1, "down_far")
        down_near = swap(down_z, "z", "down_near")
        (down_z,) = step(join_kernel, [(half, width)], [down_z, down_near], 1, "down_join")
        down_x = swap(down_z, "x", "down_x")
        up_z, *vectors, bias_g = step(
            up_last_kernel,
            [(piece, width)] + [((width,), F32)] * 6 + [((up_bias.shape[0],), F32)],
            [up_y, up_far],
            1,
            "up_far",
            scratch=[((EXTRA, width), F32)],
        )
        up_near = swap(up_z, "z", "up_near")
        (att,) = step(spread_kernel, [att.shape], [att], 1, "attend_sum")
        att = exchange(att, ("z", "x"), "att_sums")
        (up_z,) = step(join_kernel, [(half, width)], [up_z, up_near], 1, "up_join")
        up_x = swap(up_z, "x", "up_x")
        down_x = step.gate(down_x)
        (down_g,) = step(
            down_out_kernel,
            [((2 * n, width), F32)],
            [
                down_z,
                down_x,
                swap(down_z, "core", "down_core"),
                swap(down_x, "core", "down_core_x"),
            ],
            2,
            "down_out",
        )
        up_x = step.gate(up_x)
        (up_g,) = step(
            up_out_kernel,
            [((width, 2 * n), F32)],
            [up_z, up_x, swap(up_z, "core", "up_core"), swap(up_x, "core", "up_core_x")],
            2,
            "up_out",
        )
        (table,) = step(cut_kernel, [(strip, width)], [att], 1, "table_cut")
        table_y = swap(table, "mp", "table_y")
        qkv_g, out_g = step(
            attend_out_kernel,
            [((3, width, half_width), F32), ((half_width, width), F32)],
            [att, swap(att, "core", "att_core")],
            2,
            "attend_out",
        )
        (table,) = step(
            table_out_kernel,
            [((W_LONG, width), F32)],
            [
                table,
                table_y,
                swap(table, "core", "table_core"),
                swap(table_y, "core", "table_core_y"),
            ],
            1,
            "table_out",
        )
    return (
        layer_out,
        grad_tokens,
        table,
        jnp.transpose(qkv_g, (1, 0, 2)),
        out_g,
        vectors[0],
        vectors[1],
        vectors[2],
        up_g,
        bias_g,
        down_g,
        vectors[3],
        vectors[4],
        vectors[5],
    )


def reduce_plain(
    n,
    width,
    down_keep,
    down_send,
    up_keep,
    up_send,
    small,
    other_keep,
    other_send,
    own_keep,
    own_send,
    table_keep,
    table_send,
):
    def halves(keep, send):
        first = jnp.concatenate([keep[:n], send[:n]], axis=0)
        second = jnp.concatenate([keep[n : 2 * n], send[n : 2 * n]], axis=0)
        return first, second

    def summed(own, oth, make, dim):
        whole = jnp.concatenate([make(own), make(oth)], axis=dim)
        part = lax.psum_scatter(whole, "mp", scatter_dimension=dim, tiled=True)
        return lax.psum(part, "dp").astype(F32)

    def qkv_part(g):
        value = jnp.concatenate(
            [g[n : n + n // 2, : n // 2], g[n : n + n // 2, n // 2 :]], axis=0
        )
        return jnp.stack([g[:n, : n // 2], g[:n, n // 2 :], value])

    def up_part(g):
        return jnp.concatenate([g[s : s + n] for s in range(0, g.shape[0], n)], axis=1)

    att_oth = jnp.concatenate([other_keep, other_send], axis=0)
    att_own = jnp.concatenate([own_keep, own_send], axis=0)
    up_own, up_oth = halves(up_keep, up_send)
    down_own, down_oth = halves(down_keep, down_send)
    table = jnp.concatenate([table_keep, table_send], axis=0).astype(F32)
    return (
        summed(att_own, att_oth, qkv_part, 2),
        summed(att_own, att_oth, lambda g: g[n + n // 2 :], 0),
        summed(up_own, up_oth, up_part, 1),
        summed(down_own, down_oth, lambda g: g, 0),
        lax.psum(small, ("dp", "mp")),
        lax.psum(table, ("dp", "mp")),
    )


def solution(mesh):
    mp_size = mesh.shape["mp"]
    fast = mp_size == 2 and mesh.shape["dp"] == 16
    dp = "dp"
    if fast:
        shape = (mesh.shape["dp"] // 4, 2, 2, mp_size)
        mesh = Mesh(mesh.devices.reshape(shape), ("z", "x", "core", "mp"))
        dp = ("z", "x", "core")
    both = P((*dp, "mp") if fast else (dp, "mp"), None)
    placed = (
        both,
        P(),
        P(None, None, "mp"),
        P("mp", None),
        P(),
        P(),
        P(),
        P(None, "mp"),
        P("mp"),
        P("mp", None),
        P(),
        P(),
        P(),
        P(dp),
        both,
    )
    return jax.shard_map(
        functools.partial(per_device, fast, mp_size),
        mesh=mesh,
        in_specs=placed,
        out_specs=(
            both,
            both,
            P(),
            P(None, None, "mp"),
            P("mp", None),
            P(),
            P(),
            P(),
            P(None, "mp"),
            P("mp"),
            P("mp", None),
            P(),
            P(),
            P(),
        ),
        check_vma=False,
    )
```

time: 384 us -> 166 us (0.43)
  waiting for transfers between devices: 191 us -> 72.4 us
  blocking collectives: 111 us -> 0 us
  starting transfers between devices: 0.32 us -> 44.5 us
  between operations: 15.8 us -> 1.62 us
  local copies, waits for them, and re-layouts: 21.9 us -> 8.34 us
  other arithmetic: 11.9 us -> 0 us
  Pallas kernels: 31.3 us -> 38.2 us
    reduce_scatter x4 -> x0, waiting for transfers between devices: 106 us -> none  [summed(): part = lax.psum_scatter(whole, 'mp', scatter_dimension=dim, tiled=True)]
    psum x2 -> x0, blocking collectives: 89.2 us -> none  [the longest x1 56.1 us: per_device(): table = lax.psum(table.astype(F32), ('dp', 'mp'))]
    ppermute x0 -> x38, waiting for transfers between devices: none -> 72.4 us  [swap(): return lax.ppermute(value, axis, pairs)]
    all_gather x3 -> x0, waiting for transfers between devices: 68.3 us -> none  [the longest x1 31.7 us: per_device(): up_w = lax.all_gather(up_weight, 'mp', axis=1, tiled=True)]
    ppermute x0 -> x38, starting transfers between devices: none -> 34.2 us  [swap(): return lax.ppermute(value, axis, pairs)]
    all_gather x2 -> x0, blocking collectives: 17.3 us -> none  [the longest x1 12 us: per_device(): out_w = lax.all_gather(out_weight, 'mp', axis=0, tiled=True)]
    psum x1 -> x0, waiting for transfers between devices: 15.3 us -> none  [summed(): return lax.psum(part, 'dp').astype(F32)]
    slice x9 -> x0, local copies, waits for them, and re-layouts: 10.5 us -> none  [the longest x1 3.07 us: per_device(): up_own, up_oth = (up_w[:, :units], up_w[:, units:])]
  transfers between devices with their start and end apart: 8 -> 40, of which waited for: 8 -> 20; matrix products, arithmetic and copies ran while one was open for 3% -> 0% of each run, Pallas kernels for 2% -> 18%
where the time goes in v2:
time: 166 us; the launch traced here: 165 us
  waiting for transfers between devices  72.4 us (44%)
  starting transfers between devices  44.5 us (27%)
  Pallas kernels  38.2 us (23%)
  local copies, waits for them, and re-layouts  8.34 us (5%)
    ppermute x38, waiting for transfers between devices, swap(): return lax.ppermute(value, axis, pairs)  72.4 us
    pallas_call x28, Pallas kernels, call(): pl.pallas_call(flat_kernel, out_shape=[jax.ShapeDtypeStruct(out, BF16) if...  38.2 us
    ppermute x38, starting transfers between devices, swap(): return lax.ppermute(value, axis, pairs)  34.2 us
    all_to_all x2, starting transfers between devices, exchange(): return lax.all_to_all(value, axes, 0, 0, tiled=True)  10.4 us
    unnamed x42, local copies, waits for them, and re-layouts  8.34 us
  transfers between devices with their start and end apart: 40, of which 20 were waited for; matrix products, arithmetic and copies ran while one was open for 0% of the time, Pallas kernels for 18%

profile of v2, /device:TPU:0, one launch (start us, length us, event | category | flops | bytes accessed | tf_op | source)
XLA Modules:
  0.0 165.1 jit_solution(5520671106818963114)
XLA Ops:
  0.7 1.1 copy-done.2
  3.5 3.0 %collective-permute-start = (bf16[272,512]{1,0:T(8,128)(2,1)S(1)}, bf16[272,512]{1,0:T(8,128)(2,1)S(1)}, u32[]{:S(2)}, u32[]{:S(2)}) collective-permute-start(bf16[272,512]{1,0:T(8,128)(2,1)S(1)} %pack_attend.1.refs_2_), channel_id=1, source_target_pairs={{0,1},{1,0},{2,3},{3,2},{4,5},{5,4},{6,7},{7,6},{8,9},{9,8},{10,11... | collective-permute-start | bytes 835592 | tf_op jit(solution)/shard_map/attend_y_mp1/ppermute | solution.py:731
  6.5 1.5 collective-permute-start.5
  9.3 4.7 %collective-permute-done.refs_0_ = bf16[272,512]{1,0:T(8,128)(2,1)S(1)} collective-permute-done((bf16[272,512]{1,0:T(8,128)(2,1)S(1)}, bf16[272,512]{1,0:T(8,128)(2,1)S(1)}, u32[]{:S(2)}, u32[]{:S(2)}) %collective-permute-start) | collective-permute-done | bytes 278560 | tf_op jit(solution)/shard_map/attend_y_mp1/ppermute | solution.py:731
  14.0 2.0 %collective-permute-start.1 = (bf16[272,512]{1,0:T(8,128)(2,1)S(1)}, bf16[272,512]{1,0:T(8,128)(2,1)S(1)}, u32[]{:S(2)}, u32[]{:S(2)}) collective-permute-start(bf16[272,512]{1,0:T(8,128)(2,1)S(1)} %gate.8.refs_4_.refs_3_), channel_id=1, source_target_pairs={{0,4},{4,0},{1,5},{5,1},{2,6},{6,2},{3,7},{7,3},{8,12},{12,8},{9,1... | collective-permute-start | bytes 835592 | tf_op jit(solution)/shard_map/attend_x_x1/ppermute | solution.py:731
  16.0 2.6 %attend_first.1 = (bf16[3,512,256]{2,1,0:T(8,128)(2,1)S(1)}, bf16[12,256,256]{2,1,0:T(8,128)(2,1)S(1)}, bf16[512,256]{1,0:T(8,128)(2,1)S(1)}) custom-call(s32[1]{0:T(128)S(6)} %copy.45.refs_0_, bf16[512,512]{1,0:T(8,128)(2,1)S(1)} %copy-done.5, bf16[512,512]{1,0:T(8,128)(2,1)S(1)} %copy-done.6, bf16[3,512,256]{2,1,0:T(8,128)(2,1)S(1)} %bitcast.3, ...), custom_call_target="tpu_custom_call" | custom-call | flops 3000000000 | tf_op jit(solution)/shard_map/attend_first/pallas_call | solution.py:37
  18.7 5.7 %collective-permute-done.2.refs_0_ = bf16[256,512]{1,0:T(8,128)(2,1)S(1)} collective-permute-done((bf16[256,512]{1,0:T(8,128)(2,1)S(1)}, bf16[256,512]{1,0:T(8,128)(2,1)S(1)}, u32[]{:S(2)}, u32[]{:S(2)}) %collective-permute-start.2) | collective-permute-done | bytes 262176 | tf_op jit(solution)/shard_map/up_y_mp1/ppermute | solution.py:731
  25.0 1.7 %collective-permute-start.6 = (bf16[256,512]{1,0:T(8,128)(2,1)S(1)}, bf16[256,512]{1,0:T(8,128)(2,1)S(1)}, u32[]{:S(2)}, u32[]{:S(2)}) collective-permute-start(bf16[256,512]{1,0:T(8,128)(2,1)S(1)} %gate.9.refs_1_.refs_4_), channel_id=1, source_target_pairs={{0,4},{4,0},{1,5},{5,1},{2,6},{6,2},{3,7},{7,3},{8,12},{12,8},{9,1... | collective-permute-start | bytes 786440 | tf_op jit(solution)/shard_map/up_x_x1/ppermute | solution.py:731
  27.1 3.1 %attend_second.1 = (bf16[3,512,256]{2,1,0:T(8,128)(2,1)S(1)}, bf16[12,256,256]{2,1,0:T(8,128)(2,1)S(1)}, bf16[512,256]{1,0:T(8,128)(2,1)S(1)}, f32[512,512]{1,0:...) custom-call(s32[1]{0:T(128)S(6)} %copy.45.refs_0_, ...), custom_call_target="tpu_custom_call" | custom-call | flops 5000000000 | tf_op jit(solution)/shard_map/attend_second/pallas_call | solution.py:37
  30.2 4.0 %collective-permute-done.6.refs_0_ = bf16[256,512]{1,0:T(8,128)(2,1)S(1)} collective-permute-done((bf16[256,512]{1,0:T(8,128)(2,1)S(1)}, bf16[256,512]{1,0:T(8,128)(2,1)S(1)}, u32[]{:S(2)}, u32[]{:S(2)}) %collective-permute-start.6) | collective-permute-done | bytes 262176 | tf_op jit(solution)/shard_map/up_x_x1/ppermute | solution.py:731
  34.9 3.2 %ffn_own.1 = (bf16[512,512]{1,0:T(8,128)(2,1)S(1)}, bf16[512,1024]{1,0:T(8,128)(2,1)S(1)}, bf16[512,1024]{1,0:T(8,128)(2,1)S(1)}, f32[512,512]{1,0:T(8,128)S(1)}) custom-call(f32[512,512]{1,0:T(8,128)S(1)} %get-tuple-element.74.refs_0_, bf16[512,1024]{1,0:T(8,128)(2,1)S(1)} %copy-done, bf16[1024,512]{1,0:T(8,128)(2,1)S(1)} %copy-done.1, ...), custom_call_target="tpu_custom_call" | custom-call | flops 4000000000 | tf_op jit(solution)/shard_map/ffn_own/pallas_call | solution.py:37
  39.0 1.5 collective-permute-done.11.refs_11_
  40.5 4.9 %ffn_other.1 = (bf16[512,512]{1,0:T(8,128)(2,1)}, bf16[1024,512]{1,0:T(8,128)(2,1)S(1)}, bf16[1024,512]{1,0:T(8,128)(2,1)S(1)}, bf16[512,1024]{1,0:T(8,128)(2,1)...) custom-call(bf16[512,512]{1,0:T(8,128)(2,1)S(1)} %copy-done.4, ...), custom_call_target="tpu_custom_call" | custom-call | flops 6000000000 | tf_op jit(solution)/shard_map/ffn_other/pallas_call | solution.py:37
  45.7 4.2 %ffn_back.1 = (bf16[1040,512]{1,0:T(8,128)(2,1)S(1)}, bf16[1040,512]{1,0:T(8,128)(2,1)S(1)}, f32[16,512]{1,0:T(8,128)S(1)}, f32[512,512]{1,0:T(8,128)S(1)}) custom-call(f32[512,512]{1,0:T(8,128)S(1)} %get-tuple-element.74.refs_0_, f32[512,512]{1,0:T(8,128)S(1)} %get-tuple-element.80.refs_1_, bf16[512,512]{1,0:T(8,128)(2,1)S(1)} %get-tuple-element.76.refs_1_.refs_2_, ...), custom_call_target="tpu_custom_call" | custom-call | flops 6000000000 | tf_op jit(solution)/shard_map/ffn_back/pallas_call | solution.py:37
  50.5 1.8 %collective-permute-start.18 = (bf16[512,512]{1,0:T(8,128)(2,1)S(1)}, bf16[512,512]{1,0:T(8,128)(2,1)S(1)}, u32[]{:S(2)}, u32[]{:S(2)}) collective-permute-start(bf16[512,512]{1,0:T(8,128)(2,1)S(1)} %down_core.1.refs_2_), channel_id=1, source_target_pairs={{0,1},{1,0},{2,3},{3,2},{4,5},{5,4},{6,7},{7,6},{8,9},{9,8},{10,11... | collective-permute-start | bytes 1572872 | tf_op jit(solution)/shard_map/down_from_y_mp1/ppermute | solution.py:731
  53.3 1.8 %collective-permute-start.17 = (bf16[528,512]{1,0:T(8,128)(2,1)S(1)}, bf16[528,512]{1,0:T(8,128)(2,1)S(1)}, u32[]{:S(2)}, u32[]{:S(2)}) collective-permute-start(bf16[528,512]{1,0:T(8,128)(2,1)S(1)} %get-tuple-element.107), channel_id=1, source_target_pairs={{0,4},{4,0},{1,5},{5,1},{2,6},{6,2},{3,7},{7,3},{8,12},{12,8},{9,1... | collective-permute-start | bytes 1622024 | tf_op jit(solution)/shard_map/up_from_x_x1/ppermute | solution.py:731
  55.1 9.7 %attend_back.1 = (bf16[512,512]{1,0:T(8,128)(2,1)S(1)}, bf16[512,512]{1,0:T(8,128)(2,1)S(1)}, bf16[512,512]{1,0:T(8,128)(2,1)S(1)}, bf16[512,512]{1,0:T(8,128)(2...) custom-call(s32[1]{0:T(128)S(6)} %copy.45.refs_0_, ...), custom_call_target="tpu_custom_call" | custom-call | flops 12999999488 | tf_op jit(solution)/shard_map/attend_back/pallas_call | solution.py:37
  65.7 2.2 %collective-permute-done.17.refs_1_ = bf16[528,512]{1,0:T(8,128)(2,1)S(1)} collective-permute-done((bf16[528,512]{1,0:T(8,128)(2,1)S(1)}, bf16[528,512]{1,0:T(8,128)(2,1)S(1)}, u32[]{:S(2)}, u32[]{:S(2)}) %collective-permute-start.17) | collective-permute-done | bytes 540704 | tf_op jit(solution)/shard_map/up_from_x_x1/ppermute | solution.py:731
  68.6 1.8 %collective-permute-start.19 = (bf16[640,512]{1,0:T(8,128)(2,1)S(1)}, bf16[640,512]{1,0:T(8,128)(2,1)S(1)}, u32[]{:S(2)}, u32[]{:S(2)}) collective-permute-start(bf16[640,512]{1,0:T(8,128)(2,1)S(1)} %get-tuple-element.110), channel_id=1, source_target_pairs={{0,1},{1,0},{2,3},{3,2},{4,5},{5,4},{6,7},{7,6},{8,9},{9,8},{10,11... | collective-permute-start | bytes 1966088 | tf_op jit(solution)/shard_map/att_from_y_mp1/ppermute | solution.py:731
  70.4 1.5 collective-permute-start.20
  71.9 1.6 collective-permute-start.22
  73.4 4.4 %collective-permute-done.20.refs_1_ = bf16[256,512]{1,0:T(8,128)(2,1)S(1)} collective-permute-done((bf16[256,512]{1,0:T(8,128)(2,1)S(1)}, bf16[256,512]{1,0:T(8,128)(2,1)S(1)}, u32[]{:S(2)}, u32[]{:S(2)}) %collective-permute-start.20) | collective-permute-done | bytes 262176 | tf_op jit(solution)/shard_map/down_from_x_x1/ppermute | solution.py:731
  78.0 1.7 %collective-permute-start.21 = (bf16[128,512]{1,0:T(8,128)(2,1)S(1)}, bf16[128,512]{1,0:T(8,128)(2,1)S(1)}, u32[]{:S(2)}, u32[]{:S(2)}) collective-permute-start(bf16[128,512]{1,0:T(8,128)(2,1)S(1)} %get-tuple-element.114), channel_id=1, source_target_pairs={{0,8},{8,0},{16,24},{24,16},{1,9},{9,1},{17,25},{25,17},{2,10},{10... | collective-permute-start | bytes 393224 | tf_op jit(solution)/shard_map/down_from_z_z1/ppermute | solution.py:731
  79.7 1.6 collective-permute-done.22.refs_1_
  81.4 2.3 %collective-permute-done.21.refs_1_ = bf16[128,512]{1,0:T(8,128)(2,1)S(1)} collective-permute-done((bf16[128,512]{1,0:T(8,128)(2,1)S(1)}, bf16[128,512]{1,0:T(8,128)(2,1)S(1)}, u32[]{:S(2)}, u32[]{:S(2)}) %collective-permute-start.21) | collective-permute-done | bytes 131104 | tf_op jit(solution)/shard_map/down_from_z_z1/ppermute | solution.py:731
  83.8 1.1 collective-permute-done.19.refs_2_
  84.9 1.1 attend_mp.1.refs_2_
  85.9 6.0 %all-to-all-start = ((bf16[8,80,512]{2,1,0:T(8,128)(2,1)}), bf16[8,80,512]{2,1,0:T(8,128)(2,1)S(1)}, u32[]{:S(2)}, u32[]{:S(2)}) async-start(bf16[8,80,512]{2,1,0:T(8,128)(2,1)} %attend_mp.1.refs_2_), calls=%async_computation | async-start | bytes 1310720 | tf_op jit(solution)/shard_map/att_parts/all_to_all | solution.py:736
  91.9 1.5 collective-permute-start.23
  93.4 2.9 %collective-permute-start.25 = (bf16[128,512]{1,0:T(8,128)(2,1)S(1)}, bf16[128,512]{1,0:T(8,128)(2,1)S(1)}, u32[]{:S(2)}, u32[]{:S(2)}) collective-permute-start(bf16[128,512]{1,0:T(8,128)(2,1)S(1)} %down_z.1.refs_4_.refs_0_), channel_id=1, source_target_pairs={{0,16},{8,24},{16,0},{24,8},{1,17},{9,25},{17,1},{25,9},{2,18},{10... | collective-permute-start | bytes 393224 | tf_op jit(solution)/shard_map/down_far_z2/ppermute | solution.py:731
  97.1 16.6 %collective-permute-done.25.refs_1_ = bf16[128,512]{1,0:T(8,128)(2,1)S(1)} collective-permute-done((bf16[128,512]{1,0:T(8,128)(2,1)S(1)}, bf16[128,512]{1,0:T(8,128)(2,1)S(1)}, u32[]{:S(2)}, u32[]{:S(2)}) %collective-permute-start.25) | collective-permute-done | bytes 131104 | tf_op jit(solution)/shard_map/down_far_z2/ppermute | solution.py:731
  113.8 1.7 %collective-permute-start.24 = (bf16[144,512]{1,0:T(8,128)(2,1)S(1)}, bf16[144,512]{1,0:T(8,128)(2,1)S(1)}, u32[]{:S(2)}, u32[]{:S(2)}) collective-permute-start(bf16[144,512]{1,0:T(8,128)(2,1)S(1)} %up_mp.1.refs_2_.refs_0_), channel_id=1, source_target_pairs={{0,16},{8,24},{16,0},{24,8},{1,17},{9,25},{17,1},{25,9},{2,18},{10... | collective-permute-start | bytes 442376 | tf_op jit(solution)/shard_map/up_far_z2/ppermute | solution.py:731
  115.5 3.9 %collective-permute-done.26.refs_1_ = bf16[128,512]{1,0:T(8,128)(2,1)S(1)} collective-permute-done((bf16[128,512]{1,0:T(8,128)(2,1)S(1)}, bf16[128,512]{1,0:T(8,128)(2,1)S(1)}, u32[]{:S(2)}, u32[]{:S(2)}) %collective-permute-start.26) | collective-permute-done | bytes 131104 | tf_op jit(solution)/shard_map/down_near_z1/ppermute | solution.py:731
  119.5 2.8 %collective-permute-done.24.refs_1_ = bf16[144,512]{1,0:T(8,128)(2,1)S(1)} collective-permute-done((bf16[144,512]{1,0:T(8,128)(2,1)S(1)}, bf16[144,512]{1,0:T(8,128)(2,1)S(1)}, u32[]{:S(2)}, u32[]{:S(2)}) %collective-permute-start.24) | collective-permute-done | bytes 147488 | tf_op jit(solution)/shard_map/up_far_z2/ppermute | solution.py:731
  124.5 4.4 %all-to-all-start.1 = ((bf16[8,80,512]{2,1,0:T(8,128)(2,1)}), bf16[8,80,512]{2,1,0:T(8,128)(2,1)S(1)}, u32[]{:S(2)}, u32[]{:S(2)}) async-start(bf16[8,80,512]{2,1,0:T(8,128)(2,1)} %attend_sum.1.refs_2_), calls=%async_computation.1 | async-start | bytes 1310720 | tf_op jit(solution)/shard_map/att_sums/all_to_all | solution.py:736
  128.9 2.0 %collective-permute-start.29 = (bf16[256,512]{1,0:T(8,128)(2,1)S(1)}, bf16[256,512]{1,0:T(8,128)(2,1)S(1)}, u32[]{:S(2)}, u32[]{:S(2)}) collective-permute-start(bf16[256,512]{1,0:T(8,128)(2,1)S(1)} %down_join.1.refs_2_.refs_0_), channel_id=1, source_target_pairs={{0,4},{4,0},{1,5},{5,1},{2,6},{6,2},{3,7},{7,3},{8,12},{12,8},{9,1... | collective-permute-start | bytes 786440 | tf_op jit(solution)/shard_map/down_x_x1/ppermute | solution.py:731
  130.9 1.5 collective-permute-start.27
  132.4 8.4 %collective-permute-done.27.refs_1_ = bf16[128,512]{1,0:T(8,128)(2,1)S(1)} collective-permute-done((bf16[128,512]{1,0:T(8,128)(2,1)S(1)}, bf16[128,512]{1,0:T(8,128)(2,1)S(1)}, u32[]{:S(2)}, u32[]{:S(2)}) %collective-permute-start.27) | collective-permute-done | bytes 131104 | tf_op jit(solution)/shard_map/up_near_z1/ppermute | solution.py:731
  142.4 1.5 down_out.1.refs_1_
  143.8 5.7 %collective-permute-done.28.refs_0_ = bf16[256,512]{1,0:T(8,128)(2,1)S(1)} collective-permute-done((bf16[256,512]{1,0:T(8,128)(2,1)S(1)}, bf16[256,512]{1,0:T(8,128)(2,1)S(1)}, u32[]{:S(2)}, u32[]{:S(2)}) %collective-permute-start.28) | collective-permute-done | bytes 262176 | tf_op jit(solution)/shard_map/up_x_x1/ppermute | solution.py:731
  149.6 1.6 copy-done.17
  152.7 1.5 up_out.1.refs_1_
  154.2 1.6 copy-done.18
  155.8 1.6 collective-permute-start.34
  157.4 4.0 %collective-permute-done.34.refs_1_ = bf16[128,512]{1,0:T(8,128)(2,1)S(1)} collective-permute-done((bf16[128,512]{1,0:T(8,128)(2,1)S(1)}, bf16[128,512]{1,0:T(8,128)(2,1)S(1)}, u32[]{:S(2)}, u32[]{:S(2)}) %collective-permute-start.34) | collective-permute-done | bytes 131104 | tf_op jit(solution)/shard_map/table_y_mp1/ppermute | solution.py:731
  161.5 1.5 attend_out.1
  163.0 1.0 copy-done.19
  164.0 1.0 table_out.1
  (110 shorter events, 14.9 us)
Async XLA Ops:
  3.4 3.1 %copy-start = (bf16[512,1024]{1,0:T(8,128)(2,1)S(1)}, bf16[512,1024]{1,0:T(8,128)(2,1)}, u32[]{:S(2)}) copy-start(bf16[512,1024]{1,0:T(8,128)(2,1)} %refs_5_.4) | copy-start | bytes 3145732
  3.4 3.1 %copy-start.1 = (bf16[1024,512]{1,0:T(8,128)(2,1)S(1)}, bf16[1024,512]{1,0:T(8,128)(2,1)}, u32[]{:S(2)}) copy-start(bf16[1024,512]{1,0:T(8,128)(2,1)} %refs_7_.1) | copy-start | bytes 3145732
  3.5 10.5 %collective-permute-start = (bf16[272,512]{1,0:T(8,128)(2,1)S(1)}, bf16[272,512]{1,0:T(8,128)(2,1)S(1)}, u32[]{:S(2)}, u32[]{:S(2)}) collective-permute-start(bf16[272,512]{1,0:T(8,128)(2,1)S(1)} %pack_attend.1.refs_2_), channel_id=1, source_target_pairs={{0,1},{1,0},{2,3},{3,2},{4,5},{5,4},{6,7},{7,6},{8,9},{9,8},{10,11... | collective-permute-start | bytes 835592 | tf_op jit(solution)/shard_map/attend_y_mp1/ppermute | solution.py:731
  6.5 20.2 %collective-permute-start.5 = (bf16[256,512]{1,0:T(8,128)(2,1)S(1)}, bf16[256,512]{1,0:T(8,128)(2,1)S(1)}, u32[]{:S(2)}, u32[]{:S(2)}) collective-permute-start(bf16[256,512]{1,0:T(8,128)(2,1)S(1)} %get-tuple-element.73), channel_id=1, source_target_pairs={{0,1},{1,0},{2,3},{3,2},{4,5},{5,4},{6,7},{7,6},{8,9},{9,8},{10,11... | collective-permute-start | bytes 786440 | tf_op jit(solution)/shard_map/down_y_mp1/ppermute | solution.py:731
  8.0 16.4 %collective-permute-start.2 = (bf16[256,512]{1,0:T(8,128)(2,1)S(1)}, bf16[256,512]{1,0:T(8,128)(2,1)S(1)}, u32[]{:S(2)}, u32[]{:S(2)}) collective-permute-start(bf16[256,512]{1,0:T(8,128)(2,1)S(1)} %get-tuple-element.71.refs_1_), channel_id=1, source_target_pairs={{0,1},{1,0},{2,3},{3,2},{4,5},{5,4},{6,7},{7,6},{8,9},{9,8},{10,11... | collective-permute-start | bytes 786440 | tf_op jit(solution)/shard_map/up_y_mp1/ppermute | solution.py:731
  9.3 6.7 %copy-start.3 = (bf16[512,3,256]{2,0,1:T(8,128)(2,1)S(1)}, bf16[512,3,256]{2,0,1:T(8,128)(2,1)}, u32[]{:S(2)}) copy-start(bf16[512,3,256]{2,0,1:T(8,128)(2,1)} %param.17) | copy-start | bytes 2359300
  9.3 6.7 %copy-start.5 = (bf16[512,512]{1,0:T(8,128)(2,1)S(1)}, bf16[512,512]{1,0:T(8,128)(2,1)}, u32[]{:S(2)}) copy-start(bf16[512,512]{1,0:T(8,128)(2,1)} %refs_1_.11) | copy-start | bytes 1572868
  9.3 6.7 %copy-start.6 = (bf16[512,512]{1,0:T(8,128)(2,1)S(1)}, bf16[512,512]{1,0:T(8,128)(2,1)}, u32[]{:S(2)}) copy-start(bf16[512,512]{1,0:T(8,128)(2,1)} %refs_2_.9) | copy-start | bytes 1572868
  14.0 12.7 %collective-permute-start.3 = (bf16[272,512]{1,0:T(8,128)(2,1)S(1)}, bf16[272,512]{1,0:T(8,128)(2,1)S(1)}, u32[]{:S(2)}, u32[]{:S(2)}) collective-permute-start(bf16[272,512]{1,0:T(8,128)(2,1)S(1)} %gate.8.refs_4_.refs_3_), channel_id=1, source_target_pairs={{0,2},{2,0},{1,3},{3,1},{4,6},{6,4},{5,7},{7,5},{8,10},{10,8},{9,1... | collective-permute-start | bytes 835592 | tf_op jit(solution)/shard_map/attend_cy_core1/ppermute | solution.py:731
  14.0 10.4 %collective-permute-start.1 = (bf16[272,512]{1,0:T(8,128)(2,1)S(1)}, bf16[272,512]{1,0:T(8,128)(2,1)S(1)}, u32[]{:S(2)}, u32[]{:S(2)}) collective-permute-start(bf16[272,512]{1,0:T(8,128)(2,1)S(1)} %gate.8.refs_4_.refs_3_), channel_id=1, source_target_pairs={{0,4},{4,0},{1,5},{5,1},{2,6},{6,2},{3,7},{7,3},{8,12},{12,8},{9,1... | collective-permute-start | bytes 835592 | tf_op jit(solution)/shard_map/attend_x_x1/ppermute | solution.py:731
  24.4 2.7 %copy-start.8 = (bf16[256,512]{1,0:T(8,128)(2,1)S(1)}, bf16[256,512]{1,0:T(8,128)(2,1)}, u32[]{:S(2)}) copy-start(bf16[256,512]{1,0:T(8,128)(2,1)} %refs_5_.5) | copy-start | bytes 786436
  24.4 2.7 %copy-start.11 = (bf16[512]{0:T(512)(128)(2,1)S(1)}, bf16[512]{0:T(512)(128)(2,1)}, u32[]{:S(2)}) copy-start(bf16[512]{0:T(512)(128)(2,1)} %refs_9_.1) | copy-start | bytes 3076
  24.4 2.7 %collective-permute-start.4 = (bf16[272,512]{1,0:T(8,128)(2,1)S(1)}, bf16[272,512]{1,0:T(8,128)(2,1)S(1)}, u32[]{:S(2)}, u32[]{:S(2)}) collective-permute-start(bf16[272,512]{1,0:T(8,128)(2,1)S(1)} %gate.10.refs_1_.refs_4_), channel_id=1, source_target_pairs={{0,2},{2,0},{1,3},{3,1},{4,6},{6,4},{5,7},{7,5},{8,10},{10,8},{9,1... | collective-permute-start | bytes 835592 | tf_op jit(solution)/shard_map/attend_cx_core1/ppermute | solution.py:731
  24.5 14.5 %collective-permute-start.7 = (bf16[256,512]{1,0:T(8,128)(2,1)S(1)}, bf16[256,512]{1,0:T(8,128)(2,1)S(1)}, u32[]{:S(2)}, u32[]{:S(2)}) collective-permute-start(bf16[256,512]{1,0:T(8,128)(2,1)S(1)} %gate.9.refs_1_.refs_4_), channel_id=1, source_target_pairs={{0,2},{2,0},{1,3},{3,1},{4,6},{6,4},{5,7},{7,5},{8,10},{10,8},{9,1... | collective-permute-start | bytes 786440 | tf_op jit(solution)/shard_map/up_cy_core1/ppermute | solution.py:731
  25.0 9.2 %collective-permute-start.6 = (bf16[256,512]{1,0:T(8,128)(2,1)S(1)}, bf16[256,512]{1,0:T(8,128)(2,1)S(1)}, u32[]{:S(2)}, u32[]{:S(2)}) collective-permute-start(bf16[256,512]{1,0:T(8,128)(2,1)S(1)} %gate.9.refs_1_.refs_4_), channel_id=1, source_target_pairs={{0,4},{4,0},{1,5},{5,1},{2,6},{6,2},{3,7},{7,3},{8,12},{12,8},{9,1... | collective-permute-start | bytes 786440 | tf_op jit(solution)/shard_map/up_x_x1/ppermute | solution.py:731
  26.7 12.3 %collective-permute-start.10 = (bf16[256,512]{1,0:T(8,128)(2,1)S(1)}, bf16[256,512]{1,0:T(8,128)(2,1)S(1)}, u32[]{:S(2)}, u32[]{:S(2)}) collective-permute-start(bf16[256,512]{1,0:T(8,128)(2,1)S(1)} %gate.11.refs_10_.refs_8_), channel_id=1, source_target_pairs={{0,2},{2,0},{1,3},{3,1},{4,6},{6,4},{5,7},{7,5},{8,10},{10,8},{9,1... | collective-permute-start | bytes 786440 | tf_op jit(solution)/shard_map/down_cy_core1/ppermute | solution.py:731
  26.7 12.2 %collective-permute-start.9 = (bf16[256,512]{1,0:T(8,128)(2,1)S(1)}, bf16[256,512]{1,0:T(8,128)(2,1)S(1)}, u32[]{:S(2)}, u32[]{:S(2)}) collective-permute-start(bf16[256,512]{1,0:T(8,128)(2,1)S(1)} %gate.11.refs_10_.refs_8_), channel_id=1, source_target_pairs={{0,4},{4,0},{1,5},{5,1},{2,6},{6,2},{3,7},{7,3},{8,12},{12,8},{9,1... | collective-permute-start | bytes 786440 | tf_op jit(solution)/shard_map/down_x_x1/ppermute | solution.py:731
  34.1 4.9 %collective-permute-start.8 = (bf16[256,512]{1,0:T(8,128)(2,1)S(1)}, bf16[256,512]{1,0:T(8,128)(2,1)S(1)}, u32[]{:S(2)}, u32[]{:S(2)}) collective-permute-start(bf16[256,512]{1,0:T(8,128)(2,1)S(1)} %gate.12.refs_6_.refs_5_), channel_id=1, source_target_pairs={{0,2},{2,0},{1,3},{3,1},{4,6},{6,4},{5,7},{7,5},{8,10},{10,8},{9,1... | collective-permute-start | bytes 786440 | tf_op jit(solution)/shard_map/up_cx_core1/ppermute | solution.py:731
  38.9 1.6 copy-start.15
  38.9 1.6 collective-permute-start.11
  45.5 4.9 %collective-permute-start.13 = (bf16[1024,512]{1,0:T(8,128)(2,1)S(1)}, bf16[1024,512]{1,0:T(8,128)(2,1)S(1)}, u32[]{:S(2)}, u32[]{:S(2)}) collective-permute-start(bf16[1024,512]{1,0:T(8,128)(2,1)S(1)} %get-tuple-element.97), channel_id=1, source_target_pairs={{0,2},{2,0},{1,3},{3,1},{4,6},{6,4},{5,7},{7,5},{8,10},{10,8},{9,1... | collective-permute-start | bytes 3145736 | tf_op jit(solution)/shard_map/down_recv_core1/ppermute | solution.py:731
  49.9 2.8 %collective-permute-start.12 = (bf16[1040,512]{1,0:T(8,128)(2,1)S(1)}, bf16[1040,512]{1,0:T(8,128)(2,1)S(1)}, u32[]{:S(2)}, u32[]{:S(2)}) collective-permute-start(bf16[1040,512]{1,0:T(8,128)(2,1)S(1)} %get-tuple-element.95), channel_id=1, source_target_pairs={{0,2},{2,0},{1,3},{3,1},{4,6},{6,4},{5,7},{7,5},{8,10},{10,8},{9,1... | collective-permute-start | bytes 3194888 | tf_op jit(solution)/shard_map/up_recv_core1/ppermute | solution.py:731
  50.5 14.8 %collective-permute-start.18 = (bf16[512,512]{1,0:T(8,128)(2,1)S(1)}, bf16[512,512]{1,0:T(8,128)(2,1)S(1)}, u32[]{:S(2)}, u32[]{:S(2)}) collective-permute-start(bf16[512,512]{1,0:T(8,128)(2,1)S(1)} %down_core.1.refs_2_), channel_id=1, source_target_pairs={{0,1},{1,0},{2,3},{3,2},{4,5},{5,4},{6,7},{7,6},{8,9},{9,8},{10,11... | collective-permute-start | bytes 1572872 | tf_op jit(solution)/shard_map/down_from_y_mp1/ppermute | solution.py:731
  53.3 14.6 %collective-permute-start.17 = (bf16[528,512]{1,0:T(8,128)(2,1)S(1)}, bf16[528,512]{1,0:T(8,128)(2,1)S(1)}, u32[]{:S(2)}, u32[]{:S(2)}) collective-permute-start(bf16[528,512]{1,0:T(8,128)(2,1)S(1)} %get-tuple-element.107), channel_id=1, source_target_pairs={{0,4},{4,0},{1,5},{5,1},{2,6},{6,2},{3,7},{7,3},{8,12},{12,8},{9,1... | collective-permute-start | bytes 1622024 | tf_op jit(solution)/shard_map/up_from_x_x1/ppermute | solution.py:731
  64.8 3.4 %collective-permute-start.15 = (bf16[512,512]{1,0:T(8,128)(2,1)S(1)}, bf16[512,512]{1,0:T(8,128)(2,1)S(1)}, u32[]{:S(2)}, u32[]{:S(2)}) collective-permute-start(bf16[512,512]{1,0:T(8,128)(2,1)S(1)} %get-tuple-element.104), channel_id=1, source_target_pairs={{0,2},{2,0},{1,3},{3,1},{4,6},{6,4},{5,7},{7,5},{8,10},{10,8},{9,1... | collective-permute-start | bytes 1572872 | tf_op jit(solution)/shard_map/oth_recv_core1/ppermute | solution.py:731
  64.8 3.3 %collective-permute-start.16 = (bf16[256,512]{1,0:T(8,128)(2,1)S(1)}, bf16[256,512]{1,0:T(8,128)(2,1)S(1)}, u32[]{:S(2)}, u32[]{:S(2)}) collective-permute-start(bf16[256,512]{1,0:T(8,128)(2,1)S(1)} %get-tuple-element.106), channel_id=1, source_target_pairs={{0,2},{2,0},{1,3},{3,1},{4,6},{6,4},{5,7},{7,5},{8,10},{10,8},{9,1... | collective-permute-start | bytes 786440 | tf_op jit(solution)/shard_map/tab_recv_core1/ppermute | solution.py:731
  68.6 16.3 %collective-permute-start.19 = (bf16[640,512]{1,0:T(8,128)(2,1)S(1)}, bf16[640,512]{1,0:T(8,128)(2,1)S(1)}, u32[]{:S(2)}, u32[]{:S(2)}) collective-permute-start(bf16[640,512]{1,0:T(8,128)(2,1)S(1)} %get-tuple-element.110), channel_id=1, source_target_pairs={{0,1},{1,0},{2,3},{3,2},{4,5},{5,4},{6,7},{7,6},{8,9},{9,8},{10,11... | collective-permute-start | bytes 1966088 | tf_op jit(solution)/shard_map/att_from_y_mp1/ppermute | solution.py:731
  70.4 7.5 %collective-permute-start.20 = (bf16[256,512]{1,0:T(8,128)(2,1)S(1)}, bf16[256,512]{1,0:T(8,128)(2,1)S(1)}, u32[]{:S(2)}, u32[]{:S(2)}) collective-permute-start(bf16[256,512]{1,0:T(8,128)(2,1)S(1)} %get-tuple-element.112), channel_id=1, source_target_pairs={{0,4},{4,0},{1,5},{5,1},{2,6},{6,2},{3,7},{7,3},{8,12},{12,8},{9,1... | collective-permute-start | bytes 786440 | tf_op jit(solution)/shard_map/down_from_x_x1/ppermute | solution.py:731
  71.9 11.9 %collective-permute-start.14 = (bf16[512,512]{1,0:T(8,128)(2,1)S(1)}, bf16[512,512]{1,0:T(8,128)(2,1)S(1)}, u32[]{:S(2)}, u32[]{:S(2)}) collective-permute-start(bf16[512,512]{1,0:T(8,128)(2,1)S(1)} %get-tuple-element.102), channel_id=1, source_target_pairs={{0,2},{2,0},{1,3},{3,1},{4,6},{6,4},{5,7},{7,5},{8,10},{10,8},{9,1... | collective-permute-start | bytes 1572872 | tf_op jit(solution)/shard_map/own_recv_core1/ppermute | solution.py:731
  71.9 9.5 %collective-permute-start.22 = (bf16[272,512]{1,0:T(8,128)(2,1)S(1)}, bf16[272,512]{1,0:T(8,128)(2,1)S(1)}, u32[]{:S(2)}, u32[]{:S(2)}) collective-permute-start(bf16[272,512]{1,0:T(8,128)(2,1)S(1)} %get-tuple-element.115), channel_id=1, source_target_pairs={{0,8},{8,0},{16,24},{24,16},{1,9},{9,1},{17,25},{25,17},{2,10},{10... | collective-permute-start | bytes 835592 | tf_op jit(solution)/shard_map/up_from_z_z1/ppermute | solution.py:731
  78.0 5.7 %collective-permute-start.21 = (bf16[128,512]{1,0:T(8,128)(2,1)S(1)}, bf16[128,512]{1,0:T(8,128)(2,1)S(1)}, u32[]{:S(2)}, u32[]{:S(2)}) collective-permute-start(bf16[128,512]{1,0:T(8,128)(2,1)S(1)} %get-tuple-element.114), channel_id=1, source_target_pairs={{0,8},{8,0},{16,24},{24,16},{1,9},{9,1},{17,25},{25,17},{2,10},{10... | collective-permute-start | bytes 393224 | tf_op jit(solution)/shard_map/down_from_z_z1/ppermute | solution.py:731
  85.9 37.0 %all-to-all-start = ((bf16[8,80,512]{2,1,0:T(8,128)(2,1)}), bf16[8,80,512]{2,1,0:T(8,128)(2,1)S(1)}, u32[]{:S(2)}, u32[]{:S(2)}) async-start(bf16[8,80,512]{2,1,0:T(8,128)(2,1)} %attend_mp.1.refs_2_), calls=%async_computation | async-start | bytes 1310720 | tf_op jit(solution)/shard_map/att_parts/all_to_all | solution.py:736
  91.9 5.1 %collective-permute-start.23 = (bf16[144,512]{1,0:T(8,128)(2,1)S(1)}, bf16[144,512]{1,0:T(8,128)(2,1)S(1)}, u32[]{:S(2)}, u32[]{:S(2)}) collective-permute-start(bf16[144,512]{1,0:T(8,128)(2,1)S(1)} %get-tuple-element.117), channel_id=1, source_target_pairs={{0,1},{1,0},{2,3},{3,2},{4,5},{5,4},{6,7},{7,6},{8,9},{9,8},{10,11... | collective-permute-start | bytes 442376 | tf_op jit(solution)/shard_map/up_from_y_mp1/ppermute | solution.py:731
  93.4 20.3 %collective-permute-start.25 = (bf16[128,512]{1,0:T(8,128)(2,1)S(1)}, bf16[128,512]{1,0:T(8,128)(2,1)S(1)}, u32[]{:S(2)}, u32[]{:S(2)}) collective-permute-start(bf16[128,512]{1,0:T(8,128)(2,1)S(1)} %down_z.1.refs_4_.refs_0_), channel_id=1, source_target_pairs={{0,16},{8,24},{16,0},{24,8},{1,17},{9,25},{17,1},{25,9},{2,18},{10... | collective-permute-start | bytes 393224 | tf_op jit(solution)/shard_map/down_far_z2/ppermute | solution.py:731
  113.7 5.7 %collective-permute-start.26 = (bf16[128,512]{1,0:T(8,128)(2,1)S(1)}, bf16[128,512]{1,0:T(8,128)(2,1)S(1)}, u32[]{:S(2)}, u32[]{:S(2)}) collective-permute-start(bf16[128,512]{1,0:T(8,128)(2,1)S(1)} %down_far.1.refs_0_.refs_2_), channel_id=1, source_target_pairs={{0,8},{8,0},{16,24},{24,16},{1,9},{9,1},{17,25},{25,17},{2,10},{10... | collective-permute-start | bytes 393224 | tf_op jit(solution)/shard_map/down_near_z1/ppermute | solution.py:731
  113.8 8.4 %collective-permute-start.24 = (bf16[144,512]{1,0:T(8,128)(2,1)S(1)}, bf16[144,512]{1,0:T(8,128)(2,1)S(1)}, u32[]{:S(2)}, u32[]{:S(2)}) collective-permute-start(bf16[144,512]{1,0:T(8,128)(2,1)S(1)} %up_mp.1.refs_2_.refs_0_), channel_id=1, source_target_pairs={{0,16},{8,24},{16,0},{24,8},{1,17},{9,25},{17,1},{25,9},{2,18},{10... | collective-permute-start | bytes 442376 | tf_op jit(solution)/shard_map/up_far_z2/ppermute | solution.py:731
  124.5 26.7 %all-to-all-start.1 = ((bf16[8,80,512]{2,1,0:T(8,128)(2,1)}), bf16[8,80,512]{2,1,0:T(8,128)(2,1)S(1)}, u32[]{:S(2)}, u32[]{:S(2)}) async-start(bf16[8,80,512]{2,1,0:T(8,128)(2,1)} %attend_sum.1.refs_2_), calls=%async_computation.1 | async-start | bytes 1310720 | tf_op jit(solution)/shard_map/att_sums/all_to_all | solution.py:736
  128.9 11.9 %collective-permute-start.29 = (bf16[256,512]{1,0:T(8,128)(2,1)S(1)}, bf16[256,512]{1,0:T(8,128)(2,1)S(1)}, u32[]{:S(2)}, u32[]{:S(2)}) collective-permute-start(bf16[256,512]{1,0:T(8,128)(2,1)S(1)} %down_join.1.refs_2_.refs_0_), channel_id=1, source_target_pairs={{0,4},{4,0},{1,5},{5,1},{2,6},{6,2},{3,7},{7,3},{8,12},{12,8},{9,1... | collective-permute-start | bytes 786440 | tf_op jit(solution)/shard_map/down_x_x1/ppermute | solution.py:731
  130.9 9.8 %collective-permute-start.27 = (bf16[128,512]{1,0:T(8,128)(2,1)S(1)}, bf16[128,512]{1,0:T(8,128)(2,1)S(1)}, u32[]{:S(2)}, u32[]{:S(2)}) collective-permute-start(bf16[128,512]{1,0:T(8,128)(2,1)S(1)} %get-tuple-element.119.refs_0_), channel_id=1, source_target_pairs={{0,8},{8,0},{16,24},{24,16},{1,9},{9,1},{17,25},{25,17},{2,10},{10... | collective-permute-start | bytes 393224 | tf_op jit(solution)/shard_map/up_near_z1/ppermute | solution.py:731
  132.4 9.6 %collective-permute-start.30 = (bf16[256,512]{1,0:T(8,128)(2,1)S(1)}, bf16[256,512]{1,0:T(8,128)(2,1)S(1)}, u32[]{:S(2)}, u32[]{:S(2)}) collective-permute-start(bf16[256,512]{1,0:T(8,128)(2,1)S(1)} %down_join.1.refs_2_.refs_0_), channel_id=1, source_target_pairs={{0,2},{2,0},{1,3},{3,1},{4,6},{6,4},{5,7},{7,5},{8,10},{10,8},{9,1... | collective-permute-start | bytes 786440 | tf_op jit(solution)/shard_map/down_core_core1/ppermute | solution.py:731
  140.8 1.6 collective-permute-start.31
  140.9 8.7 %collective-permute-start.28 = (bf16[256,512]{1,0:T(8,128)(2,1)S(1)}, bf16[256,512]{1,0:T(8,128)(2,1)S(1)}, u32[]{:S(2)}, u32[]{:S(2)}) collective-permute-start(bf16[256,512]{1,0:T(8,128)(2,1)S(1)} %up_join.1.refs_1_.refs_0_), channel_id=1, source_target_pairs={{0,4},{4,0},{1,5},{5,1},{2,6},{6,2},{3,7},{7,3},{8,12},{12,8},{9,1... | collective-permute-start | bytes 786440 | tf_op jit(solution)/shard_map/up_x_x1/ppermute | solution.py:731
  141.8 9.9 %collective-permute-start.32 = (bf16[256,512]{1,0:T(8,128)(2,1)S(1)}, bf16[256,512]{1,0:T(8,128)(2,1)S(1)}, u32[]{:S(2)}, u32[]{:S(2)}) collective-permute-start(bf16[256,512]{1,0:T(8,128)(2,1)S(1)} %up_join.1.refs_1_.refs_0_), channel_id=1, source_target_pairs={{0,2},{2,0},{1,3},{3,1},{4,6},{6,4},{5,7},{7,5},{8,10},{10,8},{9,1... | collective-permute-start | bytes 786440 | tf_op jit(solution)/shard_map/up_core_core1/ppermute | solution.py:731
  151.2 1.5 collective-permute-start.33
  151.2 10.3 %collective-permute-start.37 = (bf16[8,80,512]{2,1,0:T(8,128)(2,1)S(1)}, bf16[8,80,512]{2,1,0:T(8,128)(2,1)S(1)}, u32[]{:S(2)}, u32[]{:S(2)}) collective-permute-start(bf16[8,80,512]{2,1,0:T(8,128)(2,1)S(1)} %all-to-all-done.1.refs_0_), channel_id=1, source_target_pairs={{0,2},{2,0},{1,3},{3,1},{4,6},{6,4},{5,7},{7,5},{8,10},{10,8},{9,1... | collective-permute-start | bytes 1966088 | tf_op jit(solution)/shard_map/att_core_core1/ppermute | solution.py:731
  155.8 5.6 %collective-permute-start.34 = (bf16[128,512]{1,0:T(8,128)(2,1)S(1)}, bf16[128,512]{1,0:T(8,128)(2,1)S(1)}, u32[]{:S(2)}, u32[]{:S(2)}) collective-permute-start(bf16[128,512]{1,0:T(8,128)(2,1)S(1)} %table_cut.1.refs_2_.refs_0_), channel_id=1, source_target_pairs={{0,1},{1,0},{2,3},{3,2},{4,5},{5,4},{6,7},{7,6},{8,9},{9,8},{10,11... | collective-permute-start | bytes 393224 | tf_op jit(solution)/shard_map/table_y_mp1/ppermute | solution.py:731
  157.4 5.5 %collective-permute-start.35 = (bf16[128,512]{1,0:T(8,128)(2,1)S(1)}, bf16[128,512]{1,0:T(8,128)(2,1)S(1)}, u32[]{:S(2)}, u32[]{:S(2)}) collective-permute-start(bf16[128,512]{1,0:T(8,128)(2,1)S(1)} %table_cut.1.refs_2_.refs_0_), channel_id=1, source_target_pairs={{0,2},{2,0},{1,3},{3,1},{4,6},{6,4},{5,7},{7,5},{8,10},{10,8},{9,1... | collective-permute-start | bytes 393224 | tf_op jit(solution)/shard_map/table_core_core1/ppermute | solution.py:731
  161.5 1.5 collective-permute-start.36
  (13 other events, 14.6 us)

commit v3 on v2

--- a/solution.py
+++ b/solution.py
@@ -27,7 +27,9 @@
 anywhere = pl.BlockSpec(memory_space=pl.ANY)
 
 
-def call(kernel, outs, args, after=(), scratch=(), us=1, mib=32, smem_args=0, name=None):
+def call(
+    kernel, outs, args, after=(), scratch=(), us=1, mib=32, smem_args=0, hbm_args=0, copies=0, name=None
+):
     flat, tree = jax.tree.flatten(tuple(args))
     count, extra = len(flat), len(after)
 
@@ -40,9 +42,12 @@
             jax.ShapeDtypeStruct(out, BF16) if isinstance(out[0], int) else jax.ShapeDtypeStruct(*out)
             for out in outs
         ],
-        in_specs=[smem] * smem_args + [vmem] * (count - smem_args) + [anywhere] * extra,
+        in_specs=[smem] * smem_args
+        + [vmem] * (count - smem_args - hbm_args)
+        + [anywhere] * (hbm_args + extra),
         out_specs=[vmem] * len(outs),
-        scratch_shapes=[pltpu.VMEM(shape, dtype) for shape, dtype in scratch],
+        scratch_shapes=[pltpu.VMEM(shape, dtype) for shape, dtype in scratch]
+        + [pltpu.SemaphoreType.DMA((copies,))] * (copies > 0),
         compiler_params=pltpu.CompilerParams(vmem_limit_bytes=mib * MIB),
         cost_estimate=pl.CostEstimate(
             flops=us * FLOPS_PER_US, bytes_accessed=0, transcendentals=0
@@ -222,49 +227,69 @@
     attend_forward(hidden_low, weight_ref, windows, mixed_ref, probs_ref, context_ref)
 
 
-def quarter():
-    return place("core") * 2 + place("x")
+def z_bit():
+    return lax.rem(place("z"), 2)
+
+
+def quarter(bit):
+    return place("core") * 2 + bit
 
 
 def part(index, size):
     return pl.ds(pl.multiple_of(index * size, size), size)
 
 
-def pack_attend_kernel(qkv_ref, out_ref, bias_ref, send_ref):
+def copy_all(pairs, sems):
+    copies = [
+        pltpu.make_async_copy(src, dst, sems.at[i]) for i, (src, dst) in enumerate(pairs)
+    ]
+    for copy in copies:
+        copy.start()
+    for copy in copies:
+        copy.wait()
+
+
+def pack_attend_kernel(bias_ref, qkv_ref, out_ref, send_ref, sems):
     _, width, half = qkv_ref.shape
-    depth, mine = width // 4, quarter()
-    send_ref[0:depth, 0:half] = qkv_ref[0, part(mine, depth), :]
-    send_ref[0:depth, half:] = qkv_ref[1, part(mine, depth), :]
-    value = qkv_ref[2, part(mine, depth), :]
-    send_ref[depth : depth + depth // 2, 0:half] = value[0 : depth // 2]
-    send_ref[depth : depth + depth // 2, half:] = value[depth // 2 :]
-    start = depth + depth // 2
-    send_ref[start : 2 * depth, :] = out_ref[part(mine, depth // 2), :]
+    depth, mine = width // 4, quarter(place("x"))
     for i in range(EXTRA):
         index = i if (i + 1) * width <= bias_ref.shape[0] else 0
         send_ref[2 * depth + i : 2 * depth + i + 1, :] = row(bias_ref, index * width, width).astype(
             BF16
         )
-
-
-def pack_ffn_kernel(up_ref, down_ref, up_to, down_to):
+    middle = depth + depth // 2
+    low, high = pl.ds(0, half), pl.ds(half, half)
+    upper, lower = part(mine * 2, depth // 2), part(mine * 2 + 1, depth // 2)
+    copy_all(
+        [
+            (qkv_ref.at[0, part(mine, depth), :], send_ref.at[pl.ds(0, depth), low]),
+            (qkv_ref.at[1, part(mine, depth), :], send_ref.at[pl.ds(0, depth), high]),
+            (qkv_ref.at[2, upper, :], send_ref.at[pl.ds(depth, depth // 2), low]),
+            (qkv_ref.at[2, lower, :], send_ref.at[pl.ds(depth, depth // 2), high]),
+            (out_ref.at[part(mine, depth // 2), :], send_ref.at[pl.ds(middle, depth // 2), :]),
+        ],
+        sems,
+    )
+
+
+def pack_ffn_kernel(up_ref, down_ref, up_to, down_to, sems):
     width, units = up_ref.shape
-    depth, mine = width // 4, quarter()
-    for i in range(units // width):
-        up_to[i * depth : (i + 1) * depth, :] = up_ref[
-            part(mine, depth), i * width : (i + 1) * width
-        ]
-    down_to[...] = down_ref[part(mine, units // 4), :]
-
-
-def places(pieces):
-    x, core = place("x"), place("core")
-    from_y, from_x, core_y, core_x = pieces
+    depth, mine = width // 4, quarter(place("x"))
+    columns = [
+        (up_ref.at[part(mine, depth), pl.ds(i * width, width)], up_to.at[pl.ds(i * depth, depth), :])
+        for i in range(units // width)
+    ]
+    copy_all([*columns, (down_ref.at[part(quarter(z_bit()), units // 4), :], down_to)], sems)
+
+
+def places(pieces, bit):
+    from_y, from_near, core_y, core_near = pieces
+    core = place("core")
     return (
-        (from_y, core * 2 + x),
-        (from_x, core * 2 + 1 - x),
-        (core_y, (1 - core) * 2 + x),
-        (core_x, (1 - core) * 2 + 1 - x),
+        (from_y, core * 2 + bit),
+        (from_near, core * 2 + 1 - bit),
+        (core_y, (1 - core) * 2 + bit),
+        (core_near, (1 - core) * 2 + 1 - bit),
     )
 
 
@@ -288,7 +313,7 @@
     half, depth = width // 2, width // 4
     windows = read_windows(win_ref, tokens_ref.shape[0])
     if len(pieces) == 4:
-        for ref, index in places(pieces):
+        for ref, index in places(pieces, place("x")):
             rows = part(index, depth)
             w_oth_ref[0, rows, :] = ref[0:depth, 0:half]
             w_oth_ref[1, rows, :] = ref[0:depth, half:]
@@ -373,13 +398,13 @@
     width = cot_ref.shape[1]
     units = up_ref.shape[1]
     if len(up_refs) == 4:
-        for ref, index in places(up_refs):
+        for ref, index in places(up_refs, place("x")):
             depth = ref.shape[0] * width // units
             for i in range(units // width):
                 up_ref[part(index, depth), i * width : (i + 1) * width] = ref[
                     i * depth : (i + 1) * depth, :
                 ]
-        for ref, index in places(down_refs):
+        for ref, index in places(down_refs, z_bit()):
             down_ref[part(index, ref.shape[0]), :] = ref[...]
     else:
         up_ref[...] = up_refs[0][...]
@@ -410,6 +435,7 @@
     slopes,
     ups,
     downs,
+    contexts,
     vec_ref,
     gain_ref,
     keep_ref,
@@ -420,9 +446,12 @@
     total_ref,
     package_ref,
     bias_sum_ref,
+    out_ref,
 ):
     width = resid_ref.shape[1]
     units = ups[0].shape[1]
+    half_width = width // 2
+    group = (units + half_width) // 2
     grad_low = grad_ref[...].astype(BF16)
     for half in range(2):
         for start in range(0, units, CHUNK):
@@ -437,7 +466,7 @@
         for start in range(0, units, width):
             cols = slice(start, start + width)
             package_ref[cols, :] = mm_tn(low_ref[...], work_ref[:, cols]).astype(BF16)
-        core_split(package_ref, keep_ref, send_ref, half * (units // 2), split)
+        core_split(package_ref, keep_ref, send_ref, half * group, split)
         before = grad_ref[...] if half == 0 else total_ref[...]
         total_ref[...] = before + mm_nt(work_ref[...], ups[half][...])
     grad = total_ref[...]
@@ -446,6 +475,10 @@
     small_ref[2:3, :] = jnp.sum(grad, axis=0, keepdims=True)
     grad = norm_grad(grad * row(gain_ref), hat, scale)
     small_ref[0:1, :] = jnp.sum(grad, axis=0, keepdims=True)
+    grad_low = grad.astype(BF16)
+    for half in range(2):
+        out_ref[...] = mm_tn(contexts[half][...], grad_low).astype(BF16)
+        core_split(out_ref, keep_ref, send_ref, half * group + units // 2, split)
     small_ref[3:6, :] = vec_ref[0:3, :]
     span = units // width
     first_half = (place("mp") if split else 0) == 0
@@ -454,8 +487,8 @@
     small_ref[6 + span : 6 + 2 * span, :] = jnp.where(first_half, theirs, ours)
     used = 6 + 2 * span
     small_ref[used:, :] = jnp.zeros((small_ref.shape[0] - used, width), F32)
-    keep_ref[units:, :] = small_ref[...].astype(BF16)
-    send_ref[units:, :] = small_ref[...].astype(BF16)
+    keep_ref[2 * group :, :] = small_ref[...].astype(BF16)
+    send_ref[2 * group :, :] = small_ref[...].astype(BF16)
     grad_resid_ref[...] = grad
 
 
@@ -467,7 +500,6 @@
     out_ref,
     mixed_ref,
     probs_ref,
-    context_ref,
     keep_ref,
     send_ref,
     gm_ref,
@@ -475,7 +507,6 @@
 ):
     rows, width = hidden_low.shape
     half_width = width // 2
-    package_ref[width + half_width :, :] = mm_tn(context_ref[...], grad_low).astype(BF16)
     grad_context = mm_nt(grad_low, out_ref[...]).astype(BF16)
     attend_backward(grad_context, mixed_ref, probs_ref, rows // W_LONG, gm_ref)
     package_ref[0:width, 0:half_width] = mm_tn(hidden_low, gm_ref[0]).astype(BF16)
@@ -553,10 +584,6 @@
     send_ref[start : start + half, :] = work_ref[part(1 - bit, half), :]
 
 
-def z_bit():
-    return lax.rem(place("z"), 2)
-
-
 def other_half_kernel(keep_ref, recv_ref, send_ref):
     start = keep_ref.shape[0] - send_ref.shape[0]
     send_ref[...] = total_of(keep_ref[start:, :], recv_ref[start:, :]).astype(BF16)
@@ -570,12 +597,6 @@
 
 def pair_kernel(a_ref, b_ref, out_ref):
     out_ref[...] = total_of(a_ref[...], b_ref[...]).astype(BF16)
-
-
-def spread_kernel(parts_ref, out_ref):
-    total = total_of(*[parts_ref[i] for i in range(parts_ref.shape[0])]).astype(BF16)
-    for i in range(out_ref.shape[0]):
-        out_ref[i] = total
 
 
 def up_split_kernel(keep_ref, recv_ref, x_keep_ref, x_send_ref, work_ref):
@@ -584,7 +605,7 @@
         rows_of = slice(half * rows, (half + 1) * rows)
         total = total_of(keep_ref[rows_of, :], recv_ref[rows_of, :])
         start = half * (rows // 2)
-        bit_split(place("x"), total, work_ref, x_keep_ref, x_send_ref, start)
+        bit_split(z_bit(), total, work_ref, x_keep_ref, x_send_ref, start)
     small = total_of(keep_ref[2 * rows :, :], recv_ref[2 * rows :, :]).astype(BF16)
     x_keep_ref[rows:, :] = small
     x_send_ref[rows:, :] = small
@@ -599,7 +620,7 @@
     for half in range(2):
         rows_of = slice(half * rows, (half + 1) * rows)
         total = total_of(keep_ref[rows_of, :], recv_ref[rows_of, :])
-        bit_split(z_bit(), total, work_ref, z_keep_ref, z_send_ref, half * (rows // 2))
+        bit_split(place("x"), total, work_ref, z_keep_ref, z_send_ref, half * (rows // 2))
     small = total_of(keep_ref[2 * rows :, :], recv_ref[2 * rows :, :]).astype(BF16)
     z_keep_ref[rows:, :] = small
     z_send_ref[rows:, :] = small
@@ -625,10 +646,11 @@
         bias_ref[i * width : (i + 1) * width] = value.reshape(width)
 
 
-def join_kernel(own_ref, recv_ref, out_ref):
+def join_kernel(axis, own_ref, recv_ref, out_ref):
     rows = own_ref.shape[0]
-    out_ref[part(z_bit(), rows), :] = own_ref[...]
-    out_ref[part(1 - z_bit(), rows), :] = recv_ref[...]
+    bit = z_bit() if axis == "z" else place("x")
+    out_ref[part(bit, rows), :] = own_ref[...]
+    out_ref[part(1 - bit, rows), :] = recv_ref[...]
 
 
 def attend_core_kernel(
@@ -640,89 +662,81 @@
     bit_split(place("mp"), total, work_ref, table_ref, to_y_ref.at[rows:, :])
 
 
-def attend_pieces_kernel(keep_ref, recv_ref, from_y_ref, table_ref, out_ref):
-    devices, rows, _ = out_ref.shape
-    size = keep_ref.shape[0]
-    piece = size // devices
-    spare = rows - piece
-    for i in range(devices):
-        rows_of = slice(i * piece, (i + 1) * piece)
-        out_ref[i, 0:piece, :] = total_of(
-            keep_ref[rows_of, :], recv_ref[rows_of, :], from_y_ref[rows_of, :]
-        ).astype(BF16)
-        rows_of = slice(i * spare, (i + 1) * spare)
-        other = from_y_ref[size + i * spare : size + (i + 1) * spare, :]
-        out_ref[i, piece:, :] = total_of(table_ref[rows_of, :], other).astype(BF16)
-
-
-def spread_kernel(parts_ref, out_ref):
-    total = total_of(*[parts_ref[i] for i in range(parts_ref.shape[0])]).astype(BF16)
-    for i in range(out_ref.shape[0]):
-        out_ref[i] = total
-
-
-def cut_kernel(parts_ref, out_ref):
-    devices, rows, _ = parts_ref.shape
-    size = out_ref.shape[0] // devices
-    for i in range(devices):
-        out_ref[i * size : (i + 1) * size, :] = parts_ref[i, rows - size :, :]
-
-
-def down_out_kernel(own_ref, from_x_ref, core_own_ref, core_x_ref, out_ref):
-    x, core = place("x"), place("core")
-    rows = own_ref.shape[0]
-    for ref, at_x, at_core in (
-        (own_ref, x, core),
-        (from_x_ref, 1 - x, core),
-        (core_own_ref, x, 1 - core),
-        (core_x_ref, 1 - x, 1 - core),
-    ):
-        start = pl.multiple_of((at_core * 2 + at_x) * rows, rows)
-        out_ref[pl.ds(start, rows), :] = ref[...].astype(F32)
-
-
-def up_out_kernel(own_ref, from_x_ref, core_own_ref, core_x_ref, out_ref):
-    x, core = place("x"), place("core")
-    rows, width = own_ref.shape
-    for index in range(2):
-        cols = slice(index * width, (index + 1) * width)
-        mine = core == index
-        for a_ref, b_ref, at_x in ((own_ref, core_own_ref, x), (from_x_ref, core_x_ref, 1 - x)):
-            start = pl.multiple_of(at_x * rows, rows)
-            out_ref[pl.ds(start, rows), cols] = jnp.where(
-                mine, a_ref[...].astype(F32), b_ref[...].astype(F32)
-            )
-
-
-def attend_out_kernel(own_ref, recv_ref, qkv_ref, out_ref):
-    first_core = place("core") == 0
-    devices, rows, width = own_ref.shape
-    half = width // 2
-    piece = width // devices
-    for i in range(devices):
-        ours, theirs = own_ref[i, 0:piece].astype(F32), recv_ref[i, 0:piece].astype(F32)
-        low = jnp.where(first_core, ours, theirs)
-        high = jnp.where(first_core, theirs, ours)
-        rows_of = slice(i * piece, (i + 1) * piece)
-        qkv_ref[0, rows_of, :] = low[:, 0:half]
-        qkv_ref[1, rows_of, :] = low[:, half:]
-        if i < devices // 2:
-            qkv_ref[2, rows_of, :] = high[:, 0:half]
-            qkv_ref[2, half + i * piece : half + (i + 1) * piece, :] = high[:, half:]
-        else:
-            out_ref[(i - devices // 2) * piece : (i - devices // 2 + 1) * piece, :] = high
-
-
-def table_out_kernel(own_ref, from_y_ref, core_own_ref, core_y_ref, out_ref):
-    y, core = place("mp"), place("core")
-    rows = own_ref.shape[0]
-    for ref, at_y, at_core in (
-        (own_ref, y, core),
-        (from_y_ref, 1 - y, core),
-        (core_own_ref, y, 1 - core),
-        (core_y_ref, 1 - y, 1 - core),
-    ):
-        out_ref[part(at_core * 2 + at_y, rows), :] = ref[...].astype(F32)
+def attend_mp_kernel(
+    keep_ref, recv_ref, from_y_ref, table_ref, x_keep_ref, x_send_ref, work_ref, spare_ref
+):
+    rows = keep_ref.shape[0]
+    total = total_of(keep_ref[...], recv_ref[...], from_y_ref[0:rows, :])
+    bit_split(place("x"), total, work_ref, x_keep_ref, x_send_ref)
+    total = total_of(table_ref[...], from_y_ref[rows:, :])
+    bit_split(place("x"), total, spare_ref, x_keep_ref, x_send_ref, rows // 2)
+
+
+def attend_x_kernel(keep_ref, recv_ref, z_keep_ref, z_send_ref, work_ref, spare_ref):
+    rows = work_ref.shape[0]
+    total = total_of(keep_ref[0:rows, :], recv_ref[0:rows, :])
+    bit_split(z_bit(), total, work_ref, z_keep_ref, z_send_ref)
+    total = total_of(keep_ref[rows:, :], recv_ref[rows:, :])
+    bit_split(z_bit(), total, spare_ref, z_keep_ref, z_send_ref, rows // 2)
+
+
+def attend_join_kernel(own_ref, recv_ref, out_ref, table_ref):
+    spare = table_ref.shape[0] // 2
+    rows = own_ref.shape[0] - spare
+    for ref, bit in ((own_ref, z_bit()), (recv_ref, 1 - z_bit())):
+        out_ref[part(bit, rows), :] = ref[0:rows, :]
+        table_ref[part(bit, spare), :] = ref[rows:, :]
+    out_ref[2 * rows :, :] = table_ref[...]
+
+
+def corners(parts, bit):
+    own_ref, near_ref, core_own_ref, core_near_ref = parts
+    core = place("core")
+    return (
+        (own_ref, core * 2 + bit),
+        (near_ref, core * 2 + 1 - bit),
+        (core_own_ref, (1 - core) * 2 + bit),
+        (core_near_ref, (1 - core) * 2 + 1 - bit),
+    )
+
+
+def down_out_kernel(*refs):
+    *parts, out_ref, token_ref = refs
+    token_ref[...] = jnp.zeros(token_ref.shape, F32)
+    for ref, index in corners(parts, place("x")):
+        out_ref[part(index, ref.shape[0]), :] = ref[...].astype(F32)
+
+
+def up_out_kernel(*refs):
+    *parts, up_ref, out_ref, token_ref, work_ref = refs
+    token_ref[...] = jnp.zeros(token_ref.shape, F32)
+    for ref, index in corners(parts, z_bit()):
+        work_ref[part(index, ref.shape[0]), :] = ref[...]
+    width, spare = up_ref.shape[0], out_ref.shape[0] // 2
+    for core in range(2):
+        start = core * (width + spare)
+        up_ref[:, core * width : (core + 1) * width] = work_ref[start : start + width, :].astype(F32)
+        start += width
+        out_ref[core * spare : (core + 1) * spare, :] = work_ref[start : start + spare, :].astype(F32)
+
+
+def attend_out_kernel(parts, table_parts, qkv_ref, table_ref, work_ref):
+    y = place("mp")
+    spare = table_parts[0].shape[0]
+    rows = parts[0].shape[0] - spare
+    half = qkv_ref.shape[2]
+    width = 2 * half
+    for ref, index in corners(parts, place("x")):
+        work_ref[part(index, rows), :] = ref[0:rows, :]
+        core, x = lax.div(index, 2), lax.rem(index, 2)
+        table_ref[part(core * 4 + y * 2 + x, spare), :] = ref[rows:, :].astype(F32)
+    for ref, index in corners(table_parts, place("x")):
+        core, x = lax.div(index, 2), lax.rem(index, 2)
+        table_ref[part(core * 4 + (1 - y) * 2 + x, spare), :] = ref[...].astype(F32)
+    qkv_ref[0] = work_ref[0:width, 0:half].astype(F32)
+    qkv_ref[1] = work_ref[0:width, half:].astype(F32)
+    qkv_ref[2, 0:half, :] = work_ref[width : width + half, 0:half].astype(F32)
+    qkv_ref[2, half:, :] = work_ref[width : width + half, half:].astype(F32)
 
 
 def swap(value, axis, name="swap", distance=1):
@@ -731,16 +745,16 @@
         return lax.ppermute(value, axis, pairs)
 
 
-def exchange(value, axes, name="exchange"):
+def swap_corner(value, name):
     with jax.named_scope(name):
-        return lax.all_to_all(value, axes, 0, 0, tiled=True)
+        return lax.ppermute(value, ("x", "mp"), [(0, 3), (1, 2), (2, 1), (3, 0)])
 
 
 class Chain:
     def __init__(self):
         self.last = ()
 
-    def gate(self, value):
+    def gate(self, value, us=1):
         value = pl.pallas_call(
             lambda *refs: None,
             out_shape=jax.ShapeDtypeStruct(value.shape, value.dtype),
@@ -749,17 +763,33 @@
             input_output_aliases={0: 0},
             compiler_params=pltpu.CompilerParams(vmem_limit_bytes=MIB),
             cost_estimate=pl.CostEstimate(
-                flops=FLOPS_PER_US, bytes_accessed=0, transcendentals=0
+                flops=us * FLOPS_PER_US, bytes_accessed=0, transcendentals=0
             ),
             name="gate",
         )(value, *self.last)
         self.last = (value,)
         return value
 
-    def __call__(self, kernel, outs, args, us, name, scratch=(), smem_args=0):
-        mib = 28 if us > 2 else 8
-        results = call(kernel, outs, args, self.last, scratch, us, mib, smem_args, name)
-        self.last = (min(results, key=lambda value: value.size),)
+    def __call__(
+        self,
+        kernel,
+        outs,
+        args,
+        us,
+        name,
+        scratch=(),
+        smem_args=0,
+        hbm_args=0,
+        copies=0,
+        mib=8,
+        token=None,
+    ):
+        results = call(
+            kernel, outs, args, self.last, scratch, us, mib, smem_args, hbm_args, copies, name
+        )
+        if token is None:
+            token = min(range(len(results)), key=lambda i: results[i].size)
+        self.last = (results[token],)
         return results
 
 
@@ -788,6 +818,7 @@
     half_width = width // 2
     units = up_weight.shape[1] * mp_size // 2
     n, spare = width, W_LONG // 2
+    group, att = (units + half_width) // 2, 3 * width // 4
     qkv_weight = jnp.transpose(qkv_weight, (1, 0, 2))
     wide = ((rows, width), F32)
 
@@ -804,6 +835,7 @@
             [window, tokens, pos_table, w_own],
             3,
             "attend_first",
+            mib=28,
             smem_args=1,
         )
 
@@ -815,6 +847,7 @@
             [window, tokens, pos_table, attend_in, context_own, out_own, out_bias],
             5,
             "attend_second",
+            mib=28,
             smem_args=1,
         )
 
@@ -825,6 +858,7 @@
             [resid, up_own, down_own, bias_own, norm1_gain, norm1_shift],
             4,
             "ffn_own",
+            mib=28,
         )
 
     if fast:
@@ -833,9 +867,12 @@
         (message,) = step(
             pack_attend_kernel,
             [(width // 2 + EXTRA, width)],
-            [qkv_weight, out_weight, up_bias],
+            [up_bias, qkv_weight, out_weight],
             1,
             "pack_attend",
+            mib=60,
+            hbm_args=2,
+            copies=5,
         )
         attend_y = swap(message, "mp", "attend_y")
         up_message, down_message = step(
@@ -844,30 +881,33 @@
             [up_weight, down_weight],
             1,
             "pack_ffn",
+            mib=60,
+            hbm_args=2,
+            copies=1 + units // width,
         )
         up_y = swap(up_message, "mp", "up_y")
         down_y = swap(down_message, "mp", "down_y")
+        mixed_own, probs_own, context_own = attend_own()
         attend_y = step.gate(attend_y)
         attend_x = swap(attend_y, "x", "attend_x")
         attend_cy = swap(attend_y, "core", "attend_cy")
-        mixed_own, probs_own, context_own = attend_own()
         up_y = step.gate(up_y)
         up_x = swap(up_y, "x", "up_x")
         up_cy = swap(up_y, "core", "up_cy")
         attend_x = step.gate(attend_x)
         attend_cx = swap(attend_x, "core", "attend_cx")
         down_y = step.gate(down_y)
-        down_x = swap(down_y, "x", "down_x")
+        down_z = swap(down_y, "z", "down_z")
         down_cy = swap(down_y, "core", "down_cy")
         attend_in = (attend_y, attend_x, attend_cy, attend_cx)
         mixed_oth, probs_oth, context_oth, resid, w_oth, out_oth, bias_oth = attend_other()
-        up_x = step.gate(up_x)
+        up_x = step.gate(up_x, 0)
         up_cx = swap(up_x, "core", "up_cx")
         low, act_own, slope_own, branch = ffn_own()
-        down_x = step.gate(down_x)
-        down_cx = swap(down_x, "core", "down_cx")
+        down_z = step.gate(down_z)
+        down_cz = swap(down_z, "core", "down_cz")
         up_in = (up_y, up_x, up_cy, up_cx)
-        down_in = (down_y, down_x, down_cy, down_cx)
+        down_in = (down_y, down_z, down_cy, down_cz)
     else:
         qkv = lax.all_gather(qkv_weight, "mp", axis=2, tiled=True)
         out_w = lax.all_gather(out_weight, "mp", axis=0, tiled=True)
@@ -909,14 +949,15 @@
         ],
         6,
         "ffn_other",
+            mib=28,
         scratch=[((rows, units), BF16), ((units, width), BF16)],
     )
     down_recv = swap(down_send, "core", "down_recv") if fast else None
     up_keep, up_send, small, grad1 = step(
         functools.partial(ffn_back_kernel, fast),
         [
-            (units + EXTRA, width),
-            (units + EXTRA, width),
+            (2 * group + EXTRA, width),
+            (2 * group + EXTRA, width),
             ((EXTRA, width), F32),
             wide,
         ],
@@ -927,37 +968,41 @@
             (slope_own, slope_oth),
             (up_own, up_oth),
             (down_own, down_oth),
+            (context_own, context_oth),
             vec,
             norm1_gain,
         ],
         6,
         "ffn_back",
+            mib=28,
         scratch=[
             ((rows, units), BF16),
             ((rows, width), F32),
             ((units, width), BF16),
             ((8, width), F32),
+            ((half_width, width), BF16),
         ],
     )
 
     def attend_back():
         return step(
             functools.partial(attend_back_kernel, fast),
-            [(n, width)] * 4 + [(spare, width)] * 2 + [(rows, width)],
+            [(att, width)] * 4 + [(spare, width)] * 2 + [(rows, width)],
             [
                 window,
                 tokens,
                 pos_table,
                 grad1,
-                (w_own, out_own, mixed_own, probs_own, context_own),
-                (w_oth, out_oth, mixed_oth, probs_oth, context_oth),
+                (w_own, out_own, mixed_own, probs_own),
+                (w_oth, out_oth, mixed_oth, probs_oth),
             ],
             13,
             "attend_back",
+            mib=28,
             scratch=[
                 ((rows, width), F32),
                 ((3, rows, half_width), BF16),
-                ((2 * n, width), BF16),
+                ((2 * att, width), BF16),
                 ((W_LONG, width), BF16),
             ],
             smem_args=1,
@@ -973,20 +1018,19 @@
         start = lax.axis_index("mp") * up_bias.shape[0]
         bias_g = lax.dynamic_slice_in_dim(bias_all, start, up_bias.shape[0])
     else:
-        zx = lax.axis_size("z") * lax.axis_size("x")
         half, piece, strip = n // 2, n // 4, spare // 2
         up_recv = swap(up_send, "core", "up_recv")
-        (to_y,) = step(other_half_kernel, [(n, width)], [down_keep, down_recv], 1, "down_core")
+        (to_y,) = step(other_half_kernel, [(n, width)], [down_keep, down_recv], 6, "down_core")
         down_from_y = swap(to_y, "mp", "down_from_y")
         up_x, to_x = step(
             up_split_kernel,
-            [(n + EXTRA, width)] * 2,
+            [(group + EXTRA, width)] * 2,
             [up_keep, up_recv],
-            2,
+            1,
             "up_core",
-            scratch=[((n, width), BF16)],
-        )
-        up_from_x = swap(to_x, "x", "up_from_x")
+            scratch=[((group, width), BF16)],
+        )
+        up_from_x = swap(to_x, "z", "up_from_z")
         oth_keep, oth_send, own_keep, own_send, tab_keep, tab_send, grad_tokens = attend_back()
         oth_recv = swap(oth_send, "core", "oth_recv")
         tab_recv = swap(tab_send, "core", "tab_recv")
@@ -995,113 +1039,142 @@
             down_split_kernel,
             [(half, width)] * 2,
             [down_keep, down_recv, down_from_y],
-            1,
+            0,
             "down_mp",
             scratch=[((n, width), BF16)],
         )
         down_from_x = swap(to_x, "x", "down_from_x")
+        to_y, table = step(
+            attend_core_kernel,
+            [(att + strip, width), (strip, width)],
+            [oth_keep, oth_recv, tab_keep, tab_recv],
+            0,
+            "attend_core",
+            scratch=[((spare, width), BF16)],
+        )
+        att_from_y = swap(to_y, "mp", "att_from_y")
         up_z, to_z = step(
             up_x_kernel,
-            [(half + EXTRA, width)] * 2,
+            [(group // 2 + EXTRA, width)] * 2,
             [up_x, up_from_x],
-            1,
+            0,
             "up_x",
-            scratch=[((half, width), BF16)],
-        )
-        up_from_z = swap(to_z, "z", "up_from_z")
-        to_y, table = step(
-            attend_core_kernel,
-            [(n + strip, width), (strip, width)],
-            [oth_keep, oth_recv, tab_keep, tab_recv],
-            1,
-            "attend_core",
-            scratch=[((spare, width), BF16)],
-        )
-        att_from_y = swap(to_y, "mp", "att_from_y")
+            scratch=[((group // 2, width), BF16)],
+        )
+        up_from_z = swap(to_z, "x", "up_from_x")
         down_z, to_z = step(
             down_x_kernel,
             [(piece, width)] * 2,
             [down_x, down_from_x],
-            1,
+            3,
             "down_x",
             scratch=[((half, width), BF16)],
         )
         down_from_z = swap(to_z, "z", "down_from_z")
+        (down_z,) = step(pair_kernel, [(piece, width)], [down_z, down_from_z], 0, "down_z")
+        down_far = swap(down_z, "z", "down_far", 2)
+        att_x, to_x = step(
+            attend_mp_kernel,
+            [((att + strip) // 2, width)] * 2,
+            [own_keep, own_recv, att_from_y, table],
+            0,
+            "attend_mp",
+            scratch=[((att, width), BF16), ((strip, width), BF16)],
+        )
+        att_from_x = swap(to_x, "x", "att_from_x")
         up_y, to_y = step(
-            up_z_kernel, [(piece + EXTRA, width)] * 2, [up_z, up_from_z], 1, "up_z"
+            up_z_kernel, [(group // 4 + EXTRA, width)] * 2, [up_z, up_from_z], 0, "up_z"
         )
         up_from_y = swap(to_y, "mp", "up_from_y")
-        (down_z,) = step(pair_kernel, [(piece, width)], [down_z, down_from_z], 1, "down_z")
-        down_far = swap(down_z, "z", "down_far", 2)
-        (att,) = step(
-            attend_pieces_kernel,
-            [(zx, (n + strip) // zx, width)],
-            [own_keep, own_recv, att_from_y, table],
-            1,
-            "attend_mp",
-        )
-        att = exchange(att, ("z", "x"), "att_parts")
-        (up_y,) = step(pair_kernel, [(piece + EXTRA, width)], [up_y, up_from_y], 1, "up_mp")
+        (down_z,) = step(pair_kernel, [(piece, width)], [down_z, down_far], 0, "down_far")
+        down_near = swap(down_z, "z", "down_near")
+        att_z, to_z = step(
+            attend_x_kernel,
+            [((att + strip) // 4, width)] * 2,
+            [att_x, att_from_x],
+            0,
+            "attend_x",
+            scratch=[((att // 2, width), BF16), ((strip // 2, width), BF16)],
+        )
+        att_from_z = swap(to_z, "z", "att_from_z")
+        (up_y,) = step(pair_kernel, [(group // 4 + EXTRA, width)], [up_y, up_from_y], 0, "up_mp")
         up_far = swap(up_y, "z", "up_far", 2)
-        (down_z,) = step(pair_kernel, [(piece, width)], [down_z, down_far], 1, "down_far")
-        down_near = swap(down_z, "z", "down_near")
-        (down_z,) = step(join_kernel, [(half, width)], [down_z, down_near], 1, "down_join")
+        (att_z,) = step(pair_kernel, [att_z.shape], [att_z, att_from_z], 0, "attend_z")
+        att_far = swap(att_z, "z", "att_far", 2)
+        (down_z,) = step(functools.partial(join_kernel, "z"), [(half, width)], [down_z, down_near], 0, "down_join")
         down_x = swap(down_z, "x", "down_x")
         up_z, *vectors, bias_g = step(
             up_last_kernel,
-            [(piece, width)] + [((width,), F32)] * 6 + [((up_bias.shape[0],), F32)],
+            [(group // 4, width)] + [((width,), F32)] * 6 + [((up_bias.shape[0],), F32)],
             [up_y, up_far],
-            1,
+            0,
             "up_far",
+            token=0,
             scratch=[((EXTRA, width), F32)],
         )
-        up_near = swap(up_z, "z", "up_near")
-        (att,) = step(spread_kernel, [att.shape], [att], 1, "attend_sum")
-        att = exchange(att, ("z", "x"), "att_sums")
-        (up_z,) = step(join_kernel, [(half, width)], [up_z, up_near], 1, "up_join")
-        up_x = swap(up_z, "x", "up_x")
-        down_x = step.gate(down_x)
-        (down_g,) = step(
+        up_near = swap(up_z, "x", "up_near")
+        (att_z,) = step(pair_kernel, [att_z.shape], [att_z, att_far], 0, "attend_far")
+        att_near = swap(att_z, "z", "att_near")
+        att_half, table = step(
+            attend_join_kernel,
+            [((att + strip) // 2, width), (strip // 2, width)],
+            [att_z, att_near],
+            0,
+            "attend_join",
+        )
+        att_x = swap(att_half, "x", "att_x")
+        table_y = swap(table, "mp", "table_y")
+        table_x = swap_corner(table, "table_x")
+        (up_z,) = step(functools.partial(join_kernel, "x"), [(group // 2, width)], [up_z, up_near], 0, "up_join")
+        up_x = swap(up_z, "z", "up_last")
+        down_x = step.gate(down_x, 0)
+        down_g, _ = step(
             down_out_kernel,
-            [((2 * n, width), F32)],
+            [((2 * n, width), F32), ((8, LANES), F32)],
             [
                 down_z,
                 down_x,
                 swap(down_z, "core", "down_core"),
                 swap(down_x, "core", "down_core_x"),
             ],
-            2,
+            0,
             "down_out",
         )
-        up_x = step.gate(up_x)
-        (up_g,) = step(
+        table_y = step.gate(table_y, 0)
+        up_x = step.gate(up_x, 0)
+        table_x = step.gate(table_x, 0)
+        att_x = step.gate(att_x, 0)
+        up_g, out_g, _ = step(
             up_out_kernel,
-            [((width, 2 * n), F32)],
+            [((width, 2 * n), F32), ((half_width, width), F32), ((8, LANES), F32)],
             [up_z, up_x, swap(up_z, "core", "up_core"), swap(up_x, "core", "up_core_x")],
-            2,
+            0,
             "up_out",
-        )
-        (table,) = step(cut_kernel, [(strip, width)], [att], 1, "table_cut")
-        table_y = swap(table, "mp", "table_y")
-        qkv_g, out_g = step(
+            scratch=[((2 * group, width), BF16)],
+        )
+        qkv_g, table = step(
             attend_out_kernel,
-            [((3, width, half_width), F32), ((half_width, width), F32)],
-            [att, swap(att, "core", "att_core")],
-            2,
+            [((3, width, half_width), F32), ((W_LONG, width), F32)],
+            [
+                (
+                    att_half,
+                    att_x,
+                    swap(att_half, "core", "att_core"),
+                    swap(att_x, "core", "att_core_x"),
+                ),
+                (
+                    table_y,
+                    table_x,
+                    swap(table_y, "core", "table_core"),
+                    swap(table_x, "core", "table_core_x"),
+                ),
+            ],
+            0,
             "attend_out",
-        )
-        (table,) = step(
-            table_out_kernel,
-            [((W_LONG, width), F32)],
-            [
-                table,
-                table_y,
-                swap(table, "core", "table_core"),
-                swap(table_y, "core", "table_core_y"),
-            ],
-            1,
-            "table_out",
-        )
+            scratch=[((2 * att, width), BF16)],
+        )
+
+
     return (
         layer_out,
         grad_tokens,
@@ -1135,35 +1208,39 @@
     table_keep,
     table_send,
 ):
-    def halves(keep, send):
-        first = jnp.concatenate([keep[:n], send[:n]], axis=0)
-        second = jnp.concatenate([keep[n : 2 * n], send[n : 2 * n]], axis=0)
-        return first, second
-
-    def summed(own, oth, make, dim):
-        whole = jnp.concatenate([make(own), make(oth)], axis=dim)
-        part = lax.psum_scatter(whole, "mp", scatter_dimension=dim, tiled=True)
-        return lax.psum(part, "dp").astype(F32)
+    half, spare = n // 2, n // 4
+    group = n + spare
+
+    def rows_of(start, size):
+        return lambda keep, send: jnp.concatenate(
+            [keep[start : start + size], send[start : start + size]], axis=0
+        )
+
+    def summed(own, oth, dim):
+        whole = jnp.concatenate([own, oth], axis=dim)
+        part_sum = lax.psum_scatter(whole, "mp", scatter_dimension=dim, tiled=True)
+        return lax.psum(part_sum, "dp").astype(F32)
 
     def qkv_part(g):
-        value = jnp.concatenate(
-            [g[n : n + n // 2, : n // 2], g[n : n + n // 2, n // 2 :]], axis=0
-        )
-        return jnp.stack([g[:n, : n // 2], g[:n, n // 2 :], value])
+        value = jnp.concatenate([g[n : n + half, :half], g[n : n + half, half:]], axis=0)
+        return jnp.stack([g[:n, :half], g[:n, half:], value])
 
     def up_part(g):
-        return jnp.concatenate([g[s : s + n] for s in range(0, g.shape[0], n)], axis=1)
-
-    att_oth = jnp.concatenate([other_keep, other_send], axis=0)
-    att_own = jnp.concatenate([own_keep, own_send], axis=0)
-    up_own, up_oth = halves(up_keep, up_send)
-    down_own, down_oth = halves(down_keep, down_send)
+        return jnp.concatenate([g[:n], g[n:]], axis=1)
+
+    down = [rows_of(start, n)(down_keep, down_send) for start in (0, n)]
+    up = [up_part(rows_of(start, n)(up_keep, up_send)) for start in (0, group)]
+    out = [rows_of(start + n, spare)(up_keep, up_send) for start in (0, group)]
+    att = [
+        qkv_part(jnp.concatenate(pair, axis=0))
+        for pair in ((own_keep, own_send), (other_keep, other_send))
+    ]
     table = jnp.concatenate([table_keep, table_send], axis=0).astype(F32)
     return (
-        summed(att_own, att_oth, qkv_part, 2),
-        summed(att_own, att_oth, lambda g: g[n + n // 2 :], 0),
-        summed(up_own, up_oth, up_part, 1),
-        summed(down_own, down_oth, lambda g: g, 0),
+        summed(*att, 2),
+        summed(*out, 0),
+        summed(*up, 1),
+        summed(*down, 0),
         lax.psum(small, ("dp", "mp")),
         lax.psum(table, ("dp", "mp")),
     )

time: 166 us -> 124 us (0.75)
  waiting for transfers between devices: 72.4 us -> 43.5 us
  local copies, waits for them, and re-layouts: 8.34 us -> 1.01 us
  starting transfers between devices: 44.5 us -> 37.6 us
  Pallas kernels: 38.2 us -> 40.2 us
    ppermute x38 -> x44, waiting for transfers between devices: 72.4 us -> 40.2 us  [swap(): return lax.ppermute(value, axis, pairs)]
    all_to_all x2 -> x0, starting transfers between devices: 10.4 us -> none  [exchange(): return lax.all_to_all(value, axes, 0, 0, tiled=True)]
    unnamed x42 -> x32, local copies, waits for them, and re-layouts: 8.34 us -> 1.01 us
    ppermute x0 -> x1, waiting for transfers between devices: none -> 3.3 us  [swap_corner(): return lax.ppermute(value, ('x', 'mp'), [(0, 3), (1, 2), (2, 1), (3, 0)])]
    pallas_call x28 -> x29, Pallas kernels: 38.2 us -> 40.2 us  [call(): pl.pallas_call(flat_kernel, out_shape=[jax.ShapeDtypeStruct(out, BF16) if...]
    ppermute x0 -> x1, starting transfers between devices: none -> 1.88 us  [swap_corner(): return lax.ppermute(value, ('x', 'mp'), [(0, 3), (1, 2), (2, 1), (3, 0)])]
    ppermute x38 -> x44, starting transfers between devices: 34.2 us -> 35.7 us  [swap(): return lax.ppermute(value, axis, pairs)]
  transfers between devices with their start and end apart: 40 -> 45, of which waited for: 20 -> 23; matrix products, arithmetic and copies ran while one was open for 0% -> 0% of each run, Pallas kernels for 18% -> 25%
where the time goes in v3:
time: 124 us
  waiting for transfers between devices  43.5 us (35%)
  Pallas kernels  40.2 us (32%)
  starting transfers between devices  37.6 us (30%)
  between operations  1.7 us (1%)
    pallas_call x29, Pallas kernels, call(): pl.pallas_call(flat_kernel, out_shape=[jax.ShapeDtypeStruct(out, BF16) if...  40.2 us
    ppermute x44, waiting for transfers between devices, swap(): return lax.ppermute(value, axis, pairs)  40.2 us
    ppermute x44, starting transfers between devices, swap(): return lax.ppermute(value, axis, pairs)  35.7 us
    ppermute x1, waiting for transfers between devices, swap_corner(): return lax.ppermute(value, ('x', 'mp'), [(0, 3), (1, 2), (2, 1), (3, 0)])  3.3 us
  transfers between devices with their start and end apart: 45, of which 23 were waited for; matrix products, arithmetic and copies ran while one was open for 0% of the time, Pallas kernels for 25%

profile of v3, /device:TPU:0, one launch (start us, length us, event | category | flops | bytes accessed | tf_op | source)
XLA Modules:
  0.0 124.0 jit_solution(17671442781032010850)
XLA Ops:
  0.6 2.4 %pack_attend.1.refs_2_ = bf16[272,512]{1,0:T(8,128)(2,1)} custom-call(bf16[1024]{0:T(1024)(128)(2,1)} %refs_3_.1, bf16[3,512,256]{2,1,0:T(8,128)(2,1)} %bitcast.2, bf16[256,512]{1,0:T(8,128)(2,1)} %refs_5_.5), custom_call_target="tpu_custom_call" | custom-call | flops 1000000000 | tf_op jit(solution)/shard_map/pack_attend/pallas_call | solution.py:39
  3.1 3.0 %collective-permute-start = (bf16[272,512]{1,0:T(8,128)(2,1)}, bf16[272,512]{1,0:T(8,128)(2,1)S(1)}, u32[]{:S(2)}, u32[]{:S(2)}) collective-permute-start(bf16[272,512]{1,0:T(8,128)(2,1)} %pack_attend.1.refs_2_), channel_id=1, source_target_pairs={{0,1},{1,0},{2,3},{3,2},{4,5},{5,4},{6,7},{7,6},{8,9},{9,8},{10,11... | collective-permute-start | bytes 835592 | tf_op jit(solution)/shard_map/attend_y_mp1/ppermute | solution.py:745
  6.1 1.9 %pack_ffn.1 = (bf16[256,512]{1,0:T(8,128)(2,1)}, bf16[256,512]{1,0:T(8,128)(2,1)}) custom-call(bf16[512,1024]{1,0:T(8,128)(2,1)} %refs_5_.4, bf16[1024,512]{1,0:T(8,128)(2,1)} %refs_7_.1, bf16[272,512]{1,0:T(8,128)(2,1)} %pack_attend.1.refs_2_), custom_call_target="tpu_custom_call" | custom-call | flops 1000000000 | tf_op jit(solution)/shard_map/pack_ffn/pallas_call | solution.py:39
  8.9 0.9 copy-done.7
  9.9 2.6 %attend_first.1 = (bf16[3,512,256]{2,1,0:T(8,128)(2,1)S(1)}, bf16[12,256,256]{2,1,0:T(8,128)(2,1)S(1)}, bf16[512,256]{1,0:T(8,128)(2,1)S(1)}) custom-call(s32[1]{0:T(128)S(6)} %copy.51.refs_0_, bf16[512,512]{1,0:T(8,128)(2,1)S(1)} %copy-done.4, bf16[512,512]{1,0:T(8,128)(2,1)S(1)} %copy-done.5, bf16[3,512,256]{2,1,0:T(8,128)(2,1)S(1)} %bitcast.3, ...), custom_call_target="tpu_custom_call" | custom-call | flops 3000000000 | tf_op jit(solution)/shard_map/attend_first/pallas_call | solution.py:39
  12.5 1.3 %collective-permute-done.refs_0_ = bf16[272,512]{1,0:T(8,128)(2,1)S(1)} collective-permute-done((bf16[272,512]{1,0:T(8,128)(2,1)}, bf16[272,512]{1,0:T(8,128)(2,1)S(1)}, u32[]{:S(2)}, u32[]{:S(2)}) %collective-permute-start) | collective-permute-done | bytes 278560 | tf_op jit(solution)/shard_map/attend_y_mp1/ppermute | solution.py:745
  13.8 2.0 %collective-permute-start.1 = (bf16[272,512]{1,0:T(8,128)(2,1)S(1)}, bf16[272,512]{1,0:T(8,128)(2,1)S(1)}, u32[]{:S(2)}, u32[]{:S(2)}) collective-permute-start(bf16[272,512]{1,0:T(8,128)(2,1)S(1)} %gate.11.refs_1_.refs_3_), channel_id=1, source_target_pairs={{0,4},{4,0},{1,5},{5,1},{2,6},{6,2},{3,7},{7,3},{8,12},{12,8},{9,1... | collective-permute-start | bytes 835592 | tf_op jit(solution)/shard_map/attend_x_x1/ppermute | solution.py:745
  15.8 1.5 %collective-permute-start.5 = (bf16[256,512]{1,0:T(8,128)(2,1)S(1)}, bf16[256,512]{1,0:T(8,128)(2,1)S(1)}, u32[]{:S(2)}, u32[]{:S(2)}) collective-permute-start(bf16[256,512]{1,0:T(8,128)(2,1)S(1)} %copy-done.15), channel_id=1, source_target_pairs={{0,1},{1,0},{2,3},{3,2},{4,5},{5,4},{6,7},{7,6},{8,9},{9,8},{10,11... | collective-permute-start | bytes 786440 | tf_op jit(solution)/shard_map/down_y_mp1/ppermute | solution.py:745
  17.4 2.1 %collective-permute-done.2.refs_0_ = bf16[256,512]{1,0:T(8,128)(2,1)S(1)} collective-permute-done((bf16[256,512]{1,0:T(8,128)(2,1)}, bf16[256,512]{1,0:T(8,128)(2,1)S(1)}, u32[]{:S(2)}, u32[]{:S(2)}) %collective-permute-start.2) | collective-permute-done | bytes 262176 | tf_op jit(solution)/shard_map/up_y_mp1/ppermute | solution.py:745
  19.4 1.4 %collective-permute-done.1.refs_0_ = bf16[272,512]{1,0:T(8,128)(2,1)S(1)} collective-permute-done((bf16[272,512]{1,0:T(8,128)(2,1)S(1)}, bf16[272,512]{1,0:T(8,128)(2,1)S(1)}, u32[]{:S(2)}, u32[]{:S(2)}) %collective-permute-start.1) | collective-permute-done | bytes 278560 | tf_op jit(solution)/shard_map/attend_x_x1/ppermute | solution.py:745
  21.3 1.6 %collective-permute-start.6 = (bf16[256,512]{1,0:T(8,128)(2,1)S(1)}, bf16[256,512]{1,0:T(8,128)(2,1)S(1)}, u32[]{:S(2)}, u32[]{:S(2)}) collective-permute-start(bf16[256,512]{1,0:T(8,128)(2,1)S(1)} %gate.12.refs_1_.refs_4_), channel_id=1, source_target_pairs={{0,4},{4,0},{1,5},{5,1},{2,6},{6,2},{3,7},{7,3},{8,12},{12,8},{9,1... | collective-permute-start | bytes 786440 | tf_op jit(solution)/shard_map/up_x_x1/ppermute | solution.py:745
  23.0 1.3 %collective-permute-done.5.refs_0_ = bf16[256,512]{1,0:T(8,128)(2,1)S(1)} collective-permute-done((bf16[256,512]{1,0:T(8,128)(2,1)S(1)}, bf16[256,512]{1,0:T(8,128)(2,1)S(1)}, u32[]{:S(2)}, u32[]{:S(2)}) %collective-permute-start.5) | collective-permute-done | bytes 262176 | tf_op jit(solution)/shard_map/down_y_mp1/ppermute | solution.py:745
  24.3 1.9 %collective-permute-start.9 = (bf16[256,512]{1,0:T(8,128)(2,1)S(1)}, bf16[256,512]{1,0:T(8,128)(2,1)S(1)}, u32[]{:S(2)}, u32[]{:S(2)}) collective-permute-start(bf16[256,512]{1,0:T(8,128)(2,1)S(1)} %gate.14.refs_10_.refs_8_), channel_id=1, source_target_pairs={{0,8},{8,0},{16,24},{24,16},{1,9},{9,1},{17,25},{25,17},{2,10},{10... | collective-permute-start | bytes 786440 | tf_op jit(solution)/shard_map/down_z_z1/ppermute | solution.py:745
  26.2 3.0 %attend_second.1 = (bf16[3,512,256]{2,1,0:T(8,128)(2,1)S(1)}, bf16[12,256,256]{2,1,0:T(8,128)(2,1)S(1)}, bf16[512,256]{1,0:T(8,128)(2,1)S(1)}, f32[512,512]{1,0:...) custom-call(s32[1]{0:T(128)S(6)} %copy.51.refs_0_, ...), custom_call_target="tpu_custom_call" | custom-call | flops 5000000000 | tf_op jit(solution)/shard_map/attend_second/pallas_call | solution.py:39
  29.7 3.2 %ffn_own.1 = (bf16[512,512]{1,0:T(8,128)(2,1)S(1)}, bf16[512,1024]{1,0:T(8,128)(2,1)S(1)}, bf16[512,1024]{1,0:T(8,128)(2,1)S(1)}, f32[512,512]{1,0:T(8,128)S(1)}) custom-call(f32[512,512]{1,0:T(8,128)S(1)} %get-tuple-element.85.refs_0_, bf16[512,1024]{1,0:T(8,128)(2,1)S(1)} %copy-done, bf16[1024,512]{1,0:T(8,128)(2,1)S(1)} %copy-done.1, ...), custom_call_target="tpu_custom_call" | custom-call | flops 4000000000 | tf_op jit(solution)/shard_map/ffn_own/pallas_call | solution.py:39
  33.5 1.2 %collective-permute-done.11.refs_11_ = bf16[256,512]{1,0:T(8,128)(2,1)S(1)} collective-permute-done((bf16[256,512]{1,0:T(8,128)(2,1)S(1)}, bf16[256,512]{1,0:T(8,128)(2,1)S(1)}, u32[]{:S(2)}, u32[]{:S(2)}) %collective-permute-start.11) | collective-permute-done | bytes 262176 | tf_op jit(solution)/shard_map/down_cz_core1/ppermute | solution.py:745
  34.7 5.0 %ffn_other.1 = (bf16[512,512]{1,0:T(8,128)(2,1)}, bf16[1024,512]{1,0:T(8,128)(2,1)S(1)}, bf16[1024,512]{1,0:T(8,128)(2,1)S(1)}, bf16[512,1024]{1,0:T(8,128)(2,1)...) custom-call(bf16[512,512]{1,0:T(8,128)(2,1)S(1)} %copy-done.3, ...), custom_call_target="tpu_custom_call" | custom-call | flops 6000000000 | tf_op jit(solution)/shard_map/ffn_other/pallas_call | solution.py:39
  40.1 4.7 %ffn_back.1 = (bf16[1296,512]{1,0:T(8,128)(2,1)S(1)}, bf16[1296,512]{1,0:T(8,128)(2,1)S(1)}, f32[16,512]{1,0:T(8,128)S(1)}, f32[512,512]{1,0:T(8,128)S(1)}) custom-call(f32[512,512]{1,0:T(8,128)S(1)} %get-tuple-element.85.refs_0_, f32[512,512]{1,0:T(8,128)S(1)} %get-tuple-element.91.refs_1_, bf16[512,512]{1,0:T(8,128)(2,1)S(1)} %get-tuple-element.87.refs_1_.refs_2_, ...), custom_call_target="tpu_custom_call" | custom-call | flops 6000000000 | tf_op jit(solution)/shard_map/ffn_back/pallas_call | solution.py:39
  45.2 1.8 %collective-permute-start.17 = (bf16[512,512]{1,0:T(8,128)(2,1)S(1)}, bf16[512,512]{1,0:T(8,128)(2,1)S(1)}, u32[]{:S(2)}, u32[]{:S(2)}) collective-permute-start(bf16[512,512]{1,0:T(8,128)(2,1)S(1)} %down_core.1.refs_2_), channel_id=1, source_target_pairs={{0,1},{1,0},{2,3},{3,2},{4,5},{5,4},{6,7},{7,6},{8,9},{9,8},{10,11... | collective-permute-start | bytes 1572872 | tf_op jit(solution)/shard_map/down_from_y_mp1/ppermute | solution.py:745
  47.0 0.9 collective-permute-done.12.refs_1_
  47.9 0.8 up_core.1
  48.7 1.8 %collective-permute-start.20 = (bf16[656,512]{1,0:T(8,128)(2,1)S(1)}, bf16[656,512]{1,0:T(8,128)(2,1)S(1)}, u32[]{:S(2)}, u32[]{:S(2)}) collective-permute-start(bf16[656,512]{1,0:T(8,128)(2,1)S(1)} %get-tuple-element.122), channel_id=1, source_target_pairs={{0,8},{8,0},{16,24},{24,16},{1,9},{9,1},{17,25},{25,17},{2,10},{10... | collective-permute-start | bytes 2015240 | tf_op jit(solution)/shard_map/up_from_z_z1/ppermute | solution.py:745
  50.5 8.9 %attend_back.1 = (bf16[384,512]{1,0:T(8,128)(2,1)S(1)}, bf16[384,512]{1,0:T(8,128)(2,1)S(1)}, bf16[384,512]{1,0:T(8,128)(2,1)S(1)}, bf16[384,512]{1,0:T(8,128)(2...) custom-call(s32[1]{0:T(128)S(6)} %copy.51.refs_0_, ...), custom_call_target="tpu_custom_call" | custom-call | flops 12999999488 | tf_op jit(solution)/shard_map/attend_back/pallas_call | solution.py:39
  60.4 1.5 %collective-permute-start.19 = (bf16[256,512]{1,0:T(8,128)(2,1)S(1)}, bf16[256,512]{1,0:T(8,128)(2,1)S(1)}, u32[]{:S(2)}, u32[]{:S(2)}) collective-permute-start(bf16[256,512]{1,0:T(8,128)(2,1)S(1)} %get-tuple-element.121), channel_id=1, source_target_pairs={{0,4},{4,0},{1,5},{5,1},{2,6},{6,2},{3,7},{7,3},{8,12},{12,8},{9,1... | collective-permute-start | bytes 786440 | tf_op jit(solution)/shard_map/down_from_x_x1/ppermute | solution.py:745
  62.2 1.5 %collective-permute-start.18 = (bf16[512,512]{1,0:T(8,128)(2,1)S(1)}, bf16[512,512]{1,0:T(8,128)(2,1)S(1)}, u32[]{:S(2)}, u32[]{:S(2)}) collective-permute-start(bf16[512,512]{1,0:T(8,128)(2,1)S(1)} %get-tuple-element.119), channel_id=1, source_target_pairs={{0,1},{1,0},{2,3},{3,2},{4,5},{5,4},{6,7},{7,6},{8,9},{9,8},{10,11... | collective-permute-start | bytes 1572872 | tf_op jit(solution)/shard_map/att_from_y_mp1/ppermute | solution.py:745
  63.7 2.3 %collective-permute-done.20.refs_1_ = bf16[656,512]{1,0:T(8,128)(2,1)S(1)} collective-permute-done((bf16[656,512]{1,0:T(8,128)(2,1)S(1)}, bf16[656,512]{1,0:T(8,128)(2,1)S(1)}, u32[]{:S(2)}, u32[]{:S(2)}) %collective-permute-start.20) | collective-permute-done | bytes 671776 | tf_op jit(solution)/shard_map/up_from_z_z1/ppermute | solution.py:745
  66.4 1.7 %collective-permute-start.24 = (bf16[336,512]{1,0:T(8,128)(2,1)S(1)}, bf16[336,512]{1,0:T(8,128)(2,1)S(1)}, u32[]{:S(2)}, u32[]{:S(2)}) collective-permute-start(bf16[336,512]{1,0:T(8,128)(2,1)S(1)} %get-tuple-element.128), channel_id=1, source_target_pairs={{0,4},{4,0},{1,5},{5,1},{2,6},{6,2},{3,7},{7,3},{8,12},{12,8},{9,1... | collective-permute-start | bytes 1032200 | tf_op jit(solution)/shard_map/up_from_x_x1/ppermute | solution.py:745
  68.8 1.0 collective-permute-start.21
  69.9 4.0 %collective-permute-done.21.refs_1_ = bf16[128,512]{1,0:T(8,128)(2,1)S(1)} collective-permute-done((bf16[128,512]{1,0:T(8,128)(2,1)S(1)}, bf16[128,512]{1,0:T(8,128)(2,1)S(1)}, u32[]{:S(2)}, u32[]{:S(2)}) %collective-permute-start.21) | collective-permute-done | bytes 131104 | tf_op jit(solution)/shard_map/down_from_z_z1/ppermute | solution.py:745
  73.9 2.0 %collective-permute-done.18.refs_2_ = bf16[512,512]{1,0:T(8,128)(2,1)S(1)} collective-permute-done((bf16[512,512]{1,0:T(8,128)(2,1)S(1)}, bf16[512,512]{1,0:T(8,128)(2,1)S(1)}, u32[]{:S(2)}, u32[]{:S(2)}) %collective-permute-start.18) | collective-permute-done | bytes 524320 | tf_op jit(solution)/shard_map/att_from_y_mp1/ppermute | solution.py:745
  76.2 1.5 %collective-permute-start.22 = (bf16[256,512]{1,0:T(8,128)(2,1)S(1)}, bf16[256,512]{1,0:T(8,128)(2,1)S(1)}, u32[]{:S(2)}, u32[]{:S(2)}) collective-permute-start(bf16[256,512]{1,0:T(8,128)(2,1)S(1)} %get-tuple-element.127), channel_id=1, source_target_pairs={{0,4},{4,0},{1,5},{5,1},{2,6},{6,2},{3,7},{7,3},{8,12},{12,8},{9,1... | collective-permute-start | bytes 786440 | tf_op jit(solution)/shard_map/att_from_x_x1/ppermute | solution.py:745
  77.8 2.6 %collective-permute-start.23 = (bf16[128,512]{1,0:T(8,128)(2,1)S(1)}, bf16[128,512]{1,0:T(8,128)(2,1)S(1)}, u32[]{:S(2)}, u32[]{:S(2)}) collective-permute-start(bf16[128,512]{1,0:T(8,128)(2,1)S(1)} %down_z.1.refs_4_.refs_0_), channel_id=1, source_target_pairs={{0,16},{8,24},{16,0},{24,8},{1,17},{9,25},{17,1},{25,9},{2,18},{10... | collective-permute-start | bytes 393224 | tf_op jit(solution)/shard_map/down_far_z2/ppermute | solution.py:745
  80.5 1.5 %collective-permute-start.26 = (bf16[176,512]{1,0:T(8,128)(2,1)S(1)}, bf16[176,512]{1,0:T(8,128)(2,1)S(1)}, u32[]{:S(2)}, u32[]{:S(2)}) collective-permute-start(bf16[176,512]{1,0:T(8,128)(2,1)S(1)} %get-tuple-element.132), channel_id=1, source_target_pairs={{0,1},{1,0},{2,3},{3,2},{4,5},{5,4},{6,7},{7,6},{8,9},{9,8},{10,11... | collective-permute-start | bytes 540680 | tf_op jit(solution)/shard_map/up_from_y_mp1/ppermute | solution.py:745
  82.0 3.5 %collective-permute-done.23.refs_1_ = bf16[128,512]{1,0:T(8,128)(2,1)S(1)} collective-permute-done((bf16[128,512]{1,0:T(8,128)(2,1)S(1)}, bf16[128,512]{1,0:T(8,128)(2,1)S(1)}, u32[]{:S(2)}, u32[]{:S(2)}) %collective-permute-start.23) | collective-permute-done | bytes 131104 | tf_op jit(solution)/shard_map/down_far_z2/ppermute | solution.py:745
  86.1 2.9 %collective-permute-start.28 = (bf16[176,512]{1,0:T(8,128)(2,1)S(1)}, bf16[176,512]{1,0:T(8,128)(2,1)S(1)}, u32[]{:S(2)}, u32[]{:S(2)}) collective-permute-start(bf16[176,512]{1,0:T(8,128)(2,1)S(1)} %up_mp.1.refs_2_.refs_0_), channel_id=1, source_target_pairs={{0,16},{8,24},{16,0},{24,8},{1,17},{9,25},{17,1},{25,9},{2,18},{10... | collective-permute-start | bytes 540680 | tf_op jit(solution)/shard_map/up_far_z2/ppermute | solution.py:745
  89.1 5.6 %collective-permute-done.25.refs_1_ = bf16[128,512]{1,0:T(8,128)(2,1)S(1)} collective-permute-done((bf16[128,512]{1,0:T(8,128)(2,1)S(1)}, bf16[128,512]{1,0:T(8,128)(2,1)S(1)}, u32[]{:S(2)}, u32[]{:S(2)}) %collective-permute-start.25) | collective-permute-done | bytes 131104 | tf_op jit(solution)/shard_map/att_from_z_z1/ppermute | solution.py:745
  94.9 2.6 %collective-permute-done.29.refs_1_ = bf16[128,512]{1,0:T(8,128)(2,1)S(1)} collective-permute-done((bf16[128,512]{1,0:T(8,128)(2,1)S(1)}, bf16[128,512]{1,0:T(8,128)(2,1)S(1)}, u32[]{:S(2)}, u32[]{:S(2)}) %collective-permute-start.29) | collective-permute-done | bytes 131104 | tf_op jit(solution)/shard_map/down_near_z1/ppermute | solution.py:745
  98.8 1.5 %collective-permute-start.33 = (bf16[160,512]{1,0:T(8,128)(2,1)S(1)}, bf16[160,512]{1,0:T(8,128)(2,1)S(1)}, u32[]{:S(2)}, u32[]{:S(2)}) collective-permute-start(bf16[160,512]{1,0:T(8,128)(2,1)S(1)} %get-tuple-element.133.refs_2_.refs_0_), channel_id=1, source_target_pairs={{0,4},{4,0},{1,5},{5,1},{2,6},{6,2},{3,7},{7,3},{8,12},{12,8},{9,1... | collective-permute-start | bytes 491528 | tf_op jit(solution)/shard_map/up_near_x1/ppermute | solution.py:745
  100.3 1.7 %collective-permute-done.27.refs_1_ = bf16[128,512]{1,0:T(8,128)(2,1)S(1)} collective-permute-done((bf16[128,512]{1,0:T(8,128)(2,1)S(1)}, bf16[128,512]{1,0:T(8,128)(2,1)S(1)}, u32[]{:S(2)}, u32[]{:S(2)}) %collective-permute-start.27) | collective-permute-done | bytes 131104 | tf_op jit(solution)/shard_map/att_far_z2/ppermute | solution.py:745
  102.1 5.0 %collective-permute-done.30.refs_1_ = bf16[128,512]{1,0:T(8,128)(2,1)S(1)} collective-permute-done((bf16[128,512]{1,0:T(8,128)(2,1)S(1)}, bf16[128,512]{1,0:T(8,128)(2,1)S(1)}, u32[]{:S(2)}, u32[]{:S(2)}) %collective-permute-start.30) | collective-permute-done | bytes 131104 | tf_op jit(solution)/shard_map/att_near_z1/ppermute | solution.py:745
  108.8 1.5 %collective-permute-start.35 = (bf16[64,512]{1,0:T(8,128)(2,1)S(1)}, bf16[64,512]{1,0:T(8,128)(2,1)S(1)}, u32[]{:S(2)}, u32[]{:S(2)}) collective-permute-start(bf16[64,512]{1,0:T(8,128)(2,1)S(1)} %get-tuple-element.135.refs_2_), channel_id=1, source_target_pairs={{0,1},{1,0},{2,3},{3,2},{4,5},{5,4},{6,7},{7,6},{8,9},{9,8},{10,11... | collective-permute-start | bytes 196616 | tf_op jit(solution)/shard_map/table_y_mp1/ppermute | solution.py:745
  110.2 1.5 %down_out.1 = (f32[1024,512]{1,0:T(8,128)}, f32[8,128]{1,0:T(8,128)S(1)}) custom-call(bf16[256,512]{1,0:T(8,128)(2,1)S(1)} %down_join.1.refs_2_.refs_0_, bf16[256,512]{1,0:T(8,128)(2,1)S(1)} %gate.17.refs_1_.refs_4_, bf16[256,512]{1,0:T(8,128)(2,1)S(1)} %collective-permute-done.37.refs_2_, bf16[256,512]{1,0:T(8,128)(2,1)S(1)} %collective-permute-done.38.refs_3_, ...), custom_call_target="tpu_custom_call" | custom-call | tf_op jit(solution)/shard_map/down_out/pallas_call | solution.py:39
  111.7 1.3 %collective-permute-done.35.refs_0_ = bf16[64,512]{1,0:T(8,128)(2,1)S(1)} collective-permute-done((bf16[64,512]{1,0:T(8,128)(2,1)S(1)}, bf16[64,512]{1,0:T(8,128)(2,1)S(1)}, u32[]{:S(2)}, u32[]{:S(2)}) %collective-permute-start.35) | collective-permute-done | bytes 65568 | tf_op jit(solution)/shard_map/table_y_mp1/ppermute | solution.py:745
  113.0 1.6 %collective-permute-done.34.refs_0_ = bf16[320,512]{1,0:T(8,128)(2,1)S(1)} collective-permute-done((bf16[320,512]{1,0:T(8,128)(2,1)S(1)}, bf16[320,512]{1,0:T(8,128)(2,1)S(1)}, u32[]{:S(2)}, u32[]{:S(2)}) %collective-permute-start.34) | collective-permute-done | bytes 327712 | tf_op jit(solution)/shard_map/up_last_z1/ppermute | solution.py:745
  114.6 1.9 %collective-permute-start.32 = (bf16[64,512]{1,0:T(8,128)(2,1)S(1)}, bf16[64,512]{1,0:T(8,128)(2,1)S(1)}, u32[]{:S(2)}, u32[]{:S(2)}) collective-permute-start(bf16[64,512]{1,0:T(8,128)(2,1)S(1)} %get-tuple-element.135.refs_2_), channel_id=1, source_target_pairs={{0,5},{1,4},{4,1},{5,0},{2,7},{3,6},{6,3},{7,2},{8,13},{9,12},{12,... | collective-permute-start | bytes 196616 | tf_op jit(solution)/shard_map/table_x/ppermute | solution.py:750
  116.8 3.3 %collective-permute-done.32.refs_0_ = bf16[64,512]{1,0:T(8,128)(2,1)S(1)} collective-permute-done((bf16[64,512]{1,0:T(8,128)(2,1)S(1)}, bf16[64,512]{1,0:T(8,128)(2,1)S(1)}, u32[]{:S(2)}, u32[]{:S(2)}) %collective-permute-start.32) | collective-permute-done | bytes 65568 | tf_op jit(solution)/shard_map/table_x/ppermute | solution.py:750
  120.6 1.7 %up_out.1 = (f32[512,1024]{1,0:T(8,128)}, f32[256,512]{1,0:T(8,128)}, f32[8,128]{1,0:T(8,128)S(1)}) custom-call(bf16[320,512]{1,0:T(8,128)(2,1)S(1)} %up_join.1.refs_1_.refs_0_, bf16[320,512]{1,0:T(8,128)(2,1)S(1)} %gate.19.refs_1_, bf16[320,512]{1,0:T(8,128)(2,1)S(1)} %collective-permute-done.43.refs_2_, ...), custom_call_target="tpu_custom_call" | custom-call | tf_op jit(solution)/shard_map/up_out/pallas_call | solution.py:39
  122.4 1.6 %attend_out.1 = (f32[3,512,256]{2,1,0:T(8,128)}, f32[512,512]{1,0:T(8,128)}) custom-call(bf16[256,512]{1,0:T(8,128)(2,1)S(1)} %get-tuple-element.134.refs_0_, bf16[256,512]{1,0:T(8,128)(2,1)S(1)} %gate.21.refs_4_.refs_1_, bf16[256,512]{1,0:T(8,128)(2,1)S(1)} %collective-permute-done.39.refs_2_, bf16[256,512]{1,0:T(8,128)(2,1)S(1)} %collective-permute-done.40.refs_3_, ...), custom_call_target="tpu_custom_call" | custom-call | tf_op jit(solution)/shard_map/attend_out/pallas_call | solution.py:39
  (114 shorter events, 10.1 us)
Async XLA Ops:
  3.0 5.8 %copy-start.2 = (bf16[512,3,256]{2,0,1:T(8,128)(2,1)S(1)}, bf16[512,3,256]{2,0,1:T(8,128)(2,1)}, u32[]{:S(2)}) copy-start(bf16[512,3,256]{2,0,1:T(8,128)(2,1)} %param.17) | copy-start | bytes 2359300
  3.1 5.8 %copy-start.4 = (bf16[512,512]{1,0:T(8,128)(2,1)S(1)}, bf16[512,512]{1,0:T(8,128)(2,1)}, u32[]{:S(2)}) copy-start(bf16[512,512]{1,0:T(8,128)(2,1)} %refs_1_.9) | copy-start | bytes 1572868
  3.1 5.8 %copy-start.5 = (bf16[512,512]{1,0:T(8,128)(2,1)S(1)}, bf16[512,512]{1,0:T(8,128)(2,1)}, u32[]{:S(2)}) copy-start(bf16[512,512]{1,0:T(8,128)(2,1)} %refs_2_.9) | copy-start | bytes 1572868
  3.1 10.7 %collective-permute-start = (bf16[272,512]{1,0:T(8,128)(2,1)}, bf16[272,512]{1,0:T(8,128)(2,1)S(1)}, u32[]{:S(2)}, u32[]{:S(2)}) collective-permute-start(bf16[272,512]{1,0:T(8,128)(2,1)} %pack_attend.1.refs_2_), channel_id=1, source_target_pairs={{0,1},{1,0},{2,3},{3,2},{4,5},{5,4},{6,7},{7,6},{8,9},{9,8},{10,11... | collective-permute-start | bytes 835592 | tf_op jit(solution)/shard_map/attend_y_mp1/ppermute | solution.py:745
  8.0 11.4 %collective-permute-start.2 = (bf16[256,512]{1,0:T(8,128)(2,1)}, bf16[256,512]{1,0:T(8,128)(2,1)S(1)}, u32[]{:S(2)}, u32[]{:S(2)}) collective-permute-start(bf16[256,512]{1,0:T(8,128)(2,1)} %get-tuple-element.82.refs_4_), channel_id=1, source_target_pairs={{0,1},{1,0},{2,3},{3,2},{4,5},{5,4},{6,7},{7,6},{8,9},{9,8},{10,11... | collective-permute-start | bytes 786440 | tf_op jit(solution)/shard_map/up_y_mp1/ppermute | solution.py:745
  13.8 7.0 %collective-permute-start.1 = (bf16[272,512]{1,0:T(8,128)(2,1)S(1)}, bf16[272,512]{1,0:T(8,128)(2,1)S(1)}, u32[]{:S(2)}, u32[]{:S(2)}) collective-permute-start(bf16[272,512]{1,0:T(8,128)(2,1)S(1)} %gate.11.refs_1_.refs_3_), channel_id=1, source_target_pairs={{0,4},{4,0},{1,5},{5,1},{2,6},{6,2},{3,7},{7,3},{8,12},{12,8},{9,1... | collective-permute-start | bytes 835592 | tf_op jit(solution)/shard_map/attend_x_x1/ppermute | solution.py:745
  15.8 8.4 %collective-permute-start.5 = (bf16[256,512]{1,0:T(8,128)(2,1)S(1)}, bf16[256,512]{1,0:T(8,128)(2,1)S(1)}, u32[]{:S(2)}, u32[]{:S(2)}) collective-permute-start(bf16[256,512]{1,0:T(8,128)(2,1)S(1)} %copy-done.15), channel_id=1, source_target_pairs={{0,1},{1,0},{2,3},{3,2},{4,5},{5,4},{6,7},{7,6},{8,9},{9,8},{10,11... | collective-permute-start | bytes 786440 | tf_op jit(solution)/shard_map/down_y_mp1/ppermute | solution.py:745
  17.4 7.0 %collective-permute-start.3 = (bf16[272,512]{1,0:T(8,128)(2,1)S(1)}, bf16[272,512]{1,0:T(8,128)(2,1)S(1)}, u32[]{:S(2)}, u32[]{:S(2)}) collective-permute-start(bf16[272,512]{1,0:T(8,128)(2,1)S(1)} %gate.11.refs_1_.refs_3_), channel_id=1, source_target_pairs={{0,2},{2,0},{1,3},{3,1},{4,6},{6,4},{5,7},{7,5},{8,10},{10,8},{9,1... | collective-permute-start | bytes 835592 | tf_op jit(solution)/shard_map/attend_cy_core1/ppermute | solution.py:745
  20.8 5.4 %collective-permute-start.4 = (bf16[272,512]{1,0:T(8,128)(2,1)S(1)}, bf16[272,512]{1,0:T(8,128)(2,1)S(1)}, u32[]{:S(2)}, u32[]{:S(2)}) collective-permute-start(bf16[272,512]{1,0:T(8,128)(2,1)S(1)} %gate.13.refs_1_.refs_4_), channel_id=1, source_target_pairs={{0,2},{2,0},{1,3},{3,1},{4,6},{6,4},{5,7},{7,5},{8,10},{10,8},{9,1... | collective-permute-start | bytes 835592 | tf_op jit(solution)/shard_map/attend_cx_core1/ppermute | solution.py:745
  20.8 12.6 %collective-permute-start.7 = (bf16[256,512]{1,0:T(8,128)(2,1)S(1)}, bf16[256,512]{1,0:T(8,128)(2,1)S(1)}, u32[]{:S(2)}, u32[]{:S(2)}) collective-permute-start(bf16[256,512]{1,0:T(8,128)(2,1)S(1)} %gate.12.refs_1_.refs_4_), channel_id=1, source_target_pairs={{0,2},{2,0},{1,3},{3,1},{4,6},{6,4},{5,7},{7,5},{8,10},{10,8},{9,1... | collective-permute-start | bytes 786440 | tf_op jit(solution)/shard_map/up_cy_core1/ppermute | solution.py:745
  21.3 8.3 %collective-permute-start.6 = (bf16[256,512]{1,0:T(8,128)(2,1)S(1)}, bf16[256,512]{1,0:T(8,128)(2,1)S(1)}, u32[]{:S(2)}, u32[]{:S(2)}) collective-permute-start(bf16[256,512]{1,0:T(8,128)(2,1)S(1)} %gate.12.refs_1_.refs_4_), channel_id=1, source_target_pairs={{0,4},{4,0},{1,5},{5,1},{2,6},{6,2},{3,7},{7,3},{8,12},{12,8},{9,1... | collective-permute-start | bytes 786440 | tf_op jit(solution)/shard_map/up_x_x1/ppermute | solution.py:745
  24.2 9.2 %collective-permute-start.10 = (bf16[256,512]{1,0:T(8,128)(2,1)S(1)}, bf16[256,512]{1,0:T(8,128)(2,1)S(1)}, u32[]{:S(2)}, u32[]{:S(2)}) collective-permute-start(bf16[256,512]{1,0:T(8,128)(2,1)S(1)} %gate.14.refs_10_.refs_8_), channel_id=1, source_target_pairs={{0,2},{2,0},{1,3},{3,1},{4,6},{6,4},{5,7},{7,5},{8,10},{10,8},{9,1... | collective-permute-start | bytes 786440 | tf_op jit(solution)/shard_map/down_cy_core1/ppermute | solution.py:745
  24.3 8.8 %collective-permute-start.9 = (bf16[256,512]{1,0:T(8,128)(2,1)S(1)}, bf16[256,512]{1,0:T(8,128)(2,1)S(1)}, u32[]{:S(2)}, u32[]{:S(2)}) collective-permute-start(bf16[256,512]{1,0:T(8,128)(2,1)S(1)} %gate.14.refs_10_.refs_8_), channel_id=1, source_target_pairs={{0,8},{8,0},{16,24},{24,16},{1,9},{9,1},{17,25},{25,17},{2,10},{10... | collective-permute-start | bytes 786440 | tf_op jit(solution)/shard_map/down_z_z1/ppermute | solution.py:745
  29.6 3.8 %collective-permute-start.8 = (bf16[256,512]{1,0:T(8,128)(2,1)S(1)}, bf16[256,512]{1,0:T(8,128)(2,1)S(1)}, u32[]{:S(2)}, u32[]{:S(2)}) collective-permute-start(bf16[256,512]{1,0:T(8,128)(2,1)S(1)} %gate.15.refs_6_.refs_5_), channel_id=1, source_target_pairs={{0,2},{2,0},{1,3},{3,1},{4,6},{6,4},{5,7},{7,5},{8,10},{10,8},{9,1... | collective-permute-start | bytes 786440 | tf_op jit(solution)/shard_map/up_cx_core1/ppermute | solution.py:745
  33.1 1.6 %collective-permute-start.11 = (bf16[256,512]{1,0:T(8,128)(2,1)S(1)}, bf16[256,512]{1,0:T(8,128)(2,1)S(1)}, u32[]{:S(2)}, u32[]{:S(2)}) collective-permute-start(bf16[256,512]{1,0:T(8,128)(2,1)S(1)} %gate.16.refs_9_.refs_16_), channel_id=1, source_target_pairs={{0,2},{2,0},{1,3},{3,1},{4,6},{6,4},{5,7},{7,5},{8,10},{10,8},{9,1... | collective-permute-start | bytes 786440 | tf_op jit(solution)/shard_map/down_cz_core1/ppermute | solution.py:745
  39.7 5.4 %collective-permute-start.13 = (bf16[1024,512]{1,0:T(8,128)(2,1)S(1)}, bf16[1024,512]{1,0:T(8,128)(2,1)S(1)}, u32[]{:S(2)}, u32[]{:S(2)}) collective-permute-start(bf16[1024,512]{1,0:T(8,128)(2,1)S(1)} %get-tuple-element.108), channel_id=1, source_target_pairs={{0,2},{2,0},{1,3},{3,1},{4,6},{6,4},{5,7},{7,5},{8,10},{10,8},{9,1... | collective-permute-start | bytes 3145736 | tf_op jit(solution)/shard_map/down_recv_core1/ppermute | solution.py:745
  44.8 3.1 %collective-permute-start.12 = (bf16[1296,512]{1,0:T(8,128)(2,1)S(1)}, bf16[1296,512]{1,0:T(8,128)(2,1)S(1)}, u32[]{:S(2)}, u32[]{:S(2)}) collective-permute-start(bf16[1296,512]{1,0:T(8,128)(2,1)S(1)} %get-tuple-element.106), channel_id=1, source_target_pairs={{0,2},{2,0},{1,3},{3,1},{4,6},{6,4},{5,7},{7,5},{8,10},{10,8},{9,1... | collective-permute-start | bytes 3981320 | tf_op jit(solution)/shard_map/up_recv_core1/ppermute | solution.py:745
  45.2 14.7 %collective-permute-start.17 = (bf16[512,512]{1,0:T(8,128)(2,1)S(1)}, bf16[512,512]{1,0:T(8,128)(2,1)S(1)}, u32[]{:S(2)}, u32[]{:S(2)}) collective-permute-start(bf16[512,512]{1,0:T(8,128)(2,1)S(1)} %down_core.1.refs_2_), channel_id=1, source_target_pairs={{0,1},{1,0},{2,3},{3,2},{4,5},{5,4},{6,7},{7,6},{8,9},{9,8},{10,11... | collective-permute-start | bytes 1572872 | tf_op jit(solution)/shard_map/down_from_y_mp1/ppermute | solution.py:745
  48.7 17.3 %collective-permute-start.20 = (bf16[656,512]{1,0:T(8,128)(2,1)S(1)}, bf16[656,512]{1,0:T(8,128)(2,1)S(1)}, u32[]{:S(2)}, u32[]{:S(2)}) collective-permute-start(bf16[656,512]{1,0:T(8,128)(2,1)S(1)} %get-tuple-element.122), channel_id=1, source_target_pairs={{0,8},{8,0},{16,24},{24,16},{1,9},{9,1},{17,25},{25,17},{2,10},{10... | collective-permute-start | bytes 2015240 | tf_op jit(solution)/shard_map/up_from_z_z1/ppermute | solution.py:745
  59.4 2.5 %collective-permute-start.15 = (bf16[384,512]{1,0:T(8,128)(2,1)S(1)}, bf16[384,512]{1,0:T(8,128)(2,1)S(1)}, u32[]{:S(2)}, u32[]{:S(2)}) collective-permute-start(bf16[384,512]{1,0:T(8,128)(2,1)S(1)} %get-tuple-element.115), channel_id=1, source_target_pairs={{0,2},{2,0},{1,3},{3,1},{4,6},{6,4},{5,7},{7,5},{8,10},{10,8},{9,1... | collective-permute-start | bytes 1179656 | tf_op jit(solution)/shard_map/oth_recv_core1/ppermute | solution.py:745
  59.4 2.5 %collective-permute-start.16 = (bf16[256,512]{1,0:T(8,128)(2,1)S(1)}, bf16[256,512]{1,0:T(8,128)(2,1)S(1)}, u32[]{:S(2)}, u32[]{:S(2)}) collective-permute-start(bf16[256,512]{1,0:T(8,128)(2,1)S(1)} %get-tuple-element.117), channel_id=1, source_target_pairs={{0,2},{2,0},{1,3},{3,1},{4,6},{6,4},{5,7},{7,5},{8,10},{10,8},{9,1... | collective-permute-start | bytes 786440 | tf_op jit(solution)/shard_map/tab_recv_core1/ppermute | solution.py:745
  60.4 8.4 %collective-permute-start.19 = (bf16[256,512]{1,0:T(8,128)(2,1)S(1)}, bf16[256,512]{1,0:T(8,128)(2,1)S(1)}, u32[]{:S(2)}, u32[]{:S(2)}) collective-permute-start(bf16[256,512]{1,0:T(8,128)(2,1)S(1)} %get-tuple-element.121), channel_id=1, source_target_pairs={{0,4},{4,0},{1,5},{5,1},{2,6},{6,2},{3,7},{7,3},{8,12},{12,8},{9,1... | collective-permute-start | bytes 786440 | tf_op jit(solution)/shard_map/down_from_x_x1/ppermute | solution.py:745
  62.2 13.6 %collective-permute-start.18 = (bf16[512,512]{1,0:T(8,128)(2,1)S(1)}, bf16[512,512]{1,0:T(8,128)(2,1)S(1)}, u32[]{:S(2)}, u32[]{:S(2)}) collective-permute-start(bf16[512,512]{1,0:T(8,128)(2,1)S(1)} %get-tuple-element.119), channel_id=1, source_target_pairs={{0,1},{1,0},{2,3},{3,2},{4,5},{5,4},{6,7},{7,6},{8,9},{9,8},{10,11... | collective-permute-start | bytes 1572872 | tf_op jit(solution)/shard_map/att_from_y_mp1/ppermute | solution.py:745
  63.7 10.2 %collective-permute-start.14 = (bf16[384,512]{1,0:T(8,128)(2,1)S(1)}, bf16[384,512]{1,0:T(8,128)(2,1)S(1)}, u32[]{:S(2)}, u32[]{:S(2)}) collective-permute-start(bf16[384,512]{1,0:T(8,128)(2,1)S(1)} %get-tuple-element.113), channel_id=1, source_target_pairs={{0,2},{2,0},{1,3},{3,1},{4,6},{6,4},{5,7},{7,5},{8,10},{10,8},{9,1... | collective-permute-start | bytes 1179656 | tf_op jit(solution)/shard_map/own_recv_core1/ppermute | solution.py:745
  66.4 14.0 %collective-permute-start.24 = (bf16[336,512]{1,0:T(8,128)(2,1)S(1)}, bf16[336,512]{1,0:T(8,128)(2,1)S(1)}, u32[]{:S(2)}, u32[]{:S(2)}) collective-permute-start(bf16[336,512]{1,0:T(8,128)(2,1)S(1)} %get-tuple-element.128), channel_id=1, source_target_pairs={{0,4},{4,0},{1,5},{5,1},{2,6},{6,2},{3,7},{7,3},{8,12},{12,8},{9,1... | collective-permute-start | bytes 1032200 | tf_op jit(solution)/shard_map/up_from_x_x1/ppermute | solution.py:745
  68.8 5.0 %collective-permute-start.21 = (bf16[128,512]{1,0:T(8,128)(2,1)S(1)}, bf16[128,512]{1,0:T(8,128)(2,1)S(1)}, u32[]{:S(2)}, u32[]{:S(2)}) collective-permute-start(bf16[128,512]{1,0:T(8,128)(2,1)S(1)} %get-tuple-element.125), channel_id=1, source_target_pairs={{0,8},{8,0},{16,24},{24,16},{1,9},{9,1},{17,25},{25,17},{2,10},{10... | collective-permute-start | bytes 393224 | tf_op jit(solution)/shard_map/down_from_z_z1/ppermute | solution.py:745
  76.2 9.3 %collective-permute-start.22 = (bf16[256,512]{1,0:T(8,128)(2,1)S(1)}, bf16[256,512]{1,0:T(8,128)(2,1)S(1)}, u32[]{:S(2)}, u32[]{:S(2)}) collective-permute-start(bf16[256,512]{1,0:T(8,128)(2,1)S(1)} %get-tuple-element.127), channel_id=1, source_target_pairs={{0,4},{4,0},{1,5},{5,1},{2,6},{6,2},{3,7},{7,3},{8,12},{12,8},{9,1... | collective-permute-start | bytes 786440 | tf_op jit(solution)/shard_map/att_from_x_x1/ppermute | solution.py:745
  77.8 7.8 %collective-permute-start.23 = (bf16[128,512]{1,0:T(8,128)(2,1)S(1)}, bf16[128,512]{1,0:T(8,128)(2,1)S(1)}, u32[]{:S(2)}, u32[]{:S(2)}) collective-permute-start(bf16[128,512]{1,0:T(8,128)(2,1)S(1)} %down_z.1.refs_4_.refs_0_), channel_id=1, source_target_pairs={{0,16},{8,24},{16,0},{24,8},{1,17},{9,25},{17,1},{25,9},{2,18},{10... | collective-permute-start | bytes 393224 | tf_op jit(solution)/shard_map/down_far_z2/ppermute | solution.py:745
  80.5 5.6 %collective-permute-start.26 = (bf16[176,512]{1,0:T(8,128)(2,1)S(1)}, bf16[176,512]{1,0:T(8,128)(2,1)S(1)}, u32[]{:S(2)}, u32[]{:S(2)}) collective-permute-start(bf16[176,512]{1,0:T(8,128)(2,1)S(1)} %get-tuple-element.132), channel_id=1, source_target_pairs={{0,1},{1,0},{2,3},{3,2},{4,5},{5,4},{6,7},{7,6},{8,9},{9,8},{10,11... | collective-permute-start | bytes 540680 | tf_op jit(solution)/shard_map/up_from_y_mp1/ppermute | solution.py:745
  85.7 9.0 %collective-permute-start.25 = (bf16[128,512]{1,0:T(8,128)(2,1)S(1)}, bf16[128,512]{1,0:T(8,128)(2,1)S(1)}, u32[]{:S(2)}, u32[]{:S(2)}) collective-permute-start(bf16[128,512]{1,0:T(8,128)(2,1)S(1)} %get-tuple-element.131), channel_id=1, source_target_pairs={{0,8},{8,0},{16,24},{24,16},{1,9},{9,1},{17,25},{25,17},{2,10},{10... | collective-permute-start | bytes 393224 | tf_op jit(solution)/shard_map/att_from_z_z1/ppermute | solution.py:745
  86.1 12.0 %collective-permute-start.28 = (bf16[176,512]{1,0:T(8,128)(2,1)S(1)}, bf16[176,512]{1,0:T(8,128)(2,1)S(1)}, u32[]{:S(2)}, u32[]{:S(2)}) collective-permute-start(bf16[176,512]{1,0:T(8,128)(2,1)S(1)} %up_mp.1.refs_2_.refs_0_), channel_id=1, source_target_pairs={{0,16},{8,24},{16,0},{24,8},{1,17},{9,25},{17,1},{25,9},{2,18},{10... | collective-permute-start | bytes 540680 | tf_op jit(solution)/shard_map/up_far_z2/ppermute | solution.py:745
  89.1 8.4 %collective-permute-start.29 = (bf16[128,512]{1,0:T(8,128)(2,1)S(1)}, bf16[128,512]{1,0:T(8,128)(2,1)S(1)}, u32[]{:S(2)}, u32[]{:S(2)}) collective-permute-start(bf16[128,512]{1,0:T(8,128)(2,1)S(1)} %down_far.1.refs_2_.refs_0_), channel_id=1, source_target_pairs={{0,8},{8,0},{16,24},{24,16},{1,9},{9,1},{17,25},{25,17},{2,10},{10... | collective-permute-start | bytes 393224 | tf_op jit(solution)/shard_map/down_near_z1/ppermute | solution.py:745
  94.8 7.3 %collective-permute-start.27 = (bf16[128,512]{1,0:T(8,128)(2,1)S(1)}, bf16[128,512]{1,0:T(8,128)(2,1)S(1)}, u32[]{:S(2)}, u32[]{:S(2)}) collective-permute-start(bf16[128,512]{1,0:T(8,128)(2,1)S(1)} %attend_z.1.refs_2_.refs_0_), channel_id=1, source_target_pairs={{0,16},{8,24},{16,0},{24,8},{1,17},{9,25},{17,1},{25,9},{2,18},{10... | collective-permute-start | bytes 393224 | tf_op jit(solution)/shard_map/att_far_z2/ppermute | solution.py:745
  97.5 10.1 %collective-permute-start.36 = (bf16[256,512]{1,0:T(8,128)(2,1)S(1)}, bf16[256,512]{1,0:T(8,128)(2,1)S(1)}, u32[]{:S(2)}, u32[]{:S(2)}) collective-permute-start(bf16[256,512]{1,0:T(8,128)(2,1)S(1)} %down_join.1.refs_2_.refs_0_), channel_id=1, source_target_pairs={{0,4},{4,0},{1,5},{5,1},{2,6},{6,2},{3,7},{7,3},{8,12},{12,8},{9,1... | collective-permute-start | bytes 786440 | tf_op jit(solution)/shard_map/down_x_x1/ppermute | solution.py:745
  98.8 8.6 %collective-permute-start.33 = (bf16[160,512]{1,0:T(8,128)(2,1)S(1)}, bf16[160,512]{1,0:T(8,128)(2,1)S(1)}, u32[]{:S(2)}, u32[]{:S(2)}) collective-permute-start(bf16[160,512]{1,0:T(8,128)(2,1)S(1)} %get-tuple-element.133.refs_2_.refs_0_), channel_id=1, source_target_pairs={{0,4},{4,0},{1,5},{5,1},{2,6},{6,2},{3,7},{7,3},{8,12},{12,8},{9,1... | collective-permute-start | bytes 491528 | tf_op jit(solution)/shard_map/up_near_x1/ppermute | solution.py:745
  102.1 5.0 %collective-permute-start.30 = (bf16[128,512]{1,0:T(8,128)(2,1)S(1)}, bf16[128,512]{1,0:T(8,128)(2,1)S(1)}, u32[]{:S(2)}, u32[]{:S(2)}) collective-permute-start(bf16[128,512]{1,0:T(8,128)(2,1)S(1)} %attend_far.1.refs_0_.refs_2_), channel_id=1, source_target_pairs={{0,8},{8,0},{16,24},{24,16},{1,9},{9,1},{17,25},{25,17},{2,10},{10... | collective-permute-start | bytes 393224 | tf_op jit(solution)/shard_map/att_near_z1/ppermute | solution.py:745
  107.5 7.1 %collective-permute-start.34 = (bf16[320,512]{1,0:T(8,128)(2,1)S(1)}, bf16[320,512]{1,0:T(8,128)(2,1)S(1)}, u32[]{:S(2)}, u32[]{:S(2)}) collective-permute-start(bf16[320,512]{1,0:T(8,128)(2,1)S(1)} %up_join.1.refs_1_.refs_0_), channel_id=1, source_target_pairs={{0,8},{8,0},{16,24},{24,16},{1,9},{9,1},{17,25},{25,17},{2,10},{10... | collective-permute-start | bytes 983048 | tf_op jit(solution)/shard_map/up_last_z1/ppermute | solution.py:745
  107.6 2.7 %collective-permute-start.37 = (bf16[256,512]{1,0:T(8,128)(2,1)S(1)}, bf16[256,512]{1,0:T(8,128)(2,1)S(1)}, u32[]{:S(2)}, u32[]{:S(2)}) collective-permute-start(bf16[256,512]{1,0:T(8,128)(2,1)S(1)} %down_join.1.refs_2_.refs_0_), channel_id=1, source_target_pairs={{0,2},{2,0},{1,3},{3,1},{4,6},{6,4},{5,7},{7,5},{8,10},{10,8},{9,1... | collective-permute-start | bytes 786440 | tf_op jit(solution)/shard_map/down_core_core1/ppermute | solution.py:745
  107.7 2.6 %collective-permute-start.38 = (bf16[256,512]{1,0:T(8,128)(2,1)S(1)}, bf16[256,512]{1,0:T(8,128)(2,1)S(1)}, u32[]{:S(2)}, u32[]{:S(2)}) collective-permute-start(bf16[256,512]{1,0:T(8,128)(2,1)S(1)} %gate.17.refs_1_.refs_4_), channel_id=1, source_target_pairs={{0,2},{2,0},{1,3},{3,1},{4,6},{6,4},{5,7},{7,5},{8,10},{10,8},{9,1... | collective-permute-start | bytes 786440 | tf_op jit(solution)/shard_map/down_core_x_core1/ppermute | solution.py:745
  108.2 11.9 %collective-permute-start.31 = (bf16[256,512]{1,0:T(8,128)(2,1)S(1)}, bf16[256,512]{1,0:T(8,128)(2,1)S(1)}, u32[]{:S(2)}, u32[]{:S(2)}) collective-permute-start(bf16[256,512]{1,0:T(8,128)(2,1)S(1)} %get-tuple-element.134.refs_0_), channel_id=1, source_target_pairs={{0,4},{4,0},{1,5},{5,1},{2,6},{6,2},{3,7},{7,3},{8,12},{12,8},{9,1... | collective-permute-start | bytes 786440 | tf_op jit(solution)/shard_map/att_x_x1/ppermute | solution.py:745
  108.8 4.3 %collective-permute-start.35 = (bf16[64,512]{1,0:T(8,128)(2,1)S(1)}, bf16[64,512]{1,0:T(8,128)(2,1)S(1)}, u32[]{:S(2)}, u32[]{:S(2)}) collective-permute-start(bf16[64,512]{1,0:T(8,128)(2,1)S(1)} %get-tuple-element.135.refs_2_), channel_id=1, source_target_pairs={{0,1},{1,0},{2,3},{3,2},{4,5},{5,4},{6,7},{7,6},{8,9},{9,8},{10,11... | collective-permute-start | bytes 196616 | tf_op jit(solution)/shard_map/table_y_mp1/ppermute | solution.py:745
  110.2 10.3 %collective-permute-start.43 = (bf16[320,512]{1,0:T(8,128)(2,1)S(1)}, bf16[320,512]{1,0:T(8,128)(2,1)S(1)}, u32[]{:S(2)}, u32[]{:S(2)}) collective-permute-start(bf16[320,512]{1,0:T(8,128)(2,1)S(1)} %up_join.1.refs_1_.refs_0_), channel_id=1, source_target_pairs={{0,2},{2,0},{1,3},{3,1},{4,6},{6,4},{5,7},{7,5},{8,10},{10,8},{9,1... | collective-permute-start | bytes 983048 | tf_op jit(solution)/shard_map/up_core_core1/ppermute | solution.py:745
  114.6 6.0 %collective-permute-start.44 = (bf16[320,512]{1,0:T(8,128)(2,1)S(1)}, bf16[320,512]{1,0:T(8,128)(2,1)S(1)}, u32[]{:S(2)}, u32[]{:S(2)}) collective-permute-start(bf16[320,512]{1,0:T(8,128)(2,1)S(1)} %gate.19.refs_1_), channel_id=1, source_target_pairs={{0,2},{2,0},{1,3},{3,1},{4,6},{6,4},{5,7},{7,5},{8,10},{10,8},{9,1... | collective-permute-start | bytes 983048 | tf_op jit(solution)/shard_map/up_core_x_core1/ppermute | solution.py:745
  114.6 5.4 %collective-permute-start.32 = (bf16[64,512]{1,0:T(8,128)(2,1)S(1)}, bf16[64,512]{1,0:T(8,128)(2,1)S(1)}, u32[]{:S(2)}, u32[]{:S(2)}) collective-permute-start(bf16[64,512]{1,0:T(8,128)(2,1)S(1)} %get-tuple-element.135.refs_2_), channel_id=1, source_target_pairs={{0,5},{1,4},{4,1},{5,0},{2,7},{3,6},{6,3},{7,2},{8,13},{9,12},{12,... | collective-permute-start | bytes 196616 | tf_op jit(solution)/shard_map/table_x/ppermute | solution.py:750
  116.5 5.9 %collective-permute-start.39 = (bf16[256,512]{1,0:T(8,128)(2,1)S(1)}, bf16[256,512]{1,0:T(8,128)(2,1)S(1)}, u32[]{:S(2)}, u32[]{:S(2)}) collective-permute-start(bf16[256,512]{1,0:T(8,128)(2,1)S(1)} %get-tuple-element.134.refs_0_), channel_id=1, source_target_pairs={{0,2},{2,0},{1,3},{3,1},{4,6},{6,4},{5,7},{7,5},{8,10},{10,8},{9,1... | collective-permute-start | bytes 786440 | tf_op jit(solution)/shard_map/att_core_core1/ppermute | solution.py:745
  120.1 2.4 %collective-permute-start.40 = (bf16[256,512]{1,0:T(8,128)(2,1)S(1)}, bf16[256,512]{1,0:T(8,128)(2,1)S(1)}, u32[]{:S(2)}, u32[]{:S(2)}) collective-permute-start(bf16[256,512]{1,0:T(8,128)(2,1)S(1)} %gate.21.refs_4_.refs_1_), channel_id=1, source_target_pairs={{0,2},{2,0},{1,3},{3,1},{4,6},{6,4},{5,7},{7,5},{8,10},{10,8},{9,1... | collective-permute-start | bytes 786440 | tf_op jit(solution)/shard_map/att_core_x_core1/ppermute | solution.py:745
  120.1 2.3 %collective-permute-start.41 = (bf16[64,512]{1,0:T(8,128)(2,1)S(1)}, bf16[64,512]{1,0:T(8,128)(2,1)S(1)}, u32[]{:S(2)}, u32[]{:S(2)}) collective-permute-start(bf16[64,512]{1,0:T(8,128)(2,1)S(1)} %gate.18.refs_1_.refs_4_), channel_id=1, source_target_pairs={{0,2},{2,0},{1,3},{3,1},{4,6},{6,4},{5,7},{7,5},{8,10},{10,8},{9,1... | collective-permute-start | bytes 196616 | tf_op jit(solution)/shard_map/table_core_core1/ppermute | solution.py:745
  120.6 1.8 %collective-permute-start.42 = (bf16[64,512]{1,0:T(8,128)(2,1)S(1)}, bf16[64,512]{1,0:T(8,128)(2,1)S(1)}, u32[]{:S(2)}, u32[]{:S(2)}) collective-permute-start(bf16[64,512]{1,0:T(8,128)(2,1)S(1)} %gate.20.refs_1_.refs_5_), channel_id=1, source_target_pairs={{0,2},{2,0},{1,3},{3,1},{4,6},{6,4},{5,7},{7,5},{8,10},{10,8},{9,1... | collective-permute-start | bytes 196616 | tf_op jit(solution)/shard_map/table_core_x_core1/ppermute | solution.py:745
  (13 other events, 47.3 us)

commit v4 on v3

--- a/solution.py
+++ b/solution.py
@@ -28,7 +28,7 @@
 
 
 def call(
-    kernel, outs, args, after=(), scratch=(), us=1, mib=32, smem_args=0, hbm_args=0, copies=0, name=None
+    kernel, outs, args, after=(), scratch=(), us=1, mib=32, smem_args=0, hbm_args=0, copies=0, hbm_outs=False, name=None
 ):
     flat, tree = jax.tree.flatten(tuple(args))
     count, extra = len(flat), len(after)
@@ -45,7 +45,7 @@
         in_specs=[smem] * smem_args
         + [vmem] * (count - smem_args - hbm_args)
         + [anywhere] * (hbm_args + extra),
-        out_specs=[vmem] * len(outs),
+        out_specs=[anywhere if hbm_outs else vmem] * len(outs),
         scratch_shapes=[pltpu.VMEM(shape, dtype) for shape, dtype in scratch]
         + [pltpu.SemaphoreType.DMA((copies,))] * (copies > 0),
         compiler_params=pltpu.CompilerParams(vmem_limit_bytes=mib * MIB),
@@ -118,113 +118,130 @@
     return lax.broadcasted_iota(jnp.int32, (rows, LANES), 1) < HD
 
 
-def own_head(value, is_low, head):
+def stack_heads(value, is_low):
     zero = jnp.zeros_like(value)
-    return jnp.where(is_low, value, zero) if head == 0 else jnp.where(is_low, zero, value)
-
-
-def attend_forward(hidden_low, weight_ref, windows, mixed_ref, probs_ref, context_ref):
+    return jnp.concatenate(
+        [jnp.where(is_low, value, zero), jnp.where(is_low, zero, value)], axis=0
+    )
+
+
+def late_rows(value):
+    return jnp.concatenate(
+        [value[W_SHORT:W_LONG], value[W_LONG + W_SHORT : 2 * W_LONG]], axis=0
+    )
+
+
+def merge_heads(first, late, is_low):
+    top = jnp.where(is_low, first[0:W_SHORT], first[W_LONG : W_LONG + W_SHORT])
+    bottom = jnp.where(
+        is_low,
+        first[W_SHORT:W_LONG] + late[0:W_SHORT],
+        first[W_LONG + W_SHORT :] + late[W_SHORT:],
+    )
+    return top, bottom
+
+
+def attend_forward(hidden_low, weight_ref, windows, mixed_ref, early_ref, late_ref, context_ref):
     rows, width = context_ref.shape
+    pairs = width // LANES
     for c in range(3):
         part = mm(hidden_low, weight_ref[c]).astype(BF16)
         mixed_ref[c] = part * BF16(HD**-0.5) if c == 0 else part
     causal = lax.broadcasted_iota(jnp.int32, (W_SHORT, W_SHORT), 0) >= lax.broadcasted_iota(
         jnp.int32, (W_SHORT, W_SHORT), 1
     )
-    is_low = head_mask(W_SHORT)
+    is_low = head_mask(W_LONG)
     for block, is_long in enumerate(windows):
+        both = slice(block * W_LONG, (block + 1) * W_LONG)
         lo = slice(block * W_LONG, block * W_LONG + W_SHORT)
         hi = slice(block * W_LONG + W_SHORT, (block + 1) * W_LONG)
-        for pair in range(width // LANES):
+        for pair in range(pairs):
             lanes = slice(pair * LANES, (pair + 1) * LANES)
-            key_lo, key_hi = mixed_ref[1, lo, lanes], mixed_ref[1, hi, lanes]
-            val_lo, val_hi = mixed_ref[2, lo, lanes], mixed_ref[2, hi, lanes]
-            query_lo, query_hi = mixed_ref[0, lo, lanes], mixed_ref[0, hi, lanes]
-            results = []
+            slot = block * pairs + pair
+            queries = stack_heads(mixed_ref[0, both, lanes], is_low)
+            scores = mm_nt(queries, mixed_ref[1, lo, lanes])
+            late = mm_nt(late_rows(queries), mixed_ref[1, hi, lanes])
             for head in range(2):
-                slot = ((block * (width // LANES) + pair) * 2 + head) * 3
-                q_lo = own_head(query_lo, is_low, head)
-                q_hi = own_head(query_hi, is_low, head)
-                s_a = jnp.where(causal, mm_nt(q_lo, key_lo), MASKED)
+                start = head * W_LONG
+                s_a = jnp.where(causal, scores[start : start + W_SHORT], MASKED)
                 e_a = jnp.exp(s_a - jnp.max(s_a, axis=-1, keepdims=True))
-                p_a = (e_a * (1.0 / jnp.sum(e_a, axis=-1, keepdims=True))).astype(BF16)
-                s_b = jnp.where(is_long, mm_nt(q_hi, key_lo), MASKED)
-                s_c = jnp.where(causal, mm_nt(q_hi, key_hi), MASKED)
+                p_a = e_a * (1.0 / jnp.sum(e_a, axis=-1, keepdims=True))
+                s_b = jnp.where(is_long, scores[start + W_SHORT : start + W_LONG], MASKED)
+                s_c = jnp.where(causal, late[head * W_SHORT : (head + 1) * W_SHORT], MASKED)
                 top = jnp.max(jnp.maximum(s_b, s_c), axis=-1, keepdims=True)
                 e_b = jnp.exp(s_b - top)
                 e_c = jnp.exp(s_c - top)
                 inverse = 1.0 / jnp.sum(e_b + e_c, axis=-1, keepdims=True)
-                p_b = (e_b * inverse).astype(BF16)
-                p_c = (e_c * inverse).astype(BF16)
-                probs_ref[slot] = p_a
-                probs_ref[slot + 1] = p_b
-                probs_ref[slot + 2] = p_c
-                results.append((mm(p_a, val_lo), mm(p_b, val_lo) + mm(p_c, val_hi)))
-            context_ref[lo, lanes] = jnp.where(is_low, results[0][0], results[1][0]).astype(BF16)
-            context_ref[hi, lanes] = jnp.where(is_low, results[0][1], results[1][1]).astype(BF16)
-
-
-def attend_backward(grad_context, mixed_ref, probs_ref, blocks, grad_mixed_ref):
+                early_ref[slot, start : start + W_SHORT, :] = p_a.astype(BF16)
+                early_ref[slot, start + W_SHORT : start + W_LONG, :] = (e_b * inverse).astype(BF16)
+                late_ref[slot, head * W_SHORT : (head + 1) * W_SHORT, :] = (e_c * inverse).astype(
+                    BF16
+                )
+            top_rows, bottom_rows = merge_heads(
+                mm(early_ref[slot], mixed_ref[2, lo, lanes]),
+                mm(late_ref[slot], mixed_ref[2, hi, lanes]),
+                head_mask(W_SHORT),
+            )
+            context_ref[lo, lanes] = top_rows.astype(BF16)
+            context_ref[hi, lanes] = bottom_rows.astype(BF16)
+
+
+def attend_backward(grad_context, mixed_ref, early_ref, late_ref, blocks, grad_mixed_ref, work):
     width = mixed_ref.shape[2]
-    is_low = head_mask(W_SHORT)
+    pairs = width // LANES
+    is_low = head_mask(W_LONG)
+    early_grad_ref, late_grad_ref = work
     for block in range(blocks):
+        both = slice(block * W_LONG, (block + 1) * W_LONG)
         lo = slice(block * W_LONG, block * W_LONG + W_SHORT)
         hi = slice(block * W_LONG + W_SHORT, (block + 1) * W_LONG)
-        for pair in range(width // LANES):
+        for pair in range(pairs):
             lanes = slice(pair * LANES, (pair + 1) * LANES)
-            q_lo, q_hi = mixed_ref[0, lo, lanes], mixed_ref[0, hi, lanes]
-            k_lo, k_hi = mixed_ref[1, lo, lanes], mixed_ref[1, hi, lanes]
-            v_lo, v_hi = mixed_ref[2, lo, lanes], mixed_ref[2, hi, lanes]
-            g_lo, g_hi = grad_context[lo, lanes], grad_context[hi, lanes]
-            results = []
+            slot = block * pairs + pair
+            queries = stack_heads(mixed_ref[0, both, lanes], is_low)
+            grads = stack_heads(grad_context[both, lanes], is_low)
+            grad_early = mm_nt(grads, mixed_ref[2, lo, lanes])
+            grad_late = mm_nt(late_rows(grads), mixed_ref[2, hi, lanes])
             for head in range(2):
-                slot = ((block * (width // LANES) + pair) * 2 + head) * 3
-                gm_lo = own_head(g_lo, is_low, head)
-                gm_hi = own_head(g_hi, is_low, head)
-                pb_a, pb_b, pb_c = probs_ref[slot], probs_ref[slot + 1], probs_ref[slot + 2]
-                p_a, p_b, p_c = pb_a.astype(F32), pb_b.astype(F32), pb_c.astype(F32)
-                g_a = mm_nt(gm_lo, v_lo)
-                g_b = mm_nt(gm_hi, v_lo)
-                g_c = mm_nt(gm_hi, v_hi)
-                inner_a = jnp.sum(p_a * g_a, axis=-1, keepdims=True)
-                inner_b = jnp.sum(p_b * g_b + p_c * g_c, axis=-1, keepdims=True)
-                s_a = (p_a * (g_a - inner_a)).astype(BF16)
-                s_b = (p_b * (g_b - inner_b)).astype(BF16)
-                s_c = (p_c * (g_c - inner_b)).astype(BF16)
-                results.append(
-                    (
-                        mm(s_a, k_lo),
-                        mm(s_b, k_lo) + mm(s_c, k_hi),
-                        mm_tn(s_a, q_lo) + mm_tn(s_b, q_hi),
-                        mm_tn(s_c, q_hi),
-                        mm_tn(pb_a, g_lo) + mm_tn(pb_b, g_hi),
-                        mm_tn(pb_c, g_hi),
-                    )
-                )
-            both = [jnp.where(is_low, a, b) for a, b in zip(*results)]
-            grad_mixed_ref[0, lo, lanes] = (both[0] * HD**-0.5).astype(BF16)
-            grad_mixed_ref[0, hi, lanes] = (both[1] * HD**-0.5).astype(BF16)
-            grad_mixed_ref[1, lo, lanes] = both[2].astype(BF16)
-            grad_mixed_ref[1, hi, lanes] = both[3].astype(BF16)
-            grad_mixed_ref[2, lo, lanes] = both[4].astype(BF16)
-            grad_mixed_ref[2, hi, lanes] = both[5].astype(BF16)
+                start = head * W_LONG
+                first = slice(start, start + W_SHORT)
+                second = slice(start + W_SHORT, start + W_LONG)
+                last = slice(head * W_SHORT, (head + 1) * W_SHORT)
+                p_a = early_ref[slot, first, :].astype(F32)
+                g_a = grad_early[first]
+                inner = jnp.sum(p_a * g_a, axis=-1, keepdims=True)
+                early_grad_ref[pair, first, :] = (p_a * (g_a - inner)).astype(BF16)
+                p_b, p_c = early_ref[slot, second, :].astype(F32), late_ref[slot, last, :].astype(F32)
+                g_b, g_c = grad_early[second], grad_late[last]
+                inner = jnp.sum(p_b * g_b + p_c * g_c, axis=-1, keepdims=True)
+                early_grad_ref[pair, second, :] = (p_b * (g_b - inner)).astype(BF16)
+                late_grad_ref[pair, last, :] = (p_c * (g_c - inner)).astype(BF16)
+            top_rows, bottom_rows = merge_heads(
+                mm(early_grad_ref[pair], mixed_ref[1, lo, lanes]),
+                mm(late_grad_ref[pair], mixed_ref[1, hi, lanes]),
+                head_mask(W_SHORT),
+            )
+            grad_mixed_ref[0, lo, lanes] = (top_rows * HD**-0.5).astype(BF16)
+            grad_mixed_ref[0, hi, lanes] = (bottom_rows * HD**-0.5).astype(BF16)
+            grad_mixed_ref[1, lo, lanes] = mm_tn(early_grad_ref[pair], queries).astype(BF16)
+            grad_mixed_ref[1, hi, lanes] = mm_tn(late_grad_ref[pair], late_rows(queries)).astype(BF16)
+            grad_mixed_ref[2, lo, lanes] = mm_tn(early_ref[slot], grads).astype(BF16)
+            grad_mixed_ref[2, hi, lanes] = mm_tn(late_ref[slot], late_rows(grads)).astype(BF16)
 
 
 def normal_parts(x):
-    density = jnp.exp(x * x * -0.5)
-    t = 1.0 / (1.0 + jnp.abs(x) * 0.23164189)
-    poly = t * (
-        0.127414796
-        + t * (-0.142248368 + t * (0.7107068705 + t * (-0.7265760135 + t * 0.5307027145)))
-    )
-    tail = poly * density
-    return jnp.where(x > 0, 1.0 - tail, tail), density * 0.3989422804
-
-
-def first_kernel(win_ref, tokens_ref, pos_ref, weight_ref, mixed_ref, probs_ref, context_ref):
+    density = jnp.exp2(x * x * -0.7213475204 - 1.3257480647)
+    return 0.5 + 0.5 * lax.erf(x * 0.7071067812), density
+
+
+def first_kernel(
+    win_ref, tokens_ref, pos_ref, weight_ref, mixed_ref, early_ref, late_ref, context_ref
+):
     windows = read_windows(win_ref, tokens_ref.shape[0])
     hidden_low = hidden_rows(tokens_ref, pos_ref, windows).astype(BF16)
-    attend_forward(hidden_low, weight_ref, windows, mixed_ref, probs_ref, context_ref)
+    attend_forward(
+        hidden_low, weight_ref, windows, mixed_ref, early_ref, late_ref, context_ref
+    )
 
 
 def z_bit():
@@ -274,12 +291,21 @@
 
 def pack_ffn_kernel(up_ref, down_ref, up_to, down_to, sems):
     width, units = up_ref.shape
-    depth, mine = width // 4, quarter(place("x"))
+    depth = width // 8
+    mine = part(quarter(place("x")) * 2 + z_bit(), depth)
     columns = [
-        (up_ref.at[part(mine, depth), pl.ds(i * width, width)], up_to.at[pl.ds(i * depth, depth), :])
+        (up_ref.at[mine, pl.ds(i * width, width)], up_to.at[pl.ds(i * depth, depth), :])
         for i in range(units // width)
     ]
     copy_all([*columns, (down_ref.at[part(quarter(z_bit()), units // 4), :], down_to)], sems)
+
+
+def z_join_kernel(own_ref, near_ref, out_ref):
+    depth = own_ref.shape[0] // 2
+    for ref, bit in ((own_ref, z_bit()), (near_ref, 1 - z_bit())):
+        for i in range(2):
+            rows = pl.ds(pl.multiple_of(i * 2 * depth + bit * depth, depth), depth)
+            out_ref[rows, :] = ref[i * depth : (i + 1) * depth, :]
 
 
 def places(pieces, bit):
@@ -302,7 +328,8 @@
     out_own_ref,
     out_bias_ref,
     mixed_ref,
-    probs_ref,
+    early_ref,
+    late_ref,
     context_ref,
     resid_ref,
     w_oth_ref,
@@ -330,7 +357,13 @@
         bias_oth_ref[...] = pieces[2][...].astype(F32)
     hidden_in = hidden_rows(tokens_ref, pos_ref, windows)
     attend_forward(
-        hidden_in.astype(BF16), w_oth_ref, windows, mixed_ref, probs_ref, context_ref
+        hidden_in.astype(BF16),
+        w_oth_ref,
+        windows,
+        mixed_ref,
+        early_ref,
+        late_ref,
+        context_ref,
     )
     branch = mm(context_own_ref[...], out_own_ref[...]) + mm(context_ref[...], out_oth_ref[...])
     hidden_in = hidden_rows(tokens_ref, pos_ref, windows)
@@ -493,33 +526,28 @@
 
 
 def half_backward(
-    split,
-    hidden_low,
-    grad_low,
-    weight_ref,
-    out_ref,
-    mixed_ref,
-    probs_ref,
-    keep_ref,
-    send_ref,
-    gm_ref,
-    package_ref,
+    grad_low, weight_ref, out_ref, mixed_ref, early_ref, late_ref, gm_ref, work
 ):
+    grad_context = mm_nt(grad_low, out_ref[...]).astype(BF16)
+    attend_backward(
+        grad_context, mixed_ref, early_ref, late_ref, grad_low.shape[0] // W_LONG, gm_ref, work
+    )
+    return (
+        mm_nt(gm_ref[0], weight_ref[0])
+        + mm_nt(gm_ref[1], weight_ref[1])
+        + mm_nt(gm_ref[2], weight_ref[2])
+    )
+
+
+def projection_grads(hidden_low, gm_ref, package_ref, keep_ref, send_ref, split):
     rows, width = hidden_low.shape
     half_width = width // 2
-    grad_context = mm_nt(grad_low, out_ref[...]).astype(BF16)
-    attend_backward(grad_context, mixed_ref, probs_ref, rows // W_LONG, gm_ref)
     package_ref[0:width, 0:half_width] = mm_tn(hidden_low, gm_ref[0]).astype(BF16)
     package_ref[0:width, half_width:] = mm_tn(hidden_low, gm_ref[1]).astype(BF16)
     value_grad = mm_tn(hidden_low, gm_ref[2]).astype(BF16)
     package_ref[width : width + half_width, 0:half_width] = value_grad[0:half_width, :]
     package_ref[width : width + half_width, half_width:] = value_grad[half_width:, :]
     core_split(package_ref, keep_ref, send_ref, 0, split)
-    return (
-        mm_nt(gm_ref[0], weight_ref[0])
-        + mm_nt(gm_ref[1], weight_ref[1])
-        + mm_nt(gm_ref[2], weight_ref[2])
-    )
 
 
 def attend_back_kernel(
@@ -532,28 +560,25 @@
     other_refs,
     other_keep_ref,
     other_send_ref,
-    own_keep_ref,
-    own_send_ref,
     table_keep_ref,
     table_send_ref,
     tokens_grad_ref,
+    hidden_ref,
+    own_gm_ref,
     grad_ref,
     gm_ref,
     package_ref,
     table_ref,
+    *work,
 ):
     rows, width = tokens_ref.shape
     windows = read_windows(win_ref, rows)
     hidden_low = hidden_rows(tokens_ref, pos_ref, windows).astype(BF16)
+    hidden_ref[...] = hidden_low
     grad_low = grad_resid_ref[...].astype(BF16)
-    for before_ref, refs, to_refs in (
-        (grad_resid_ref, other_refs, (other_keep_ref, other_send_ref)),
-        (grad_ref, own_refs, (own_keep_ref, own_send_ref)),
-    ):
-        part_grad = half_backward(
-            split, hidden_low, grad_low, *refs, *to_refs, gm_ref, package_ref
-        )
-        grad_ref[...] = before_ref[...] + part_grad
+    grad_ref[...] = grad_resid_ref[...] + half_backward(grad_low, *other_refs, gm_ref, work)
+    projection_grads(hidden_low, gm_ref, package_ref, other_keep_ref, other_send_ref, split)
+    grad_ref[...] += half_backward(grad_low, *own_refs, own_gm_ref, work)
     grad = grad_ref[...]
     tokens_grad_ref[...] = grad.astype(BF16)
     first, second = None, None
@@ -570,6 +595,10 @@
     core_split(table_ref, table_keep_ref, table_send_ref, 0, split)
 
 
+def project_back_kernel(split, hidden_ref, gm_ref, keep_ref, send_ref, package_ref):
+    projection_grads(hidden_ref[...], gm_ref, package_ref, keep_ref, send_ref, split)
+
+
 def total_of(*values):
     total = values[0].astype(F32)
     for value in values[1:]:
@@ -577,11 +606,13 @@
     return total
 
 
-def bit_split(bit, value, work_ref, keep_ref, send_ref, start=0):
-    half = value.shape[0] // 2
-    work_ref[...] = value.astype(BF16)
-    keep_ref[start : start + half, :] = work_ref[part(bit, half), :]
-    send_ref[start : start + half, :] = work_ref[part(1 - bit, half), :]
+def bit_split(bit, size, terms, keep_ref, send_ref, start=0):
+    half = size // 2
+    for index, to_ref in ((bit, keep_ref), (1 - bit, send_ref)):
+        rows = [pl.ds(pl.multiple_of(first + index * half, 16), half) for _, first in terms]
+        to_ref[start : start + half, :] = total_of(
+            *[ref[row_range, :] for (ref, _), row_range in zip(terms, rows)]
+        ).astype(BF16)
 
 
 def other_half_kernel(keep_ref, recv_ref, send_ref):
@@ -589,41 +620,36 @@
     send_ref[...] = total_of(keep_ref[start:, :], recv_ref[start:, :]).astype(BF16)
 
 
-def down_split_kernel(keep_ref, recv_ref, from_y_ref, x_keep_ref, x_send_ref, work_ref):
-    rows = from_y_ref.shape[0]
-    total = total_of(keep_ref[0:rows, :], recv_ref[0:rows, :], from_y_ref[...])
-    bit_split(place("x"), total, work_ref, x_keep_ref, x_send_ref)
+def down_split_kernel(keep_ref, recv_ref, from_y_ref, x_keep_ref, x_send_ref):
+    terms = [(keep_ref, 0), (recv_ref, 0), (from_y_ref, 0)]
+    bit_split(place("x"), from_y_ref.shape[0], terms, x_keep_ref, x_send_ref)
 
 
 def pair_kernel(a_ref, b_ref, out_ref):
     out_ref[...] = total_of(a_ref[...], b_ref[...]).astype(BF16)
 
 
-def up_split_kernel(keep_ref, recv_ref, x_keep_ref, x_send_ref, work_ref):
-    rows = work_ref.shape[0]
+def halves_split(bit, keep_ref, recv_ref, to_keep_ref, to_send_ref):
+    rows = (keep_ref.shape[0] - EXTRA) // 2
     for half in range(2):
-        rows_of = slice(half * rows, (half + 1) * rows)
-        total = total_of(keep_ref[rows_of, :], recv_ref[rows_of, :])
-        start = half * (rows // 2)
-        bit_split(z_bit(), total, work_ref, x_keep_ref, x_send_ref, start)
+        terms = [(keep_ref, half * rows), (recv_ref, half * rows)]
+        bit_split(bit, rows, terms, to_keep_ref, to_send_ref, half * (rows // 2))
     small = total_of(keep_ref[2 * rows :, :], recv_ref[2 * rows :, :]).astype(BF16)
-    x_keep_ref[rows:, :] = small
-    x_send_ref[rows:, :] = small
-
-
-def down_x_kernel(keep_ref, recv_ref, z_keep_ref, z_send_ref, work_ref):
-    bit_split(z_bit(), total_of(keep_ref[...], recv_ref[...]), work_ref, z_keep_ref, z_send_ref)
-
-
-def up_x_kernel(keep_ref, recv_ref, z_keep_ref, z_send_ref, work_ref):
-    rows = work_ref.shape[0]
-    for half in range(2):
-        rows_of = slice(half * rows, (half + 1) * rows)
-        total = total_of(keep_ref[rows_of, :], recv_ref[rows_of, :])
-        bit_split(place("x"), total, work_ref, z_keep_ref, z_send_ref, half * (rows // 2))
-    small = total_of(keep_ref[2 * rows :, :], recv_ref[2 * rows :, :]).astype(BF16)
-    z_keep_ref[rows:, :] = small
-    z_send_ref[rows:, :] = small
+    to_keep_ref[rows:, :] = small
+    to_send_ref[rows:, :] = small
+
+
+def up_split_kernel(keep_ref, recv_ref, z_keep_ref, z_send_ref):
+    halves_split(z_bit(), keep_ref, recv_ref, z_keep_ref, z_send_ref)
+
+
+def down_x_kernel(keep_ref, recv_ref, z_keep_ref, z_send_ref):
+    terms = [(keep_ref, 0), (recv_ref, 0)]
+    bit_split(z_bit(), keep_ref.shape[0], terms, z_keep_ref, z_send_ref)
+
+
+def up_x_kernel(keep_ref, recv_ref, x_keep_ref, x_send_ref):
+    halves_split(place("x"), keep_ref, recv_ref, x_keep_ref, x_send_ref)
 
 
 def up_z_kernel(keep_ref, recv_ref, y_keep_ref, y_send_ref):
@@ -633,16 +659,21 @@
     y_keep_ref[rows:, :] = y_send_ref[rows:, :]
 
 
-def up_last_kernel(own_ref, recv_ref, out_ref, *small_refs):
-    *vector_refs, bias_ref, work_ref = small_refs
-    rows, width = out_ref.shape
+def up_last_kernel(own_ref, recv_ref, out_ref, small_ref):
+    rows = out_ref.shape[0]
     out_ref[...] = total_of(own_ref[0:rows, :], recv_ref[0:rows, :]).astype(BF16)
-    work_ref[...] = total_of(own_ref[rows:, :], recv_ref[rows:, :])
+    small_ref[...] = total_of(own_ref[rows:, :], recv_ref[rows:, :])
+
+
+def small_out_kernel(small_ref, *refs):
+    *vector_refs, bias_ref, token_ref = refs
+    width = small_ref.shape[1]
+    token_ref[...] = jnp.zeros(token_ref.shape, F32)
     for i, ref in enumerate(vector_refs):
-        ref[...] = work_ref[i : i + 1, :].reshape(width)
+        ref[...] = small_ref[i : i + 1, :].reshape(width)
     span = bias_ref.shape[0] // width
     for i in range(span):
-        value = work_ref[pl.ds(6 + place("mp") * span + i, 1), :]
+        value = small_ref[pl.ds(6 + place("mp") * span + i, 1), :]
         bias_ref[i * width : (i + 1) * width] = value.reshape(width)
 
 
@@ -653,31 +684,27 @@
     out_ref[part(1 - bit, rows), :] = recv_ref[...]
 
 
-def attend_core_kernel(
-    keep_ref, recv_ref, table_keep_ref, table_recv_ref, to_y_ref, table_ref, work_ref
-):
+def attend_core_kernel(keep_ref, recv_ref, table_keep_ref, table_recv_ref, to_y_ref, table_ref):
     rows = keep_ref.shape[0]
     to_y_ref[0:rows, :] = total_of(keep_ref[...], recv_ref[...]).astype(BF16)
-    total = total_of(table_keep_ref[...], table_recv_ref[...])
-    bit_split(place("mp"), total, work_ref, table_ref, to_y_ref.at[rows:, :])
-
-
-def attend_mp_kernel(
-    keep_ref, recv_ref, from_y_ref, table_ref, x_keep_ref, x_send_ref, work_ref, spare_ref
-):
-    rows = keep_ref.shape[0]
-    total = total_of(keep_ref[...], recv_ref[...], from_y_ref[0:rows, :])
-    bit_split(place("x"), total, work_ref, x_keep_ref, x_send_ref)
-    total = total_of(table_ref[...], from_y_ref[rows:, :])
-    bit_split(place("x"), total, spare_ref, x_keep_ref, x_send_ref, rows // 2)
-
-
-def attend_x_kernel(keep_ref, recv_ref, z_keep_ref, z_send_ref, work_ref, spare_ref):
-    rows = work_ref.shape[0]
-    total = total_of(keep_ref[0:rows, :], recv_ref[0:rows, :])
-    bit_split(z_bit(), total, work_ref, z_keep_ref, z_send_ref)
-    total = total_of(keep_ref[rows:, :], recv_ref[rows:, :])
-    bit_split(z_bit(), total, spare_ref, z_keep_ref, z_send_ref, rows // 2)
+    terms = [(table_keep_ref, 0), (table_recv_ref, 0)]
+    size = table_keep_ref.shape[0]
+    bit_split(place("mp"), size, terms, table_ref, to_y_ref.at[rows:, :])
+
+
+def attend_mp_kernel(keep_ref, recv_ref, from_y_ref, table_ref, x_keep_ref, x_send_ref):
+    rows, spare = keep_ref.shape[0], table_ref.shape[0]
+    terms = [(keep_ref, 0), (recv_ref, 0), (from_y_ref, 0)]
+    bit_split(place("x"), rows, terms, x_keep_ref, x_send_ref)
+    terms = [(table_ref, 0), (from_y_ref, rows)]
+    bit_split(place("x"), spare, terms, x_keep_ref, x_send_ref, rows // 2)
+
+
+def attend_x_kernel(spare, keep_ref, recv_ref, z_keep_ref, z_send_ref):
+    rows = keep_ref.shape[0] - spare
+    for start, size in ((0, rows), (rows, spare)):
+        terms = [(keep_ref, start), (recv_ref, start)]
+        bit_split(z_bit(), size, terms, z_keep_ref, z_send_ref, start // 2)
 
 
 def attend_join_kernel(own_ref, recv_ref, out_ref, table_ref):
@@ -720,7 +747,9 @@
         out_ref[core * spare : (core + 1) * spare, :] = work_ref[start : start + spare, :].astype(F32)
 
 
-def attend_out_kernel(parts, table_parts, qkv_ref, table_ref, work_ref):
+def attend_out_kernel(
+    parts, table_parts, qkv_ref, table_ref, work_ref, qkv_out_ref, table_out_ref, sems
+):
     y = place("mp")
     spare = table_parts[0].shape[0]
     rows = parts[0].shape[0] - spare
@@ -729,14 +758,22 @@
     for ref, index in corners(parts, place("x")):
         work_ref[part(index, rows), :] = ref[0:rows, :]
         core, x = lax.div(index, 2), lax.rem(index, 2)
-        table_ref[part(core * 4 + y * 2 + x, spare), :] = ref[rows:, :].astype(F32)
+        table_out_ref[part(core * 4 + y * 2 + x, spare), :] = ref[rows:, :].astype(F32)
     for ref, index in corners(table_parts, place("x")):
         core, x = lax.div(index, 2), lax.rem(index, 2)
-        table_ref[part(core * 4 + (1 - y) * 2 + x, spare), :] = ref[...].astype(F32)
-    qkv_ref[0] = work_ref[0:width, 0:half].astype(F32)
-    qkv_ref[1] = work_ref[0:width, half:].astype(F32)
-    qkv_ref[2, 0:half, :] = work_ref[width : width + half, 0:half].astype(F32)
-    qkv_ref[2, half:, :] = work_ref[width : width + half, half:].astype(F32)
+        table_out_ref[part(core * 4 + (1 - y) * 2 + x, spare), :] = ref[...].astype(F32)
+    copies = [pltpu.make_async_copy(table_out_ref, table_ref, sems.at[3])]
+    copies[0].start()
+    for i in range(3):
+        if i < 2:
+            qkv_out_ref[i] = work_ref[0:width, i * half : (i + 1) * half].astype(F32)
+        else:
+            qkv_out_ref[i, 0:half, :] = work_ref[width : width + half, 0:half].astype(F32)
+            qkv_out_ref[i, half:, :] = work_ref[width : width + half, half:].astype(F32)
+        copies.append(pltpu.make_async_copy(qkv_out_ref.at[i], qkv_ref.at[i], sems.at[i]))
+        copies[-1].start()
+    for copy in copies:
+        copy.wait()
 
 
 def swap(value, axis, name="swap", distance=1):
@@ -783,9 +820,10 @@
         copies=0,
         mib=8,
         token=None,
+        hbm_outs=False,
     ):
         results = call(
-            kernel, outs, args, self.last, scratch, us, mib, smem_args, hbm_args, copies, name
+            kernel, outs, args, self.last, scratch, us, mib, smem_args, hbm_args, copies, hbm_outs, name
         )
         if token is None:
             token = min(range(len(results)), key=lambda i: results[i].size)
@@ -824,7 +862,8 @@
 
     attend_outs = [
         (3, rows, half_width),
-        (blocks * half_width // HD * 3, W_SHORT, W_SHORT),
+        (blocks * half_width // LANES, 2 * W_LONG, W_SHORT),
+        (blocks * half_width // LANES, W_LONG, W_SHORT),
         (rows, half_width),
     ]
 
@@ -870,14 +909,14 @@
             [up_bias, qkv_weight, out_weight],
             1,
             "pack_attend",
-            mib=60,
+            mib=63,
             hbm_args=2,
             copies=5,
         )
         attend_y = swap(message, "mp", "attend_y")
         up_message, down_message = step(
             pack_ffn_kernel,
-            [(units // 4, width), (units // 4, width)],
+            [(units // 8, width), (units // 4, width)],
             [up_weight, down_weight],
             1,
             "pack_ffn",
@@ -887,24 +926,26 @@
         )
         up_y = swap(up_message, "mp", "up_y")
         down_y = swap(down_message, "mp", "down_y")
-        mixed_own, probs_own, context_own = attend_own()
-        attend_y = step.gate(attend_y)
+        mixed_own, early_own, late_own, context_own = attend_own()
+        attend_y = step.gate(attend_y, 0)
         attend_x = swap(attend_y, "x", "attend_x")
         attend_cy = swap(attend_y, "core", "attend_cy")
         up_y = step.gate(up_y)
+        up_z = swap(up_y, "z", "up_z")
+        (up_y,) = step(z_join_kernel, [(units // 4, width)], [up_y, up_z], 0, "up_pair")
         up_x = swap(up_y, "x", "up_x")
         up_cy = swap(up_y, "core", "up_cy")
         attend_x = step.gate(attend_x)
         attend_cx = swap(attend_x, "core", "attend_cx")
-        down_y = step.gate(down_y)
+        down_y = step.gate(down_y, 2)
         down_z = swap(down_y, "z", "down_z")
         down_cy = swap(down_y, "core", "down_cy")
         attend_in = (attend_y, attend_x, attend_cy, attend_cx)
-        mixed_oth, probs_oth, context_oth, resid, w_oth, out_oth, bias_oth = attend_other()
+        mixed_oth, early_oth, late_oth, context_oth, resid, w_oth, out_oth, bias_oth = attend_other()
+        low, act_own, slope_own, branch = ffn_own()
         up_x = step.gate(up_x, 0)
         up_cx = swap(up_x, "core", "up_cx")
-        low, act_own, slope_own, branch = ffn_own()
-        down_z = step.gate(down_z)
+        down_z = step.gate(down_z, 4)
         down_cz = swap(down_z, "core", "down_cz")
         up_in = (up_y, up_x, up_cy, up_cx)
         down_in = (down_y, down_z, down_cy, down_cz)
@@ -919,8 +960,8 @@
         up_own, up_in = up_w[:, :units], (up_w[:, units:],)
         down_own, down_in = down_w[:units], (down_w[units:],)
         bias_own = bias[:units]
-        mixed_own, probs_own, context_own = attend_own()
-        mixed_oth, probs_oth, context_oth, resid, w_oth, out_oth, bias_oth = attend_other()
+        mixed_own, early_own, late_own, context_own = attend_own()
+        mixed_oth, early_oth, late_oth, context_oth, resid, w_oth, out_oth, bias_oth = attend_other()
         low, act_own, slope_own, branch = ffn_own()
 
     layer_out, down_keep, down_send, slope_oth, up_oth, down_oth, grad2, vec = step(
@@ -987,14 +1028,17 @@
     def attend_back():
         return step(
             functools.partial(attend_back_kernel, fast),
-            [(att, width)] * 4 + [(spare, width)] * 2 + [(rows, width)],
+            [(att, width)] * 2
+            + [(spare, width)] * 2
+            + [(rows, width)] * 2
+            + [(3, rows, half_width)],
             [
                 window,
                 tokens,
                 pos_table,
                 grad1,
-                (w_own, out_own, mixed_own, probs_own),
-                (w_oth, out_oth, mixed_oth, probs_oth),
+                (w_own, out_own, mixed_own, early_own, late_own),
+                (w_oth, out_oth, mixed_oth, early_oth, late_oth),
             ],
             13,
             "attend_back",
@@ -1004,12 +1048,26 @@
                 ((3, rows, half_width), BF16),
                 ((2 * att, width), BF16),
                 ((W_LONG, width), BF16),
+                ((half_width // LANES, 2 * W_LONG, W_SHORT), BF16),
+                ((half_width // LANES, W_LONG, W_SHORT), BF16),
             ],
             smem_args=1,
         )
 
+    def project_back(hidden, own_gm):
+        return step(
+            functools.partial(project_back_kernel, fast),
+            [(att, width)] * 2,
+            [hidden, own_gm],
+            0,
+            "project_back",
+            mib=16,
+            scratch=[((2 * att, width), BF16)],
+        )
+
     if not fast:
-        *att_parts, grad_tokens = attend_back()
+        *oth_parts, grad_tokens, hidden, own_gm = attend_back()
+        att_parts = (*oth_parts[:2], *project_back(hidden, own_gm), *oth_parts[2:])
         qkv_g, out_g, up_g, down_g, small, table = reduce_plain(
             n, width, down_keep, down_send, up_keep, up_send, small, *att_parts
         )
@@ -1026,14 +1084,14 @@
             up_split_kernel,
             [(group + EXTRA, width)] * 2,
             [up_keep, up_recv],
-            1,
+            5,
             "up_core",
-            scratch=[((group, width), BF16)],
         )
         up_from_x = swap(to_x, "z", "up_from_z")
-        oth_keep, oth_send, own_keep, own_send, tab_keep, tab_send, grad_tokens = attend_back()
+        oth_keep, oth_send, tab_keep, tab_send, grad_tokens, hidden, own_gm = attend_back()
         oth_recv = swap(oth_send, "core", "oth_recv")
         tab_recv = swap(tab_send, "core", "tab_recv")
+        own_keep, own_send = project_back(hidden, own_gm)
         own_recv = swap(own_send, "core", "own_recv")
         down_x, to_x = step(
             down_split_kernel,
@@ -1041,7 +1099,6 @@
             [down_keep, down_recv, down_from_y],
             0,
             "down_mp",
-            scratch=[((n, width), BF16)],
         )
         down_from_x = swap(to_x, "x", "down_from_x")
         to_y, table = step(
@@ -1050,16 +1107,14 @@
             [oth_keep, oth_recv, tab_keep, tab_recv],
             0,
             "attend_core",
-            scratch=[((spare, width), BF16)],
         )
         att_from_y = swap(to_y, "mp", "att_from_y")
         up_z, to_z = step(
             up_x_kernel,
             [(group // 2 + EXTRA, width)] * 2,
             [up_x, up_from_x],
-            0,
+            5,
             "up_x",
-            scratch=[((group // 2, width), BF16)],
         )
         up_from_z = swap(to_z, "x", "up_from_x")
         down_z, to_z = step(
@@ -1068,7 +1123,6 @@
             [down_x, down_from_x],
             3,
             "down_x",
-            scratch=[((half, width), BF16)],
         )
         down_from_z = swap(to_z, "z", "down_from_z")
         (down_z,) = step(pair_kernel, [(piece, width)], [down_z, down_from_z], 0, "down_z")
@@ -1079,38 +1133,34 @@
             [own_keep, own_recv, att_from_y, table],
             0,
             "attend_mp",
-            scratch=[((att, width), BF16), ((strip, width), BF16)],
         )
         att_from_x = swap(to_x, "x", "att_from_x")
         up_y, to_y = step(
-            up_z_kernel, [(group // 4 + EXTRA, width)] * 2, [up_z, up_from_z], 0, "up_z"
+            up_z_kernel, [(group // 4 + EXTRA, width)] * 2, [up_z, up_from_z], 3, "up_z"
         )
         up_from_y = swap(to_y, "mp", "up_from_y")
         (down_z,) = step(pair_kernel, [(piece, width)], [down_z, down_far], 0, "down_far")
         down_near = swap(down_z, "z", "down_near")
         att_z, to_z = step(
-            attend_x_kernel,
+            functools.partial(attend_x_kernel, strip // 2),
             [((att + strip) // 4, width)] * 2,
             [att_x, att_from_x],
             0,
             "attend_x",
-            scratch=[((att // 2, width), BF16), ((strip // 2, width), BF16)],
         )
         att_from_z = swap(to_z, "z", "att_from_z")
         (up_y,) = step(pair_kernel, [(group // 4 + EXTRA, width)], [up_y, up_from_y], 0, "up_mp")
         up_far = swap(up_y, "z", "up_far", 2)
+        (down_z,) = step(functools.partial(join_kernel, "z"), [(half, width)], [down_z, down_near], 0, "down_join")
+        down_x = swap(down_z, "x", "down_x")
         (att_z,) = step(pair_kernel, [att_z.shape], [att_z, att_from_z], 0, "attend_z")
         att_far = swap(att_z, "z", "att_far", 2)
-        (down_z,) = step(functools.partial(join_kernel, "z"), [(half, width)], [down_z, down_near], 0, "down_join")
-        down_x = swap(down_z, "x", "down_x")
-        up_z, *vectors, bias_g = step(
+        up_z, small = step(
             up_last_kernel,
-            [(group // 4, width)] + [((width,), F32)] * 6 + [((up_bias.shape[0],), F32)],
+            [(group // 4, width), ((EXTRA, width), F32)],
             [up_y, up_far],
             0,
             "up_far",
-            token=0,
-            scratch=[((EXTRA, width), F32)],
         )
         up_near = swap(up_z, "x", "up_near")
         (att_z,) = step(pair_kernel, [att_z.shape], [att_z, att_far], 0, "attend_far")
@@ -1128,6 +1178,14 @@
         (up_z,) = step(functools.partial(join_kernel, "x"), [(group // 2, width)], [up_z, up_near], 0, "up_join")
         up_x = swap(up_z, "z", "up_last")
         down_x = step.gate(down_x, 0)
+        *vectors, bias_g, _ = step(
+            small_out_kernel,
+            [((width,), F32)] * 6 + [((up_bias.shape[0],), F32), ((8, LANES), F32)],
+            [small],
+            0,
+            "small_out",
+            token=7,
+        )
         down_g, _ = step(
             down_out_kernel,
             [((2 * n, width), F32), ((8, LANES), F32)],
@@ -1142,8 +1200,8 @@
         )
         table_y = step.gate(table_y, 0)
         up_x = step.gate(up_x, 0)
-        table_x = step.gate(table_x, 0)
-        att_x = step.gate(att_x, 0)
+        table_x = step.gate(table_x, 2)
+        att_x = step.gate(att_x, 1)
         up_g, out_g, _ = step(
             up_out_kernel,
             [((width, 2 * n), F32), ((half_width, width), F32), ((8, LANES), F32)],
@@ -1171,7 +1229,13 @@
             ],
             0,
             "attend_out",
-            scratch=[((2 * att, width), BF16)],
+            scratch=[
+                ((2 * att, width), BF16),
+                ((3, width, half_width), F32),
+                ((W_LONG, width), F32),
+            ],
+            copies=4,
+            hbm_outs=True,
         )
 
 

time: 124 us -> 118 us (0.952)
  waiting for transfers between devices: 43.5 us -> 38.2 us
  Pallas kernels: 40.2 us -> 35.7 us
  starting transfers between devices: 37.6 us -> 41 us
    ppermute x44 -> x45, waiting for transfers between devices: 40.2 us -> 34.8 us  [swap(): return lax.ppermute(value, axis, pairs)]
    ppermute x44 -> x45, starting transfers between devices: 35.7 us -> 40.6 us  [swap(): return lax.ppermute(value, axis, pairs)]
    pallas_call x29 -> x32, Pallas kernels: 40.2 us -> 35.7 us  [call(): pl.pallas_call(flat_kernel, out_shape=[jax.ShapeDtypeStruct(out, BF16) if...]
    ppermute x1, starting transfers between devices: 1.88 us -> 0.45 us  [swap_corner(): return lax.ppermute(value, ('x', 'mp'), [(0, 3), (1, 2), (2, 1), (3, 0)])]
  transfers between devices with their start and end apart: 45 -> 46, of which waited for: 23 -> 20; matrix products, arithmetic and copies ran while one was open for 0% -> 0% of each run, Pallas kernels for 25% -> 23%
where the time goes in v4:
time: 118 us
  starting transfers between devices  41 us (35%)
  waiting for transfers between devices  38.2 us (32%)
  Pallas kernels  35.7 us (30%)
  between operations  1.95 us (2%)
    ppermute x45, starting transfers between devices, swap(): return lax.ppermute(value, axis, pairs)  40.6 us
    pallas_call x32, Pallas kernels, call(): pl.pallas_call(flat_kernel, out_shape=[jax.ShapeDtypeStruct(out, BF16) if...  35.7 us
    ppermute x45, waiting for transfers between devices, swap(): return lax.ppermute(value, axis, pairs)  34.8 us
    ppermute x1, waiting for transfers between devices, swap_corner(): return lax.ppermute(value, ('x', 'mp'), [(0, 3), (1, 2), (2, 1), (3, 0)])  3.36 us
  transfers between devices with their start and end apart: 46, of which 20 were waited for; matrix products, arithmetic and copies ran while one was open for 0% of the time, Pallas kernels for 23%

profile of v4, /device:TPU:0, one launch (start us, length us, event | category | flops | bytes accessed | tf_op | source)
XLA Modules:
  0.0 117.9 jit_solution(14441788049474405148)
XLA Ops:
  0.6 2.4 %pack_attend.1.refs_2_ = bf16[272,512]{1,0:T(8,128)(2,1)} custom-call(bf16[1024]{0:T(1024)(128)(2,1)} %refs_3_.1, bf16[3,512,256]{2,1,0:T(8,128)(2,1)} %bitcast.2, bf16[256,512]{1,0:T(8,128)(2,1)} %refs_5_.5), custom_call_target="tpu_custom_call" | custom-call | flops 1000000000 | tf_op jit(solution)/shard_map/pack_attend/pallas_call | solution.py:39
  3.1 3.0 %collective-permute-start = (bf16[272,512]{1,0:T(8,128)(2,1)}, bf16[272,512]{1,0:T(8,128)(2,1)S(1)}, u32[]{:S(2)}, u32[]{:S(2)}) collective-permute-start(bf16[272,512]{1,0:T(8,128)(2,1)} %pack_attend.1.refs_2_), channel_id=1, source_target_pairs={{0,1},{1,0},{2,3},{3,2},{4,5},{5,4},{6,7},{7,6},{8,9},{9,8},{10,11... | collective-permute-start | bytes 835592 | tf_op jit(solution)/shard_map/attend_y_mp1/ppermute | solution.py:782
  6.1 1.8 %pack_ffn.1 = (bf16[128,512]{1,0:T(8,128)(2,1)}, bf16[256,512]{1,0:T(8,128)(2,1)}) custom-call(bf16[512,1024]{1,0:T(8,128)(2,1)} %refs_5_.4, bf16[1024,512]{1,0:T(8,128)(2,1)} %refs_7_.1, bf16[272,512]{1,0:T(8,128)(2,1)} %pack_attend.1.refs_2_), custom_call_target="tpu_custom_call" | custom-call | flops 1000000000 | tf_op jit(solution)/shard_map/pack_ffn/pallas_call | solution.py:39
  8.8 0.9 copy-done.7
  9.7 2.3 %attend_first.1 = (bf16[3,512,256]{2,1,0:T(8,128)(2,1)S(1)}, bf16[2,1024,256]{2,1,0:T(8,128)(2,1)S(1)}, bf16[2,512,256]{2,1,0:T(8,128)(2,1)S(1)}, bf16[512,256]{1,0:T(8,128)(2,1)S(1)}) custom-call(s32[1]{0:T(128)S(6)} %copy.51.refs_0_, bf16[512,512]{1,0:T(8,128)(2,1)S(1)} %copy-done.4, bf16[512,512]{1,0:T(8,128)(2,1)S(1)} %copy-done.5, ...), custom_call_target="tpu_custom_call" | custom-call | flops 3000000000 | tf_op jit(solution)/shard_map/attend_first/pallas_call | solution.py:39
  12.0 1.8 %collective-permute-done.refs_0_ = bf16[272,512]{1,0:T(8,128)(2,1)S(1)} collective-permute-done((bf16[272,512]{1,0:T(8,128)(2,1)}, bf16[272,512]{1,0:T(8,128)(2,1)S(1)}, u32[]{:S(2)}, u32[]{:S(2)}) %collective-permute-start) | collective-permute-done | bytes 278560 | tf_op jit(solution)/shard_map/attend_y_mp1/ppermute | solution.py:782
  13.8 2.0 %collective-permute-start.1 = (bf16[272,512]{1,0:T(8,128)(2,1)S(1)}, bf16[272,512]{1,0:T(8,128)(2,1)S(1)}, u32[]{:S(2)}, u32[]{:S(2)}) collective-permute-start(bf16[272,512]{1,0:T(8,128)(2,1)S(1)} %gate.11.refs_1_.refs_3_), channel_id=1, source_target_pairs={{0,4},{4,0},{1,5},{5,1},{2,6},{6,2},{3,7},{7,3},{8,12},{12,8},{9,1... | collective-permute-start | bytes 835592 | tf_op jit(solution)/shard_map/attend_x_x1/ppermute | solution.py:782
  15.9 1.7 %collective-permute-start.3 = (bf16[128,512]{1,0:T(8,128)(2,1)S(1)}, bf16[128,512]{1,0:T(8,128)(2,1)S(1)}, u32[]{:S(2)}, u32[]{:S(2)}) collective-permute-start(bf16[128,512]{1,0:T(8,128)(2,1)S(1)} %gate.12.refs_0_.refs_2_), channel_id=1, source_target_pairs={{0,8},{8,0},{16,24},{24,16},{1,9},{9,1},{17,25},{25,17},{2,10},{10... | collective-permute-start | bytes 393224 | tf_op jit(solution)/shard_map/up_z_z1/ppermute | solution.py:782
  17.6 1.5 %collective-permute-start.6 = (bf16[256,512]{1,0:T(8,128)(2,1)S(1)}, bf16[256,512]{1,0:T(8,128)(2,1)S(1)}, u32[]{:S(2)}, u32[]{:S(2)}) collective-permute-start(bf16[256,512]{1,0:T(8,128)(2,1)S(1)} %copy-done.15), channel_id=1, source_target_pairs={{0,1},{1,0},{2,3},{3,2},{4,5},{5,4},{6,7},{7,6},{8,9},{9,8},{10,11... | collective-permute-start | bytes 786440 | tf_op jit(solution)/shard_map/down_y_mp1/ppermute | solution.py:782
  19.1 1.7 %collective-permute-done.3.refs_1_ = bf16[128,512]{1,0:T(8,128)(2,1)S(1)} collective-permute-done((bf16[128,512]{1,0:T(8,128)(2,1)S(1)}, bf16[128,512]{1,0:T(8,128)(2,1)S(1)}, u32[]{:S(2)}, u32[]{:S(2)}) %collective-permute-start.3) | collective-permute-done | bytes 131104 | tf_op jit(solution)/shard_map/up_z_z1/ppermute | solution.py:782
  21.5 1.7 %collective-permute-start.7 = (bf16[256,512]{1,0:T(8,128)(2,1)S(1)}, bf16[256,512]{1,0:T(8,128)(2,1)S(1)}, u32[]{:S(2)}, u32[]{:S(2)}) collective-permute-start(bf16[256,512]{1,0:T(8,128)(2,1)S(1)} %up_pair.1.refs_1_.refs_4_), channel_id=1, source_target_pairs={{0,4},{4,0},{1,5},{5,1},{2,6},{6,2},{3,7},{7,3},{8,12},{12,8},{9,1... | collective-permute-start | bytes 786440 | tf_op jit(solution)/shard_map/up_x_x1/ppermute | solution.py:782
  23.1 1.4 %collective-permute-done.6.refs_0_ = bf16[256,512]{1,0:T(8,128)(2,1)S(1)} collective-permute-done((bf16[256,512]{1,0:T(8,128)(2,1)S(1)}, bf16[256,512]{1,0:T(8,128)(2,1)S(1)}, u32[]{:S(2)}, u32[]{:S(2)}) %collective-permute-start.6) | collective-permute-done | bytes 262176 | tf_op jit(solution)/shard_map/down_y_mp1/ppermute | solution.py:782
  25.2 2.9 %attend_second.1 = (bf16[3,512,256]{2,1,0:T(8,128)(2,1)S(1)}, bf16[2,1024,256]{2,1,0:T(8,128)(2,1)S(1)}, bf16[2,512,256]{2,1,0:T(8,128)(2,1)S(1)}, bf16[512,256]...) custom-call(s32[1]{0:T(128)S(6)} %copy.51.refs_0_, ...), custom_call_target="tpu_custom_call" | custom-call | flops 5000000000 | tf_op jit(solution)/shard_map/attend_second/pallas_call | solution.py:39
  28.2 2.2 %ffn_own.1 = (bf16[512,512]{1,0:T(8,128)(2,1)S(1)}, bf16[512,1024]{1,0:T(8,128)(2,1)S(1)}, bf16[512,1024]{1,0:T(8,128)(2,1)S(1)}, f32[512,512]{1,0:T(8,128)S(1)}) custom-call(f32[512,512]{1,0:T(8,128)S(1)} %get-tuple-element.91.refs_0_, bf16[512,1024]{1,0:T(8,128)(2,1)S(1)} %copy-done, bf16[1024,512]{1,0:T(8,128)(2,1)S(1)} %copy-done.1, ...), custom_call_target="tpu_custom_call" | custom-call | flops 4000000000 | tf_op jit(solution)/shard_map/ffn_own/pallas_call | solution.py:39
  30.5 2.9 %collective-permute-done.10.refs_0_ = bf16[256,512]{1,0:T(8,128)(2,1)S(1)} collective-permute-done((bf16[256,512]{1,0:T(8,128)(2,1)S(1)}, bf16[256,512]{1,0:T(8,128)(2,1)S(1)}, u32[]{:S(2)}, u32[]{:S(2)}) %collective-permute-start.10) | collective-permute-done | bytes 262176 | tf_op jit(solution)/shard_map/down_z_z1/ppermute | solution.py:782
  33.8 1.0 collective-permute-done.12.refs_11_
  35.3 4.0 %ffn_other.1 = (bf16[512,512]{1,0:T(8,128)(2,1)}, bf16[1024,512]{1,0:T(8,128)(2,1)S(1)}, bf16[1024,512]{1,0:T(8,128)(2,1)S(1)}, bf16[512,1024]{1,0:T(8,128)(2,1)...) custom-call(bf16[512,512]{1,0:T(8,128)(2,1)S(1)} %copy-done.3, ...), custom_call_target="tpu_custom_call" | custom-call | flops 6000000000 | tf_op jit(solution)/shard_map/ffn_other/pallas_call | solution.py:39
  39.4 4.9 %ffn_back.1 = (bf16[1296,512]{1,0:T(8,128)(2,1)S(1)}, bf16[1296,512]{1,0:T(8,128)(2,1)S(1)}, f32[16,512]{1,0:T(8,128)S(1)}, f32[512,512]{1,0:T(8,128)S(1)}) custom-call(f32[512,512]{1,0:T(8,128)S(1)} %get-tuple-element.91.refs_0_, f32[512,512]{1,0:T(8,128)S(1)} %get-tuple-element.97.refs_1_, bf16[512,512]{1,0:T(8,128)(2,1)S(1)} %get-tuple-element.93.refs_1_.refs_2_, ...), custom_call_target="tpu_custom_call" | custom-call | flops 6000000000 | tf_op jit(solution)/shard_map/ffn_back/pallas_call | solution.py:39
  45.0 1.6 %collective-permute-start.18 = (bf16[512,512]{1,0:T(8,128)(2,1)S(1)}, bf16[512,512]{1,0:T(8,128)(2,1)S(1)}, u32[]{:S(2)}, u32[]{:S(2)}) collective-permute-start(bf16[512,512]{1,0:T(8,128)(2,1)S(1)} %down_core.1.refs_2_), channel_id=1, source_target_pairs={{0,1},{1,0},{2,3},{3,2},{4,5},{5,4},{6,7},{7,6},{8,9},{9,8},{10,11... | collective-permute-start | bytes 1572872 | tf_op jit(solution)/shard_map/down_from_y_mp1/ppermute | solution.py:782
  46.5 1.0 collective-permute-done.13.refs_1_
  48.4 7.3 %attend_back.1 = (bf16[384,512]{1,0:T(8,128)(2,1)S(1)}, bf16[384,512]{1,0:T(8,128)(2,1)S(1)}, bf16[256,512]{1,0:T(8,128)(2,1)S(1)}, bf16[256,512]{1,0:T(8,128)(2...) custom-call(s32[1]{0:T(128)S(6)} %copy.51.refs_0_, ...), custom_call_target="tpu_custom_call" | custom-call | flops 12999999488 | tf_op jit(solution)/shard_map/attend_back/pallas_call | solution.py:39
  56.2 0.7 project_back.1
  57.1 1.9 %collective-permute-done.18.refs_2_ = bf16[512,512]{1,0:T(8,128)(2,1)S(1)} collective-permute-done((bf16[512,512]{1,0:T(8,128)(2,1)S(1)}, bf16[512,512]{1,0:T(8,128)(2,1)S(1)}, u32[]{:S(2)}, u32[]{:S(2)}) %collective-permute-start.18) | collective-permute-done | bytes 524320 | tf_op jit(solution)/shard_map/down_from_y_mp1/ppermute | solution.py:782
  59.2 1.6 %collective-permute-start.20 = (bf16[256,512]{1,0:T(8,128)(2,1)S(1)}, bf16[256,512]{1,0:T(8,128)(2,1)S(1)}, u32[]{:S(2)}, u32[]{:S(2)}) collective-permute-start(bf16[256,512]{1,0:T(8,128)(2,1)S(1)} %get-tuple-element.131), channel_id=1, source_target_pairs={{0,4},{4,0},{1,5},{5,1},{2,6},{6,2},{3,7},{7,3},{8,12},{12,8},{9,1... | collective-permute-start | bytes 786440 | tf_op jit(solution)/shard_map/down_from_x_x1/ppermute | solution.py:782
  60.9 1.6 %collective-permute-start.19 = (bf16[512,512]{1,0:T(8,128)(2,1)S(1)}, bf16[512,512]{1,0:T(8,128)(2,1)S(1)}, u32[]{:S(2)}, u32[]{:S(2)}) collective-permute-start(bf16[512,512]{1,0:T(8,128)(2,1)S(1)} %get-tuple-element.129), channel_id=1, source_target_pairs={{0,1},{1,0},{2,3},{3,2},{4,5},{5,4},{6,7},{7,6},{8,9},{9,8},{10,11... | collective-permute-start | bytes 1572872 | tf_op jit(solution)/shard_map/att_from_y_mp1/ppermute | solution.py:782
  62.5 2.8 %collective-permute-done.21.refs_1_ = bf16[656,512]{1,0:T(8,128)(2,1)S(1)} collective-permute-done((bf16[656,512]{1,0:T(8,128)(2,1)S(1)}, bf16[656,512]{1,0:T(8,128)(2,1)S(1)}, u32[]{:S(2)}, u32[]{:S(2)}) %collective-permute-start.21) | collective-permute-done | bytes 671776 | tf_op jit(solution)/shard_map/up_from_z_z1/ppermute | solution.py:782
  65.4 1.6 %collective-permute-start.25 = (bf16[336,512]{1,0:T(8,128)(2,1)S(1)}, bf16[336,512]{1,0:T(8,128)(2,1)S(1)}, u32[]{:S(2)}, u32[]{:S(2)}) collective-permute-start(bf16[336,512]{1,0:T(8,128)(2,1)S(1)} %get-tuple-element.138), channel_id=1, source_target_pairs={{0,4},{4,0},{1,5},{5,1},{2,6},{6,2},{3,7},{7,3},{8,12},{12,8},{9,1... | collective-permute-start | bytes 1032200 | tf_op jit(solution)/shard_map/up_from_x_x1/ppermute | solution.py:782
  67.6 4.5 %collective-permute-done.22.refs_1_ = bf16[128,512]{1,0:T(8,128)(2,1)S(1)} collective-permute-done((bf16[128,512]{1,0:T(8,128)(2,1)S(1)}, bf16[128,512]{1,0:T(8,128)(2,1)S(1)}, u32[]{:S(2)}, u32[]{:S(2)}) %collective-permute-start.22) | collective-permute-done | bytes 131104 | tf_op jit(solution)/shard_map/down_from_z_z1/ppermute | solution.py:782
  72.1 2.8 %collective-permute-start.24 = (bf16[128,512]{1,0:T(8,128)(2,1)S(1)}, bf16[128,512]{1,0:T(8,128)(2,1)S(1)}, u32[]{:S(2)}, u32[]{:S(2)}) collective-permute-start(bf16[128,512]{1,0:T(8,128)(2,1)S(1)} %down_z.1.refs_4_.refs_0_), channel_id=1, source_target_pairs={{0,16},{8,24},{16,0},{24,8},{1,17},{9,25},{17,1},{25,9},{2,18},{10... | collective-permute-start | bytes 393224 | tf_op jit(solution)/shard_map/down_far_z2/ppermute | solution.py:782
  75.1 1.9 %collective-permute-start.23 = (bf16[256,512]{1,0:T(8,128)(2,1)S(1)}, bf16[256,512]{1,0:T(8,128)(2,1)S(1)}, u32[]{:S(2)}, u32[]{:S(2)}) collective-permute-start(bf16[256,512]{1,0:T(8,128)(2,1)S(1)} %get-tuple-element.137), channel_id=1, source_target_pairs={{0,4},{4,0},{1,5},{5,1},{2,6},{6,2},{3,7},{7,3},{8,12},{12,8},{9,1... | collective-permute-start | bytes 786440 | tf_op jit(solution)/shard_map/att_from_x_x1/ppermute | solution.py:782
  77.1 1.6 %collective-permute-start.28 = (bf16[176,512]{1,0:T(8,128)(2,1)S(1)}, bf16[176,512]{1,0:T(8,128)(2,1)S(1)}, u32[]{:S(2)}, u32[]{:S(2)}) collective-permute-start(bf16[176,512]{1,0:T(8,128)(2,1)S(1)} %get-tuple-element.142), channel_id=1, source_target_pairs={{0,1},{1,0},{2,3},{3,2},{4,5},{5,4},{6,7},{7,6},{8,9},{9,8},{10,11... | collective-permute-start | bytes 540680 | tf_op jit(solution)/shard_map/up_from_y_mp1/ppermute | solution.py:782
  78.7 0.9 collective-permute-done.24.refs_1_
  79.8 1.9 %collective-permute-done.23.refs_1_ = bf16[256,512]{1,0:T(8,128)(2,1)S(1)} collective-permute-done((bf16[256,512]{1,0:T(8,128)(2,1)S(1)}, bf16[256,512]{1,0:T(8,128)(2,1)S(1)}, u32[]{:S(2)}, u32[]{:S(2)}) %collective-permute-start.23) | collective-permute-done | bytes 262176 | tf_op jit(solution)/shard_map/att_from_x_x1/ppermute | solution.py:782
  82.7 1.7 %collective-permute-start.30 = (bf16[176,512]{1,0:T(8,128)(2,1)S(1)}, bf16[176,512]{1,0:T(8,128)(2,1)S(1)}, u32[]{:S(2)}, u32[]{:S(2)}) collective-permute-start(bf16[176,512]{1,0:T(8,128)(2,1)S(1)} %up_mp.1.refs_2_.refs_0_), channel_id=1, source_target_pairs={{0,16},{8,24},{16,0},{24,8},{1,17},{9,25},{17,1},{25,9},{2,18},{10... | collective-permute-start | bytes 540680 | tf_op jit(solution)/shard_map/up_far_z2/ppermute | solution.py:782
  84.5 2.9 %collective-permute-done.27.refs_1_ = bf16[128,512]{1,0:T(8,128)(2,1)S(1)} collective-permute-done((bf16[128,512]{1,0:T(8,128)(2,1)S(1)}, bf16[128,512]{1,0:T(8,128)(2,1)S(1)}, u32[]{:S(2)}, u32[]{:S(2)}) %collective-permute-start.27) | collective-permute-done | bytes 131104 | tf_op jit(solution)/shard_map/down_near_z1/ppermute | solution.py:782
  87.4 2.6 %collective-permute-done.26.refs_1_ = bf16[128,512]{1,0:T(8,128)(2,1)S(1)} collective-permute-done((bf16[128,512]{1,0:T(8,128)(2,1)S(1)}, bf16[128,512]{1,0:T(8,128)(2,1)S(1)}, u32[]{:S(2)}, u32[]{:S(2)}) %collective-permute-start.26) | collective-permute-done | bytes 131104 | tf_op jit(solution)/shard_map/att_from_z_z1/ppermute | solution.py:782
  90.1 2.8 %collective-permute-start.37 = (bf16[256,512]{1,0:T(8,128)(2,1)S(1)}, bf16[256,512]{1,0:T(8,128)(2,1)S(1)}, u32[]{:S(2)}, u32[]{:S(2)}) collective-permute-start(bf16[256,512]{1,0:T(8,128)(2,1)S(1)} %down_join.1.refs_2_.refs_0_), channel_id=1, source_target_pairs={{0,4},{4,0},{1,5},{5,1},{2,6},{6,2},{3,7},{7,3},{8,12},{12,8},{9,1... | collective-permute-start | bytes 786440 | tf_op jit(solution)/shard_map/down_x_x1/ppermute | solution.py:782
  93.0 0.6 collective-permute-done.30.refs_1_
  93.6 3.5 %collective-permute-start.34 = (bf16[160,512]{1,0:T(8,128)(2,1)S(1)}, bf16[160,512]{1,0:T(8,128)(2,1)S(1)}, u32[]{:S(2)}, u32[]{:S(2)}) collective-permute-start(bf16[160,512]{1,0:T(8,128)(2,1)S(1)} %get-tuple-element.146.refs_0_), channel_id=1, source_target_pairs={{0,4},{4,0},{1,5},{5,1},{2,6},{6,2},{3,7},{7,3},{8,12},{12,8},{9,1... | collective-permute-start | bytes 491528 | tf_op jit(solution)/shard_map/up_near_x1/ppermute | solution.py:782
  97.3 5.0 %collective-permute-done.31.refs_1_ = bf16[128,512]{1,0:T(8,128)(2,1)S(1)} collective-permute-done((bf16[128,512]{1,0:T(8,128)(2,1)S(1)}, bf16[128,512]{1,0:T(8,128)(2,1)S(1)}, u32[]{:S(2)}, u32[]{:S(2)}) %collective-permute-start.31) | collective-permute-done | bytes 131104 | tf_op jit(solution)/shard_map/att_near_z1/ppermute | solution.py:782
  103.0 1.7 %collective-permute-start.32 = (bf16[256,512]{1,0:T(8,128)(2,1)S(1)}, bf16[256,512]{1,0:T(8,128)(2,1)S(1)}, u32[]{:S(2)}, u32[]{:S(2)}) collective-permute-start(bf16[256,512]{1,0:T(8,128)(2,1)S(1)} %get-tuple-element.144.refs_0_), channel_id=1, source_target_pairs={{0,4},{4,0},{1,5},{5,1},{2,6},{6,2},{3,7},{7,3},{8,12},{12,8},{9,1... | collective-permute-start | bytes 786440 | tf_op jit(solution)/shard_map/att_x_x1/ppermute | solution.py:782
  104.7 1.5 %collective-permute-start.36 = (bf16[64,512]{1,0:T(8,128)(2,1)S(1)}, bf16[64,512]{1,0:T(8,128)(2,1)S(1)}, u32[]{:S(2)}, u32[]{:S(2)}) collective-permute-start(bf16[64,512]{1,0:T(8,128)(2,1)S(1)} %get-tuple-element.145.refs_2_), channel_id=1, source_target_pairs={{0,1},{1,0},{2,3},{3,2},{4,5},{5,4},{6,7},{7,6},{8,9},{9,8},{10,11... | collective-permute-start | bytes 196616 | tf_op jit(solution)/shard_map/table_y_mp1/ppermute | solution.py:782
  106.7 0.6 small_out.1
  107.4 1.5 %down_out.1 = (f32[1024,512]{1,0:T(8,128)}, f32[8,128]{1,0:T(8,128)S(1)}) custom-call(bf16[256,512]{1,0:T(8,128)(2,1)S(1)} %down_join.1.refs_2_.refs_0_, bf16[256,512]{1,0:T(8,128)(2,1)S(1)} %gate.17.refs_1_, bf16[256,512]{1,0:T(8,128)(2,1)S(1)} %collective-permute-done.38.refs_2_, bf16[256,512]{1,0:T(8,128)(2,1)S(1)} %collective-permute-done.39.refs_3_, ...), custom_call_target="tpu_custom_call" | custom-call | tf_op jit(solution)/shard_map/down_out/pallas_call | solution.py:39
  109.3 1.0 collective-permute-done.35.refs_0_
  110.3 3.4 %collective-permute-done.33.refs_0_ = bf16[64,512]{1,0:T(8,128)(2,1)S(1)} collective-permute-done((bf16[64,512]{1,0:T(8,128)(2,1)S(1)}, bf16[64,512]{1,0:T(8,128)(2,1)S(1)}, u32[]{:S(2)}, u32[]{:S(2)}) %collective-permute-start.33) | collective-permute-done | bytes 65568 | tf_op jit(solution)/shard_map/table_x/ppermute | solution.py:787
  114.3 1.7 %up_out.1 = (f32[512,1024]{1,0:T(8,128)}, f32[256,512]{1,0:T(8,128)}, f32[8,128]{1,0:T(8,128)S(1)}) custom-call(bf16[320,512]{1,0:T(8,128)(2,1)S(1)} %up_join.1.refs_1_.refs_0_, bf16[320,512]{1,0:T(8,128)(2,1)S(1)} %gate.19.refs_1_, bf16[320,512]{1,0:T(8,128)(2,1)S(1)} %collective-permute-done.44.refs_2_, ...), custom_call_target="tpu_custom_call" | custom-call | tf_op jit(solution)/shard_map/up_out/pallas_call | solution.py:39
  116.0 1.7 %attend_out.1 = (f32[3,512,256]{2,1,0:T(8,128)}, f32[512,512]{1,0:T(8,128)}) custom-call(bf16[256,512]{1,0:T(8,128)(2,1)S(1)} %get-tuple-element.144.refs_0_, bf16[256,512]{1,0:T(8,128)(2,1)S(1)} %gate.21.refs_4_.refs_1_, bf16[256,512]{1,0:T(8,128)(2,1)S(1)} %collective-permute-done.40.refs_2_, bf16[256,512]{1,0:T(8,128)(2,1)S(1)} %collective-permute-done.41.refs_3_, ...), custom_call_target="tpu_custom_call" | custom-call | tf_op jit(solution)/shard_map/attend_out/pallas_call | solution.py:39
  (119 shorter events, 10.1 us)
Async XLA Ops:
  3.0 5.7 %copy-start.2 = (bf16[512,3,256]{2,0,1:T(8,128)(2,1)S(1)}, bf16[512,3,256]{2,0,1:T(8,128)(2,1)}, u32[]{:S(2)}) copy-start(bf16[512,3,256]{2,0,1:T(8,128)(2,1)} %param.17) | copy-start | bytes 2359300
  3.1 5.7 %copy-start.4 = (bf16[512,512]{1,0:T(8,128)(2,1)S(1)}, bf16[512,512]{1,0:T(8,128)(2,1)}, u32[]{:S(2)}) copy-start(bf16[512,512]{1,0:T(8,128)(2,1)} %refs_1_.9) | copy-start | bytes 1572868
  3.1 10.7 %collective-permute-start = (bf16[272,512]{1,0:T(8,128)(2,1)}, bf16[272,512]{1,0:T(8,128)(2,1)S(1)}, u32[]{:S(2)}, u32[]{:S(2)}) collective-permute-start(bf16[272,512]{1,0:T(8,128)(2,1)} %pack_attend.1.refs_2_), channel_id=1, source_target_pairs={{0,1},{1,0},{2,3},{3,2},{4,5},{5,4},{6,7},{7,6},{8,9},{9,8},{10,11... | collective-permute-start | bytes 835592 | tf_op jit(solution)/shard_map/attend_y_mp1/ppermute | solution.py:782
  7.9 7.9 %collective-permute-start.2 = (bf16[128,512]{1,0:T(8,128)(2,1)}, bf16[128,512]{1,0:T(8,128)(2,1)S(1)}, u32[]{:S(2)}, u32[]{:S(2)}) collective-permute-start(bf16[128,512]{1,0:T(8,128)(2,1)} %get-tuple-element.88.refs_4_), channel_id=1, source_target_pairs={{0,1},{1,0},{2,3},{3,2},{4,5},{5,4},{6,7},{7,6},{8,9},{9,8},{10,11... | collective-permute-start | bytes 393224 | tf_op jit(solution)/shard_map/up_y_mp1/ppermute | solution.py:782
  13.8 7.0 %collective-permute-start.1 = (bf16[272,512]{1,0:T(8,128)(2,1)S(1)}, bf16[272,512]{1,0:T(8,128)(2,1)S(1)}, u32[]{:S(2)}, u32[]{:S(2)}) collective-permute-start(bf16[272,512]{1,0:T(8,128)(2,1)S(1)} %gate.11.refs_1_.refs_3_), channel_id=1, source_target_pairs={{0,4},{4,0},{1,5},{5,1},{2,6},{6,2},{3,7},{7,3},{8,12},{12,8},{9,1... | collective-permute-start | bytes 835592 | tf_op jit(solution)/shard_map/attend_x_x1/ppermute | solution.py:782
  15.9 5.0 %collective-permute-start.3 = (bf16[128,512]{1,0:T(8,128)(2,1)S(1)}, bf16[128,512]{1,0:T(8,128)(2,1)S(1)}, u32[]{:S(2)}, u32[]{:S(2)}) collective-permute-start(bf16[128,512]{1,0:T(8,128)(2,1)S(1)} %gate.12.refs_0_.refs_2_), channel_id=1, source_target_pairs={{0,8},{8,0},{16,24},{24,16},{1,9},{9,1},{17,25},{25,17},{2,10},{10... | collective-permute-start | bytes 393224 | tf_op jit(solution)/shard_map/up_z_z1/ppermute | solution.py:782
  17.6 6.9 %collective-permute-start.6 = (bf16[256,512]{1,0:T(8,128)(2,1)S(1)}, bf16[256,512]{1,0:T(8,128)(2,1)S(1)}, u32[]{:S(2)}, u32[]{:S(2)}) collective-permute-start(bf16[256,512]{1,0:T(8,128)(2,1)S(1)} %copy-done.15), channel_id=1, source_target_pairs={{0,1},{1,0},{2,3},{3,2},{4,5},{5,4},{6,7},{7,6},{8,9},{9,8},{10,11... | collective-permute-start | bytes 786440 | tf_op jit(solution)/shard_map/down_y_mp1/ppermute | solution.py:782
  19.1 5.5 %collective-permute-start.4 = (bf16[272,512]{1,0:T(8,128)(2,1)S(1)}, bf16[272,512]{1,0:T(8,128)(2,1)S(1)}, u32[]{:S(2)}, u32[]{:S(2)}) collective-permute-start(bf16[272,512]{1,0:T(8,128)(2,1)S(1)} %gate.11.refs_1_.refs_3_), channel_id=1, source_target_pairs={{0,2},{2,0},{1,3},{3,1},{4,6},{6,4},{5,7},{7,5},{8,10},{10,8},{9,1... | collective-permute-start | bytes 835592 | tf_op jit(solution)/shard_map/attend_cy_core1/ppermute | solution.py:782
  20.9 4.3 %collective-permute-start.5 = (bf16[272,512]{1,0:T(8,128)(2,1)S(1)}, bf16[272,512]{1,0:T(8,128)(2,1)S(1)}, u32[]{:S(2)}, u32[]{:S(2)}) collective-permute-start(bf16[272,512]{1,0:T(8,128)(2,1)S(1)} %gate.13.refs_1_.refs_4_), channel_id=1, source_target_pairs={{0,2},{2,0},{1,3},{3,1},{4,6},{6,4},{5,7},{7,5},{8,10},{10,8},{9,1... | collective-permute-start | bytes 835592 | tf_op jit(solution)/shard_map/attend_cx_core1/ppermute | solution.py:782
  21.0 12.9 %collective-permute-start.8 = (bf16[256,512]{1,0:T(8,128)(2,1)S(1)}, bf16[256,512]{1,0:T(8,128)(2,1)S(1)}, u32[]{:S(2)}, u32[]{:S(2)}) collective-permute-start(bf16[256,512]{1,0:T(8,128)(2,1)S(1)} %up_pair.1.refs_1_.refs_4_), channel_id=1, source_target_pairs={{0,2},{2,0},{1,3},{3,1},{4,6},{6,4},{5,7},{7,5},{8,10},{10,8},{9,1... | collective-permute-start | bytes 786440 | tf_op jit(solution)/shard_map/up_cy_core1/ppermute | solution.py:782
  21.5 8.9 %collective-permute-start.7 = (bf16[256,512]{1,0:T(8,128)(2,1)S(1)}, bf16[256,512]{1,0:T(8,128)(2,1)S(1)}, u32[]{:S(2)}, u32[]{:S(2)}) collective-permute-start(bf16[256,512]{1,0:T(8,128)(2,1)S(1)} %up_pair.1.refs_1_.refs_4_), channel_id=1, source_target_pairs={{0,4},{4,0},{1,5},{5,1},{2,6},{6,2},{3,7},{7,3},{8,12},{12,8},{9,1... | collective-permute-start | bytes 786440 | tf_op jit(solution)/shard_map/up_x_x1/ppermute | solution.py:782
  24.5 9.3 %collective-permute-start.11 = (bf16[256,512]{1,0:T(8,128)(2,1)S(1)}, bf16[256,512]{1,0:T(8,128)(2,1)S(1)}, u32[]{:S(2)}, u32[]{:S(2)}) collective-permute-start(bf16[256,512]{1,0:T(8,128)(2,1)S(1)} %gate.14.refs_10_.refs_8_), channel_id=1, source_target_pairs={{0,2},{2,0},{1,3},{3,1},{4,6},{6,4},{5,7},{7,5},{8,10},{10,8},{9,1... | collective-permute-start | bytes 786440 | tf_op jit(solution)/shard_map/down_cy_core1/ppermute | solution.py:782
  24.6 8.7 %collective-permute-start.10 = (bf16[256,512]{1,0:T(8,128)(2,1)S(1)}, bf16[256,512]{1,0:T(8,128)(2,1)S(1)}, u32[]{:S(2)}, u32[]{:S(2)}) collective-permute-start(bf16[256,512]{1,0:T(8,128)(2,1)S(1)} %gate.14.refs_10_.refs_8_), channel_id=1, source_target_pairs={{0,8},{8,0},{16,24},{24,16},{1,9},{9,1},{17,25},{25,17},{2,10},{10... | collective-permute-start | bytes 786440 | tf_op jit(solution)/shard_map/down_z_z1/ppermute | solution.py:782
  33.3 1.5 %collective-permute-start.12 = (bf16[256,512]{1,0:T(8,128)(2,1)S(1)}, bf16[256,512]{1,0:T(8,128)(2,1)S(1)}, u32[]{:S(2)}, u32[]{:S(2)}) collective-permute-start(bf16[256,512]{1,0:T(8,128)(2,1)S(1)} %gate.16.refs_9_.refs_16_), channel_id=1, source_target_pairs={{0,2},{2,0},{1,3},{3,1},{4,6},{6,4},{5,7},{7,5},{8,10},{10,8},{9,1... | collective-permute-start | bytes 786440 | tf_op jit(solution)/shard_map/down_cz_core1/ppermute | solution.py:782
  33.3 1.9 %collective-permute-start.9 = (bf16[256,512]{1,0:T(8,128)(2,1)S(1)}, bf16[256,512]{1,0:T(8,128)(2,1)S(1)}, u32[]{:S(2)}, u32[]{:S(2)}) collective-permute-start(bf16[256,512]{1,0:T(8,128)(2,1)S(1)} %gate.15.refs_1_.refs_5_), channel_id=1, source_target_pairs={{0,2},{2,0},{1,3},{3,1},{4,6},{6,4},{5,7},{7,5},{8,10},{10,8},{9,1... | collective-permute-start | bytes 786440 | tf_op jit(solution)/shard_map/up_cx_core1/ppermute | solution.py:782
  39.2 5.6 %collective-permute-start.14 = (bf16[1024,512]{1,0:T(8,128)(2,1)S(1)}, bf16[1024,512]{1,0:T(8,128)(2,1)S(1)}, u32[]{:S(2)}, u32[]{:S(2)}) collective-permute-start(bf16[1024,512]{1,0:T(8,128)(2,1)S(1)} %get-tuple-element.116), channel_id=1, source_target_pairs={{0,2},{2,0},{1,3},{3,1},{4,6},{6,4},{5,7},{7,5},{8,10},{10,8},{9,1... | collective-permute-start | bytes 3145736 | tf_op jit(solution)/shard_map/down_recv_core1/ppermute | solution.py:782
  44.4 3.2 %collective-permute-start.13 = (bf16[1296,512]{1,0:T(8,128)(2,1)S(1)}, bf16[1296,512]{1,0:T(8,128)(2,1)S(1)}, u32[]{:S(2)}, u32[]{:S(2)}) collective-permute-start(bf16[1296,512]{1,0:T(8,128)(2,1)S(1)} %get-tuple-element.114), channel_id=1, source_target_pairs={{0,2},{2,0},{1,3},{3,1},{4,6},{6,4},{5,7},{7,5},{8,10},{10,8},{9,1... | collective-permute-start | bytes 3981320 | tf_op jit(solution)/shard_map/up_recv_core1/ppermute | solution.py:782
  45.0 14.0 %collective-permute-start.18 = (bf16[512,512]{1,0:T(8,128)(2,1)S(1)}, bf16[512,512]{1,0:T(8,128)(2,1)S(1)}, u32[]{:S(2)}, u32[]{:S(2)}) collective-permute-start(bf16[512,512]{1,0:T(8,128)(2,1)S(1)} %down_core.1.refs_2_), channel_id=1, source_target_pairs={{0,1},{1,0},{2,3},{3,2},{4,5},{5,4},{6,7},{7,6},{8,9},{9,8},{10,11... | collective-permute-start | bytes 1572872 | tf_op jit(solution)/shard_map/down_from_y_mp1/ppermute | solution.py:782
  47.8 17.4 %collective-permute-start.21 = (bf16[656,512]{1,0:T(8,128)(2,1)S(1)}, bf16[656,512]{1,0:T(8,128)(2,1)S(1)}, u32[]{:S(2)}, u32[]{:S(2)}) collective-permute-start(bf16[656,512]{1,0:T(8,128)(2,1)S(1)} %get-tuple-element.132), channel_id=1, source_target_pairs={{0,8},{8,0},{16,24},{24,16},{1,9},{9,1},{17,25},{25,17},{2,10},{10... | collective-permute-start | bytes 2015240 | tf_op jit(solution)/shard_map/up_from_z_z1/ppermute | solution.py:782
  55.7 5.1 %collective-permute-start.16 = (bf16[384,512]{1,0:T(8,128)(2,1)S(1)}, bf16[384,512]{1,0:T(8,128)(2,1)S(1)}, u32[]{:S(2)}, u32[]{:S(2)}) collective-permute-start(bf16[384,512]{1,0:T(8,128)(2,1)S(1)} %get-tuple-element.126), channel_id=1, source_target_pairs={{0,2},{2,0},{1,3},{3,1},{4,6},{6,4},{5,7},{7,5},{8,10},{10,8},{9,1... | collective-permute-start | bytes 1179656 | tf_op jit(solution)/shard_map/oth_recv_core1/ppermute | solution.py:782
  55.8 5.0 %collective-permute-start.17 = (bf16[256,512]{1,0:T(8,128)(2,1)S(1)}, bf16[256,512]{1,0:T(8,128)(2,1)S(1)}, u32[]{:S(2)}, u32[]{:S(2)}) collective-permute-start(bf16[256,512]{1,0:T(8,128)(2,1)S(1)} %get-tuple-element.127), channel_id=1, source_target_pairs={{0,2},{2,0},{1,3},{3,1},{4,6},{6,4},{5,7},{7,5},{8,10},{10,8},{9,1... | collective-permute-start | bytes 786440 | tf_op jit(solution)/shard_map/tab_recv_core1/ppermute | solution.py:782
  56.9 17.9 %collective-permute-start.15 = (bf16[384,512]{1,0:T(8,128)(2,1)S(1)}, bf16[384,512]{1,0:T(8,128)(2,1)S(1)}, u32[]{:S(2)}, u32[]{:S(2)}) collective-permute-start(bf16[384,512]{1,0:T(8,128)(2,1)S(1)} %get-tuple-element.124), channel_id=1, source_target_pairs={{0,2},{2,0},{1,3},{3,1},{4,6},{6,4},{5,7},{7,5},{8,10},{10,8},{9,1... | collective-permute-start | bytes 1179656 | tf_op jit(solution)/shard_map/own_recv_core1/ppermute | solution.py:782
  59.2 7.8 %collective-permute-start.20 = (bf16[256,512]{1,0:T(8,128)(2,1)S(1)}, bf16[256,512]{1,0:T(8,128)(2,1)S(1)}, u32[]{:S(2)}, u32[]{:S(2)}) collective-permute-start(bf16[256,512]{1,0:T(8,128)(2,1)S(1)} %get-tuple-element.131), channel_id=1, source_target_pairs={{0,4},{4,0},{1,5},{5,1},{2,6},{6,2},{3,7},{7,3},{8,12},{12,8},{9,1... | collective-permute-start | bytes 786440 | tf_op jit(solution)/shard_map/down_from_x_x1/ppermute | solution.py:782
  60.9 14.0 %collective-permute-start.19 = (bf16[512,512]{1,0:T(8,128)(2,1)S(1)}, bf16[512,512]{1,0:T(8,128)(2,1)S(1)}, u32[]{:S(2)}, u32[]{:S(2)}) collective-permute-start(bf16[512,512]{1,0:T(8,128)(2,1)S(1)} %get-tuple-element.129), channel_id=1, source_target_pairs={{0,1},{1,0},{2,3},{3,2},{4,5},{5,4},{6,7},{7,6},{8,9},{9,8},{10,11... | collective-permute-start | bytes 1572872 | tf_op jit(solution)/shard_map/att_from_y_mp1/ppermute | solution.py:782
  65.4 11.6 %collective-permute-start.25 = (bf16[336,512]{1,0:T(8,128)(2,1)S(1)}, bf16[336,512]{1,0:T(8,128)(2,1)S(1)}, u32[]{:S(2)}, u32[]{:S(2)}) collective-permute-start(bf16[336,512]{1,0:T(8,128)(2,1)S(1)} %get-tuple-element.138), channel_id=1, source_target_pairs={{0,4},{4,0},{1,5},{5,1},{2,6},{6,2},{3,7},{7,3},{8,12},{12,8},{9,1... | collective-permute-start | bytes 1032200 | tf_op jit(solution)/shard_map/up_from_x_x1/ppermute | solution.py:782
  67.0 5.0 %collective-permute-start.22 = (bf16[128,512]{1,0:T(8,128)(2,1)S(1)}, bf16[128,512]{1,0:T(8,128)(2,1)S(1)}, u32[]{:S(2)}, u32[]{:S(2)}) collective-permute-start(bf16[128,512]{1,0:T(8,128)(2,1)S(1)} %get-tuple-element.135), channel_id=1, source_target_pairs={{0,8},{8,0},{16,24},{24,16},{1,9},{9,1},{17,25},{25,17},{2,10},{10... | collective-permute-start | bytes 393224 | tf_op jit(solution)/shard_map/down_from_z_z1/ppermute | solution.py:782
  72.1 7.5 %collective-permute-start.24 = (bf16[128,512]{1,0:T(8,128)(2,1)S(1)}, bf16[128,512]{1,0:T(8,128)(2,1)S(1)}, u32[]{:S(2)}, u32[]{:S(2)}) collective-permute-start(bf16[128,512]{1,0:T(8,128)(2,1)S(1)} %down_z.1.refs_4_.refs_0_), channel_id=1, source_target_pairs={{0,16},{8,24},{16,0},{24,8},{1,17},{9,25},{17,1},{25,9},{2,18},{10... | collective-permute-start | bytes 393224 | tf_op jit(solution)/shard_map/down_far_z2/ppermute | solution.py:782
  75.1 6.7 %collective-permute-start.23 = (bf16[256,512]{1,0:T(8,128)(2,1)S(1)}, bf16[256,512]{1,0:T(8,128)(2,1)S(1)}, u32[]{:S(2)}, u32[]{:S(2)}) collective-permute-start(bf16[256,512]{1,0:T(8,128)(2,1)S(1)} %get-tuple-element.137), channel_id=1, source_target_pairs={{0,4},{4,0},{1,5},{5,1},{2,6},{6,2},{3,7},{7,3},{8,12},{12,8},{9,1... | collective-permute-start | bytes 786440 | tf_op jit(solution)/shard_map/att_from_x_x1/ppermute | solution.py:782
  77.1 5.6 %collective-permute-start.28 = (bf16[176,512]{1,0:T(8,128)(2,1)S(1)}, bf16[176,512]{1,0:T(8,128)(2,1)S(1)}, u32[]{:S(2)}, u32[]{:S(2)}) collective-permute-start(bf16[176,512]{1,0:T(8,128)(2,1)S(1)} %get-tuple-element.142), channel_id=1, source_target_pairs={{0,1},{1,0},{2,3},{3,2},{4,5},{5,4},{6,7},{7,6},{8,9},{9,8},{10,11... | collective-permute-start | bytes 540680 | tf_op jit(solution)/shard_map/up_from_y_mp1/ppermute | solution.py:782
  79.7 7.7 %collective-permute-start.27 = (bf16[128,512]{1,0:T(8,128)(2,1)S(1)}, bf16[128,512]{1,0:T(8,128)(2,1)S(1)}, u32[]{:S(2)}, u32[]{:S(2)}) collective-permute-start(bf16[128,512]{1,0:T(8,128)(2,1)S(1)} %down_far.1.refs_2_.refs_0_), channel_id=1, source_target_pairs={{0,8},{8,0},{16,24},{24,16},{1,9},{9,1},{17,25},{25,17},{2,10},{10... | collective-permute-start | bytes 393224 | tf_op jit(solution)/shard_map/down_near_z1/ppermute | solution.py:782
  81.8 8.2 %collective-permute-start.26 = (bf16[128,512]{1,0:T(8,128)(2,1)S(1)}, bf16[128,512]{1,0:T(8,128)(2,1)S(1)}, u32[]{:S(2)}, u32[]{:S(2)}) collective-permute-start(bf16[128,512]{1,0:T(8,128)(2,1)S(1)} %get-tuple-element.141), channel_id=1, source_target_pairs={{0,8},{8,0},{16,24},{24,16},{1,9},{9,1},{17,25},{25,17},{2,10},{10... | collective-permute-start | bytes 393224 | tf_op jit(solution)/shard_map/att_from_z_z1/ppermute | solution.py:782
  82.7 10.8 %collective-permute-start.30 = (bf16[176,512]{1,0:T(8,128)(2,1)S(1)}, bf16[176,512]{1,0:T(8,128)(2,1)S(1)}, u32[]{:S(2)}, u32[]{:S(2)}) collective-permute-start(bf16[176,512]{1,0:T(8,128)(2,1)S(1)} %up_mp.1.refs_2_.refs_0_), channel_id=1, source_target_pairs={{0,16},{8,24},{16,0},{24,8},{1,17},{9,25},{17,1},{25,9},{2,18},{10... | collective-permute-start | bytes 540680 | tf_op jit(solution)/shard_map/up_far_z2/ppermute | solution.py:782
  90.0 7.1 %collective-permute-start.29 = (bf16[128,512]{1,0:T(8,128)(2,1)S(1)}, bf16[128,512]{1,0:T(8,128)(2,1)S(1)}, u32[]{:S(2)}, u32[]{:S(2)}) collective-permute-start(bf16[128,512]{1,0:T(8,128)(2,1)S(1)} %attend_z.1.refs_2_.refs_0_), channel_id=1, source_target_pairs={{0,16},{8,24},{16,0},{24,8},{1,17},{9,25},{17,1},{25,9},{2,18},{10... | collective-permute-start | bytes 393224 | tf_op jit(solution)/shard_map/att_far_z2/ppermute | solution.py:782
  90.1 12.4 %collective-permute-start.37 = (bf16[256,512]{1,0:T(8,128)(2,1)S(1)}, bf16[256,512]{1,0:T(8,128)(2,1)S(1)}, u32[]{:S(2)}, u32[]{:S(2)}) collective-permute-start(bf16[256,512]{1,0:T(8,128)(2,1)S(1)} %down_join.1.refs_2_.refs_0_), channel_id=1, source_target_pairs={{0,4},{4,0},{1,5},{5,1},{2,6},{6,2},{3,7},{7,3},{8,12},{12,8},{9,1... | collective-permute-start | bytes 786440 | tf_op jit(solution)/shard_map/down_x_x1/ppermute | solution.py:782
  93.6 8.6 %collective-permute-start.34 = (bf16[160,512]{1,0:T(8,128)(2,1)S(1)}, bf16[160,512]{1,0:T(8,128)(2,1)S(1)}, u32[]{:S(2)}, u32[]{:S(2)}) collective-permute-start(bf16[160,512]{1,0:T(8,128)(2,1)S(1)} %get-tuple-element.146.refs_0_), channel_id=1, source_target_pairs={{0,4},{4,0},{1,5},{5,1},{2,6},{6,2},{3,7},{7,3},{8,12},{12,8},{9,1... | collective-permute-start | bytes 491528 | tf_op jit(solution)/shard_map/up_near_x1/ppermute | solution.py:782
  97.2 5.0 %collective-permute-start.31 = (bf16[128,512]{1,0:T(8,128)(2,1)S(1)}, bf16[128,512]{1,0:T(8,128)(2,1)S(1)}, u32[]{:S(2)}, u32[]{:S(2)}) collective-permute-start(bf16[128,512]{1,0:T(8,128)(2,1)S(1)} %attend_far.1.refs_0_.refs_2_), channel_id=1, source_target_pairs={{0,8},{8,0},{16,24},{24,16},{1,9},{9,1},{17,25},{25,17},{2,10},{10... | collective-permute-start | bytes 393224 | tf_op jit(solution)/shard_map/att_near_z1/ppermute | solution.py:782
  102.3 8.0 %collective-permute-start.35 = (bf16[320,512]{1,0:T(8,128)(2,1)S(1)}, bf16[320,512]{1,0:T(8,128)(2,1)S(1)}, u32[]{:S(2)}, u32[]{:S(2)}) collective-permute-start(bf16[320,512]{1,0:T(8,128)(2,1)S(1)} %up_join.1.refs_1_.refs_0_), channel_id=1, source_target_pairs={{0,8},{8,0},{16,24},{24,16},{1,9},{9,1},{17,25},{25,17},{2,10},{10... | collective-permute-start | bytes 983048 | tf_op jit(solution)/shard_map/up_last_z1/ppermute | solution.py:782
  102.5 3.8 %collective-permute-start.38 = (bf16[256,512]{1,0:T(8,128)(2,1)S(1)}, bf16[256,512]{1,0:T(8,128)(2,1)S(1)}, u32[]{:S(2)}, u32[]{:S(2)}) collective-permute-start(bf16[256,512]{1,0:T(8,128)(2,1)S(1)} %down_join.1.refs_2_.refs_0_), channel_id=1, source_target_pairs={{0,2},{2,0},{1,3},{3,1},{4,6},{6,4},{5,7},{7,5},{8,10},{10,8},{9,1... | collective-permute-start | bytes 786440 | tf_op jit(solution)/shard_map/down_core_core1/ppermute | solution.py:782
  102.5 4.8 %collective-permute-start.39 = (bf16[256,512]{1,0:T(8,128)(2,1)S(1)}, bf16[256,512]{1,0:T(8,128)(2,1)S(1)}, u32[]{:S(2)}, u32[]{:S(2)}) collective-permute-start(bf16[256,512]{1,0:T(8,128)(2,1)S(1)} %gate.17.refs_1_), channel_id=1, source_target_pairs={{0,2},{2,0},{1,3},{3,1},{4,6},{6,4},{5,7},{7,5},{8,10},{10,8},{9,1... | collective-permute-start | bytes 786440 | tf_op jit(solution)/shard_map/down_core_x_core1/ppermute | solution.py:782
  103.0 10.7 %collective-permute-start.32 = (bf16[256,512]{1,0:T(8,128)(2,1)S(1)}, bf16[256,512]{1,0:T(8,128)(2,1)S(1)}, u32[]{:S(2)}, u32[]{:S(2)}) collective-permute-start(bf16[256,512]{1,0:T(8,128)(2,1)S(1)} %get-tuple-element.144.refs_0_), channel_id=1, source_target_pairs={{0,4},{4,0},{1,5},{5,1},{2,6},{6,2},{3,7},{7,3},{8,12},{12,8},{9,1... | collective-permute-start | bytes 786440 | tf_op jit(solution)/shard_map/att_x_x1/ppermute | solution.py:782
  104.7 4.3 %collective-permute-start.36 = (bf16[64,512]{1,0:T(8,128)(2,1)S(1)}, bf16[64,512]{1,0:T(8,128)(2,1)S(1)}, u32[]{:S(2)}, u32[]{:S(2)}) collective-permute-start(bf16[64,512]{1,0:T(8,128)(2,1)S(1)} %get-tuple-element.145.refs_2_), channel_id=1, source_target_pairs={{0,1},{1,0},{2,3},{3,2},{4,5},{5,4},{6,7},{7,6},{8,9},{9,8},{10,11... | collective-permute-start | bytes 196616 | tf_op jit(solution)/shard_map/table_y_mp1/ppermute | solution.py:782
  106.2 7.4 %collective-permute-start.33 = (bf16[64,512]{1,0:T(8,128)(2,1)S(1)}, bf16[64,512]{1,0:T(8,128)(2,1)S(1)}, u32[]{:S(2)}, u32[]{:S(2)}) collective-permute-start(bf16[64,512]{1,0:T(8,128)(2,1)S(1)} %get-tuple-element.145.refs_2_), channel_id=1, source_target_pairs={{0,5},{1,4},{4,1},{5,0},{2,7},{3,6},{6,3},{7,2},{8,13},{9,12},{12,... | collective-permute-start | bytes 196616 | tf_op jit(solution)/shard_map/table_x/ppermute | solution.py:787
  107.3 8.7 %collective-permute-start.40 = (bf16[256,512]{1,0:T(8,128)(2,1)S(1)}, bf16[256,512]{1,0:T(8,128)(2,1)S(1)}, u32[]{:S(2)}, u32[]{:S(2)}) collective-permute-start(bf16[256,512]{1,0:T(8,128)(2,1)S(1)} %get-tuple-element.144.refs_0_), channel_id=1, source_target_pairs={{0,2},{2,0},{1,3},{3,1},{4,6},{6,4},{5,7},{7,5},{8,10},{10,8},{9,1... | collective-permute-start | bytes 786440 | tf_op jit(solution)/shard_map/att_core_core1/ppermute | solution.py:782
  109.0 5.2 %collective-permute-start.44 = (bf16[320,512]{1,0:T(8,128)(2,1)S(1)}, bf16[320,512]{1,0:T(8,128)(2,1)S(1)}, u32[]{:S(2)}, u32[]{:S(2)}) collective-permute-start(bf16[320,512]{1,0:T(8,128)(2,1)S(1)} %up_join.1.refs_1_.refs_0_), channel_id=1, source_target_pairs={{0,2},{2,0},{1,3},{3,1},{4,6},{6,4},{5,7},{7,5},{8,10},{10,8},{9,1... | collective-permute-start | bytes 983048 | tf_op jit(solution)/shard_map/up_core_core1/ppermute | solution.py:782
  110.3 4.0 %collective-permute-start.45 = (bf16[320,512]{1,0:T(8,128)(2,1)S(1)}, bf16[320,512]{1,0:T(8,128)(2,1)S(1)}, u32[]{:S(2)}, u32[]{:S(2)}) collective-permute-start(bf16[320,512]{1,0:T(8,128)(2,1)S(1)} %gate.19.refs_1_), channel_id=1, source_target_pairs={{0,2},{2,0},{1,3},{3,1},{4,6},{6,4},{5,7},{7,5},{8,10},{10,8},{9,1... | collective-permute-start | bytes 983048 | tf_op jit(solution)/shard_map/up_core_x_core1/ppermute | solution.py:782
  113.7 2.4 %collective-permute-start.41 = (bf16[256,512]{1,0:T(8,128)(2,1)S(1)}, bf16[256,512]{1,0:T(8,128)(2,1)S(1)}, u32[]{:S(2)}, u32[]{:S(2)}) collective-permute-start(bf16[256,512]{1,0:T(8,128)(2,1)S(1)} %gate.21.refs_4_.refs_1_), channel_id=1, source_target_pairs={{0,2},{2,0},{1,3},{3,1},{4,6},{6,4},{5,7},{7,5},{8,10},{10,8},{9,1... | collective-permute-start | bytes 786440 | tf_op jit(solution)/shard_map/att_core_x_core1/ppermute | solution.py:782
  113.7 2.3 %collective-permute-start.42 = (bf16[64,512]{1,0:T(8,128)(2,1)S(1)}, bf16[64,512]{1,0:T(8,128)(2,1)S(1)}, u32[]{:S(2)}, u32[]{:S(2)}) collective-permute-start(bf16[64,512]{1,0:T(8,128)(2,1)S(1)} %gate.18.refs_1_.refs_4_), channel_id=1, source_target_pairs={{0,2},{2,0},{1,3},{3,1},{4,6},{6,4},{5,7},{7,5},{8,10},{10,8},{9,1... | collective-permute-start | bytes 196616 | tf_op jit(solution)/shard_map/table_core_core1/ppermute | solution.py:782
  114.2 1.8 %collective-permute-start.43 = (bf16[64,512]{1,0:T(8,128)(2,1)S(1)}, bf16[64,512]{1,0:T(8,128)(2,1)S(1)}, u32[]{:S(2)}, u32[]{:S(2)}) collective-permute-start(bf16[64,512]{1,0:T(8,128)(2,1)S(1)} %gate.20.refs_1_.refs_5_), channel_id=1, source_target_pairs={{0,2},{2,0},{1,3},{3,1},{4,6},{6,4},{5,7},{7,5},{8,10},{10,8},{9,1... | collective-permute-start | bytes 196616 | tf_op jit(solution)/shard_map/table_core_x_core1/ppermute | solution.py:782
  (14 other events, 56.7 us)

commit v5 on v4

--- a/solution.py
+++ b/solution.py
@@ -929,23 +929,23 @@
         mixed_own, early_own, late_own, context_own = attend_own()
         attend_y = step.gate(attend_y, 0)
         attend_x = swap(attend_y, "x", "attend_x")
-        attend_cy = swap(attend_y, "core", "attend_cy")
-        up_y = step.gate(up_y)
+        up_y = step.gate(up_y, 0)
         up_z = swap(up_y, "z", "up_z")
         (up_y,) = step(z_join_kernel, [(units // 4, width)], [up_y, up_z], 0, "up_pair")
         up_x = swap(up_y, "x", "up_x")
         up_cy = swap(up_y, "core", "up_cy")
-        attend_x = step.gate(attend_x)
+        down_y = step.gate(down_y, 1)
+        down_z = swap(down_y, "z", "down_z")
+        attend_x = step.gate(attend_x, 0)
         attend_cx = swap(attend_x, "core", "attend_cx")
-        down_y = step.gate(down_y, 2)
-        down_z = swap(down_y, "z", "down_z")
-        down_cy = swap(down_y, "core", "down_cy")
+        attend_cy = swap(attend_y, "core", "attend_cy")
         attend_in = (attend_y, attend_x, attend_cy, attend_cx)
         mixed_oth, early_oth, late_oth, context_oth, resid, w_oth, out_oth, bias_oth = attend_other()
         low, act_own, slope_own, branch = ffn_own()
         up_x = step.gate(up_x, 0)
         up_cx = swap(up_x, "core", "up_cx")
         down_z = step.gate(down_z, 4)
+        down_cy = swap(down_y, "core", "down_cy")
         down_cz = swap(down_z, "core", "down_cz")
         up_in = (up_y, up_x, up_cy, up_cx)
         down_in = (down_y, down_z, down_cy, down_cz)
@@ -1136,7 +1136,7 @@
         )
         att_from_x = swap(to_x, "x", "att_from_x")
         up_y, to_y = step(
-            up_z_kernel, [(group // 4 + EXTRA, width)] * 2, [up_z, up_from_z], 3, "up_z"
+            up_z_kernel, [(group // 4 + EXTRA, width)] * 2, [up_z, up_from_z], 1, "up_z"
         )
         up_from_y = swap(to_y, "mp", "up_from_y")
         (down_z,) = step(pair_kernel, [(piece, width)], [down_z, down_far], 0, "down_far")
@@ -1151,7 +1151,7 @@
         att_from_z = swap(to_z, "z", "att_from_z")
         (up_y,) = step(pair_kernel, [(group // 4 + EXTRA, width)], [up_y, up_from_y], 0, "up_mp")
         up_far = swap(up_y, "z", "up_far", 2)
-        (down_z,) = step(functools.partial(join_kernel, "z"), [(half, width)], [down_z, down_near], 0, "down_join")
+        (down_z,) = step(functools.partial(join_kernel, "z"), [(half, width)], [down_z, down_near], 7, "down_join")
         down_x = swap(down_z, "x", "down_x")
         (att_z,) = step(pair_kernel, [att_z.shape], [att_z, att_from_z], 0, "attend_z")
         att_far = swap(att_z, "z", "att_far", 2)

time: 118 us -> 118 us (level)
  starting transfers between devices: 41 us -> 42.2 us
  waiting for transfers between devices: 38.2 us -> 37 us
    ppermute x45, waiting for transfers between devices: 34.8 us -> 33.6 us  [swap(): return lax.ppermute(value, axis, pairs)]
    ppermute x45, starting transfers between devices: 40.6 us -> 41.8 us  [swap(): return lax.ppermute(value, axis, pairs)]
where the time goes in v5:
time: 118 us
  starting transfers between devices  42.2 us (36%)
  waiting for transfers between devices  37 us (31%)
  Pallas kernels  35.7 us (30%)
  between operations  1.95 us (2%)
    ppermute x45, starting transfers between devices, swap(): return lax.ppermute(value, axis, pairs)  41.8 us
    pallas_call x32, Pallas kernels, call(): pl.pallas_call(flat_kernel, out_shape=[jax.ShapeDtypeStruct(out, BF16) if...  35.7 us
    ppermute x45, waiting for transfers between devices, swap(): return lax.ppermute(value, axis, pairs)  33.6 us
    ppermute x1, waiting for transfers between devices, swap_corner(): return lax.ppermute(value, ('x', 'mp'), [(0, 3), (1, 2), (2, 1), (3, 0)])  3.4 us
  transfers between devices with their start and end apart: 46, of which 20 were waited for; matrix products, arithmetic and copies ran while one was open for 0% of the time, Pallas kernels for 23%

profile of v5, /device:TPU:0, one launch (start us, length us, event | category | flops | bytes accessed | tf_op | source)
XLA Modules:
  0.0 117.8 jit_solution(15184393553206075960)
XLA Ops:
  0.6 2.4 %pack_attend.1.refs_2_ = bf16[272,512]{1,0:T(8,128)(2,1)} custom-call(bf16[1024]{0:T(1024)(128)(2,1)} %refs_3_.1, bf16[3,512,256]{2,1,0:T(8,128)(2,1)} %bitcast.2, bf16[256,512]{1,0:T(8,128)(2,1)} %refs_5_.5), custom_call_target="tpu_custom_call" | custom-call | flops 1000000000 | tf_op jit(solution)/shard_map/pack_attend/pallas_call | solution.py:39
  3.1 3.0 %collective-permute-start = (bf16[272,512]{1,0:T(8,128)(2,1)}, bf16[272,512]{1,0:T(8,128)(2,1)S(1)}, u32[]{:S(2)}, u32[]{:S(2)}) collective-permute-start(bf16[272,512]{1,0:T(8,128)(2,1)} %pack_attend.1.refs_2_), channel_id=1, source_target_pairs={{0,1},{1,0},{2,3},{3,2},{4,5},{5,4},{6,7},{7,6},{8,9},{9,8},{10,11... | collective-permute-start | bytes 835592 | tf_op jit(solution)/shard_map/attend_y_mp1/ppermute | solution.py:782
  6.1 1.8 %pack_ffn.1 = (bf16[128,512]{1,0:T(8,128)(2,1)}, bf16[256,512]{1,0:T(8,128)(2,1)}) custom-call(bf16[512,1024]{1,0:T(8,128)(2,1)} %refs_5_.4, bf16[1024,512]{1,0:T(8,128)(2,1)} %refs_7_.1, bf16[272,512]{1,0:T(8,128)(2,1)} %pack_attend.1.refs_2_), custom_call_target="tpu_custom_call" | custom-call | flops 1000000000 | tf_op jit(solution)/shard_map/pack_ffn/pallas_call | solution.py:39
  8.1 1.9 %collective-permute-start.2 = (bf16[256,512]{1,0:T(8,128)(2,1)}, bf16[256,512]{1,0:T(8,128)(2,1)S(1)}, u32[]{:S(2)}, u32[]{:S(2)}) collective-permute-start(bf16[256,512]{1,0:T(8,128)(2,1)} %get-tuple-element.90), channel_id=1, source_target_pairs={{0,1},{1,0},{2,3},{3,2},{4,5},{5,4},{6,7},{7,6},{8,9},{9,8},{10,11... | collective-permute-start | bytes 786440 | tf_op jit(solution)/shard_map/down_y_mp1/ppermute | solution.py:782
  10.7 0.9 copy-done.7
  11.6 2.3 %attend_first.1 = (bf16[3,512,256]{2,1,0:T(8,128)(2,1)S(1)}, bf16[2,1024,256]{2,1,0:T(8,128)(2,1)S(1)}, bf16[2,512,256]{2,1,0:T(8,128)(2,1)S(1)}, bf16[512,256]{1,0:T(8,128)(2,1)S(1)}) custom-call(s32[1]{0:T(128)S(6)} %copy.51.refs_0_, bf16[512,512]{1,0:T(8,128)(2,1)S(1)} %copy-done.4, bf16[512,512]{1,0:T(8,128)(2,1)S(1)} %copy-done.5, ...), custom_call_target="tpu_custom_call" | custom-call | flops 3000000000 | tf_op jit(solution)/shard_map/attend_first/pallas_call | solution.py:39
  13.9 1.9 %collective-permute-start.1 = (bf16[272,512]{1,0:T(8,128)(2,1)S(1)}, bf16[272,512]{1,0:T(8,128)(2,1)S(1)}, u32[]{:S(2)}, u32[]{:S(2)}) collective-permute-start(bf16[272,512]{1,0:T(8,128)(2,1)S(1)} %gate.11.refs_1_.refs_3_), channel_id=1, source_target_pairs={{0,4},{4,0},{1,5},{5,1},{2,6},{6,2},{3,7},{7,3},{8,12},{12,8},{9,1... | collective-permute-start | bytes 835592 | tf_op jit(solution)/shard_map/attend_x_x1/ppermute | solution.py:782
  15.8 0.8 collective-permute-done.3.refs_0_
  16.6 2.1 %collective-permute-start.4 = (bf16[128,512]{1,0:T(8,128)(2,1)S(1)}, bf16[128,512]{1,0:T(8,128)(2,1)S(1)}, u32[]{:S(2)}, u32[]{:S(2)}) collective-permute-start(bf16[128,512]{1,0:T(8,128)(2,1)S(1)} %gate.12.refs_0_.refs_2_), channel_id=1, source_target_pairs={{0,8},{8,0},{16,24},{24,16},{1,9},{9,1},{17,25},{25,17},{2,10},{10... | collective-permute-start | bytes 393224 | tf_op jit(solution)/shard_map/up_z_z1/ppermute | solution.py:782
  18.7 2.9 %collective-permute-done.4.refs_1_ = bf16[128,512]{1,0:T(8,128)(2,1)S(1)} collective-permute-done((bf16[128,512]{1,0:T(8,128)(2,1)S(1)}, bf16[128,512]{1,0:T(8,128)(2,1)S(1)}, u32[]{:S(2)}, u32[]{:S(2)}) %collective-permute-start.4) | collective-permute-done | bytes 131104 | tf_op jit(solution)/shard_map/up_z_z1/ppermute | solution.py:782
  22.4 2.0 %collective-permute-start.10 = (bf16[256,512]{1,0:T(8,128)(2,1)S(1)}, bf16[256,512]{1,0:T(8,128)(2,1)S(1)}, u32[]{:S(2)}, u32[]{:S(2)}) collective-permute-start(bf16[256,512]{1,0:T(8,128)(2,1)S(1)} %gate.13.refs_1_.refs_8_), channel_id=1, source_target_pairs={{0,8},{8,0},{16,24},{24,16},{1,9},{9,1},{17,25},{25,17},{2,10},{10... | collective-permute-start | bytes 786440 | tf_op jit(solution)/shard_map/down_z_z1/ppermute | solution.py:782
  24.5 1.5 %collective-permute-start.7 = (bf16[256,512]{1,0:T(8,128)(2,1)S(1)}, bf16[256,512]{1,0:T(8,128)(2,1)S(1)}, u32[]{:S(2)}, u32[]{:S(2)}) collective-permute-start(bf16[256,512]{1,0:T(8,128)(2,1)S(1)} %up_pair.1.refs_1_.refs_4_), channel_id=1, source_target_pairs={{0,4},{4,0},{1,5},{5,1},{2,6},{6,2},{3,7},{7,3},{8,12},{12,8},{9,1... | collective-permute-start | bytes 786440 | tf_op jit(solution)/shard_map/up_x_x1/ppermute | solution.py:782
  26.0 2.9 %attend_second.1 = (bf16[3,512,256]{2,1,0:T(8,128)(2,1)S(1)}, bf16[2,1024,256]{2,1,0:T(8,128)(2,1)S(1)}, bf16[2,512,256]{2,1,0:T(8,128)(2,1)S(1)}, bf16[512,256]...) custom-call(s32[1]{0:T(128)S(6)} %copy.51.refs_0_, ...), custom_call_target="tpu_custom_call" | custom-call | flops 5000000000 | tf_op jit(solution)/shard_map/attend_second/pallas_call | solution.py:39
  28.9 2.2 %ffn_own.1 = (bf16[512,512]{1,0:T(8,128)(2,1)S(1)}, bf16[512,1024]{1,0:T(8,128)(2,1)S(1)}, bf16[512,1024]{1,0:T(8,128)(2,1)S(1)}, f32[512,512]{1,0:T(8,128)S(1)}) custom-call(f32[512,512]{1,0:T(8,128)S(1)} %get-tuple-element.91.refs_0_, bf16[512,1024]{1,0:T(8,128)(2,1)S(1)} %copy-done, bf16[1024,512]{1,0:T(8,128)(2,1)S(1)} %copy-done.1, ...), custom_call_target="tpu_custom_call" | custom-call | flops 4000000000 | tf_op jit(solution)/shard_map/ffn_own/pallas_call | solution.py:39
  31.1 2.1 %collective-permute-done.7.refs_0_ = bf16[256,512]{1,0:T(8,128)(2,1)S(1)} collective-permute-done((bf16[256,512]{1,0:T(8,128)(2,1)S(1)}, bf16[256,512]{1,0:T(8,128)(2,1)S(1)}, u32[]{:S(2)}, u32[]{:S(2)}) %collective-permute-start.7) | collective-permute-done | bytes 262176 | tf_op jit(solution)/shard_map/up_x_x1/ppermute | solution.py:782
  33.8 1.0 collective-permute-done.12.refs_11_
  35.2 3.9 %ffn_other.1 = (bf16[512,512]{1,0:T(8,128)(2,1)}, bf16[1024,512]{1,0:T(8,128)(2,1)S(1)}, bf16[1024,512]{1,0:T(8,128)(2,1)S(1)}, bf16[512,1024]{1,0:T(8,128)(2,1)...) custom-call(bf16[512,512]{1,0:T(8,128)(2,1)S(1)} %copy-done.3, ...), custom_call_target="tpu_custom_call" | custom-call | flops 6000000000 | tf_op jit(solution)/shard_map/ffn_other/pallas_call | solution.py:39
  39.4 4.9 %ffn_back.1 = (bf16[1296,512]{1,0:T(8,128)(2,1)S(1)}, bf16[1296,512]{1,0:T(8,128)(2,1)S(1)}, f32[16,512]{1,0:T(8,128)S(1)}, f32[512,512]{1,0:T(8,128)S(1)}) custom-call(f32[512,512]{1,0:T(8,128)S(1)} %get-tuple-element.91.refs_0_, f32[512,512]{1,0:T(8,128)S(1)} %get-tuple-element.97.refs_1_, bf16[512,512]{1,0:T(8,128)(2,1)S(1)} %get-tuple-element.93.refs_1_.refs_2_, ...), custom_call_target="tpu_custom_call" | custom-call | flops 6000000000 | tf_op jit(solution)/shard_map/ffn_back/pallas_call | solution.py:39
  44.9 1.6 %collective-permute-start.18 = (bf16[512,512]{1,0:T(8,128)(2,1)S(1)}, bf16[512,512]{1,0:T(8,128)(2,1)S(1)}, u32[]{:S(2)}, u32[]{:S(2)}) collective-permute-start(bf16[512,512]{1,0:T(8,128)(2,1)S(1)} %down_core.1.refs_2_), channel_id=1, source_target_pairs={{0,1},{1,0},{2,3},{3,2},{4,5},{5,4},{6,7},{7,6},{8,9},{9,8},{10,11... | collective-permute-start | bytes 1572872 | tf_op jit(solution)/shard_map/down_from_y_mp1/ppermute | solution.py:782
  46.5 1.0 collective-permute-done.13.refs_1_
  48.1 7.3 %attend_back.1 = (bf16[384,512]{1,0:T(8,128)(2,1)S(1)}, bf16[384,512]{1,0:T(8,128)(2,1)S(1)}, bf16[256,512]{1,0:T(8,128)(2,1)S(1)}, bf16[256,512]{1,0:T(8,128)(2...) custom-call(s32[1]{0:T(128)S(6)} %copy.51.refs_0_, ...), custom_call_target="tpu_custom_call" | custom-call | flops 12999999488 | tf_op jit(solution)/shard_map/attend_back/pallas_call | solution.py:39
  55.8 0.7 project_back.1
  56.8 2.1 %collective-permute-done.18.refs_2_ = bf16[512,512]{1,0:T(8,128)(2,1)S(1)} collective-permute-done((bf16[512,512]{1,0:T(8,128)(2,1)S(1)}, bf16[512,512]{1,0:T(8,128)(2,1)S(1)}, u32[]{:S(2)}, u32[]{:S(2)}) %collective-permute-start.18) | collective-permute-done | bytes 524320 | tf_op jit(solution)/shard_map/down_from_y_mp1/ppermute | solution.py:782
  59.1 1.5 %collective-permute-start.20 = (bf16[256,512]{1,0:T(8,128)(2,1)S(1)}, bf16[256,512]{1,0:T(8,128)(2,1)S(1)}, u32[]{:S(2)}, u32[]{:S(2)}) collective-permute-start(bf16[256,512]{1,0:T(8,128)(2,1)S(1)} %get-tuple-element.131), channel_id=1, source_target_pairs={{0,4},{4,0},{1,5},{5,1},{2,6},{6,2},{3,7},{7,3},{8,12},{12,8},{9,1... | collective-permute-start | bytes 786440 | tf_op jit(solution)/shard_map/down_from_x_x1/ppermute | solution.py:782
  60.8 1.6 %collective-permute-start.19 = (bf16[512,512]{1,0:T(8,128)(2,1)S(1)}, bf16[512,512]{1,0:T(8,128)(2,1)S(1)}, u32[]{:S(2)}, u32[]{:S(2)}) collective-permute-start(bf16[512,512]{1,0:T(8,128)(2,1)S(1)} %get-tuple-element.129), channel_id=1, source_target_pairs={{0,1},{1,0},{2,3},{3,2},{4,5},{5,4},{6,7},{7,6},{8,9},{9,8},{10,11... | collective-permute-start | bytes 1572872 | tf_op jit(solution)/shard_map/att_from_y_mp1/ppermute | solution.py:782
  62.4 2.7 %collective-permute-done.21.refs_1_ = bf16[656,512]{1,0:T(8,128)(2,1)S(1)} collective-permute-done((bf16[656,512]{1,0:T(8,128)(2,1)S(1)}, bf16[656,512]{1,0:T(8,128)(2,1)S(1)}, u32[]{:S(2)}, u32[]{:S(2)}) %collective-permute-start.21) | collective-permute-done | bytes 671776 | tf_op jit(solution)/shard_map/up_from_z_z1/ppermute | solution.py:782
  65.3 1.6 %collective-permute-start.25 = (bf16[336,512]{1,0:T(8,128)(2,1)S(1)}, bf16[336,512]{1,0:T(8,128)(2,1)S(1)}, u32[]{:S(2)}, u32[]{:S(2)}) collective-permute-start(bf16[336,512]{1,0:T(8,128)(2,1)S(1)} %get-tuple-element.138), channel_id=1, source_target_pairs={{0,4},{4,0},{1,5},{5,1},{2,6},{6,2},{3,7},{7,3},{8,12},{12,8},{9,1... | collective-permute-start | bytes 1032200 | tf_op jit(solution)/shard_map/up_from_x_x1/ppermute | solution.py:782
  67.0 0.6 collective-permute-start.22
  67.6 4.4 %collective-permute-done.22.refs_1_ = bf16[128,512]{1,0:T(8,128)(2,1)S(1)} collective-permute-done((bf16[128,512]{1,0:T(8,128)(2,1)S(1)}, bf16[128,512]{1,0:T(8,128)(2,1)S(1)}, u32[]{:S(2)}, u32[]{:S(2)}) %collective-permute-start.22) | collective-permute-done | bytes 131104 | tf_op jit(solution)/shard_map/down_from_z_z1/ppermute | solution.py:782
  72.0 2.7 %collective-permute-start.24 = (bf16[128,512]{1,0:T(8,128)(2,1)S(1)}, bf16[128,512]{1,0:T(8,128)(2,1)S(1)}, u32[]{:S(2)}, u32[]{:S(2)}) collective-permute-start(bf16[128,512]{1,0:T(8,128)(2,1)S(1)} %down_z.1.refs_4_.refs_0_), channel_id=1, source_target_pairs={{0,16},{8,24},{16,0},{24,8},{1,17},{9,25},{17,1},{25,9},{2,18},{10... | collective-permute-start | bytes 393224 | tf_op jit(solution)/shard_map/down_far_z2/ppermute | solution.py:782
  75.0 2.0 %collective-permute-start.23 = (bf16[256,512]{1,0:T(8,128)(2,1)S(1)}, bf16[256,512]{1,0:T(8,128)(2,1)S(1)}, u32[]{:S(2)}, u32[]{:S(2)}) collective-permute-start(bf16[256,512]{1,0:T(8,128)(2,1)S(1)} %get-tuple-element.137), channel_id=1, source_target_pairs={{0,4},{4,0},{1,5},{5,1},{2,6},{6,2},{3,7},{7,3},{8,12},{12,8},{9,1... | collective-permute-start | bytes 786440 | tf_op jit(solution)/shard_map/att_from_x_x1/ppermute | solution.py:782
  77.1 1.4 %collective-permute-start.28 = (bf16[176,512]{1,0:T(8,128)(2,1)S(1)}, bf16[176,512]{1,0:T(8,128)(2,1)S(1)}, u32[]{:S(2)}, u32[]{:S(2)}) collective-permute-start(bf16[176,512]{1,0:T(8,128)(2,1)S(1)} %get-tuple-element.142), channel_id=1, source_target_pairs={{0,1},{1,0},{2,3},{3,2},{4,5},{5,4},{6,7},{7,6},{8,9},{9,8},{10,11... | collective-permute-start | bytes 540680 | tf_op jit(solution)/shard_map/up_from_y_mp1/ppermute | solution.py:782
  78.5 1.1 collective-permute-done.24.refs_1_
  79.7 1.9 %collective-permute-done.23.refs_1_ = bf16[256,512]{1,0:T(8,128)(2,1)S(1)} collective-permute-done((bf16[256,512]{1,0:T(8,128)(2,1)S(1)}, bf16[256,512]{1,0:T(8,128)(2,1)S(1)}, u32[]{:S(2)}, u32[]{:S(2)}) %collective-permute-start.23) | collective-permute-done | bytes 262176 | tf_op jit(solution)/shard_map/att_from_x_x1/ppermute | solution.py:782
  82.7 1.6 %collective-permute-start.30 = (bf16[176,512]{1,0:T(8,128)(2,1)S(1)}, bf16[176,512]{1,0:T(8,128)(2,1)S(1)}, u32[]{:S(2)}, u32[]{:S(2)}) collective-permute-start(bf16[176,512]{1,0:T(8,128)(2,1)S(1)} %up_mp.1.refs_2_.refs_0_), channel_id=1, source_target_pairs={{0,16},{8,24},{16,0},{24,8},{1,17},{9,25},{17,1},{25,9},{2,18},{10... | collective-permute-start | bytes 540680 | tf_op jit(solution)/shard_map/up_far_z2/ppermute | solution.py:782
  84.4 3.0 %collective-permute-done.27.refs_1_ = bf16[128,512]{1,0:T(8,128)(2,1)S(1)} collective-permute-done((bf16[128,512]{1,0:T(8,128)(2,1)S(1)}, bf16[128,512]{1,0:T(8,128)(2,1)S(1)}, u32[]{:S(2)}, u32[]{:S(2)}) %collective-permute-start.27) | collective-permute-done | bytes 131104 | tf_op jit(solution)/shard_map/down_near_z1/ppermute | solution.py:782
  87.4 2.5 %collective-permute-done.26.refs_1_ = bf16[128,512]{1,0:T(8,128)(2,1)S(1)} collective-permute-done((bf16[128,512]{1,0:T(8,128)(2,1)S(1)}, bf16[128,512]{1,0:T(8,128)(2,1)S(1)}, u32[]{:S(2)}, u32[]{:S(2)}) %collective-permute-start.26) | collective-permute-done | bytes 131104 | tf_op jit(solution)/shard_map/att_from_z_z1/ppermute | solution.py:782
  90.0 3.0 %collective-permute-start.37 = (bf16[256,512]{1,0:T(8,128)(2,1)S(1)}, bf16[256,512]{1,0:T(8,128)(2,1)S(1)}, u32[]{:S(2)}, u32[]{:S(2)}) collective-permute-start(bf16[256,512]{1,0:T(8,128)(2,1)S(1)} %down_join.1.refs_2_.refs_0_), channel_id=1, source_target_pairs={{0,4},{4,0},{1,5},{5,1},{2,6},{6,2},{3,7},{7,3},{8,12},{12,8},{9,1... | collective-permute-start | bytes 786440 | tf_op jit(solution)/shard_map/down_x_x1/ppermute | solution.py:782
  93.6 3.2 %collective-permute-start.34 = (bf16[160,512]{1,0:T(8,128)(2,1)S(1)}, bf16[160,512]{1,0:T(8,128)(2,1)S(1)}, u32[]{:S(2)}, u32[]{:S(2)}) collective-permute-start(bf16[160,512]{1,0:T(8,128)(2,1)S(1)} %get-tuple-element.146.refs_0_), channel_id=1, source_target_pairs={{0,4},{4,0},{1,5},{5,1},{2,6},{6,2},{3,7},{7,3},{8,12},{12,8},{9,1... | collective-permute-start | bytes 491528 | tf_op jit(solution)/shard_map/up_near_x1/ppermute | solution.py:782
  97.2 5.0 %collective-permute-done.31.refs_1_ = bf16[128,512]{1,0:T(8,128)(2,1)S(1)} collective-permute-done((bf16[128,512]{1,0:T(8,128)(2,1)S(1)}, bf16[128,512]{1,0:T(8,128)(2,1)S(1)}, u32[]{:S(2)}, u32[]{:S(2)}) %collective-permute-start.31) | collective-permute-done | bytes 131104 | tf_op jit(solution)/shard_map/att_near_z1/ppermute | solution.py:782
  103.0 2.1 %collective-permute-start.32 = (bf16[256,512]{1,0:T(8,128)(2,1)S(1)}, bf16[256,512]{1,0:T(8,128)(2,1)S(1)}, u32[]{:S(2)}, u32[]{:S(2)}) collective-permute-start(bf16[256,512]{1,0:T(8,128)(2,1)S(1)} %get-tuple-element.144.refs_0_), channel_id=1, source_target_pairs={{0,4},{4,0},{1,5},{5,1},{2,6},{6,2},{3,7},{7,3},{8,12},{12,8},{9,1... | collective-permute-start | bytes 786440 | tf_op jit(solution)/shard_map/att_x_x1/ppermute | solution.py:782
  105.1 1.1 collective-permute-start.36
  106.7 0.6 small_out.1
  107.4 1.5 %down_out.1 = (f32[1024,512]{1,0:T(8,128)}, f32[8,128]{1,0:T(8,128)S(1)}) custom-call(bf16[256,512]{1,0:T(8,128)(2,1)S(1)} %down_join.1.refs_2_.refs_0_, bf16[256,512]{1,0:T(8,128)(2,1)S(1)} %gate.17.refs_1_, bf16[256,512]{1,0:T(8,128)(2,1)S(1)} %collective-permute-done.38.refs_2_, bf16[256,512]{1,0:T(8,128)(2,1)S(1)} %collective-permute-done.39.refs_3_, ...), custom_call_target="tpu_custom_call" | custom-call | tf_op jit(solution)/shard_map/down_out/pallas_call | solution.py:39
  109.4 0.8 collective-permute-done.35.refs_0_
  110.2 3.4 %collective-permute-done.33.refs_0_ = bf16[64,512]{1,0:T(8,128)(2,1)S(1)} collective-permute-done((bf16[64,512]{1,0:T(8,128)(2,1)S(1)}, bf16[64,512]{1,0:T(8,128)(2,1)S(1)}, u32[]{:S(2)}, u32[]{:S(2)}) %collective-permute-start.33) | collective-permute-done | bytes 65568 | tf_op jit(solution)/shard_map/table_x/ppermute | solution.py:787
  114.2 1.7 %up_out.1 = (f32[512,1024]{1,0:T(8,128)}, f32[256,512]{1,0:T(8,128)}, f32[8,128]{1,0:T(8,128)S(1)}) custom-call(bf16[320,512]{1,0:T(8,128)(2,1)S(1)} %up_join.1.refs_1_.refs_0_, bf16[320,512]{1,0:T(8,128)(2,1)S(1)} %gate.19.refs_1_, bf16[320,512]{1,0:T(8,128)(2,1)S(1)} %collective-permute-done.44.refs_2_, ...), custom_call_target="tpu_custom_call" | custom-call | tf_op jit(solution)/shard_map/up_out/pallas_call | solution.py:39
  116.0 1.7 %attend_out.1 = (f32[3,512,256]{2,1,0:T(8,128)}, f32[512,512]{1,0:T(8,128)}) custom-call(bf16[256,512]{1,0:T(8,128)(2,1)S(1)} %get-tuple-element.144.refs_0_, bf16[256,512]{1,0:T(8,128)(2,1)S(1)} %gate.21.refs_4_.refs_1_, bf16[256,512]{1,0:T(8,128)(2,1)S(1)} %collective-permute-done.40.refs_2_, bf16[256,512]{1,0:T(8,128)(2,1)S(1)} %collective-permute-done.41.refs_3_, ...), custom_call_target="tpu_custom_call" | custom-call | tf_op jit(solution)/shard_map/attend_out/pallas_call | solution.py:39
  (117 shorter events, 9.6 us)
Async XLA Ops:
  3.0 7.6 %copy-start.2 = (bf16[512,3,256]{2,0,1:T(8,128)(2,1)S(1)}, bf16[512,3,256]{2,0,1:T(8,128)(2,1)}, u32[]{:S(2)}) copy-start(bf16[512,3,256]{2,0,1:T(8,128)(2,1)} %param.17) | copy-start | bytes 2359300
  3.1 7.6 %copy-start.4 = (bf16[512,512]{1,0:T(8,128)(2,1)S(1)}, bf16[512,512]{1,0:T(8,128)(2,1)}, u32[]{:S(2)}) copy-start(bf16[512,512]{1,0:T(8,128)(2,1)} %refs_1_.9) | copy-start | bytes 1572868
  3.1 10.8 %collective-permute-start = (bf16[272,512]{1,0:T(8,128)(2,1)}, bf16[272,512]{1,0:T(8,128)(2,1)S(1)}, u32[]{:S(2)}, u32[]{:S(2)}) collective-permute-start(bf16[272,512]{1,0:T(8,128)(2,1)} %pack_attend.1.refs_2_), channel_id=1, source_target_pairs={{0,1},{1,0},{2,3},{3,2},{4,5},{5,4},{6,7},{7,6},{8,9},{9,8},{10,11... | collective-permute-start | bytes 835592 | tf_op jit(solution)/shard_map/attend_y_mp1/ppermute | solution.py:782
  7.9 8.7 %collective-permute-start.3 = (bf16[128,512]{1,0:T(8,128)(2,1)}, bf16[128,512]{1,0:T(8,128)(2,1)S(1)}, u32[]{:S(2)}, u32[]{:S(2)}) collective-permute-start(bf16[128,512]{1,0:T(8,128)(2,1)} %get-tuple-element.88.refs_4_), channel_id=1, source_target_pairs={{0,1},{1,0},{2,3},{3,2},{4,5},{5,4},{6,7},{7,6},{8,9},{9,8},{10,11... | collective-permute-start | bytes 393224 | tf_op jit(solution)/shard_map/up_y_mp1/ppermute | solution.py:782
  8.1 13.6 %collective-permute-start.2 = (bf16[256,512]{1,0:T(8,128)(2,1)}, bf16[256,512]{1,0:T(8,128)(2,1)S(1)}, u32[]{:S(2)}, u32[]{:S(2)}) collective-permute-start(bf16[256,512]{1,0:T(8,128)(2,1)} %get-tuple-element.90), channel_id=1, source_target_pairs={{0,1},{1,0},{2,3},{3,2},{4,5},{5,4},{6,7},{7,6},{8,9},{9,8},{10,11... | collective-permute-start | bytes 786440 | tf_op jit(solution)/shard_map/down_y_mp1/ppermute | solution.py:782
  13.9 7.8 %collective-permute-start.1 = (bf16[272,512]{1,0:T(8,128)(2,1)S(1)}, bf16[272,512]{1,0:T(8,128)(2,1)S(1)}, u32[]{:S(2)}, u32[]{:S(2)}) collective-permute-start(bf16[272,512]{1,0:T(8,128)(2,1)S(1)} %gate.11.refs_1_.refs_3_), channel_id=1, source_target_pairs={{0,4},{4,0},{1,5},{5,1},{2,6},{6,2},{3,7},{7,3},{8,12},{12,8},{9,1... | collective-permute-start | bytes 835592 | tf_op jit(solution)/shard_map/attend_x_x1/ppermute | solution.py:782
  16.6 5.1 %collective-permute-start.4 = (bf16[128,512]{1,0:T(8,128)(2,1)S(1)}, bf16[128,512]{1,0:T(8,128)(2,1)S(1)}, u32[]{:S(2)}, u32[]{:S(2)}) collective-permute-start(bf16[128,512]{1,0:T(8,128)(2,1)S(1)} %gate.12.refs_0_.refs_2_), channel_id=1, source_target_pairs={{0,8},{8,0},{16,24},{24,16},{1,9},{9,1},{17,25},{25,17},{2,10},{10... | collective-permute-start | bytes 393224 | tf_op jit(solution)/shard_map/up_z_z1/ppermute | solution.py:782
  18.7 5.7 %collective-permute-start.5 = (bf16[272,512]{1,0:T(8,128)(2,1)S(1)}, bf16[272,512]{1,0:T(8,128)(2,1)S(1)}, u32[]{:S(2)}, u32[]{:S(2)}) collective-permute-start(bf16[272,512]{1,0:T(8,128)(2,1)S(1)} %gate.11.refs_1_.refs_3_), channel_id=1, source_target_pairs={{0,2},{2,0},{1,3},{3,1},{4,6},{6,4},{5,7},{7,5},{8,10},{10,8},{9,1... | collective-permute-start | bytes 835592 | tf_op jit(solution)/shard_map/attend_cy_core1/ppermute | solution.py:782
  21.8 4.1 %collective-permute-start.6 = (bf16[272,512]{1,0:T(8,128)(2,1)S(1)}, bf16[272,512]{1,0:T(8,128)(2,1)S(1)}, u32[]{:S(2)}, u32[]{:S(2)}) collective-permute-start(bf16[272,512]{1,0:T(8,128)(2,1)S(1)} %gate.14.refs_4_.refs_10_), channel_id=1, source_target_pairs={{0,2},{2,0},{1,3},{3,1},{4,6},{6,4},{5,7},{7,5},{8,10},{10,8},{9,1... | collective-permute-start | bytes 835592 | tf_op jit(solution)/shard_map/attend_cx_core1/ppermute | solution.py:782
  21.9 11.9 %collective-permute-start.11 = (bf16[256,512]{1,0:T(8,128)(2,1)S(1)}, bf16[256,512]{1,0:T(8,128)(2,1)S(1)}, u32[]{:S(2)}, u32[]{:S(2)}) collective-permute-start(bf16[256,512]{1,0:T(8,128)(2,1)S(1)} %gate.13.refs_1_.refs_8_), channel_id=1, source_target_pairs={{0,2},{2,0},{1,3},{3,1},{4,6},{6,4},{5,7},{7,5},{8,10},{10,8},{9,1... | collective-permute-start | bytes 786440 | tf_op jit(solution)/shard_map/down_cy_core1/ppermute | solution.py:782
  22.4 10.8 %collective-permute-start.10 = (bf16[256,512]{1,0:T(8,128)(2,1)S(1)}, bf16[256,512]{1,0:T(8,128)(2,1)S(1)}, u32[]{:S(2)}, u32[]{:S(2)}) collective-permute-start(bf16[256,512]{1,0:T(8,128)(2,1)S(1)} %gate.13.refs_1_.refs_8_), channel_id=1, source_target_pairs={{0,8},{8,0},{16,24},{24,16},{1,9},{9,1},{17,25},{25,17},{2,10},{10... | collective-permute-start | bytes 786440 | tf_op jit(solution)/shard_map/down_z_z1/ppermute | solution.py:782
  24.4 9.3 %collective-permute-start.8 = (bf16[256,512]{1,0:T(8,128)(2,1)S(1)}, bf16[256,512]{1,0:T(8,128)(2,1)S(1)}, u32[]{:S(2)}, u32[]{:S(2)}) collective-permute-start(bf16[256,512]{1,0:T(8,128)(2,1)S(1)} %up_pair.1.refs_1_.refs_4_), channel_id=1, source_target_pairs={{0,2},{2,0},{1,3},{3,1},{4,6},{6,4},{5,7},{7,5},{8,10},{10,8},{9,1... | collective-permute-start | bytes 786440 | tf_op jit(solution)/shard_map/up_cy_core1/ppermute | solution.py:782
  24.5 8.7 %collective-permute-start.7 = (bf16[256,512]{1,0:T(8,128)(2,1)S(1)}, bf16[256,512]{1,0:T(8,128)(2,1)S(1)}, u32[]{:S(2)}, u32[]{:S(2)}) collective-permute-start(bf16[256,512]{1,0:T(8,128)(2,1)S(1)} %up_pair.1.refs_1_.refs_4_), channel_id=1, source_target_pairs={{0,4},{4,0},{1,5},{5,1},{2,6},{6,2},{3,7},{7,3},{8,12},{12,8},{9,1... | collective-permute-start | bytes 786440 | tf_op jit(solution)/shard_map/up_x_x1/ppermute | solution.py:782
  33.2 1.6 %collective-permute-start.12 = (bf16[256,512]{1,0:T(8,128)(2,1)S(1)}, bf16[256,512]{1,0:T(8,128)(2,1)S(1)}, u32[]{:S(2)}, u32[]{:S(2)}) collective-permute-start(bf16[256,512]{1,0:T(8,128)(2,1)S(1)} %gate.16.refs_9_.refs_16_), channel_id=1, source_target_pairs={{0,2},{2,0},{1,3},{3,1},{4,6},{6,4},{5,7},{7,5},{8,10},{10,8},{9,1... | collective-permute-start | bytes 786440 | tf_op jit(solution)/shard_map/down_cz_core1/ppermute | solution.py:782
  33.3 1.9 %collective-permute-start.9 = (bf16[256,512]{1,0:T(8,128)(2,1)S(1)}, bf16[256,512]{1,0:T(8,128)(2,1)S(1)}, u32[]{:S(2)}, u32[]{:S(2)}) collective-permute-start(bf16[256,512]{1,0:T(8,128)(2,1)S(1)} %gate.15.refs_1_.refs_5_), channel_id=1, source_target_pairs={{0,2},{2,0},{1,3},{3,1},{4,6},{6,4},{5,7},{7,5},{8,10},{10,8},{9,1... | collective-permute-start | bytes 786440 | tf_op jit(solution)/shard_map/up_cx_core1/ppermute | solution.py:782
  39.2 5.6 %collective-permute-start.14 = (bf16[1024,512]{1,0:T(8,128)(2,1)S(1)}, bf16[1024,512]{1,0:T(8,128)(2,1)S(1)}, u32[]{:S(2)}, u32[]{:S(2)}) collective-permute-start(bf16[1024,512]{1,0:T(8,128)(2,1)S(1)} %get-tuple-element.116), channel_id=1, source_target_pairs={{0,2},{2,0},{1,3},{3,1},{4,6},{6,4},{5,7},{7,5},{8,10},{10,8},{9,1... | collective-permute-start | bytes 3145736 | tf_op jit(solution)/shard_map/down_recv_core1/ppermute | solution.py:782
  44.3 3.1 %collective-permute-start.13 = (bf16[1296,512]{1,0:T(8,128)(2,1)S(1)}, bf16[1296,512]{1,0:T(8,128)(2,1)S(1)}, u32[]{:S(2)}, u32[]{:S(2)}) collective-permute-start(bf16[1296,512]{1,0:T(8,128)(2,1)S(1)} %get-tuple-element.114), channel_id=1, source_target_pairs={{0,2},{2,0},{1,3},{3,1},{4,6},{6,4},{5,7},{7,5},{8,10},{10,8},{9,1... | collective-permute-start | bytes 3981320 | tf_op jit(solution)/shard_map/up_recv_core1/ppermute | solution.py:782
  44.9 14.0 %collective-permute-start.18 = (bf16[512,512]{1,0:T(8,128)(2,1)S(1)}, bf16[512,512]{1,0:T(8,128)(2,1)S(1)}, u32[]{:S(2)}, u32[]{:S(2)}) collective-permute-start(bf16[512,512]{1,0:T(8,128)(2,1)S(1)} %down_core.1.refs_2_), channel_id=1, source_target_pairs={{0,1},{1,0},{2,3},{3,2},{4,5},{5,4},{6,7},{7,6},{8,9},{9,8},{10,11... | collective-permute-start | bytes 1572872 | tf_op jit(solution)/shard_map/down_from_y_mp1/ppermute | solution.py:782
  47.8 17.4 %collective-permute-start.21 = (bf16[656,512]{1,0:T(8,128)(2,1)S(1)}, bf16[656,512]{1,0:T(8,128)(2,1)S(1)}, u32[]{:S(2)}, u32[]{:S(2)}) collective-permute-start(bf16[656,512]{1,0:T(8,128)(2,1)S(1)} %get-tuple-element.132), channel_id=1, source_target_pairs={{0,8},{8,0},{16,24},{24,16},{1,9},{9,1},{17,25},{25,17},{2,10},{10... | collective-permute-start | bytes 2015240 | tf_op jit(solution)/shard_map/up_from_z_z1/ppermute | solution.py:782
  55.3 5.4 %collective-permute-start.16 = (bf16[384,512]{1,0:T(8,128)(2,1)S(1)}, bf16[384,512]{1,0:T(8,128)(2,1)S(1)}, u32[]{:S(2)}, u32[]{:S(2)}) collective-permute-start(bf16[384,512]{1,0:T(8,128)(2,1)S(1)} %get-tuple-element.126), channel_id=1, source_target_pairs={{0,2},{2,0},{1,3},{3,1},{4,6},{6,4},{5,7},{7,5},{8,10},{10,8},{9,1... | collective-permute-start | bytes 1179656 | tf_op jit(solution)/shard_map/oth_recv_core1/ppermute | solution.py:782
  55.5 5.2 %collective-permute-start.17 = (bf16[256,512]{1,0:T(8,128)(2,1)S(1)}, bf16[256,512]{1,0:T(8,128)(2,1)S(1)}, u32[]{:S(2)}, u32[]{:S(2)}) collective-permute-start(bf16[256,512]{1,0:T(8,128)(2,1)S(1)} %get-tuple-element.127), channel_id=1, source_target_pairs={{0,2},{2,0},{1,3},{3,1},{4,6},{6,4},{5,7},{7,5},{8,10},{10,8},{9,1... | collective-permute-start | bytes 786440 | tf_op jit(solution)/shard_map/tab_recv_core1/ppermute | solution.py:782
  56.6 18.2 %collective-permute-start.15 = (bf16[384,512]{1,0:T(8,128)(2,1)S(1)}, bf16[384,512]{1,0:T(8,128)(2,1)S(1)}, u32[]{:S(2)}, u32[]{:S(2)}) collective-permute-start(bf16[384,512]{1,0:T(8,128)(2,1)S(1)} %get-tuple-element.124), channel_id=1, source_target_pairs={{0,2},{2,0},{1,3},{3,1},{4,6},{6,4},{5,7},{7,5},{8,10},{10,8},{9,1... | collective-permute-start | bytes 1179656 | tf_op jit(solution)/shard_map/own_recv_core1/ppermute | solution.py:782
  59.1 7.8 %collective-permute-start.20 = (bf16[256,512]{1,0:T(8,128)(2,1)S(1)}, bf16[256,512]{1,0:T(8,128)(2,1)S(1)}, u32[]{:S(2)}, u32[]{:S(2)}) collective-permute-start(bf16[256,512]{1,0:T(8,128)(2,1)S(1)} %get-tuple-element.131), channel_id=1, source_target_pairs={{0,4},{4,0},{1,5},{5,1},{2,6},{6,2},{3,7},{7,3},{8,12},{12,8},{9,1... | collective-permute-start | bytes 786440 | tf_op jit(solution)/shard_map/down_from_x_x1/ppermute | solution.py:782
  60.8 14.0 %collective-permute-start.19 = (bf16[512,512]{1,0:T(8,128)(2,1)S(1)}, bf16[512,512]{1,0:T(8,128)(2,1)S(1)}, u32[]{:S(2)}, u32[]{:S(2)}) collective-permute-start(bf16[512,512]{1,0:T(8,128)(2,1)S(1)} %get-tuple-element.129), channel_id=1, source_target_pairs={{0,1},{1,0},{2,3},{3,2},{4,5},{5,4},{6,7},{7,6},{8,9},{9,8},{10,11... | collective-permute-start | bytes 1572872 | tf_op jit(solution)/shard_map/att_from_y_mp1/ppermute | solution.py:782
  65.3 11.6 %collective-permute-start.25 = (bf16[336,512]{1,0:T(8,128)(2,1)S(1)}, bf16[336,512]{1,0:T(8,128)(2,1)S(1)}, u32[]{:S(2)}, u32[]{:S(2)}) collective-permute-start(bf16[336,512]{1,0:T(8,128)(2,1)S(1)} %get-tuple-element.138), channel_id=1, source_target_pairs={{0,4},{4,0},{1,5},{5,1},{2,6},{6,2},{3,7},{7,3},{8,12},{12,8},{9,1... | collective-permute-start | bytes 1032200 | tf_op jit(solution)/shard_map/up_from_x_x1/ppermute | solution.py:782
  67.0 5.0 %collective-permute-start.22 = (bf16[128,512]{1,0:T(8,128)(2,1)S(1)}, bf16[128,512]{1,0:T(8,128)(2,1)S(1)}, u32[]{:S(2)}, u32[]{:S(2)}) collective-permute-start(bf16[128,512]{1,0:T(8,128)(2,1)S(1)} %get-tuple-element.135), channel_id=1, source_target_pairs={{0,8},{8,0},{16,24},{24,16},{1,9},{9,1},{17,25},{25,17},{2,10},{10... | collective-permute-start | bytes 393224 | tf_op jit(solution)/shard_map/down_from_z_z1/ppermute | solution.py:782
  72.0 7.5 %collective-permute-start.24 = (bf16[128,512]{1,0:T(8,128)(2,1)S(1)}, bf16[128,512]{1,0:T(8,128)(2,1)S(1)}, u32[]{:S(2)}, u32[]{:S(2)}) collective-permute-start(bf16[128,512]{1,0:T(8,128)(2,1)S(1)} %down_z.1.refs_4_.refs_0_), channel_id=1, source_target_pairs={{0,16},{8,24},{16,0},{24,8},{1,17},{9,25},{17,1},{25,9},{2,18},{10... | collective-permute-start | bytes 393224 | tf_op jit(solution)/shard_map/down_far_z2/ppermute | solution.py:782
  75.0 6.7 %collective-permute-start.23 = (bf16[256,512]{1,0:T(8,128)(2,1)S(1)}, bf16[256,512]{1,0:T(8,128)(2,1)S(1)}, u32[]{:S(2)}, u32[]{:S(2)}) collective-permute-start(bf16[256,512]{1,0:T(8,128)(2,1)S(1)} %get-tuple-element.137), channel_id=1, source_target_pairs={{0,4},{4,0},{1,5},{5,1},{2,6},{6,2},{3,7},{7,3},{8,12},{12,8},{9,1... | collective-permute-start | bytes 786440 | tf_op jit(solution)/shard_map/att_from_x_x1/ppermute | solution.py:782
  77.1 5.6 %collective-permute-start.28 = (bf16[176,512]{1,0:T(8,128)(2,1)S(1)}, bf16[176,512]{1,0:T(8,128)(2,1)S(1)}, u32[]{:S(2)}, u32[]{:S(2)}) collective-permute-start(bf16[176,512]{1,0:T(8,128)(2,1)S(1)} %get-tuple-element.142), channel_id=1, source_target_pairs={{0,1},{1,0},{2,3},{3,2},{4,5},{5,4},{6,7},{7,6},{8,9},{9,8},{10,11... | collective-permute-start | bytes 540680 | tf_op jit(solution)/shard_map/up_from_y_mp1/ppermute | solution.py:782
  79.6 7.7 %collective-permute-start.27 = (bf16[128,512]{1,0:T(8,128)(2,1)S(1)}, bf16[128,512]{1,0:T(8,128)(2,1)S(1)}, u32[]{:S(2)}, u32[]{:S(2)}) collective-permute-start(bf16[128,512]{1,0:T(8,128)(2,1)S(1)} %down_far.1.refs_2_.refs_0_), channel_id=1, source_target_pairs={{0,8},{8,0},{16,24},{24,16},{1,9},{9,1},{17,25},{25,17},{2,10},{10... | collective-permute-start | bytes 393224 | tf_op jit(solution)/shard_map/down_near_z1/ppermute | solution.py:782
  81.7 8.2 %collective-permute-start.26 = (bf16[128,512]{1,0:T(8,128)(2,1)S(1)}, bf16[128,512]{1,0:T(8,128)(2,1)S(1)}, u32[]{:S(2)}, u32[]{:S(2)}) collective-permute-start(bf16[128,512]{1,0:T(8,128)(2,1)S(1)} %get-tuple-element.141), channel_id=1, source_target_pairs={{0,8},{8,0},{16,24},{24,16},{1,9},{9,1},{17,25},{25,17},{2,10},{10... | collective-permute-start | bytes 393224 | tf_op jit(solution)/shard_map/att_from_z_z1/ppermute | solution.py:782
  82.7 10.9 %collective-permute-start.30 = (bf16[176,512]{1,0:T(8,128)(2,1)S(1)}, bf16[176,512]{1,0:T(8,128)(2,1)S(1)}, u32[]{:S(2)}, u32[]{:S(2)}) collective-permute-start(bf16[176,512]{1,0:T(8,128)(2,1)S(1)} %up_mp.1.refs_2_.refs_0_), channel_id=1, source_target_pairs={{0,16},{8,24},{16,0},{24,8},{1,17},{9,25},{17,1},{25,9},{2,18},{10... | collective-permute-start | bytes 540680 | tf_op jit(solution)/shard_map/up_far_z2/ppermute | solution.py:782
  90.0 7.2 %collective-permute-start.29 = (bf16[128,512]{1,0:T(8,128)(2,1)S(1)}, bf16[128,512]{1,0:T(8,128)(2,1)S(1)}, u32[]{:S(2)}, u32[]{:S(2)}) collective-permute-start(bf16[128,512]{1,0:T(8,128)(2,1)S(1)} %attend_z.1.refs_2_.refs_0_), channel_id=1, source_target_pairs={{0,16},{8,24},{16,0},{24,8},{1,17},{9,25},{17,1},{25,9},{2,18},{10... | collective-permute-start | bytes 393224 | tf_op jit(solution)/shard_map/att_far_z2/ppermute | solution.py:782
  90.0 12.5 %collective-permute-start.37 = (bf16[256,512]{1,0:T(8,128)(2,1)S(1)}, bf16[256,512]{1,0:T(8,128)(2,1)S(1)}, u32[]{:S(2)}, u32[]{:S(2)}) collective-permute-start(bf16[256,512]{1,0:T(8,128)(2,1)S(1)} %down_join.1.refs_2_.refs_0_), channel_id=1, source_target_pairs={{0,4},{4,0},{1,5},{5,1},{2,6},{6,2},{3,7},{7,3},{8,12},{12,8},{9,1... | collective-permute-start | bytes 786440 | tf_op jit(solution)/shard_map/down_x_x1/ppermute | solution.py:782
  93.6 8.6 %collective-permute-start.34 = (bf16[160,512]{1,0:T(8,128)(2,1)S(1)}, bf16[160,512]{1,0:T(8,128)(2,1)S(1)}, u32[]{:S(2)}, u32[]{:S(2)}) collective-permute-start(bf16[160,512]{1,0:T(8,128)(2,1)S(1)} %get-tuple-element.146.refs_0_), channel_id=1, source_target_pairs={{0,4},{4,0},{1,5},{5,1},{2,6},{6,2},{3,7},{7,3},{8,12},{12,8},{9,1... | collective-permute-start | bytes 491528 | tf_op jit(solution)/shard_map/up_near_x1/ppermute | solution.py:782
  97.2 5.0 %collective-permute-start.31 = (bf16[128,512]{1,0:T(8,128)(2,1)S(1)}, bf16[128,512]{1,0:T(8,128)(2,1)S(1)}, u32[]{:S(2)}, u32[]{:S(2)}) collective-permute-start(bf16[128,512]{1,0:T(8,128)(2,1)S(1)} %attend_far.1.refs_0_.refs_2_), channel_id=1, source_target_pairs={{0,8},{8,0},{16,24},{24,16},{1,9},{9,1},{17,25},{25,17},{2,10},{10... | collective-permute-start | bytes 393224 | tf_op jit(solution)/shard_map/att_near_z1/ppermute | solution.py:782
  102.3 7.9 %collective-permute-start.35 = (bf16[320,512]{1,0:T(8,128)(2,1)S(1)}, bf16[320,512]{1,0:T(8,128)(2,1)S(1)}, u32[]{:S(2)}, u32[]{:S(2)}) collective-permute-start(bf16[320,512]{1,0:T(8,128)(2,1)S(1)} %up_join.1.refs_1_.refs_0_), channel_id=1, source_target_pairs={{0,8},{8,0},{16,24},{24,16},{1,9},{9,1},{17,25},{25,17},{2,10},{10... | collective-permute-start | bytes 983048 | tf_op jit(solution)/shard_map/up_last_z1/ppermute | solution.py:782
  102.5 3.7 %collective-permute-start.38 = (bf16[256,512]{1,0:T(8,128)(2,1)S(1)}, bf16[256,512]{1,0:T(8,128)(2,1)S(1)}, u32[]{:S(2)}, u32[]{:S(2)}) collective-permute-start(bf16[256,512]{1,0:T(8,128)(2,1)S(1)} %down_join.1.refs_2_.refs_0_), channel_id=1, source_target_pairs={{0,2},{2,0},{1,3},{3,1},{4,6},{6,4},{5,7},{7,5},{8,10},{10,8},{9,1... | collective-permute-start | bytes 786440 | tf_op jit(solution)/shard_map/down_core_core1/ppermute | solution.py:782
  102.5 4.8 %collective-permute-start.39 = (bf16[256,512]{1,0:T(8,128)(2,1)S(1)}, bf16[256,512]{1,0:T(8,128)(2,1)S(1)}, u32[]{:S(2)}, u32[]{:S(2)}) collective-permute-start(bf16[256,512]{1,0:T(8,128)(2,1)S(1)} %gate.17.refs_1_), channel_id=1, source_target_pairs={{0,2},{2,0},{1,3},{3,1},{4,6},{6,4},{5,7},{7,5},{8,10},{10,8},{9,1... | collective-permute-start | bytes 786440 | tf_op jit(solution)/shard_map/down_core_x_core1/ppermute | solution.py:782
  103.0 10.6 %collective-permute-start.32 = (bf16[256,512]{1,0:T(8,128)(2,1)S(1)}, bf16[256,512]{1,0:T(8,128)(2,1)S(1)}, u32[]{:S(2)}, u32[]{:S(2)}) collective-permute-start(bf16[256,512]{1,0:T(8,128)(2,1)S(1)} %get-tuple-element.144.refs_0_), channel_id=1, source_target_pairs={{0,4},{4,0},{1,5},{5,1},{2,6},{6,2},{3,7},{7,3},{8,12},{12,8},{9,1... | collective-permute-start | bytes 786440 | tf_op jit(solution)/shard_map/att_x_x1/ppermute | solution.py:782
  105.1 4.3 %collective-permute-start.36 = (bf16[64,512]{1,0:T(8,128)(2,1)S(1)}, bf16[64,512]{1,0:T(8,128)(2,1)S(1)}, u32[]{:S(2)}, u32[]{:S(2)}) collective-permute-start(bf16[64,512]{1,0:T(8,128)(2,1)S(1)} %get-tuple-element.145.refs_2_), channel_id=1, source_target_pairs={{0,1},{1,0},{2,3},{3,2},{4,5},{5,4},{6,7},{7,6},{8,9},{9,8},{10,11... | collective-permute-start | bytes 196616 | tf_op jit(solution)/shard_map/table_y_mp1/ppermute | solution.py:782
  106.2 7.4 %collective-permute-start.33 = (bf16[64,512]{1,0:T(8,128)(2,1)S(1)}, bf16[64,512]{1,0:T(8,128)(2,1)S(1)}, u32[]{:S(2)}, u32[]{:S(2)}) collective-permute-start(bf16[64,512]{1,0:T(8,128)(2,1)S(1)} %get-tuple-element.145.refs_2_), channel_id=1, source_target_pairs={{0,5},{1,4},{4,1},{5,0},{2,7},{3,6},{6,3},{7,2},{8,13},{9,12},{12,... | collective-permute-start | bytes 196616 | tf_op jit(solution)/shard_map/table_x/ppermute | solution.py:787
  107.3 8.7 %collective-permute-start.40 = (bf16[256,512]{1,0:T(8,128)(2,1)S(1)}, bf16[256,512]{1,0:T(8,128)(2,1)S(1)}, u32[]{:S(2)}, u32[]{:S(2)}) collective-permute-start(bf16[256,512]{1,0:T(8,128)(2,1)S(1)} %get-tuple-element.144.refs_0_), channel_id=1, source_target_pairs={{0,2},{2,0},{1,3},{3,1},{4,6},{6,4},{5,7},{7,5},{8,10},{10,8},{9,1... | collective-permute-start | bytes 786440 | tf_op jit(solution)/shard_map/att_core_core1/ppermute | solution.py:782
  109.4 4.8 %collective-permute-start.44 = (bf16[320,512]{1,0:T(8,128)(2,1)S(1)}, bf16[320,512]{1,0:T(8,128)(2,1)S(1)}, u32[]{:S(2)}, u32[]{:S(2)}) collective-permute-start(bf16[320,512]{1,0:T(8,128)(2,1)S(1)} %up_join.1.refs_1_.refs_0_), channel_id=1, source_target_pairs={{0,2},{2,0},{1,3},{3,1},{4,6},{6,4},{5,7},{7,5},{8,10},{10,8},{9,1... | collective-permute-start | bytes 983048 | tf_op jit(solution)/shard_map/up_core_core1/ppermute | solution.py:782
  110.2 4.0 %collective-permute-start.45 = (bf16[320,512]{1,0:T(8,128)(2,1)S(1)}, bf16[320,512]{1,0:T(8,128)(2,1)S(1)}, u32[]{:S(2)}, u32[]{:S(2)}) collective-permute-start(bf16[320,512]{1,0:T(8,128)(2,1)S(1)} %gate.19.refs_1_), channel_id=1, source_target_pairs={{0,2},{2,0},{1,3},{3,1},{4,6},{6,4},{5,7},{7,5},{8,10},{10,8},{9,1... | collective-permute-start | bytes 983048 | tf_op jit(solution)/shard_map/up_core_x_core1/ppermute | solution.py:782
  113.6 2.4 %collective-permute-start.41 = (bf16[256,512]{1,0:T(8,128)(2,1)S(1)}, bf16[256,512]{1,0:T(8,128)(2,1)S(1)}, u32[]{:S(2)}, u32[]{:S(2)}) collective-permute-start(bf16[256,512]{1,0:T(8,128)(2,1)S(1)} %gate.21.refs_4_.refs_1_), channel_id=1, source_target_pairs={{0,2},{2,0},{1,3},{3,1},{4,6},{6,4},{5,7},{7,5},{8,10},{10,8},{9,1... | collective-permute-start | bytes 786440 | tf_op jit(solution)/shard_map/att_core_x_core1/ppermute | solution.py:782
  113.6 2.3 %collective-permute-start.42 = (bf16[64,512]{1,0:T(8,128)(2,1)S(1)}, bf16[64,512]{1,0:T(8,128)(2,1)S(1)}, u32[]{:S(2)}, u32[]{:S(2)}) collective-permute-start(bf16[64,512]{1,0:T(8,128)(2,1)S(1)} %gate.18.refs_1_.refs_4_), channel_id=1, source_target_pairs={{0,2},{2,0},{1,3},{3,1},{4,6},{6,4},{5,7},{7,5},{8,10},{10,8},{9,1... | collective-permute-start | bytes 196616 | tf_op jit(solution)/shard_map/table_core_core1/ppermute | solution.py:782
  114.2 1.8 %collective-permute-start.43 = (bf16[64,512]{1,0:T(8,128)(2,1)S(1)}, bf16[64,512]{1,0:T(8,128)(2,1)S(1)}, u32[]{:S(2)}, u32[]{:S(2)}) collective-permute-start(bf16[64,512]{1,0:T(8,128)(2,1)S(1)} %gate.20.refs_1_.refs_5_), channel_id=1, source_target_pairs={{0,2},{2,0},{1,3},{3,1},{4,6},{6,4},{5,7},{7,5},{8,10},{10,8},{9,1... | collective-permute-start | bytes 196616 | tf_op jit(solution)/shard_map/table_core_x_core1/ppermute | solution.py:782
  (13 other events, 60.5 us)

commit v6 on v5

--- a/solution.py
+++ b/solution.py
@@ -256,12 +256,14 @@
     return pl.ds(pl.multiple_of(index * size, size), size)
 
 
-def copy_all(pairs, sems):
+def copy_all(pairs, sems, meanwhile=None):
     copies = [
         pltpu.make_async_copy(src, dst, sems.at[i]) for i, (src, dst) in enumerate(pairs)
     ]
     for copy in copies:
         copy.start()
+    if meanwhile is not None:
+        meanwhile()
     for copy in copies:
         copy.wait()
 
@@ -269,11 +271,14 @@
 def pack_attend_kernel(bias_ref, qkv_ref, out_ref, send_ref, sems):
     _, width, half = qkv_ref.shape
     depth, mine = width // 4, quarter(place("x"))
-    for i in range(EXTRA):
-        index = i if (i + 1) * width <= bias_ref.shape[0] else 0
-        send_ref[2 * depth + i : 2 * depth + i + 1, :] = row(bias_ref, index * width, width).astype(
-            BF16
-        )
+
+    def write_bias():
+        used = bias_ref.shape[0] // width
+        send_ref[2 * depth :, :] = jnp.zeros((EXTRA, width), BF16)
+        for i in range(used):
+            at = 2 * depth + i
+            send_ref[at : at + 1, :] = row(bias_ref, i * width, width).astype(BF16)
+
     middle = depth + depth // 2
     low, high = pl.ds(0, half), pl.ds(half, half)
     upper, lower = part(mine * 2, depth // 2), part(mine * 2 + 1, depth // 2)
@@ -286,6 +291,7 @@
             (out_ref.at[part(mine, depth // 2), :], send_ref.at[pl.ds(middle, depth // 2), :]),
         ],
         sems,
+        write_bias,
     )
 
 

time: 118 us -> 118 us (level)
  no operation moved by 1% of the time
where the time goes in v6:
time: 118 us
  starting transfers between devices  42.6 us (36%)
  waiting for transfers between devices  36.6 us (31%)
  Pallas kernels  35.7 us (30%)
  between operations  1.97 us (2%)
    ppermute x45, starting transfers between devices, swap(): return lax.ppermute(value, axis, pairs)  42.1 us
    pallas_call x32, Pallas kernels, call(): pl.pallas_call(flat_kernel, out_shape=[jax.ShapeDtypeStruct(out, BF16) if...  35.6 us
    ppermute x45, waiting for transfers between devices, swap(): return lax.ppermute(value, axis, pairs)  33.2 us
    ppermute x1, waiting for transfers between devices, swap_corner(): return lax.ppermute(value, ('x', 'mp'), [(0, 3), (1, 2), (2, 1), (3, 0)])  3.43 us
  transfers between devices with their start and end apart: 46, of which 20 were waited for; matrix products, arithmetic and copies ran while one was open for 0% of the time, Pallas kernels for 23%

profile of v6, /device:TPU:0, one launch (start us, length us, event | category | flops | bytes accessed | tf_op | source)
XLA Modules:
  0.0 117.8 jit_solution(12658296947342876582)
XLA Ops:
  0.6 2.4 %pack_attend.1.refs_2_ = bf16[272,512]{1,0:T(8,128)(2,1)} custom-call(bf16[1024]{0:T(1024)(128)(2,1)} %refs_3_.1, bf16[3,512,256]{2,1,0:T(8,128)(2,1)} %bitcast.2, bf16[256,512]{1,0:T(8,128)(2,1)} %refs_5_.5), custom_call_target="tpu_custom_call" | custom-call | flops 1000000000 | tf_op jit(solution)/shard_map/pack_attend/pallas_call | solution.py:39
  3.1 3.0 %collective-permute-start = (bf16[272,512]{1,0:T(8,128)(2,1)}, bf16[272,512]{1,0:T(8,128)(2,1)S(1)}, u32[]{:S(2)}, u32[]{:S(2)}) collective-permute-start(bf16[272,512]{1,0:T(8,128)(2,1)} %pack_attend.1.refs_2_), channel_id=1, source_target_pairs={{0,1},{1,0},{2,3},{3,2},{4,5},{5,4},{6,7},{7,6},{8,9},{9,8},{10,11... | collective-permute-start | bytes 835592 | tf_op jit(solution)/shard_map/attend_y_mp1/ppermute | solution.py:788
  6.1 1.8 %pack_ffn.1 = (bf16[128,512]{1,0:T(8,128)(2,1)}, bf16[256,512]{1,0:T(8,128)(2,1)}) custom-call(bf16[512,1024]{1,0:T(8,128)(2,1)} %refs_5_.4, bf16[1024,512]{1,0:T(8,128)(2,1)} %refs_7_.1, bf16[272,512]{1,0:T(8,128)(2,1)} %pack_attend.1.refs_2_), custom_call_target="tpu_custom_call" | custom-call | flops 1000000000 | tf_op jit(solution)/shard_map/pack_ffn/pallas_call | solution.py:39
  8.1 1.9 %collective-permute-start.2 = (bf16[256,512]{1,0:T(8,128)(2,1)}, bf16[256,512]{1,0:T(8,128)(2,1)S(1)}, u32[]{:S(2)}, u32[]{:S(2)}) collective-permute-start(bf16[256,512]{1,0:T(8,128)(2,1)} %get-tuple-element.90), channel_id=1, source_target_pairs={{0,1},{1,0},{2,3},{3,2},{4,5},{5,4},{6,7},{7,6},{8,9},{9,8},{10,11... | collective-permute-start | bytes 786440 | tf_op jit(solution)/shard_map/down_y_mp1/ppermute | solution.py:788
  10.7 0.9 copy-done.7
  11.6 2.3 %attend_first.1 = (bf16[3,512,256]{2,1,0:T(8,128)(2,1)S(1)}, bf16[2,1024,256]{2,1,0:T(8,128)(2,1)S(1)}, bf16[2,512,256]{2,1,0:T(8,128)(2,1)S(1)}, bf16[512,256]{1,0:T(8,128)(2,1)S(1)}) custom-call(s32[1]{0:T(128)S(6)} %copy.51.refs_0_, bf16[512,512]{1,0:T(8,128)(2,1)S(1)} %copy-done.4, bf16[512,512]{1,0:T(8,128)(2,1)S(1)} %copy-done.5, ...), custom_call_target="tpu_custom_call" | custom-call | flops 3000000000 | tf_op jit(solution)/shard_map/attend_first/pallas_call | solution.py:39
  13.9 1.9 %collective-permute-start.1 = (bf16[272,512]{1,0:T(8,128)(2,1)S(1)}, bf16[272,512]{1,0:T(8,128)(2,1)S(1)}, u32[]{:S(2)}, u32[]{:S(2)}) collective-permute-start(bf16[272,512]{1,0:T(8,128)(2,1)S(1)} %gate.11.refs_1_.refs_3_), channel_id=1, source_target_pairs={{0,4},{4,0},{1,5},{5,1},{2,6},{6,2},{3,7},{7,3},{8,12},{12,8},{9,1... | collective-permute-start | bytes 835592 | tf_op jit(solution)/shard_map/attend_x_x1/ppermute | solution.py:788
  15.8 0.8 collective-permute-done.3.refs_0_
  16.6 2.1 %collective-permute-start.4 = (bf16[128,512]{1,0:T(8,128)(2,1)S(1)}, bf16[128,512]{1,0:T(8,128)(2,1)S(1)}, u32[]{:S(2)}, u32[]{:S(2)}) collective-permute-start(bf16[128,512]{1,0:T(8,128)(2,1)S(1)} %gate.12.refs_0_.refs_2_), channel_id=1, source_target_pairs={{0,8},{8,0},{16,24},{24,16},{1,9},{9,1},{17,25},{25,17},{2,10},{10... | collective-permute-start | bytes 393224 | tf_op jit(solution)/shard_map/up_z_z1/ppermute | solution.py:788
  18.7 2.9 %collective-permute-done.4.refs_1_ = bf16[128,512]{1,0:T(8,128)(2,1)S(1)} collective-permute-done((bf16[128,512]{1,0:T(8,128)(2,1)S(1)}, bf16[128,512]{1,0:T(8,128)(2,1)S(1)}, u32[]{:S(2)}, u32[]{:S(2)}) %collective-permute-start.4) | collective-permute-done | bytes 131104 | tf_op jit(solution)/shard_map/up_z_z1/ppermute | solution.py:788
  22.4 2.0 %collective-permute-start.10 = (bf16[256,512]{1,0:T(8,128)(2,1)S(1)}, bf16[256,512]{1,0:T(8,128)(2,1)S(1)}, u32[]{:S(2)}, u32[]{:S(2)}) collective-permute-start(bf16[256,512]{1,0:T(8,128)(2,1)S(1)} %gate.13.refs_1_.refs_8_), channel_id=1, source_target_pairs={{0,8},{8,0},{16,24},{24,16},{1,9},{9,1},{17,25},{25,17},{2,10},{10... | collective-permute-start | bytes 786440 | tf_op jit(solution)/shard_map/down_z_z1/ppermute | solution.py:788
  24.4 1.5 %collective-permute-start.7 = (bf16[256,512]{1,0:T(8,128)(2,1)S(1)}, bf16[256,512]{1,0:T(8,128)(2,1)S(1)}, u32[]{:S(2)}, u32[]{:S(2)}) collective-permute-start(bf16[256,512]{1,0:T(8,128)(2,1)S(1)} %up_pair.1.refs_1_.refs_4_), channel_id=1, source_target_pairs={{0,4},{4,0},{1,5},{5,1},{2,6},{6,2},{3,7},{7,3},{8,12},{12,8},{9,1... | collective-permute-start | bytes 786440 | tf_op jit(solution)/shard_map/up_x_x1/ppermute | solution.py:788
  25.9 2.9 %attend_second.1 = (bf16[3,512,256]{2,1,0:T(8,128)(2,1)S(1)}, bf16[2,1024,256]{2,1,0:T(8,128)(2,1)S(1)}, bf16[2,512,256]{2,1,0:T(8,128)(2,1)S(1)}, bf16[512,256]...) custom-call(s32[1]{0:T(128)S(6)} %copy.51.refs_0_, ...), custom_call_target="tpu_custom_call" | custom-call | flops 5000000000 | tf_op jit(solution)/shard_map/attend_second/pallas_call | solution.py:39
  28.9 2.2 %ffn_own.1 = (bf16[512,512]{1,0:T(8,128)(2,1)S(1)}, bf16[512,1024]{1,0:T(8,128)(2,1)S(1)}, bf16[512,1024]{1,0:T(8,128)(2,1)S(1)}, f32[512,512]{1,0:T(8,128)S(1)}) custom-call(f32[512,512]{1,0:T(8,128)S(1)} %get-tuple-element.91.refs_0_, bf16[512,1024]{1,0:T(8,128)(2,1)S(1)} %copy-done, bf16[1024,512]{1,0:T(8,128)(2,1)S(1)} %copy-done.1, ...), custom_call_target="tpu_custom_call" | custom-call | flops 4000000000 | tf_op jit(solution)/shard_map/ffn_own/pallas_call | solution.py:39
  31.1 2.1 %collective-permute-done.7.refs_0_ = bf16[256,512]{1,0:T(8,128)(2,1)S(1)} collective-permute-done((bf16[256,512]{1,0:T(8,128)(2,1)S(1)}, bf16[256,512]{1,0:T(8,128)(2,1)S(1)}, u32[]{:S(2)}, u32[]{:S(2)}) %collective-permute-start.7) | collective-permute-done | bytes 262176 | tf_op jit(solution)/shard_map/up_x_x1/ppermute | solution.py:788
  33.8 1.0 collective-permute-done.12.refs_11_
  35.2 4.0 %ffn_other.1 = (bf16[512,512]{1,0:T(8,128)(2,1)}, bf16[1024,512]{1,0:T(8,128)(2,1)S(1)}, bf16[1024,512]{1,0:T(8,128)(2,1)S(1)}, bf16[512,1024]{1,0:T(8,128)(2,1)...) custom-call(bf16[512,512]{1,0:T(8,128)(2,1)S(1)} %copy-done.3, ...), custom_call_target="tpu_custom_call" | custom-call | flops 6000000000 | tf_op jit(solution)/shard_map/ffn_other/pallas_call | solution.py:39
  39.4 4.9 %ffn_back.1 = (bf16[1296,512]{1,0:T(8,128)(2,1)S(1)}, bf16[1296,512]{1,0:T(8,128)(2,1)S(1)}, f32[16,512]{1,0:T(8,128)S(1)}, f32[512,512]{1,0:T(8,128)S(1)}) custom-call(f32[512,512]{1,0:T(8,128)S(1)} %get-tuple-element.91.refs_0_, f32[512,512]{1,0:T(8,128)S(1)} %get-tuple-element.97.refs_1_, bf16[512,512]{1,0:T(8,128)(2,1)S(1)} %get-tuple-element.93.refs_1_.refs_2_, ...), custom_call_target="tpu_custom_call" | custom-call | flops 6000000000 | tf_op jit(solution)/shard_map/ffn_back/pallas_call | solution.py:39
  44.9 1.6 %collective-permute-start.18 = (bf16[512,512]{1,0:T(8,128)(2,1)S(1)}, bf16[512,512]{1,0:T(8,128)(2,1)S(1)}, u32[]{:S(2)}, u32[]{:S(2)}) collective-permute-start(bf16[512,512]{1,0:T(8,128)(2,1)S(1)} %down_core.1.refs_2_), channel_id=1, source_target_pairs={{0,1},{1,0},{2,3},{3,2},{4,5},{5,4},{6,7},{7,6},{8,9},{9,8},{10,11... | collective-permute-start | bytes 1572872 | tf_op jit(solution)/shard_map/down_from_y_mp1/ppermute | solution.py:788
  46.5 1.0 collective-permute-done.13.refs_1_
  48.0 7.3 %attend_back.1 = (bf16[384,512]{1,0:T(8,128)(2,1)S(1)}, bf16[384,512]{1,0:T(8,128)(2,1)S(1)}, bf16[256,512]{1,0:T(8,128)(2,1)S(1)}, bf16[256,512]{1,0:T(8,128)(2...) custom-call(s32[1]{0:T(128)S(6)} %copy.51.refs_0_, ...), custom_call_target="tpu_custom_call" | custom-call | flops 12999999488 | tf_op jit(solution)/shard_map/attend_back/pallas_call | solution.py:39
  55.8 0.7 project_back.1
  56.8 2.1 %collective-permute-done.18.refs_2_ = bf16[512,512]{1,0:T(8,128)(2,1)S(1)} collective-permute-done((bf16[512,512]{1,0:T(8,128)(2,1)S(1)}, bf16[512,512]{1,0:T(8,128)(2,1)S(1)}, u32[]{:S(2)}, u32[]{:S(2)}) %collective-permute-start.18) | collective-permute-done | bytes 524320 | tf_op jit(solution)/shard_map/down_from_y_mp1/ppermute | solution.py:788
  59.1 1.6 %collective-permute-start.20 = (bf16[256,512]{1,0:T(8,128)(2,1)S(1)}, bf16[256,512]{1,0:T(8,128)(2,1)S(1)}, u32[]{:S(2)}, u32[]{:S(2)}) collective-permute-start(bf16[256,512]{1,0:T(8,128)(2,1)S(1)} %get-tuple-element.131), channel_id=1, source_target_pairs={{0,4},{4,0},{1,5},{5,1},{2,6},{6,2},{3,7},{7,3},{8,12},{12,8},{9,1... | collective-permute-start | bytes 786440 | tf_op jit(solution)/shard_map/down_from_x_x1/ppermute | solution.py:788
  60.8 1.6 %collective-permute-start.19 = (bf16[512,512]{1,0:T(8,128)(2,1)S(1)}, bf16[512,512]{1,0:T(8,128)(2,1)S(1)}, u32[]{:S(2)}, u32[]{:S(2)}) collective-permute-start(bf16[512,512]{1,0:T(8,128)(2,1)S(1)} %get-tuple-element.129), channel_id=1, source_target_pairs={{0,1},{1,0},{2,3},{3,2},{4,5},{5,4},{6,7},{7,6},{8,9},{9,8},{10,11... | collective-permute-start | bytes 1572872 | tf_op jit(solution)/shard_map/att_from_y_mp1/ppermute | solution.py:788
  62.4 2.8 %collective-permute-done.21.refs_1_ = bf16[656,512]{1,0:T(8,128)(2,1)S(1)} collective-permute-done((bf16[656,512]{1,0:T(8,128)(2,1)S(1)}, bf16[656,512]{1,0:T(8,128)(2,1)S(1)}, u32[]{:S(2)}, u32[]{:S(2)}) %collective-permute-start.21) | collective-permute-done | bytes 671776 | tf_op jit(solution)/shard_map/up_from_z_z1/ppermute | solution.py:788
  65.3 1.5 %collective-permute-start.25 = (bf16[336,512]{1,0:T(8,128)(2,1)S(1)}, bf16[336,512]{1,0:T(8,128)(2,1)S(1)}, u32[]{:S(2)}, u32[]{:S(2)}) collective-permute-start(bf16[336,512]{1,0:T(8,128)(2,1)S(1)} %get-tuple-element.138), channel_id=1, source_target_pairs={{0,4},{4,0},{1,5},{5,1},{2,6},{6,2},{3,7},{7,3},{8,12},{12,8},{9,1... | collective-permute-start | bytes 1032200 | tf_op jit(solution)/shard_map/up_from_x_x1/ppermute | solution.py:788
  66.9 0.6 collective-permute-start.22
  67.5 4.4 %collective-permute-done.22.refs_1_ = bf16[128,512]{1,0:T(8,128)(2,1)S(1)} collective-permute-done((bf16[128,512]{1,0:T(8,128)(2,1)S(1)}, bf16[128,512]{1,0:T(8,128)(2,1)S(1)}, u32[]{:S(2)}, u32[]{:S(2)}) %collective-permute-start.22) | collective-permute-done | bytes 131104 | tf_op jit(solution)/shard_map/down_from_z_z1/ppermute | solution.py:788
  72.0 2.7 %collective-permute-start.24 = (bf16[128,512]{1,0:T(8,128)(2,1)S(1)}, bf16[128,512]{1,0:T(8,128)(2,1)S(1)}, u32[]{:S(2)}, u32[]{:S(2)}) collective-permute-start(bf16[128,512]{1,0:T(8,128)(2,1)S(1)} %down_z.1.refs_4_.refs_0_), channel_id=1, source_target_pairs={{0,16},{8,24},{16,0},{24,8},{1,17},{9,25},{17,1},{25,9},{2,18},{10... | collective-permute-start | bytes 393224 | tf_op jit(solution)/shard_map/down_far_z2/ppermute | solution.py:788
  74.9 2.0 %collective-permute-start.23 = (bf16[256,512]{1,0:T(8,128)(2,1)S(1)}, bf16[256,512]{1,0:T(8,128)(2,1)S(1)}, u32[]{:S(2)}, u32[]{:S(2)}) collective-permute-start(bf16[256,512]{1,0:T(8,128)(2,1)S(1)} %get-tuple-element.137), channel_id=1, source_target_pairs={{0,4},{4,0},{1,5},{5,1},{2,6},{6,2},{3,7},{7,3},{8,12},{12,8},{9,1... | collective-permute-start | bytes 786440 | tf_op jit(solution)/shard_map/att_from_x_x1/ppermute | solution.py:788
  77.1 1.6 %collective-permute-start.28 = (bf16[176,512]{1,0:T(8,128)(2,1)S(1)}, bf16[176,512]{1,0:T(8,128)(2,1)S(1)}, u32[]{:S(2)}, u32[]{:S(2)}) collective-permute-start(bf16[176,512]{1,0:T(8,128)(2,1)S(1)} %get-tuple-element.142), channel_id=1, source_target_pairs={{0,1},{1,0},{2,3},{3,2},{4,5},{5,4},{6,7},{7,6},{8,9},{9,8},{10,11... | collective-permute-start | bytes 540680 | tf_op jit(solution)/shard_map/up_from_y_mp1/ppermute | solution.py:788
  78.6 0.9 collective-permute-done.24.refs_1_
  79.7 1.9 %collective-permute-done.23.refs_1_ = bf16[256,512]{1,0:T(8,128)(2,1)S(1)} collective-permute-done((bf16[256,512]{1,0:T(8,128)(2,1)S(1)}, bf16[256,512]{1,0:T(8,128)(2,1)S(1)}, u32[]{:S(2)}, u32[]{:S(2)}) %collective-permute-start.23) | collective-permute-done | bytes 262176 | tf_op jit(solution)/shard_map/att_from_x_x1/ppermute | solution.py:788
  82.7 1.7 %collective-permute-start.30 = (bf16[176,512]{1,0:T(8,128)(2,1)S(1)}, bf16[176,512]{1,0:T(8,128)(2,1)S(1)}, u32[]{:S(2)}, u32[]{:S(2)}) collective-permute-start(bf16[176,512]{1,0:T(8,128)(2,1)S(1)} %up_mp.1.refs_2_.refs_0_), channel_id=1, source_target_pairs={{0,16},{8,24},{16,0},{24,8},{1,17},{9,25},{17,1},{25,9},{2,18},{10... | collective-permute-start | bytes 540680 | tf_op jit(solution)/shard_map/up_far_z2/ppermute | solution.py:788
  84.4 3.0 %collective-permute-done.27.refs_1_ = bf16[128,512]{1,0:T(8,128)(2,1)S(1)} collective-permute-done((bf16[128,512]{1,0:T(8,128)(2,1)S(1)}, bf16[128,512]{1,0:T(8,128)(2,1)S(1)}, u32[]{:S(2)}, u32[]{:S(2)}) %collective-permute-start.27) | collective-permute-done | bytes 131104 | tf_op jit(solution)/shard_map/down_near_z1/ppermute | solution.py:788
  87.4 2.5 %collective-permute-done.26.refs_1_ = bf16[128,512]{1,0:T(8,128)(2,1)S(1)} collective-permute-done((bf16[128,512]{1,0:T(8,128)(2,1)S(1)}, bf16[128,512]{1,0:T(8,128)(2,1)S(1)}, u32[]{:S(2)}, u32[]{:S(2)}) %collective-permute-start.26) | collective-permute-done | bytes 131104 | tf_op jit(solution)/shard_map/att_from_z_z1/ppermute | solution.py:788
  90.0 2.9 %collective-permute-start.37 = (bf16[256,512]{1,0:T(8,128)(2,1)S(1)}, bf16[256,512]{1,0:T(8,128)(2,1)S(1)}, u32[]{:S(2)}, u32[]{:S(2)}) collective-permute-start(bf16[256,512]{1,0:T(8,128)(2,1)S(1)} %down_join.1.refs_2_.refs_0_), channel_id=1, source_target_pairs={{0,4},{4,0},{1,5},{5,1},{2,6},{6,2},{3,7},{7,3},{8,12},{12,8},{9,1... | collective-permute-start | bytes 786440 | tf_op jit(solution)/shard_map/down_x_x1/ppermute | solution.py:788
  93.6 3.4 %collective-permute-start.34 = (bf16[160,512]{1,0:T(8,128)(2,1)S(1)}, bf16[160,512]{1,0:T(8,128)(2,1)S(1)}, u32[]{:S(2)}, u32[]{:S(2)}) collective-permute-start(bf16[160,512]{1,0:T(8,128)(2,1)S(1)} %get-tuple-element.146.refs_0_), channel_id=1, source_target_pairs={{0,4},{4,0},{1,5},{5,1},{2,6},{6,2},{3,7},{7,3},{8,12},{12,8},{9,1... | collective-permute-start | bytes 491528 | tf_op jit(solution)/shard_map/up_near_x1/ppermute | solution.py:788
  97.2 5.0 %collective-permute-done.31.refs_1_ = bf16[128,512]{1,0:T(8,128)(2,1)S(1)} collective-permute-done((bf16[128,512]{1,0:T(8,128)(2,1)S(1)}, bf16[128,512]{1,0:T(8,128)(2,1)S(1)}, u32[]{:S(2)}, u32[]{:S(2)}) %collective-permute-start.31) | collective-permute-done | bytes 131104 | tf_op jit(solution)/shard_map/att_near_z1/ppermute | solution.py:788
  102.9 1.7 %collective-permute-start.32 = (bf16[256,512]{1,0:T(8,128)(2,1)S(1)}, bf16[256,512]{1,0:T(8,128)(2,1)S(1)}, u32[]{:S(2)}, u32[]{:S(2)}) collective-permute-start(bf16[256,512]{1,0:T(8,128)(2,1)S(1)} %get-tuple-element.144.refs_0_), channel_id=1, source_target_pairs={{0,4},{4,0},{1,5},{5,1},{2,6},{6,2},{3,7},{7,3},{8,12},{12,8},{9,1... | collective-permute-start | bytes 786440 | tf_op jit(solution)/shard_map/att_x_x1/ppermute | solution.py:788
  104.6 1.5 %collective-permute-start.36 = (bf16[64,512]{1,0:T(8,128)(2,1)S(1)}, bf16[64,512]{1,0:T(8,128)(2,1)S(1)}, u32[]{:S(2)}, u32[]{:S(2)}) collective-permute-start(bf16[64,512]{1,0:T(8,128)(2,1)S(1)} %get-tuple-element.145.refs_2_), channel_id=1, source_target_pairs={{0,1},{1,0},{2,3},{3,2},{4,5},{5,4},{6,7},{7,6},{8,9},{9,8},{10,11... | collective-permute-start | bytes 196616 | tf_op jit(solution)/shard_map/table_y_mp1/ppermute | solution.py:788
  106.5 0.6 small_out.1
  107.2 1.5 %down_out.1 = (f32[1024,512]{1,0:T(8,128)}, f32[8,128]{1,0:T(8,128)S(1)}) custom-call(bf16[256,512]{1,0:T(8,128)(2,1)S(1)} %down_join.1.refs_2_.refs_0_, bf16[256,512]{1,0:T(8,128)(2,1)S(1)} %gate.17.refs_1_, bf16[256,512]{1,0:T(8,128)(2,1)S(1)} %collective-permute-done.38.refs_2_, bf16[256,512]{1,0:T(8,128)(2,1)S(1)} %collective-permute-done.39.refs_3_, ...), custom_call_target="tpu_custom_call" | custom-call | tf_op jit(solution)/shard_map/down_out/pallas_call | solution.py:39
  109.2 1.0 collective-permute-done.35.refs_0_
  110.2 3.4 %collective-permute-done.33.refs_0_ = bf16[64,512]{1,0:T(8,128)(2,1)S(1)} collective-permute-done((bf16[64,512]{1,0:T(8,128)(2,1)S(1)}, bf16[64,512]{1,0:T(8,128)(2,1)S(1)}, u32[]{:S(2)}, u32[]{:S(2)}) %collective-permute-start.33) | collective-permute-done | bytes 65568 | tf_op jit(solution)/shard_map/table_x/ppermute | solution.py:793
  114.2 1.7 %up_out.1 = (f32[512,1024]{1,0:T(8,128)}, f32[256,512]{1,0:T(8,128)}, f32[8,128]{1,0:T(8,128)S(1)}) custom-call(bf16[320,512]{1,0:T(8,128)(2,1)S(1)} %up_join.1.refs_1_.refs_0_, bf16[320,512]{1,0:T(8,128)(2,1)S(1)} %gate.19.refs_1_, bf16[320,512]{1,0:T(8,128)(2,1)S(1)} %collective-permute-done.44.refs_2_, ...), custom_call_target="tpu_custom_call" | custom-call | tf_op jit(solution)/shard_map/up_out/pallas_call | solution.py:39
  116.0 1.7 %attend_out.1 = (f32[3,512,256]{2,1,0:T(8,128)}, f32[512,512]{1,0:T(8,128)}) custom-call(bf16[256,512]{1,0:T(8,128)(2,1)S(1)} %get-tuple-element.144.refs_0_, bf16[256,512]{1,0:T(8,128)(2,1)S(1)} %gate.21.refs_4_.refs_1_, bf16[256,512]{1,0:T(8,128)(2,1)S(1)} %collective-permute-done.40.refs_2_, bf16[256,512]{1,0:T(8,128)(2,1)S(1)} %collective-permute-done.41.refs_3_, ...), custom_call_target="tpu_custom_call" | custom-call | tf_op jit(solution)/shard_map/attend_out/pallas_call | solution.py:39
  (117 shorter events, 9.4 us)
Async XLA Ops:
  3.0 7.6 %copy-start.2 = (bf16[512,3,256]{2,0,1:T(8,128)(2,1)S(1)}, bf16[512,3,256]{2,0,1:T(8,128)(2,1)}, u32[]{:S(2)}) copy-start(bf16[512,3,256]{2,0,1:T(8,128)(2,1)} %param.17) | copy-start | bytes 2359300
  3.0 7.6 %copy-start.4 = (bf16[512,512]{1,0:T(8,128)(2,1)S(1)}, bf16[512,512]{1,0:T(8,128)(2,1)}, u32[]{:S(2)}) copy-start(bf16[512,512]{1,0:T(8,128)(2,1)} %refs_1_.9) | copy-start | bytes 1572868
  3.1 10.8 %collective-permute-start = (bf16[272,512]{1,0:T(8,128)(2,1)}, bf16[272,512]{1,0:T(8,128)(2,1)S(1)}, u32[]{:S(2)}, u32[]{:S(2)}) collective-permute-start(bf16[272,512]{1,0:T(8,128)(2,1)} %pack_attend.1.refs_2_), channel_id=1, source_target_pairs={{0,1},{1,0},{2,3},{3,2},{4,5},{5,4},{6,7},{7,6},{8,9},{9,8},{10,11... | collective-permute-start | bytes 835592 | tf_op jit(solution)/shard_map/attend_y_mp1/ppermute | solution.py:788
  7.9 8.7 %collective-permute-start.3 = (bf16[128,512]{1,0:T(8,128)(2,1)}, bf16[128,512]{1,0:T(8,128)(2,1)S(1)}, u32[]{:S(2)}, u32[]{:S(2)}) collective-permute-start(bf16[128,512]{1,0:T(8,128)(2,1)} %get-tuple-element.88.refs_4_), channel_id=1, source_target_pairs={{0,1},{1,0},{2,3},{3,2},{4,5},{5,4},{6,7},{7,6},{8,9},{9,8},{10,11... | collective-permute-start | bytes 393224 | tf_op jit(solution)/shard_map/up_y_mp1/ppermute | solution.py:788
  8.1 13.6 %collective-permute-start.2 = (bf16[256,512]{1,0:T(8,128)(2,1)}, bf16[256,512]{1,0:T(8,128)(2,1)S(1)}, u32[]{:S(2)}, u32[]{:S(2)}) collective-permute-start(bf16[256,512]{1,0:T(8,128)(2,1)} %get-tuple-element.90), channel_id=1, source_target_pairs={{0,1},{1,0},{2,3},{3,2},{4,5},{5,4},{6,7},{7,6},{8,9},{9,8},{10,11... | collective-permute-start | bytes 786440 | tf_op jit(solution)/shard_map/down_y_mp1/ppermute | solution.py:788
  13.9 7.8 %collective-permute-start.1 = (bf16[272,512]{1,0:T(8,128)(2,1)S(1)}, bf16[272,512]{1,0:T(8,128)(2,1)S(1)}, u32[]{:S(2)}, u32[]{:S(2)}) collective-permute-start(bf16[272,512]{1,0:T(8,128)(2,1)S(1)} %gate.11.refs_1_.refs_3_), channel_id=1, source_target_pairs={{0,4},{4,0},{1,5},{5,1},{2,6},{6,2},{3,7},{7,3},{8,12},{12,8},{9,1... | collective-permute-start | bytes 835592 | tf_op jit(solution)/shard_map/attend_x_x1/ppermute | solution.py:788
  16.6 5.1 %collective-permute-start.4 = (bf16[128,512]{1,0:T(8,128)(2,1)S(1)}, bf16[128,512]{1,0:T(8,128)(2,1)S(1)}, u32[]{:S(2)}, u32[]{:S(2)}) collective-permute-start(bf16[128,512]{1,0:T(8,128)(2,1)S(1)} %gate.12.refs_0_.refs_2_), channel_id=1, source_target_pairs={{0,8},{8,0},{16,24},{24,16},{1,9},{9,1},{17,25},{25,17},{2,10},{10... | collective-permute-start | bytes 393224 | tf_op jit(solution)/shard_map/up_z_z1/ppermute | solution.py:788
  18.7 5.7 %collective-permute-start.5 = (bf16[272,512]{1,0:T(8,128)(2,1)S(1)}, bf16[272,512]{1,0:T(8,128)(2,1)S(1)}, u32[]{:S(2)}, u32[]{:S(2)}) collective-permute-start(bf16[272,512]{1,0:T(8,128)(2,1)S(1)} %gate.11.refs_1_.refs_3_), channel_id=1, source_target_pairs={{0,2},{2,0},{1,3},{3,1},{4,6},{6,4},{5,7},{7,5},{8,10},{10,8},{9,1... | collective-permute-start | bytes 835592 | tf_op jit(solution)/shard_map/attend_cy_core1/ppermute | solution.py:788
  21.8 4.1 %collective-permute-start.6 = (bf16[272,512]{1,0:T(8,128)(2,1)S(1)}, bf16[272,512]{1,0:T(8,128)(2,1)S(1)}, u32[]{:S(2)}, u32[]{:S(2)}) collective-permute-start(bf16[272,512]{1,0:T(8,128)(2,1)S(1)} %gate.14.refs_4_.refs_10_), channel_id=1, source_target_pairs={{0,2},{2,0},{1,3},{3,1},{4,6},{6,4},{5,7},{7,5},{8,10},{10,8},{9,1... | collective-permute-start | bytes 835592 | tf_op jit(solution)/shard_map/attend_cx_core1/ppermute | solution.py:788
  21.9 11.9 %collective-permute-start.11 = (bf16[256,512]{1,0:T(8,128)(2,1)S(1)}, bf16[256,512]{1,0:T(8,128)(2,1)S(1)}, u32[]{:S(2)}, u32[]{:S(2)}) collective-permute-start(bf16[256,512]{1,0:T(8,128)(2,1)S(1)} %gate.13.refs_1_.refs_8_), channel_id=1, source_target_pairs={{0,2},{2,0},{1,3},{3,1},{4,6},{6,4},{5,7},{7,5},{8,10},{10,8},{9,1... | collective-permute-start | bytes 786440 | tf_op jit(solution)/shard_map/down_cy_core1/ppermute | solution.py:788
  22.4 10.8 %collective-permute-start.10 = (bf16[256,512]{1,0:T(8,128)(2,1)S(1)}, bf16[256,512]{1,0:T(8,128)(2,1)S(1)}, u32[]{:S(2)}, u32[]{:S(2)}) collective-permute-start(bf16[256,512]{1,0:T(8,128)(2,1)S(1)} %gate.13.refs_1_.refs_8_), channel_id=1, source_target_pairs={{0,8},{8,0},{16,24},{24,16},{1,9},{9,1},{17,25},{25,17},{2,10},{10... | collective-permute-start | bytes 786440 | tf_op jit(solution)/shard_map/down_z_z1/ppermute | solution.py:788
  24.4 9.3 %collective-permute-start.8 = (bf16[256,512]{1,0:T(8,128)(2,1)S(1)}, bf16[256,512]{1,0:T(8,128)(2,1)S(1)}, u32[]{:S(2)}, u32[]{:S(2)}) collective-permute-start(bf16[256,512]{1,0:T(8,128)(2,1)S(1)} %up_pair.1.refs_1_.refs_4_), channel_id=1, source_target_pairs={{0,2},{2,0},{1,3},{3,1},{4,6},{6,4},{5,7},{7,5},{8,10},{10,8},{9,1... | collective-permute-start | bytes 786440 | tf_op jit(solution)/shard_map/up_cy_core1/ppermute | solution.py:788
  24.4 8.7 %collective-permute-start.7 = (bf16[256,512]{1,0:T(8,128)(2,1)S(1)}, bf16[256,512]{1,0:T(8,128)(2,1)S(1)}, u32[]{:S(2)}, u32[]{:S(2)}) collective-permute-start(bf16[256,512]{1,0:T(8,128)(2,1)S(1)} %up_pair.1.refs_1_.refs_4_), channel_id=1, source_target_pairs={{0,4},{4,0},{1,5},{5,1},{2,6},{6,2},{3,7},{7,3},{8,12},{12,8},{9,1... | collective-permute-start | bytes 786440 | tf_op jit(solution)/shard_map/up_x_x1/ppermute | solution.py:788
  33.2 1.6 %collective-permute-start.12 = (bf16[256,512]{1,0:T(8,128)(2,1)S(1)}, bf16[256,512]{1,0:T(8,128)(2,1)S(1)}, u32[]{:S(2)}, u32[]{:S(2)}) collective-permute-start(bf16[256,512]{1,0:T(8,128)(2,1)S(1)} %gate.16.refs_9_.refs_16_), channel_id=1, source_target_pairs={{0,2},{2,0},{1,3},{3,1},{4,6},{6,4},{5,7},{7,5},{8,10},{10,8},{9,1... | collective-permute-start | bytes 786440 | tf_op jit(solution)/shard_map/down_cz_core1/ppermute | solution.py:788
  33.3 1.9 %collective-permute-start.9 = (bf16[256,512]{1,0:T(8,128)(2,1)S(1)}, bf16[256,512]{1,0:T(8,128)(2,1)S(1)}, u32[]{:S(2)}, u32[]{:S(2)}) collective-permute-start(bf16[256,512]{1,0:T(8,128)(2,1)S(1)} %gate.15.refs_1_.refs_5_), channel_id=1, source_target_pairs={{0,2},{2,0},{1,3},{3,1},{4,6},{6,4},{5,7},{7,5},{8,10},{10,8},{9,1... | collective-permute-start | bytes 786440 | tf_op jit(solution)/shard_map/up_cx_core1/ppermute | solution.py:788
  39.1 5.6 %collective-permute-start.14 = (bf16[1024,512]{1,0:T(8,128)(2,1)S(1)}, bf16[1024,512]{1,0:T(8,128)(2,1)S(1)}, u32[]{:S(2)}, u32[]{:S(2)}) collective-permute-start(bf16[1024,512]{1,0:T(8,128)(2,1)S(1)} %get-tuple-element.116), channel_id=1, source_target_pairs={{0,2},{2,0},{1,3},{3,1},{4,6},{6,4},{5,7},{7,5},{8,10},{10,8},{9,1... | collective-permute-start | bytes 3145736 | tf_op jit(solution)/shard_map/down_recv_core1/ppermute | solution.py:788
  44.3 3.1 %collective-permute-start.13 = (bf16[1296,512]{1,0:T(8,128)(2,1)S(1)}, bf16[1296,512]{1,0:T(8,128)(2,1)S(1)}, u32[]{:S(2)}, u32[]{:S(2)}) collective-permute-start(bf16[1296,512]{1,0:T(8,128)(2,1)S(1)} %get-tuple-element.114), channel_id=1, source_target_pairs={{0,2},{2,0},{1,3},{3,1},{4,6},{6,4},{5,7},{7,5},{8,10},{10,8},{9,1... | collective-permute-start | bytes 3981320 | tf_op jit(solution)/shard_map/up_recv_core1/ppermute | solution.py:788
  44.9 14.0 %collective-permute-start.18 = (bf16[512,512]{1,0:T(8,128)(2,1)S(1)}, bf16[512,512]{1,0:T(8,128)(2,1)S(1)}, u32[]{:S(2)}, u32[]{:S(2)}) collective-permute-start(bf16[512,512]{1,0:T(8,128)(2,1)S(1)} %down_core.1.refs_2_), channel_id=1, source_target_pairs={{0,1},{1,0},{2,3},{3,2},{4,5},{5,4},{6,7},{7,6},{8,9},{9,8},{10,11... | collective-permute-start | bytes 1572872 | tf_op jit(solution)/shard_map/down_from_y_mp1/ppermute | solution.py:788
  47.7 17.4 %collective-permute-start.21 = (bf16[656,512]{1,0:T(8,128)(2,1)S(1)}, bf16[656,512]{1,0:T(8,128)(2,1)S(1)}, u32[]{:S(2)}, u32[]{:S(2)}) collective-permute-start(bf16[656,512]{1,0:T(8,128)(2,1)S(1)} %get-tuple-element.132), channel_id=1, source_target_pairs={{0,8},{8,0},{16,24},{24,16},{1,9},{9,1},{17,25},{25,17},{2,10},{10... | collective-permute-start | bytes 2015240 | tf_op jit(solution)/shard_map/up_from_z_z1/ppermute | solution.py:788
  55.3 5.4 %collective-permute-start.16 = (bf16[384,512]{1,0:T(8,128)(2,1)S(1)}, bf16[384,512]{1,0:T(8,128)(2,1)S(1)}, u32[]{:S(2)}, u32[]{:S(2)}) collective-permute-start(bf16[384,512]{1,0:T(8,128)(2,1)S(1)} %get-tuple-element.126), channel_id=1, source_target_pairs={{0,2},{2,0},{1,3},{3,1},{4,6},{6,4},{5,7},{7,5},{8,10},{10,8},{9,1... | collective-permute-start | bytes 1179656 | tf_op jit(solution)/shard_map/oth_recv_core1/ppermute | solution.py:788
  55.5 5.2 %collective-permute-start.17 = (bf16[256,512]{1,0:T(8,128)(2,1)S(1)}, bf16[256,512]{1,0:T(8,128)(2,1)S(1)}, u32[]{:S(2)}, u32[]{:S(2)}) collective-permute-start(bf16[256,512]{1,0:T(8,128)(2,1)S(1)} %get-tuple-element.127), channel_id=1, source_target_pairs={{0,2},{2,0},{1,3},{3,1},{4,6},{6,4},{5,7},{7,5},{8,10},{10,8},{9,1... | collective-permute-start | bytes 786440 | tf_op jit(solution)/shard_map/tab_recv_core1/ppermute | solution.py:788
  56.5 18.2 %collective-permute-start.15 = (bf16[384,512]{1,0:T(8,128)(2,1)S(1)}, bf16[384,512]{1,0:T(8,128)(2,1)S(1)}, u32[]{:S(2)}, u32[]{:S(2)}) collective-permute-start(bf16[384,512]{1,0:T(8,128)(2,1)S(1)} %get-tuple-element.124), channel_id=1, source_target_pairs={{0,2},{2,0},{1,3},{3,1},{4,6},{6,4},{5,7},{7,5},{8,10},{10,8},{9,1... | collective-permute-start | bytes 1179656 | tf_op jit(solution)/shard_map/own_recv_core1/ppermute | solution.py:788
  59.1 7.8 %collective-permute-start.20 = (bf16[256,512]{1,0:T(8,128)(2,1)S(1)}, bf16[256,512]{1,0:T(8,128)(2,1)S(1)}, u32[]{:S(2)}, u32[]{:S(2)}) collective-permute-start(bf16[256,512]{1,0:T(8,128)(2,1)S(1)} %get-tuple-element.131), channel_id=1, source_target_pairs={{0,4},{4,0},{1,5},{5,1},{2,6},{6,2},{3,7},{7,3},{8,12},{12,8},{9,1... | collective-permute-start | bytes 786440 | tf_op jit(solution)/shard_map/down_from_x_x1/ppermute | solution.py:788
  60.8 13.9 %collective-permute-start.19 = (bf16[512,512]{1,0:T(8,128)(2,1)S(1)}, bf16[512,512]{1,0:T(8,128)(2,1)S(1)}, u32[]{:S(2)}, u32[]{:S(2)}) collective-permute-start(bf16[512,512]{1,0:T(8,128)(2,1)S(1)} %get-tuple-element.129), channel_id=1, source_target_pairs={{0,1},{1,0},{2,3},{3,2},{4,5},{5,4},{6,7},{7,6},{8,9},{9,8},{10,11... | collective-permute-start | bytes 1572872 | tf_op jit(solution)/shard_map/att_from_y_mp1/ppermute | solution.py:788
  65.3 11.6 %collective-permute-start.25 = (bf16[336,512]{1,0:T(8,128)(2,1)S(1)}, bf16[336,512]{1,0:T(8,128)(2,1)S(1)}, u32[]{:S(2)}, u32[]{:S(2)}) collective-permute-start(bf16[336,512]{1,0:T(8,128)(2,1)S(1)} %get-tuple-element.138), channel_id=1, source_target_pairs={{0,4},{4,0},{1,5},{5,1},{2,6},{6,2},{3,7},{7,3},{8,12},{12,8},{9,1... | collective-permute-start | bytes 1032200 | tf_op jit(solution)/shard_map/up_from_x_x1/ppermute | solution.py:788
  66.9 5.0 %collective-permute-start.22 = (bf16[128,512]{1,0:T(8,128)(2,1)S(1)}, bf16[128,512]{1,0:T(8,128)(2,1)S(1)}, u32[]{:S(2)}, u32[]{:S(2)}) collective-permute-start(bf16[128,512]{1,0:T(8,128)(2,1)S(1)} %get-tuple-element.135), channel_id=1, source_target_pairs={{0,8},{8,0},{16,24},{24,16},{1,9},{9,1},{17,25},{25,17},{2,10},{10... | collective-permute-start | bytes 393224 | tf_op jit(solution)/shard_map/down_from_z_z1/ppermute | solution.py:788
  72.0 7.6 %collective-permute-start.24 = (bf16[128,512]{1,0:T(8,128)(2,1)S(1)}, bf16[128,512]{1,0:T(8,128)(2,1)S(1)}, u32[]{:S(2)}, u32[]{:S(2)}) collective-permute-start(bf16[128,512]{1,0:T(8,128)(2,1)S(1)} %down_z.1.refs_4_.refs_0_), channel_id=1, source_target_pairs={{0,16},{8,24},{16,0},{24,8},{1,17},{9,25},{17,1},{25,9},{2,18},{10... | collective-permute-start | bytes 393224 | tf_op jit(solution)/shard_map/down_far_z2/ppermute | solution.py:788
  74.9 6.7 %collective-permute-start.23 = (bf16[256,512]{1,0:T(8,128)(2,1)S(1)}, bf16[256,512]{1,0:T(8,128)(2,1)S(1)}, u32[]{:S(2)}, u32[]{:S(2)}) collective-permute-start(bf16[256,512]{1,0:T(8,128)(2,1)S(1)} %get-tuple-element.137), channel_id=1, source_target_pairs={{0,4},{4,0},{1,5},{5,1},{2,6},{6,2},{3,7},{7,3},{8,12},{12,8},{9,1... | collective-permute-start | bytes 786440 | tf_op jit(solution)/shard_map/att_from_x_x1/ppermute | solution.py:788
  77.1 5.6 %collective-permute-start.28 = (bf16[176,512]{1,0:T(8,128)(2,1)S(1)}, bf16[176,512]{1,0:T(8,128)(2,1)S(1)}, u32[]{:S(2)}, u32[]{:S(2)}) collective-permute-start(bf16[176,512]{1,0:T(8,128)(2,1)S(1)} %get-tuple-element.142), channel_id=1, source_target_pairs={{0,1},{1,0},{2,3},{3,2},{4,5},{5,4},{6,7},{7,6},{8,9},{9,8},{10,11... | collective-permute-start | bytes 540680 | tf_op jit(solution)/shard_map/up_from_y_mp1/ppermute | solution.py:788
  79.6 7.7 %collective-permute-start.27 = (bf16[128,512]{1,0:T(8,128)(2,1)S(1)}, bf16[128,512]{1,0:T(8,128)(2,1)S(1)}, u32[]{:S(2)}, u32[]{:S(2)}) collective-permute-start(bf16[128,512]{1,0:T(8,128)(2,1)S(1)} %down_far.1.refs_2_.refs_0_), channel_id=1, source_target_pairs={{0,8},{8,0},{16,24},{24,16},{1,9},{9,1},{17,25},{25,17},{2,10},{10... | collective-permute-start | bytes 393224 | tf_op jit(solution)/shard_map/down_near_z1/ppermute | solution.py:788
  81.7 8.3 %collective-permute-start.26 = (bf16[128,512]{1,0:T(8,128)(2,1)S(1)}, bf16[128,512]{1,0:T(8,128)(2,1)S(1)}, u32[]{:S(2)}, u32[]{:S(2)}) collective-permute-start(bf16[128,512]{1,0:T(8,128)(2,1)S(1)} %get-tuple-element.141), channel_id=1, source_target_pairs={{0,8},{8,0},{16,24},{24,16},{1,9},{9,1},{17,25},{25,17},{2,10},{10... | collective-permute-start | bytes 393224 | tf_op jit(solution)/shard_map/att_from_z_z1/ppermute | solution.py:788
  82.7 10.8 %collective-permute-start.30 = (bf16[176,512]{1,0:T(8,128)(2,1)S(1)}, bf16[176,512]{1,0:T(8,128)(2,1)S(1)}, u32[]{:S(2)}, u32[]{:S(2)}) collective-permute-start(bf16[176,512]{1,0:T(8,128)(2,1)S(1)} %up_mp.1.refs_2_.refs_0_), channel_id=1, source_target_pairs={{0,16},{8,24},{16,0},{24,8},{1,17},{9,25},{17,1},{25,9},{2,18},{10... | collective-permute-start | bytes 540680 | tf_op jit(solution)/shard_map/up_far_z2/ppermute | solution.py:788
  90.0 7.1 %collective-permute-start.29 = (bf16[128,512]{1,0:T(8,128)(2,1)S(1)}, bf16[128,512]{1,0:T(8,128)(2,1)S(1)}, u32[]{:S(2)}, u32[]{:S(2)}) collective-permute-start(bf16[128,512]{1,0:T(8,128)(2,1)S(1)} %attend_z.1.refs_2_.refs_0_), channel_id=1, source_target_pairs={{0,16},{8,24},{16,0},{24,8},{1,17},{9,25},{17,1},{25,9},{2,18},{10... | collective-permute-start | bytes 393224 | tf_op jit(solution)/shard_map/att_far_z2/ppermute | solution.py:788
  90.0 12.4 %collective-permute-start.37 = (bf16[256,512]{1,0:T(8,128)(2,1)S(1)}, bf16[256,512]{1,0:T(8,128)(2,1)S(1)}, u32[]{:S(2)}, u32[]{:S(2)}) collective-permute-start(bf16[256,512]{1,0:T(8,128)(2,1)S(1)} %down_join.1.refs_2_.refs_0_), channel_id=1, source_target_pairs={{0,4},{4,0},{1,5},{5,1},{2,6},{6,2},{3,7},{7,3},{8,12},{12,8},{9,1... | collective-permute-start | bytes 786440 | tf_op jit(solution)/shard_map/down_x_x1/ppermute | solution.py:788
  93.6 8.6 %collective-permute-start.34 = (bf16[160,512]{1,0:T(8,128)(2,1)S(1)}, bf16[160,512]{1,0:T(8,128)(2,1)S(1)}, u32[]{:S(2)}, u32[]{:S(2)}) collective-permute-start(bf16[160,512]{1,0:T(8,128)(2,1)S(1)} %get-tuple-element.146.refs_0_), channel_id=1, source_target_pairs={{0,4},{4,0},{1,5},{5,1},{2,6},{6,2},{3,7},{7,3},{8,12},{12,8},{9,1... | collective-permute-start | bytes 491528 | tf_op jit(solution)/shard_map/up_near_x1/ppermute | solution.py:788
  97.1 5.0 %collective-permute-start.31 = (bf16[128,512]{1,0:T(8,128)(2,1)S(1)}, bf16[128,512]{1,0:T(8,128)(2,1)S(1)}, u32[]{:S(2)}, u32[]{:S(2)}) collective-permute-start(bf16[128,512]{1,0:T(8,128)(2,1)S(1)} %attend_far.1.refs_0_.refs_2_), channel_id=1, source_target_pairs={{0,8},{8,0},{16,24},{24,16},{1,9},{9,1},{17,25},{25,17},{2,10},{10... | collective-permute-start | bytes 393224 | tf_op jit(solution)/shard_map/att_near_z1/ppermute | solution.py:788
  102.3 7.9 %collective-permute-start.35 = (bf16[320,512]{1,0:T(8,128)(2,1)S(1)}, bf16[320,512]{1,0:T(8,128)(2,1)S(1)}, u32[]{:S(2)}, u32[]{:S(2)}) collective-permute-start(bf16[320,512]{1,0:T(8,128)(2,1)S(1)} %up_join.1.refs_1_.refs_0_), channel_id=1, source_target_pairs={{0,8},{8,0},{16,24},{24,16},{1,9},{9,1},{17,25},{25,17},{2,10},{10... | collective-permute-start | bytes 983048 | tf_op jit(solution)/shard_map/up_last_z1/ppermute | solution.py:788
  102.4 3.7 %collective-permute-start.38 = (bf16[256,512]{1,0:T(8,128)(2,1)S(1)}, bf16[256,512]{1,0:T(8,128)(2,1)S(1)}, u32[]{:S(2)}, u32[]{:S(2)}) collective-permute-start(bf16[256,512]{1,0:T(8,128)(2,1)S(1)} %down_join.1.refs_2_.refs_0_), channel_id=1, source_target_pairs={{0,2},{2,0},{1,3},{3,1},{4,6},{6,4},{5,7},{7,5},{8,10},{10,8},{9,1... | collective-permute-start | bytes 786440 | tf_op jit(solution)/shard_map/down_core_core1/ppermute | solution.py:788
  102.4 4.7 %collective-permute-start.39 = (bf16[256,512]{1,0:T(8,128)(2,1)S(1)}, bf16[256,512]{1,0:T(8,128)(2,1)S(1)}, u32[]{:S(2)}, u32[]{:S(2)}) collective-permute-start(bf16[256,512]{1,0:T(8,128)(2,1)S(1)} %gate.17.refs_1_), channel_id=1, source_target_pairs={{0,2},{2,0},{1,3},{3,1},{4,6},{6,4},{5,7},{7,5},{8,10},{10,8},{9,1... | collective-permute-start | bytes 786440 | tf_op jit(solution)/shard_map/down_core_x_core1/ppermute | solution.py:788
  102.9 10.7 %collective-permute-start.32 = (bf16[256,512]{1,0:T(8,128)(2,1)S(1)}, bf16[256,512]{1,0:T(8,128)(2,1)S(1)}, u32[]{:S(2)}, u32[]{:S(2)}) collective-permute-start(bf16[256,512]{1,0:T(8,128)(2,1)S(1)} %get-tuple-element.144.refs_0_), channel_id=1, source_target_pairs={{0,4},{4,0},{1,5},{5,1},{2,6},{6,2},{3,7},{7,3},{8,12},{12,8},{9,1... | collective-permute-start | bytes 786440 | tf_op jit(solution)/shard_map/att_x_x1/ppermute | solution.py:788
  104.6 4.3 %collective-permute-start.36 = (bf16[64,512]{1,0:T(8,128)(2,1)S(1)}, bf16[64,512]{1,0:T(8,128)(2,1)S(1)}, u32[]{:S(2)}, u32[]{:S(2)}) collective-permute-start(bf16[64,512]{1,0:T(8,128)(2,1)S(1)} %get-tuple-element.145.refs_2_), channel_id=1, source_target_pairs={{0,1},{1,0},{2,3},{3,2},{4,5},{5,4},{6,7},{7,6},{8,9},{9,8},{10,11... | collective-permute-start | bytes 196616 | tf_op jit(solution)/shard_map/table_y_mp1/ppermute | solution.py:788
  106.1 7.5 %collective-permute-start.33 = (bf16[64,512]{1,0:T(8,128)(2,1)S(1)}, bf16[64,512]{1,0:T(8,128)(2,1)S(1)}, u32[]{:S(2)}, u32[]{:S(2)}) collective-permute-start(bf16[64,512]{1,0:T(8,128)(2,1)S(1)} %get-tuple-element.145.refs_2_), channel_id=1, source_target_pairs={{0,5},{1,4},{4,1},{5,0},{2,7},{3,6},{6,3},{7,2},{8,13},{9,12},{12,... | collective-permute-start | bytes 196616 | tf_op jit(solution)/shard_map/table_x/ppermute | solution.py:793
  107.1 8.8 %collective-permute-start.40 = (bf16[256,512]{1,0:T(8,128)(2,1)S(1)}, bf16[256,512]{1,0:T(8,128)(2,1)S(1)}, u32[]{:S(2)}, u32[]{:S(2)}) collective-permute-start(bf16[256,512]{1,0:T(8,128)(2,1)S(1)} %get-tuple-element.144.refs_0_), channel_id=1, source_target_pairs={{0,2},{2,0},{1,3},{3,1},{4,6},{6,4},{5,7},{7,5},{8,10},{10,8},{9,1... | collective-permute-start | bytes 786440 | tf_op jit(solution)/shard_map/att_core_core1/ppermute | solution.py:788
  108.8 5.3 %collective-permute-start.44 = (bf16[320,512]{1,0:T(8,128)(2,1)S(1)}, bf16[320,512]{1,0:T(8,128)(2,1)S(1)}, u32[]{:S(2)}, u32[]{:S(2)}) collective-permute-start(bf16[320,512]{1,0:T(8,128)(2,1)S(1)} %up_join.1.refs_1_.refs_0_), channel_id=1, source_target_pairs={{0,2},{2,0},{1,3},{3,1},{4,6},{6,4},{5,7},{7,5},{8,10},{10,8},{9,1... | collective-permute-start | bytes 983048 | tf_op jit(solution)/shard_map/up_core_core1/ppermute | solution.py:788
  110.2 4.0 %collective-permute-start.45 = (bf16[320,512]{1,0:T(8,128)(2,1)S(1)}, bf16[320,512]{1,0:T(8,128)(2,1)S(1)}, u32[]{:S(2)}, u32[]{:S(2)}) collective-permute-start(bf16[320,512]{1,0:T(8,128)(2,1)S(1)} %gate.19.refs_1_), channel_id=1, source_target_pairs={{0,2},{2,0},{1,3},{3,1},{4,6},{6,4},{5,7},{7,5},{8,10},{10,8},{9,1... | collective-permute-start | bytes 983048 | tf_op jit(solution)/shard_map/up_core_x_core1/ppermute | solution.py:788
  113.6 2.4 %collective-permute-start.41 = (bf16[256,512]{1,0:T(8,128)(2,1)S(1)}, bf16[256,512]{1,0:T(8,128)(2,1)S(1)}, u32[]{:S(2)}, u32[]{:S(2)}) collective-permute-start(bf16[256,512]{1,0:T(8,128)(2,1)S(1)} %gate.21.refs_4_.refs_1_), channel_id=1, source_target_pairs={{0,2},{2,0},{1,3},{3,1},{4,6},{6,4},{5,7},{7,5},{8,10},{10,8},{9,1... | collective-permute-start | bytes 786440 | tf_op jit(solution)/shard_map/att_core_x_core1/ppermute | solution.py:788
  113.6 2.3 %collective-permute-start.42 = (bf16[64,512]{1,0:T(8,128)(2,1)S(1)}, bf16[64,512]{1,0:T(8,128)(2,1)S(1)}, u32[]{:S(2)}, u32[]{:S(2)}) collective-permute-start(bf16[64,512]{1,0:T(8,128)(2,1)S(1)} %gate.18.refs_1_.refs_4_), channel_id=1, source_target_pairs={{0,2},{2,0},{1,3},{3,1},{4,6},{6,4},{5,7},{7,5},{8,10},{10,8},{9,1... | collective-permute-start | bytes 196616 | tf_op jit(solution)/shard_map/table_core_core1/ppermute | solution.py:788
  114.1 1.8 %collective-permute-start.43 = (bf16[64,512]{1,0:T(8,128)(2,1)S(1)}, bf16[64,512]{1,0:T(8,128)(2,1)S(1)}, u32[]{:S(2)}, u32[]{:S(2)}) collective-permute-start(bf16[64,512]{1,0:T(8,128)(2,1)S(1)} %gate.20.refs_1_.refs_5_), channel_id=1, source_target_pairs={{0,2},{2,0},{1,3},{3,1},{4,6},{6,4},{5,7},{7,5},{8,10},{10,8},{9,1... | collective-permute-start | bytes 196616 | tf_op jit(solution)/shard_map/table_core_x_core1/ppermute | solution.py:788
  (13 other events, 60.5 us)
